TPU v7x, 32 devices: a whole 2x2x4 slice. The times are simulated.
32 devices in a mesh: grp: 4 (over y, x), col: 8 (over z, core).
Axes of the slice: x: 2, y: 2, z: 4, core: 2. Of those that a mesh axis runs over, the one named last changes fastest.
Arguments:
- state_now: float32 [6, 512, 2048], P(None, 'col', 'grp'), may hold values from -6 to 6
- force_now: float32 [6, 512, 2048], P(None, 'col', 'grp'), may hold values from -6 to 6
- force_old: float32 [6, 512, 2048], P(None, 'col', 'grp'), may hold values from -6 to 6
- velocity: float32 [6, 512, 2048], P(None, 'col', 'grp'), may hold values from -0.125 to 0.125
- second_deriv: float32 [512, 512], replicated, may hold values from -0.25 to 0.25
- eig_basis: float32 [512, 512], replicated, may hold values from -0.25 to 0.25
- eig_inverse: float32 [512, 512], replicated, may hold values from -0.25 to 0.25
- eig_values: float32 [512], replicated, may hold values from 0.1 to 10
- kept_modes: int32 [2, 2048], P(None, 'grp'), may hold values from 0 to 2047
- col_owner: int32 [2048, 1], P('grp'), may hold values from 0 to 7; in each aligned block of 512 rows (0 to 511, 512 to 1023, ...) at most 128 rows name the same one
Outputs:
- state_next: float32 [6, 512, 2048], P(None, 'col', 'grp')
- owned_columns: float32 [6, 512, 4096], P(None, None, ('grp', 'col'))
- mean_emf: float32 [3, 512], P(None, 'col')
Inputs may be any that keep to these rules, and one draw needn't show every extreme that they name: `col_owner`: in each group of 512 consecutive columns no owner gets more than 128 columns, and some owner gets exactly 128.
All inputs are finite; a program needn't handle non-finite values.
Results may differ from a plain program's by a relative error of at most 0.000073.
Values sent between devices are 32-bit elements; how exact they have to be, the bound alone decides.
No kernel may reach another device: no remote copies, remote signals or barrier semaphores. Data moves between devices by JAX's collectives and lax.ppermute only.
A program may use at most 128 MiB of HBM per device.

v0:
```python
import jax
import jax.numpy as jnp
from jax import lax
from jax.sharding import PartitionSpec as P

KMAX = 2048
TESTS = 1


TIME_STEP = 2.0
RK_ALPHA = -3.0 / 40.0
RK_BETA = 5.0 / 24.0
RK_GAMMA = 5.0 / 12.0
RK_ZETA = -17.0 / 60.0
WAVE_SCALE = 8.0


def wave_squares(kept_modes):
    wave_x = kept_modes[0].astype(jnp.float32)
    wave_z = kept_modes[1].astype(jnp.float32)
    return (wave_x * wave_x + wave_z * wave_z) * (WAVE_SCALE / (KMAX * KMAX))


def advance(columns, forcing, wave, second_deriv, eig_basis, eig_inverse, eig_values):
    lap_term = (
        jnp.einsum("yz,czs->cys", second_deriv, columns, precision=lax.Precision.HIGHEST)
        - wave[None, None, :] * columns
    )
    rhs_term = columns + TIME_STEP * (RK_ALPHA * lap_term + forcing)
    project = jnp.einsum("yz,czs->cys", eig_inverse, rhs_term, precision=lax.Precision.HIGHEST)
    project = project / (1.0 + TIME_STEP * RK_BETA * (eig_values[:, None] + wave[None, :]))
    return jnp.einsum("yz,czs->cys", eig_basis, project, precision=lax.Precision.HIGHEST)


def emf_of(velocity, state, kept_modes):
    weight = jnp.where(kept_modes[0] > 0, 2.0, 1.0).astype(jnp.float32)
    speed = velocity.reshape(3, 2, velocity.shape[1], velocity.shape[2])
    parts = state.reshape(TESTS, 3, 2, state.shape[1], state.shape[2])
    pairs = jnp.einsum("jrym,fkrym,m->fjky", speed, parts, weight, precision=lax.Precision.HIGHEST)
    result = jnp.stack(
        [
            pairs[:, 1, 2] - pairs[:, 2, 1],
            pairs[:, 2, 0] - pairs[:, 0, 2],
            pairs[:, 0, 1] - pairs[:, 1, 0],
        ],
        axis=1,
    )
    return result.reshape(3 * TESTS, state.shape[1])


def on_device(
    state_now,
    force_now,
    force_old,
    velocity,
    second_deriv,
    eig_basis,
    eig_inverse,
    eig_values,
    kept_modes,
    col_owner,
):
    group_cols = state_now.shape[2]
    comps = state_now.shape[0]
    devices = lax.axis_size("col")
    position = lax.axis_index("col")
    capacity = 2 * group_cols // devices
    ksq = wave_squares(kept_modes)
    forcing = RK_GAMMA * force_now + RK_ZETA * force_old
    owners = col_owner[:, 0]
    onehot = (owners[:, None] == jnp.arange(devices, dtype=jnp.int32)[None, :]).astype(jnp.int32)
    ranks = jnp.sum(jnp.cumsum(onehot, axis=0) * onehot, axis=1) - 1
    slots = owners * capacity + ranks
    slot_column = (
        jnp.zeros((devices * capacity,), jnp.int32)
        .at[slots]
        .set(jnp.arange(group_cols, dtype=jnp.int32))
    )
    slot_used = jnp.zeros((devices * capacity,), jnp.int32).at[slots].set(1) > 0
    mine = lax.dynamic_slice_in_dim(slot_column, position * capacity, capacity)
    wave = ksq[mine]
    taken = jnp.take(jnp.concatenate([state_now, forcing], axis=0), slot_column, axis=2)
    stacked = jnp.where(slot_used[None, None, :], taken, jnp.zeros_like(taken))
    arrived = lax.all_to_all(stacked, "col", split_axis=2, concat_axis=1, tiled=True)
    solved = advance(
        arrived[:comps], arrived[comps:], wave, second_deriv, eig_basis, eig_inverse, eig_values
    )
    returned = lax.all_to_all(solved, "col", split_axis=1, concat_axis=2, tiled=True)
    state_next = jnp.take(returned, slots, axis=2)
    partial_emf = emf_of(velocity, state_next, kept_modes)
    mean_emf = lax.psum(partial_emf, "grp")
    return (state_next, solved, mean_emf)


def solution(mesh):
    return jax.shard_map(
        on_device,
        mesh=mesh,
        in_specs=(
            P(None, "col", "grp"),
            P(None, "col", "grp"),
            P(None, "col", "grp"),
            P(None, "col", "grp"),
            P(),
            P(),
            P(),
            P(),
            P(None, "grp"),
            P("grp", None),
        ),
        out_specs=(P(None, "col", "grp"), P(None, None, ("grp", "col")), P(None, "col")),
        check_vma=False,
    )
```

profile of v0, /device:TPU:0, one launch (start us, length us, event | category | flops | bytes accessed | tf_op | source)
XLA Modules:
  0.0 254.2 jit_solution(9855481268123576011)
XLA Ops:
  0.6 0.0 copy-start
  0.7 0.8 fusion.23
  1.5 1.1 reduce-window.6
  2.6 0.2 slice_reduce_fusion
  2.9 0.8 fusion.22
  3.6 0.7 and_reduce_fusion
  4.4 1.5 multiply_add_fusion
  5.9 0.1 pad_maximum_fusion
  6.1 3.7 %copy.58 = f32[12,64,512]{1,0,2:T(8,128)} copy(f32[12,64,512]{2,1,0:T(8,128)S(1)} %pad_maximum_fusion) | data formatting | bytes 3145728 | tf_op jit(solution)/shard_map/concatenate | solution.py:82
  9.8 2.4 scatter_custom_fusion.1
  12.2 2.4 scatter_custom_fusion
  14.7 11.9 %gather_fusion = f32[1024,12,64]{2,1,0:T(8,128)} fusion(f32[12,64,512]{1,0,2:T(8,128)} %copy.58, s32[1024]{0:T(1024)S(1)} %fusion.24), kind=kCustom, calls=%fused_computation | custom fusion | bytes 6295552 | tf_op jit(solution)/shard_map/jit(_take)/gather | solution.py:82
  26.6 7.5 %fusion.32 = f32[1024,12,64]{2,1,0:T(8,128)} fusion(f32[1024,12,64]{2,1,0:T(8,128)} %gather_fusion, pred[1024]{0:T(1024)(128)(4,1)S(1)} %get-tuple-element.27, pred[1024]{0:T(1024)(128)(4,1)S(1)} %get-tuple-element.28), kind=kLoop, calls=%fused_computation.65 | loop fusion | flops 1572864 | bytes 6293504
  34.1 9.1 %reshape.224 = f32[8,1,98304]{2,1,0:T(1,128)} reshape(f32[1024,12,64]{2,1,0:T(8,128)} %fusion.32) | data formatting | bytes 6291456
  43.2 6.7 %all-to-all-start = ((f32[8,1,98304]{2,1,0:T(1,128)}), f32[8,1,98304]{2,1,0:T(1,128)}, u32[]{:S(2)}, u32[]{:S(2)}) async-start(f32[8,1,98304]{2,1,0:T(1,128)} %reshape.224), calls=%async_computation | async-start | bytes 6291456 | tf_op jit(solution)/shard_map/all_to_all | solution.py:84
  49.9 0.1 compare_select_fusion.3
  50.0 1.3 gather_fusion.1
  51.3 0.0 copy-done.8
  51.3 0.1 multiply_add_fusion.1
  51.4 70.1 %all-to-all-done = f32[8,1,98304]{2,1,0:T(1,128)} async-done(((f32[8,1,98304]{2,1,0:T(1,128)}), f32[8,1,98304]{2,1,0:T(1,128)}, u32[]{:S(2)}, u32[]{:S(2)}) %all-to-all-start) | async-done | bytes 3145760 | tf_op jit(solution)/shard_map/all_to_all | solution.py:84
  121.5 0.5 broadcast.142
  122.0 11.8 %reduce.10 = f32[8,98304]{1,0:T(8,128)} reduce(f32[8,1,98304]{2,1,0:T(1,128)} %all-to-all-done, f32[]{:T(128)} %broadcast.142), dimensions={1}, to_apply=%all_to_all.24.reduce_sub_computation | reduce | bytes 6291460 | tf_op jit(solution)/shard_map/all_to_all | solution.py:84
  133.7 7.6 %reshape.225 = f32[1024,12,64]{2,1,0:T(8,128)} reshape(f32[8,98304]{1,0:T(8,128)} %reduce.10) | data formatting | bytes 6291456
  141.3 7.1 %copy.59 = f32[12,64,8,128]{3,1,2,0:T(8,128)} copy(f32[12,64,8,128]{1,0,3,2:T(8,128)} %bitcast.73) | data formatting | bytes 6291456 | tf_op jit(solution)/shard_map/all_to_all | solution.py:84
  148.4 3.3 %fusion.31 = (f32[6,8,64,128]{3,2,1,0:T(8,128)}, f32[6,8,64,128]{3,2,1,0:T(8,128)S(1)}) fusion(f32[12,8,64,128]{3,2,1,0:T(8,128)} %bitcast.76), kind=kLoop, calls=%fused_computation.64 | loop fusion | bytes 6291456 | tf_op jit(solution)/shard_map/slice | solution.py:86
  151.8 1.6 copy.63
  153.4 3.0 %copy.62 = f32[6,512,128]{1,2,0:T(8,128)} copy(f32[6,512,128]{2,1,0:T(8,128)} %bitcast.79) | data formatting | bytes 3145728 | tf_op jit(solution)/shard_map/slice | solution.py:86
  156.4 0.0 copy-done
  156.4 5.1 %fusion.11 = f32[6,128,512]{2,1,0:T(8,128)S(1)} fusion(f32[6,512,128]{2,1,0:T(8,128)S(1)} %bitcast.75, f32[512,512]{1,0:T(8,128)S(1)} %copy-done), kind=kOutput, calls=%fused_computation.20 | convolution fusion | flops 2415919104 | bytes 4194304 | tf_op jit(solution)/shard_map/yz,czs->cys/dot_general | solution.py:26
  161.5 0.0 copy-start.9
  161.6 2.9 %fusion.5 = f32[6,128,512]{2,1,0:T(8,128)S(1)} fusion(f32[6,512,128]{1,2,0:T(8,128)S(1)} %copy-done.2, f32[6,512,128]{1,2,0:T(8,128)S(1)} %copy-done.3, f32[6,128,512]{2,1,0:T(8,128)S(1)} %fusion.11, f32[512,512]{1,0:T(8,128)S(1)} %copy-done.5, f32[128]{0:T(128)S(1)} %gather_fusion.1), kind=kOutput, calls=%fused_computation.14 | convolution fusion | flops 2418278400 | bytes 7340544 | tf_op jit(solution)/shard_map/yz,czs->cys/dot_general | solution.py:30
  164.5 2.7 %fusion.8 = f32[6,512,128]{1,2,0:T(8,128)S(1)} fusion(f32[6,128,512]{2,1,0:T(8,128)S(1)} %fusion.5, f32[512,512]{1,0:T(8,128)S(1)} %copy-done.9, f32[512,128]{0,1:T(8,128)S(1)} %multiply_add_fusion.1), kind=kOutput, calls=%fused_computation.16 | convolution fusion | flops 2416312320 | bytes 4456448 | tf_op jit(solution)/shard_map/yz,czs->cys/dot_general | solution.py:32
  167.2 0.0 copy-start.1
  167.2 1.9 copy.64
  169.1 3.9 %all-to-all-start.1 = ((f32[6,512,128]{2,0,1:T(8,128)}), f32[6,512,128]{2,0,1:T(8,128)S(1)}, u32[]{:S(2)}, u32[]{:S(2)}) async-start(f32[6,512,128]{2,0,1:T(8,128)} %copy.64), calls=%async_computation.1 | async-start | bytes 4194304 | tf_op jit(solution)/shard_map/all_to_all | solution.py:88
  173.0 2.1 multiply_bitcast_fusion
  175.1 3.0 %copy.72 = f32[6,512,128]{2,1,0:T(8,128)} copy(f32[6,512,128]{1,2,0:T(8,128)} %copy-done.1) | data formatting | bytes 3145728
  178.1 43.8 %all-to-all-done.1 = f32[6,512,128]{2,0,1:T(8,128)S(1)} async-done(((f32[6,512,128]{2,0,1:T(8,128)}), f32[6,512,128]{2,0,1:T(8,128)S(1)}, u32[]{:S(2)}, u32[]{:S(2)}) %all-to-all-start.1) | async-done | bytes 1572896 | tf_op jit(solution)/shard_map/all_to_all | solution.py:88
  221.9 2.7 %copy.76 = f32[6,64,8,128]{1,0,3,2:T(8,128)} copy(f32[6,64,8,128]{3,0,1,2:T(8,128)S(1)} %bitcast.78) | data formatting | bytes 3145728 | tf_op jit(solution)/shard_map/all_to_all | solution.py:88
  224.6 3.2 %gather_fusion.2 = f32[512,6,64]{2,1,0:T(8,128)S(1)} fusion(f32[6,64,1024]{1,0,2:T(8,128)} %bitcast.80, s32[1024]{0:T(1024)S(1)} %pad_clamp_fusion), kind=kCustom, calls=%fused_computation.2 | custom fusion | bytes 1574912 | tf_op jit(solution)/shard_map/jit(_take)/gather | solution.py:89
  227.8 2.9 %broadcast_select_fusion = f32[6,64,512]{1,0,2:T(8,128)} fusion(pred[512]{0:T(512)(128)(4,1)S(1)} %get-tuple-element.21, f32[512,6,64]{2,1,0:T(8,128)S(1)} %gather_fusion.2), kind=kLoop, calls=%fused_computation.24 | loop fusion | flops 196608 | bytes 1573376 | tf_op jit(solution)/shard_map/jit(_take)/select_n | solution.py:89
  230.7 2.9 %copy.71 = f32[6,64,512]{2,1,0:T(8,128)} copy(f32[6,64,512]{1,0,2:T(8,128)} %broadcast_select_fusion) | data formatting | bytes 1572864
  233.6 1.4 copy.68
  235.1 1.3 broadcast_select_fusion.1
  236.3 0.1 copy-done.4
  236.4 5.1 %convolution_bitcast_fusion = f32[1,3,3,64]{2,1,3,0:T(4,128)S(1)} fusion(f32[3,2,64,512]{3,2,1,0:T(8,128)S(1)} %broadcast_select_fusion.1, f32[512,3,2,64]{0,3,2,1:T(8,128)S(1)} %copy-done.4), kind=kOutput, calls=%fused_computation.17 | convolution fusion | flops 7077888 | bytes 1575168 | tf_op jit(solution)/shard_map/jrym,fkrym,m->fjky/dot_general | solution.py:39
  241.5 1.8 fusion.19
  243.3 10.5 %psum.7 = f32[3,64]{1,0:T(4,128)} all-reduce(f32[3,64]{1,0:T(4,128)S(1)} %maximum_bitcast_fusion), channel_id=1, replica_groups=mesh['grp'=4,'col'=8] {'grp'}, use_global_device_ids=true, to_apply=%region_5.6 | all-reduce | flops 192 | bytes 1536 | tf_op jit(solution)/shard_map/psum | solution.py:91
  (25 shorter events, 0.1 us)
Async XLA Ops:
  0.6 155.8 %copy-start = (f32[512,512]{1,0:T(8,128)S(1)}, f32[512,512]{1,0:T(8,128)}, u32[]{:S(2)}) copy-start(f32[512,512]{1,0:T(8,128)} %param.14) | copy-start | bytes 3145732
  0.6 5.3 %copy-start.6 = (f32[6,64,512]{2,1,0:T(8,128)S(1)}, f32[6,64,512]{2,1,0:T(8,128)}, u32[]{:S(2)}) copy-start(f32[6,64,512]{2,1,0:T(8,128)} %param.10) | copy-start | bytes 2359300
  43.2 6.8 %copy-start.7 = (s32[2,512]{1,0:T(2,128)S(1)}, s32[2,512]{1,0:T(2,128)}, u32[]{:S(2)}) copy-start(s32[2,512]{1,0:T(2,128)} %param.18) | copy-start | bytes 12292
  43.2 8.1 %copy-start.8 = (f32[512]{0:T(512)S(1)}, f32[512]{0:T(512)}, u32[]{:S(2)}) copy-start(f32[512]{0:T(512)} %param.17) | copy-start | bytes 6148
  43.2 78.3 %all-to-all-start = ((f32[8,1,98304]{2,1,0:T(1,128)}), f32[8,1,98304]{2,1,0:T(1,128)}, u32[]{:S(2)}, u32[]{:S(2)}) async-start(f32[8,1,98304]{2,1,0:T(1,128)} %reshape.224), calls=%async_computation | async-start | bytes 6291456 | tf_op jit(solution)/shard_map/all_to_all | solution.py:84
  156.4 5.1 %copy-start.2 = (f32[6,512,128]{1,2,0:T(8,128)S(1)}, f32[6,512,128]{1,2,0:T(8,128)}, u32[]{:S(2)}) copy-start(f32[6,512,128]{1,2,0:T(8,128)} %copy.63) | copy-start | bytes 4718596
  156.4 5.1 %copy-start.3 = (f32[6,512,128]{1,2,0:T(8,128)S(1)}, f32[6,512,128]{1,2,0:T(8,128)}, u32[]{:S(2)}) copy-start(f32[6,512,128]{1,2,0:T(8,128)} %copy.62) | copy-start | bytes 4718596
  156.4 5.1 %copy-start.5 = (f32[512,512]{1,0:T(8,128)S(1)}, f32[512,512]{1,0:T(8,128)}, u32[]{:S(2)}) copy-start(f32[512,512]{1,0:T(8,128)} %param.16) | copy-start | bytes 3145732
  161.5 3.0 %copy-start.9 = (f32[512,512]{1,0:T(8,128)S(1)}, f32[512,512]{1,0:T(8,128)}, u32[]{:S(2)}) copy-start(f32[512,512]{1,0:T(8,128)} %param.15) | copy-start | bytes 3145732
  167.2 1.9 copy-start.1
  169.1 52.8 %all-to-all-start.1 = ((f32[6,512,128]{2,0,1:T(8,128)}), f32[6,512,128]{2,0,1:T(8,128)S(1)}, u32[]{:S(2)}, u32[]{:S(2)}) async-start(f32[6,512,128]{2,0,1:T(8,128)} %copy.64), calls=%async_computation.1 | async-start | bytes 4194304 | tf_op jit(solution)/shard_map/all_to_all | solution.py:88
  235.1 1.4 copy-start.4
where the time goes:
time: 259 us; the launch traced here: 254 us
  waiting for transfers between devices  114 us (44%)
  local copies, waits for them, and re-layouts  69.4 us (27%)
  other arithmetic  32.8 us (13%)
  matrix products  15.8 us (6%)
  starting transfers between devices  10.5 us (4%)
  blocking collectives  10.5 us (4%)
    all_to_all x1, waiting for transfers between devices, on_device(): lax.all_to_all(stacked, 'col', split_axis=2, concat_axis=1, tiled=True)  70.1 us
    all_to_all x1, waiting for transfers between devices, on_device(): lax.all_to_all(solved, 'col', split_axis=1, concat_axis=2, tiled=True)  43.8 us
    unnamed x24, local copies, waits for them, and re-layouts  22.7 us
    gather x1, local copies, waits for them, and re-layouts, on_device(): jnp.take(jnp.concatenate([state_now, forcing], axis=0), slot_column, axis=2)  11.9 us
    all_to_all x1, other arithmetic, on_device(): lax.all_to_all(stacked, 'col', split_axis=2, concat_axis=1, tiled=True)  11.8 us
    psum x1, blocking collectives, on_device(): mean_emf = lax.psum(partial_emf, 'grp')  10.5 us
    all_to_all x2, local copies, waits for them, and re-layouts, on_device(): lax.all_to_all(stacked, 'col', split_axis=2, concat_axis=1, tiled=True)  7.6 us
    unnamed x1, other arithmetic  7.54 us
  transfers between devices with their start and end apart: 2, of which 2 were waited for; matrix products, arithmetic and copies ran while one was open for 3% of the time, Pallas kernels for 0%

commit v1 on v0

v1 whole, which is shorter than its diff:
```python
import functools

import jax
import jax.numpy as jnp
from jax import lax
from jax.experimental import pallas as pl
from jax.experimental.pallas import tpu as pltpu
from jax.sharding import PartitionSpec as P

KMAX = 2048
TIME_STEP = 2.0
RK_ALPHA = -3.0 / 40.0
RK_BETA = 5.0 / 24.0
RK_GAMMA = 5.0 / 12.0
RK_ZETA = -17.0 / 60.0
WAVE_SCALE = 8.0
VMEM_LIMIT = 56 * 1024 * 1024
GROUPS = 3
LANES = 128

F32 = jnp.float32
BF16 = jnp.bfloat16


def call(body, out_shape, in_specs, out_specs, flops, nbytes, scratch=(), aliases=None):
    return pl.pallas_call(
        body,
        grid=(1,),
        out_shape=out_shape,
        in_specs=in_specs,
        out_specs=out_specs,
        scratch_shapes=list(scratch),
        input_output_aliases=aliases or {},
        cost_estimate=pl.CostEstimate(flops=flops, bytes_accessed=nbytes, transcendentals=0),
        compiler_params=pltpu.CompilerParams(vmem_limit_bytes=VMEM_LIMIT),
    )


def whole(shape):
    return pl.BlockSpec(shape, lambda i: (0,) * len(shape))


def part(shape, at):
    return pl.BlockSpec(shape, lambda i: (at,) + (0,) * (len(shape) - 1))


def scalar():
    return pl.BlockSpec(memory_space=pltpu.SMEM)


def untouched():
    return pl.BlockSpec(memory_space=pl.ANY)


def shaped(shape, dtype=F32):
    return jax.ShapeDtypeStruct(shape, dtype)


def three_parts(x):
    high = x.astype(BF16)
    rest = x - high.astype(F32)
    middle = rest.astype(BF16)
    low = (rest - middle.astype(F32)).astype(BF16)
    return jnp.concatenate([high, middle, low], axis=0)


def sum_parts(x):
    rows = x.shape[0] // 3
    return x[:rows] + x[rows : 2 * rows] + x[2 * rows :]


def two_parts(x):
    high = x.astype(BF16)
    low = (x - high.astype(F32)).astype(BF16)
    return high, low


def selector(places, rows):
    columns = places.shape[1]
    return (lax.broadcasted_iota(jnp.int32, (rows, columns), 0) == places).astype(F32).astype(BF16)


def wave_row(modes):
    wave_x = modes[0:1, :].astype(F32)
    wave_z = modes[1:2, :].astype(F32)
    return (wave_x * wave_x + wave_z * wave_z) * (WAVE_SCALE / (KMAX * KMAX))


NT = (((1,), (1,)), ((), ()))


def plan_kernel(devices, me_ref, owner_ref, modes_ref, info_ref, wave_ref):
    columns = owner_ref.shape[1]
    share = columns // devices
    rows = -(-devices // 8) * 8
    me = me_ref[0]
    owner = owner_ref[...]
    owned = (lax.broadcasted_iota(jnp.int32, (rows, columns), 0) == owner).astype(F32)
    before = (
        lax.broadcasted_iota(jnp.int32, (LANES, LANES), 0) < lax.broadcasted_iota(jnp.int32, (LANES, LANES), 1)
    ).astype(F32)
    carry = jnp.zeros((rows, 1), F32)
    earlier = []
    for at in range(columns // LANES):
        block = owned[:, at * LANES : (at + 1) * LANES]
        earlier.append(jnp.dot(block, before, preferred_element_type=F32) + carry)
        carry = carry + jnp.sum(block, axis=1, keepdims=True)
    counts = carry
    rank = jnp.sum(owned * jnp.concatenate(earlier, axis=1), axis=0, keepdims=True)
    surplus = jnp.maximum(counts - share, 0.0)
    lower = (lax.broadcasted_iota(jnp.int32, (rows, columns), 0) < owner).astype(F32)
    number = jnp.sum(lower * surplus, axis=0, keepdims=True) + (rank - share)
    free = share - jnp.minimum(counts, share)
    start = jnp.zeros((1, 1), F32)
    solver = owner
    slot = rank
    beyond = rank >= share
    for device in range(devices):
        here = free[device : device + 1, :]
        inside = beyond & (number >= start) & (number < start + here)
        solver = jnp.where(inside, device, solver)
        slot = jnp.where(inside, share - here + number - start, slot)
        start = start + here
    place = (solver ^ me) * share + slot.astype(jnp.int32)
    extra = jnp.where(beyond, (owner ^ me) * share + rank.astype(jnp.int32) - share, -1)
    mine = jnp.sum((owner == me).astype(F32), axis=1, keepdims=True).astype(jnp.int32)
    info_ref[...] = jnp.concatenate(
        [place, extra, jnp.broadcast_to(mine, (1, columns)), jnp.zeros((5, columns), jnp.int32)], axis=0
    )
    wave = jnp.broadcast_to(wave_row(modes_ref[...]), (16, columns))
    picked = sum_parts(
        lax.dot_general(three_parts(wave), selector(place, share), NT, preferred_element_type=F32)
    )
    wave_ref[...] = jnp.concatenate([picked, picked], axis=1)[:8]


def pack_kernel(devices, info_ref, modes_ref, state_ref, now_ref, old_ref, *out_refs):
    comps, points, columns = state_ref.shape
    share = columns // devices
    wave = wave_row(modes_ref[...]).reshape(1, 1, columns)
    state = state_ref[...]
    forcing = RK_GAMMA * now_ref[...] + RK_ZETA * old_ref[...]
    local = state + TIME_STEP * (forcing - RK_ALPHA * (wave * state))
    rows = comps * points
    both = jnp.concatenate([state.reshape(rows, columns), local.reshape(rows, columns)], axis=0)
    placed = sum_parts(
        lax.dot_general(
            three_parts(both), selector(info_ref[0:1, :], columns), NT, preferred_element_type=F32
        )
    )
    for step, out in enumerate(out_refs):
        taken = placed[:, step * share : (step + 1) * share]
        for kind in range(2):
            for pair in range(comps // 2):
                real = (kind * comps + 2 * pair) * points
                imag = real + points
                out[kind, pair] = jnp.concatenate(
                    [taken[real : real + points], taken[imag : imag + points]], axis=1
                )


def operators_kernel(deriv_ref, inverse_ref, basis_ref, values_ref, deriv_out, inverse_out, basis_out, values_out):
    for source, target in ((deriv_ref, deriv_out), (inverse_ref, inverse_out), (basis_ref, basis_out)):
        high, low = two_parts(source[...])
        target[...] = jnp.concatenate([high, high, low], axis=1)
    lanes = values_out.shape[1]
    values_out[...] = jnp.transpose(jnp.broadcast_to(values_ref[...], (lanes, values_ref.shape[1])))


def apply(operator, x):
    high, low = two_parts(x)
    return jnp.dot(operator, jnp.concatenate([high, low, high], axis=0), preferred_element_type=F32)


def solve_kernel(devices, me_ref, wave_ref, values_ref, deriv_ref, inverse_ref, basis_ref, *refs):
    in_refs, refs = refs[:devices], refs[devices:]
    out_refs, (solved_ref, state, local, after) = refs[:devices], refs[devices:]
    me = me_ref[0]
    _, pairs, points, lanes = in_refs[0].shape
    for step, block in enumerate(in_refs):
        rows = pl.ds(pl.multiple_of((me ^ step) * points, points), points)
        for pair in range(pairs):
            state[rows, pair * lanes : (pair + 1) * lanes] = block[0, pair]
            local[rows, pair * lanes : (pair + 1) * lanes] = block[1, pair]
    rhs = local[...] + (TIME_STEP * RK_ALPHA) * apply(deriv_ref[...], state[...])
    project = apply(inverse_ref[...], rhs)
    damping = 1.0 + TIME_STEP * RK_BETA * (values_ref[...] + wave_ref[0:1, :])
    project = project / jnp.concatenate([damping] * pairs, axis=1)
    after[...] = apply(basis_ref[...], project)
    for pair in range(pairs):
        solved_ref[pair] = after[:, pair * lanes : (pair + 1) * lanes]
    for step, block in enumerate(out_refs):
        rows = pl.ds(pl.multiple_of((me ^ step) * points, points), points)
        for pair in range(pairs):
            block[pair] = after[rows, pair * lanes : (pair + 1) * lanes]


def unpack_kernel(devices, chunk, first, info_ref, modes_ref, velocity_ref, *refs):
    in_refs, refs = refs[:devices], refs[devices:]
    if not first:
        (_, emf_in), refs = refs[:2], refs[2:]
    (state_ref, emf_ref), out_refs = refs[:2], refs[2:]
    pairs, points, lanes = in_refs[0].shape
    share = lanes // 2
    columns = devices * share
    got = []
    for pair in range(pairs):
        for half in range(2):
            got.append(
                jnp.concatenate(
                    [block[pair][:, half * share : (half + 1) * share] for block in in_refs], axis=1
                )
            )
    got = jnp.concatenate(got, axis=0)
    state = sum_parts(
        jnp.dot(three_parts(got), selector(info_ref[0:1, :], columns), preferred_element_type=F32)
    )
    state_ref[...] = state.reshape(2 * pairs, points, columns)
    extra = sum_parts(
        lax.dot_general(
            three_parts(state), selector(info_ref[1:2, :], columns), NT, preferred_element_type=F32
        )
    )
    for step, out in enumerate(out_refs):
        taken = extra[:, step * share : (step + 1) * share]
        for pair in range(pairs):
            real = 2 * pair * points
            imag = real + points
            out[pair] = jnp.concatenate([taken[real : real + points], taken[imag : imag + points]], axis=1)
    weight = jnp.where(modes_ref[0:1, :] > 0, 2.0, 1.0).astype(F32)
    totals = [jnp.zeros((points, columns), F32)] * 3
    for pair in range(pairs):
        field = chunk * pairs + pair
        real = weight * state[2 * pair * points : (2 * pair + 1) * points]
        imag = weight * state[(2 * pair + 1) * points : (2 * pair + 2) * points]
        for sign, i, j in ((1.0, (field + 1) % 3, (field + 2) % 3), (-1.0, (field + 2) % 3, (field + 1) % 3)):
            totals[i] = totals[i] + sign * (velocity_ref[2 * j] * real + velocity_ref[2 * j + 1] * imag)
    rows = []
    for total in totals:
        folded = total[:, :LANES]
        for at in range(1, columns // LANES):
            folded = folded + total[:, at * LANES : (at + 1) * LANES]
        rows.append(jnp.sum(jnp.transpose(folded), axis=0, keepdims=True))
    rows = jnp.concatenate(rows, axis=0)
    emf_ref[...] = rows if first else rows + emf_in[...]


def assemble_kernel(devices, first, me_ref, info_ref, solved_ref, *refs):
    in_refs, refs = refs[:devices], refs[devices:]
    if not first:
        refs = refs[1:]
    (out_ref,) = refs
    me = me_ref[0]
    pairs, points, lanes = in_refs[0].shape
    share = lanes // 2
    depth = solved_ref.shape[1]
    used = lax.broadcasted_iota(jnp.int32, (depth, share), 1) < info_ref[2:3, :share]
    for pair in range(pairs):
        for half in range(2):
            kept = jnp.where(used, solved_ref[pair][:, half * share : (half + 1) * share], 0.0)
            out_ref[2 * pair + half, :, :share] = kept
            for step, block in enumerate(in_refs):
                rows = pl.ds(pl.multiple_of((me ^ step) * points, points), points)
                out_ref[2 * pair + half, rows, share:] = block[pair][:, half * share : (half + 1) * share]


def exchange(blocks):
    devices = len(blocks)
    return [blocks[0]] + [
        lax.ppermute(blocks[step], "col", [(i, i ^ step) for i in range(devices)]) for step in range(1, devices)
    ]


def sum_over_groups(value):
    groups = lax.axis_size("grp")
    terms = [value] + [
        lax.ppermute(value, "grp", [(i, i ^ step) for i in range(groups)]) for step in range(1, groups)
    ]
    while len(terms) > 1:
        terms = [terms[at] + terms[at + 1] for at in range(0, len(terms), 2)]
    return terms[0]


def on_device(
    state_now,
    force_now,
    force_old,
    velocity,
    second_deriv,
    eig_basis,
    eig_inverse,
    eig_values,
    kept_modes,
    col_owner,
):
    comps, points, columns = state_now.shape
    devices = lax.axis_size("col")
    depth = devices * points
    share = columns // devices
    lanes = 2 * share
    pairs = GROUPS
    chunks = comps // (2 * pairs)
    me = lax.axis_index("col").astype(jnp.int32).reshape(1)
    owner = col_owner.reshape(1, columns)

    info, wave = call(
        functools.partial(plan_kernel, devices),
        [shaped((8, columns), jnp.int32), shaped((8, lanes))],
        [scalar(), whole((1, columns)), whole((2, columns))],
        [whole((8, columns)), whole((8, lanes))],
        1000000,
        100000,
    )(me, owner, kept_modes)

    field = (2 * pairs, points, columns)
    sent = (2, pairs, points, lanes)
    back = (pairs, points, lanes)
    moved = 4 * 2 * pairs * points * columns

    forward = []
    for chunk in range(chunks):
        forward.append(
            exchange(
                call(
                    functools.partial(pack_kernel, devices),
                    [shaped(sent)] * devices,
                    [whole((8, columns)), whole((2, columns))] + [part(field, chunk)] * 3,
                    [whole(sent)] * devices,
                    12 * 2 * pairs * points * columns * columns,
                    5 * moved,
                )(info, kept_modes, state_now, force_now, force_old)
            )
        )

    operator = shaped((depth, 3 * depth), BF16)
    operators = call(
        operators_kernel,
        [operator, operator, operator, shaped((depth, lanes))],
        [whole((depth, depth))] * 3 + [whole((1, depth))],
        [whole((depth, 3 * depth))] * 3 + [whole((depth, lanes))],
        1000000,
        30 * depth * depth,
    )(second_deriv, eig_inverse, eig_basis, eig_values.reshape(1, depth))
    values = operators[3]

    solved, returned = [], []
    for chunk in range(chunks):
        width = pairs * lanes
        outs = call(
            functools.partial(solve_kernel, devices),
            [shaped(back)] * devices + [shaped((pairs, depth, lanes))],
            [scalar(), whole((8, lanes)), whole((depth, lanes))]
            + [whole((depth, 3 * depth))] * 3
            + [whole(sent)] * devices,
            [whole(back)] * devices + [whole((pairs, depth, lanes))],
            18 * depth * depth * width,
            18 * depth * depth + 16 * depth * width,
            [pltpu.VMEM((depth, width), F32)] * 3,
        )(me, wave, values, *operators[:3], *forward[chunk])
        solved.append(outs[devices])
        returned.append(exchange(outs[:devices]))

    state_next, emf, extra = None, None, []
    for chunk in range(chunks):
        first = chunk == 0
        outs = call(
            functools.partial(unpack_kernel, devices, chunk, first),
            [shaped(state_now.shape), shaped((3, points))] + [shaped(back)] * devices,
            [whole((8, columns)), whole((2, columns)), whole(velocity.shape)]
            + [whole(back)] * devices
            + ([] if first else [untouched(), whole((3, points))]),
            [part(field, chunk), whole((3, points))] + [whole(back)] * devices,
            12 * 2 * pairs * points * columns * columns,
            6 * moved,
            aliases={} if first else {3 + devices: 0},
        )(info, kept_modes, velocity, *returned[chunk], *([] if first else [state_next, emf]))
        state_next, emf = outs[:2]
        extra.append(exchange(outs[2:]))
    mean_emf = sum_over_groups(emf)

    owned = None
    for chunk in range(chunks):
        first = chunk == 0
        owned = call(
            functools.partial(assemble_kernel, devices, first),
            shaped((comps, depth, lanes)),
            [scalar(), whole((8, columns)), whole((pairs, depth, lanes))]
            + [whole(back)] * devices
            + ([] if first else [untouched()]),
            part((2 * pairs, depth, lanes), chunk),
            1000000,
            16 * pairs * depth * lanes,
            aliases={} if first else {3 + devices: 0},
        )(me, info, solved[chunk], *extra[chunk], *([] if first else [owned]))
    return (state_next, owned, mean_emf)


def solution(mesh):
    return jax.shard_map(
        on_device,
        mesh=mesh,
        in_specs=(
            P(None, "col", "grp"),
            P(None, "col", "grp"),
            P(None, "col", "grp"),
            P(None, "col", "grp"),
            P(),
            P(),
            P(),
            P(),
            P(None, "grp"),
            P("grp", None),
        ),
        out_specs=(P(None, "col", "grp"), P(None, None, ("grp", "col")), P(None, "col")),
        check_vma=False,
    )
```

time: 259 us -> 111 us (0.43)
  the two profiles are of different devices: /device:TPU:0 before, /device:TPU:9 now
where the time goes in v1:
time: 111 us; the launch traced here: 110 us
  waiting for transfers between devices  55.1 us (50%)
  starting transfers between devices  26.7 us (24%)
  Pallas kernels  24.6 us (22%)
  local copies, waits for them, and re-layouts  1.9 us (2%)
  other arithmetic  1.26 us (1%)
    ppermute x21, waiting for transfers between devices, exchange(): lax.ppermute(blocks[step], 'col', [(i, i ^ step) for i in range(devices)])  54.2 us
    ppermute x21, starting transfers between devices, exchange(): lax.ppermute(blocks[step], 'col', [(i, i ^ step) for i in range(devices)])  24.1 us
    pallas_call x1, Pallas kernels, on_device(): call(functools.partial(solve_kernel, devices), [shaped(back)] * devices +...  6.85 us
    pallas_call x1, Pallas kernels, on_device(): call(operators_kernel, [operator, operator, operator, shaped((depth, lane...  4.49 us
    pallas_call x1, Pallas kernels, on_device(): call(functools.partial(pack_kernel, devices), [shaped(sent)] * devices, [...  4.42 us
    pallas_call x1, Pallas kernels, on_device(): call(functools.partial(unpack_kernel, devices, chunk, first), [shaped(sta...  4.1 us
    pallas_call x1, Pallas kernels, on_device(): call(functools.partial(assemble_kernel, devices, first), shaped((comps, d...  3.04 us
    ppermute x3, starting transfers between devices, sum_over_groups(): lax.ppermute(value, 'grp', [(i, i ^ step) for i in range(groups)])  2.65 us
  transfers between devices with their start and end apart: 24, of which 12 were waited for; matrix products, arithmetic and copies ran while one was open for 1% of the time, Pallas kernels for 4%

profile of v1, /device:TPU:9, one launch (start us, length us, event | category | flops | bytes accessed | tf_op | source)
XLA Modules:
  0.0 110.4 jit_solution(1121918629943893899)
XLA Ops:
  0.6 1.7 %shard_map.121 = (s32[8,512]{1,0:T(8,128)}, f32[8,128]{1,0:T(8,128)}) custom-call(s32[1]{0:T(128)} %bitcast.me_ref, s32[1,512]{1,0:T(1,128)} %bitcast.3, s32[2,512]{1,0:T(2,128)} %modes_ref.5), custom_call_target="tpu_custom_call" | custom-call | flops 1000000 | bytes 100000 | tf_op jit(solution)/shard_map/pallas_call | solution.py:306
  2.4 4.4 %shard_map.123 = (f32[2,3,64,128]{3,2,1,0:T(8,128)}, f32[2,3,64,128]{3,2,1,0:T(8,128)}, f32[2,3,64,128]{3,2,1,0:T(8,128)}, f32[2,3,64,128]{3,2,1,0:T(8,128)}, f3...) custom-call(s32[8,512]{1,0:T(8,128)} %get-tuple-element.36.info_ref,, ...), custom_call_target="tpu_custom_call" | custom-call | flops 1207959552 | bytes 3932160 | tf_op jit(solution)/shard_map/pallas_call | solution.py:324
  6.8 0.7 collective-permute-start
  7.5 0.0 collective-permute-start.1
  7.5 1.6 %collective-permute-start.2 = (f32[2,3,64,128]{3,2,1,0:T(8,128)}, f32[2,3,64,128]{3,2,1,0:T(8,128)S(1)}, u32[]{:S(2)}, u32[]{:S(2)}) collective-permute-start(f32[2,3,64,128]{3,2,1,0:T(8,128)} %get-tuple-element.45), channel_id=1, source_target_pairs={{0,3},{1,2},{2,1},{3,0},{4,7},{5,6},{6,5},{7,4},{8,11},{9,10},{10,... | collective-permute-start | bytes 589832 | tf_op jit(solution)/shard_map/ppermute | solution.py:270
  9.1 2.3 %collective-permute-start.3 = (f32[2,3,64,128]{3,2,1,0:T(8,128)}, f32[2,3,64,128]{3,2,1,0:T(8,128)S(1)}, u32[]{:S(2)}, u32[]{:S(2)}) collective-permute-start(f32[2,3,64,128]{3,2,1,0:T(8,128)} %get-tuple-element.46), channel_id=1, source_target_pairs={{0,4},{1,5},{2,6},{3,7},{4,0},{5,1},{6,2},{7,3},{8,12},{9,13},{10,... | collective-permute-start | bytes 589832 | tf_op jit(solution)/shard_map/ppermute | solution.py:270
  11.4 0.4 collective-permute-start.4
  11.9 0.0 collective-permute-done.refs_1_
  11.9 1.3 %collective-permute-start.5 = (f32[2,3,64,128]{3,2,1,0:T(8,128)}, f32[2,3,64,128]{3,2,1,0:T(8,128)S(1)}, u32[]{:S(2)}, u32[]{:S(2)}) collective-permute-start(f32[2,3,64,128]{3,2,1,0:T(8,128)} %get-tuple-element.48), channel_id=1, source_target_pairs={{0,6},{1,7},{2,4},{3,5},{4,2},{5,3},{6,0},{7,1},{8,14},{9,15},{10,... | collective-permute-start | bytes 589832 | tf_op jit(solution)/shard_map/ppermute | solution.py:270
  13.2 7.1 %collective-permute-done.1.refs_2_ = f32[2,3,64,128]{3,2,1,0:T(8,128)S(1)} collective-permute-done((f32[2,3,64,128]{3,2,1,0:T(8,128)}, f32[2,3,64,128]{3,2,1,0:T(8,128)S(1)}, u32[]{:S(2)}, u32[]{:S(2)}) %collective-permute-start.1) | collective-permute-done | bytes 196640 | tf_op jit(solution)/shard_map/ppermute | solution.py:270
  20.3 1.2 %collective-permute-start.6 = (f32[2,3,64,128]{3,2,1,0:T(8,128)}, f32[2,3,64,128]{3,2,1,0:T(8,128)S(1)}, u32[]{:S(2)}, u32[]{:S(2)}) collective-permute-start(f32[2,3,64,128]{3,2,1,0:T(8,128)} %get-tuple-element.49), channel_id=1, source_target_pairs={{0,7},{1,6},{2,5},{3,4},{4,3},{5,2},{6,1},{7,0},{8,15},{9,14},{10,... | collective-permute-start | bytes 589832 | tf_op jit(solution)/shard_map/ppermute | solution.py:270
  21.5 4.5 %shard_map.122 = (bf16[512,1536]{1,0:T(8,128)(2,1)}, bf16[512,1536]{1,0:T(8,128)(2,1)}, bf16[512,1536]{1,0:T(8,128)(2,1)}, f32[512,128]{1,0:T(8,128)}) custom-call(f32[512,512]{1,0:T(8,128)} %deriv_ref.1, f32[512,512]{1,0:T(8,128)} %inverse_ref.1, f32[512,512]{1,0:T(8,128)} %basis_ref.1, f32[1,512]{1,0:T(1,128)} %bitcast.4), custom_call_target="tpu_custom_call" | custom-call | flops 1000000 | bytes 7864320 | tf_op jit(solution)/shard_map/pallas_call | solution.py:336
  26.0 0.0 collective-permute-done.2.refs_3_
  26.0 0.0 collective-permute-done.3.refs_4_
  26.0 10.9 %collective-permute-done.4.refs_5_ = f32[2,3,64,128]{3,2,1,0:T(8,128)S(1)} collective-permute-done((f32[2,3,64,128]{3,2,1,0:T(8,128)}, f32[2,3,64,128]{3,2,1,0:T(8,128)S(1)}, u32[]{:S(2)}, u32[]{:S(2)}) %collective-permute-start.4) | collective-permute-done | bytes 196640 | tf_op jit(solution)/shard_map/ppermute | solution.py:270
  36.9 4.2 %collective-permute-done.5.refs_6_ = f32[2,3,64,128]{3,2,1,0:T(8,128)S(1)} collective-permute-done((f32[2,3,64,128]{3,2,1,0:T(8,128)}, f32[2,3,64,128]{3,2,1,0:T(8,128)S(1)}, u32[]{:S(2)}, u32[]{:S(2)}) %collective-permute-start.5) | collective-permute-done | bytes 196640 | tf_op jit(solution)/shard_map/ppermute | solution.py:270
  41.2 4.2 %collective-permute-done.6.refs_7_ = f32[2,3,64,128]{3,2,1,0:T(8,128)S(1)} collective-permute-done((f32[2,3,64,128]{3,2,1,0:T(8,128)}, f32[2,3,64,128]{3,2,1,0:T(8,128)S(1)}, u32[]{:S(2)}, u32[]{:S(2)}) %collective-permute-start.6) | collective-permute-done | bytes 196640 | tf_op jit(solution)/shard_map/ppermute | solution.py:270
  45.4 0.6 copy-done.13
  46.0 6.8 %shard_map.124 = (f32[3,64,128]{2,1,0:T(8,128)}, f32[3,64,128]{2,1,0:T(8,128)}, f32[3,64,128]{2,1,0:T(8,128)}, f32[3,64,128]{2,1,0:T(8,128)}, f32[3,64,128]{2,1,...) custom-call(s32[1]{0:T(128)} %bitcast.me_ref, ...), custom_call_target="tpu_custom_call" | custom-call | flops 1811939328 | bytes 7864320 | tf_op jit(solution)/shard_map/pallas_call | solution.py:349
  52.9 1.0 collective-permute-start.7
  53.9 0.0 collective-permute-start.8
  53.9 1.7 %collective-permute-start.9 = (f32[3,64,128]{2,1,0:T(8,128)}, f32[3,64,128]{2,1,0:T(8,128)S(1)}, u32[]{:S(2)}, u32[]{:S(2)}) collective-permute-start(f32[3,64,128]{2,1,0:T(8,128)} %get-tuple-element.53), channel_id=1, source_target_pairs={{0,3},{1,2},{2,1},{3,0},{4,7},{5,6},{6,5},{7,4},{8,11},{9,10},{10,... | collective-permute-start | bytes 294920 | tf_op jit(solution)/shard_map/ppermute | solution.py:270
  55.6 1.3 %collective-permute-start.10 = (f32[3,64,128]{2,1,0:T(8,128)}, f32[3,64,128]{2,1,0:T(8,128)S(1)}, u32[]{:S(2)}, u32[]{:S(2)}) collective-permute-start(f32[3,64,128]{2,1,0:T(8,128)} %get-tuple-element.54), channel_id=1, source_target_pairs={{0,4},{1,5},{2,6},{3,7},{4,0},{5,1},{6,2},{7,3},{8,12},{9,13},{10,... | collective-permute-start | bytes 294920 | tf_op jit(solution)/shard_map/ppermute | solution.py:270
  56.9 1.4 %collective-permute-start.11 = (f32[3,64,128]{2,1,0:T(8,128)}, f32[3,64,128]{2,1,0:T(8,128)S(1)}, u32[]{:S(2)}, u32[]{:S(2)}) collective-permute-start(f32[3,64,128]{2,1,0:T(8,128)} %get-tuple-element.55), channel_id=1, source_target_pairs={{0,5},{1,4},{2,7},{3,6},{4,1},{5,0},{6,3},{7,2},{8,13},{9,12},{10,... | collective-permute-start | bytes 294920 | tf_op jit(solution)/shard_map/ppermute | solution.py:270
  58.3 1.5 %collective-permute-start.12 = (f32[3,64,128]{2,1,0:T(8,128)}, f32[3,64,128]{2,1,0:T(8,128)S(1)}, u32[]{:S(2)}, u32[]{:S(2)}) collective-permute-start(f32[3,64,128]{2,1,0:T(8,128)} %get-tuple-element.56), channel_id=1, source_target_pairs={{0,6},{1,7},{2,4},{3,5},{4,2},{5,3},{6,0},{7,1},{8,14},{9,15},{10,... | collective-permute-start | bytes 294920 | tf_op jit(solution)/shard_map/ppermute | solution.py:270
  59.8 1.8 %collective-permute-start.13 = (f32[3,64,128]{2,1,0:T(8,128)}, f32[3,64,128]{2,1,0:T(8,128)S(1)}, u32[]{:S(2)}, u32[]{:S(2)}) collective-permute-start(f32[3,64,128]{2,1,0:T(8,128)} %get-tuple-element.57), channel_id=1, source_target_pairs={{0,7},{1,6},{2,5},{3,4},{4,3},{5,2},{6,1},{7,0},{8,15},{9,14},{10,... | collective-permute-start | bytes 294920 | tf_op jit(solution)/shard_map/ppermute | solution.py:270
  61.6 1.9 %collective-permute-done.10.refs_4_ = f32[3,64,128]{2,1,0:T(8,128)S(1)} collective-permute-done((f32[3,64,128]{2,1,0:T(8,128)}, f32[3,64,128]{2,1,0:T(8,128)S(1)}, u32[]{:S(2)}, u32[]{:S(2)}) %collective-permute-start.10) | collective-permute-done | bytes 98336 | tf_op jit(solution)/shard_map/ppermute | solution.py:270
  63.5 6.2 %collective-permute-done.11.refs_5_ = f32[3,64,128]{2,1,0:T(8,128)S(1)} collective-permute-done((f32[3,64,128]{2,1,0:T(8,128)}, f32[3,64,128]{2,1,0:T(8,128)S(1)}, u32[]{:S(2)}, u32[]{:S(2)}) %collective-permute-start.11) | collective-permute-done | bytes 98336 | tf_op jit(solution)/shard_map/ppermute | solution.py:270
  69.7 3.9 %collective-permute-done.12.refs_6_ = f32[3,64,128]{2,1,0:T(8,128)S(1)} collective-permute-done((f32[3,64,128]{2,1,0:T(8,128)}, f32[3,64,128]{2,1,0:T(8,128)S(1)}, u32[]{:S(2)}, u32[]{:S(2)}) %collective-permute-start.12) | collective-permute-done | bytes 98336 | tf_op jit(solution)/shard_map/ppermute | solution.py:270
  73.6 2.1 %collective-permute-done.13.refs_7_ = f32[3,64,128]{2,1,0:T(8,128)S(1)} collective-permute-done((f32[3,64,128]{2,1,0:T(8,128)}, f32[3,64,128]{2,1,0:T(8,128)S(1)}, u32[]{:S(2)}, u32[]{:S(2)}) %collective-permute-start.13) | collective-permute-done | bytes 98336 | tf_op jit(solution)/shard_map/ppermute | solution.py:270
  75.7 0.6 copy-done.20
  76.3 4.1 %shard_map.125 = (f32[6,64,512]{2,1,0:T(8,128)}, f32[3,64]{1,0:T(4,128)}, f32[3,64,128]{2,1,0:T(8,128)}, f32[3,64,128]{2,1,0:T(8,128)}, f32[3,64,128]{2,1,0:T(8,...) custom-call(s32[8,512]{1,0:T(8,128)} %get-tuple-element.36.info_ref,, ...), custom_call_target="tpu_custom_call" | custom-call | flops 1207959552 | bytes 4718592 | tf_op jit(solution)/shard_map/pallas_call | solution.py:366
  80.4 0.4 collective-permute-start.14
  80.9 2.2 %collective-permute-start.23 = (f32[3,64]{1,0:T(4,128)}, f32[3,64]{1,0:T(4,128)S(1)}, u32[]{:S(2)}, u32[]{:S(2)}) collective-permute-start(f32[3,64]{1,0:T(4,128)} %get-tuple-element.68), channel_id=1, source_target_pairs={{0,24},{8,16},{16,8},{24,0},{1,25},{9,17},{17,9},{25,1},{2,26},{10... | collective-permute-start | bytes 2312 | tf_op jit(solution)/shard_map/ppermute | solution.py:277
  83.1 0.2 collective-permute-start.22
  83.3 0.3 collective-permute-start.21
  83.5 0.9 collective-permute-done.23
  84.4 2.9 %collective-permute-start.16 = (f32[3,64,128]{2,1,0:T(8,128)}, f32[3,64,128]{2,1,0:T(8,128)S(1)}, u32[]{:S(2)}, u32[]{:S(2)}) collective-permute-start(f32[3,64,128]{2,1,0:T(8,128)} %get-tuple-element.63), channel_id=1, source_target_pairs={{0,3},{1,2},{2,1},{3,0},{4,7},{5,6},{6,5},{7,4},{8,11},{9,10},{10,... | collective-permute-start | bytes 294920 | tf_op jit(solution)/shard_map/ppermute | solution.py:270
  87.4 0.2 collective-permute-start.17
  87.6 2.3 %collective-permute-start.18 = (f32[3,64,128]{2,1,0:T(8,128)}, f32[3,64,128]{2,1,0:T(8,128)S(1)}, u32[]{:S(2)}, u32[]{:S(2)}) collective-permute-start(f32[3,64,128]{2,1,0:T(8,128)} %get-tuple-element.65), channel_id=1, source_target_pairs={{0,5},{1,4},{2,7},{3,6},{4,1},{5,0},{6,3},{7,2},{8,13},{9,12},{10,... | collective-permute-start | bytes 294920 | tf_op jit(solution)/shard_map/ppermute | solution.py:270
  89.9 0.7 collective-permute-start.19
  90.6 1.2 %collective-permute-start.20 = (f32[3,64,128]{2,1,0:T(8,128)}, f32[3,64,128]{2,1,0:T(8,128)S(1)}, u32[]{:S(2)}, u32[]{:S(2)}) collective-permute-start(f32[3,64,128]{2,1,0:T(8,128)} %get-tuple-element.67), channel_id=1, source_target_pairs={{0,7},{1,6},{2,5},{3,4},{4,3},{5,2},{6,1},{7,0},{8,15},{9,14},{10,... | collective-permute-start | bytes 294920 | tf_op jit(solution)/shard_map/ppermute | solution.py:270
  91.8 1.3 %add_add_fusion = f32[3,64]{1,0:T(4,128)} fusion(f32[3,64]{1,0:T(4,128)S(1)} %collective-permute-done.22, f32[3,64]{1,0:T(4,128)S(1)} %collective-permute-done.23, f32[3,64]{1,0:T(4,128)} %get-tuple-element.68, f32[3,64]{1,0:T(4,128)S(1)} %collective-permute-done.21), kind=kLoop, calls=%fused_computation | loop fusion | flops 576 | bytes 3840 | tf_op jit(solution)/shard_map/add | solution.py:280
  93.1 7.3 %collective-permute-done.18.refs_5_ = f32[3,64,128]{2,1,0:T(8,128)S(1)} collective-permute-done((f32[3,64,128]{2,1,0:T(8,128)}, f32[3,64,128]{2,1,0:T(8,128)S(1)}, u32[]{:S(2)}, u32[]{:S(2)}) %collective-permute-start.18) | collective-permute-done | bytes 98336 | tf_op jit(solution)/shard_map/ppermute | solution.py:270
  100.4 3.2 %collective-permute-done.19.refs_6_ = f32[3,64,128]{2,1,0:T(8,128)S(1)} collective-permute-done((f32[3,64,128]{2,1,0:T(8,128)}, f32[3,64,128]{2,1,0:T(8,128)S(1)}, u32[]{:S(2)}, u32[]{:S(2)}) %collective-permute-start.19) | collective-permute-done | bytes 98336 | tf_op jit(solution)/shard_map/ppermute | solution.py:270
  103.5 3.2 %collective-permute-done.20.refs_7_ = f32[3,64,128]{2,1,0:T(8,128)S(1)} collective-permute-done((f32[3,64,128]{2,1,0:T(8,128)}, f32[3,64,128]{2,1,0:T(8,128)S(1)}, u32[]{:S(2)}, u32[]{:S(2)}) %collective-permute-start.20) | collective-permute-done | bytes 98336 | tf_op jit(solution)/shard_map/ppermute | solution.py:270
  106.7 0.6 copy-done.6
  107.3 3.0 %shard_map.126 = f32[6,512,128]{2,1,0:T(8,128)} custom-call(s32[1]{0:T(128)} %bitcast.me_ref, s32[8,512]{1,0:T(8,128)} %get-tuple-element.36.info_ref, f32[3,512,128]{2,1,0:T(8,128)} %get-tuple-element.59.solved_ref, f32[3,64,128]{2,1,0:T(8,128)} %get-tuple-element.60.refs_0_, f32[3,64,128]{2,1,0:T(8,128)} %copy-done, f32[3,64,128]{2,1,0:T(8,128)} %copy-done.1, ...), custom_call_target="tpu_custom_call" | custom-call | flops 1000000 | bytes 3145728 | tf_op jit(solution)/shard_map/pallas_call | solution.py:384
  (49 shorter events, 0.1 us)
Async XLA Ops:
  6.8 5.1 %collective-permute-start = (f32[2,3,64,128]{3,2,1,0:T(8,128)}, f32[2,3,64,128]{3,2,1,0:T(8,128)S(1)}, u32[]{:S(2)}, u32[]{:S(2)}) collective-permute-start(f32[2,3,64,128]{3,2,1,0:T(8,128)} %get-tuple-element.43), channel_id=1, source_target_pairs={{0,1},{1,0},{2,3},{3,2},{4,5},{5,4},{6,7},{7,6},{8,9},{9,8},{10,11... | collective-permute-start | bytes 589832 | tf_op jit(solution)/shard_map/ppermute | solution.py:270
  7.5 12.8 %collective-permute-start.1 = (f32[2,3,64,128]{3,2,1,0:T(8,128)}, f32[2,3,64,128]{3,2,1,0:T(8,128)S(1)}, u32[]{:S(2)}, u32[]{:S(2)}) collective-permute-start(f32[2,3,64,128]{3,2,1,0:T(8,128)} %get-tuple-element.44), channel_id=1, source_target_pairs={{0,2},{1,3},{2,0},{3,1},{4,6},{5,7},{6,4},{7,5},{8,10},{9,11},{10,... | collective-permute-start | bytes 589832 | tf_op jit(solution)/shard_map/ppermute | solution.py:270
  7.5 18.5 %collective-permute-start.2 = (f32[2,3,64,128]{3,2,1,0:T(8,128)}, f32[2,3,64,128]{3,2,1,0:T(8,128)S(1)}, u32[]{:S(2)}, u32[]{:S(2)}) collective-permute-start(f32[2,3,64,128]{3,2,1,0:T(8,128)} %get-tuple-element.45), channel_id=1, source_target_pairs={{0,3},{1,2},{2,1},{3,0},{4,7},{5,6},{6,5},{7,4},{8,11},{9,10},{10,... | collective-permute-start | bytes 589832 | tf_op jit(solution)/shard_map/ppermute | solution.py:270
  9.1 16.9 %collective-permute-start.3 = (f32[2,3,64,128]{3,2,1,0:T(8,128)}, f32[2,3,64,128]{3,2,1,0:T(8,128)S(1)}, u32[]{:S(2)}, u32[]{:S(2)}) collective-permute-start(f32[2,3,64,128]{3,2,1,0:T(8,128)} %get-tuple-element.46), channel_id=1, source_target_pairs={{0,4},{1,5},{2,6},{3,7},{4,0},{5,1},{6,2},{7,3},{8,12},{9,13},{10,... | collective-permute-start | bytes 589832 | tf_op jit(solution)/shard_map/ppermute | solution.py:270
  11.4 25.5 %collective-permute-start.4 = (f32[2,3,64,128]{3,2,1,0:T(8,128)}, f32[2,3,64,128]{3,2,1,0:T(8,128)S(1)}, u32[]{:S(2)}, u32[]{:S(2)}) collective-permute-start(f32[2,3,64,128]{3,2,1,0:T(8,128)} %get-tuple-element.47), channel_id=1, source_target_pairs={{0,5},{1,4},{2,7},{3,6},{4,1},{5,0},{6,3},{7,2},{8,13},{9,12},{10,... | collective-permute-start | bytes 589832 | tf_op jit(solution)/shard_map/ppermute | solution.py:270
  11.9 14.1 %copy-start.7 = (f32[2,3,64,128]{3,2,1,0:T(8,128)}, f32[2,3,64,128]{3,2,1,0:T(8,128)S(1)}, u32[]{:S(2)}) copy-start(f32[2,3,64,128]{3,2,1,0:T(8,128)S(1)} %collective-permute-done.refs_1_) | copy-start | bytes 589828
  11.9 29.3 %collective-permute-start.5 = (f32[2,3,64,128]{3,2,1,0:T(8,128)}, f32[2,3,64,128]{3,2,1,0:T(8,128)S(1)}, u32[]{:S(2)}, u32[]{:S(2)}) collective-permute-start(f32[2,3,64,128]{3,2,1,0:T(8,128)} %get-tuple-element.48), channel_id=1, source_target_pairs={{0,6},{1,7},{2,4},{3,5},{4,2},{5,3},{6,0},{7,1},{8,14},{9,15},{10,... | collective-permute-start | bytes 589832 | tf_op jit(solution)/shard_map/ppermute | solution.py:270
  20.3 5.7 %copy-start.8 = (f32[2,3,64,128]{3,2,1,0:T(8,128)}, f32[2,3,64,128]{3,2,1,0:T(8,128)S(1)}, u32[]{:S(2)}) copy-start(f32[2,3,64,128]{3,2,1,0:T(8,128)S(1)} %collective-permute-done.1.refs_2_) | copy-start | bytes 589828
  20.3 25.1 %collective-permute-start.6 = (f32[2,3,64,128]{3,2,1,0:T(8,128)}, f32[2,3,64,128]{3,2,1,0:T(8,128)S(1)}, u32[]{:S(2)}, u32[]{:S(2)}) collective-permute-start(f32[2,3,64,128]{3,2,1,0:T(8,128)} %get-tuple-element.49), channel_id=1, source_target_pairs={{0,7},{1,6},{2,5},{3,4},{4,3},{5,2},{6,1},{7,0},{8,15},{9,14},{10,... | collective-permute-start | bytes 589832 | tf_op jit(solution)/shard_map/ppermute | solution.py:270
  26.0 19.4 %copy-start.9 = (f32[2,3,64,128]{3,2,1,0:T(8,128)}, f32[2,3,64,128]{3,2,1,0:T(8,128)S(1)}, u32[]{:S(2)}) copy-start(f32[2,3,64,128]{3,2,1,0:T(8,128)S(1)} %collective-permute-done.2.refs_3_) | copy-start | bytes 589828
  26.0 19.3 %copy-start.10 = (f32[2,3,64,128]{3,2,1,0:T(8,128)}, f32[2,3,64,128]{3,2,1,0:T(8,128)S(1)}, u32[]{:S(2)}) copy-start(f32[2,3,64,128]{3,2,1,0:T(8,128)S(1)} %collective-permute-done.3.refs_4_) | copy-start | bytes 589828
  36.9 8.4 %copy-start.11 = (f32[2,3,64,128]{3,2,1,0:T(8,128)}, f32[2,3,64,128]{3,2,1,0:T(8,128)S(1)}, u32[]{:S(2)}) copy-start(f32[2,3,64,128]{3,2,1,0:T(8,128)S(1)} %collective-permute-done.4.refs_5_) | copy-start | bytes 589828
  41.2 4.2 %copy-start.12 = (f32[2,3,64,128]{3,2,1,0:T(8,128)}, f32[2,3,64,128]{3,2,1,0:T(8,128)S(1)}, u32[]{:S(2)}) copy-start(f32[2,3,64,128]{3,2,1,0:T(8,128)S(1)} %collective-permute-done.5.refs_6_) | copy-start | bytes 589828
  45.4 0.7 copy-start.13
  52.9 5.4 %collective-permute-start.7 = (f32[3,64,128]{2,1,0:T(8,128)}, f32[3,64,128]{2,1,0:T(8,128)S(1)}, u32[]{:S(2)}, u32[]{:S(2)}) collective-permute-start(f32[3,64,128]{2,1,0:T(8,128)} %get-tuple-element.51), channel_id=1, source_target_pairs={{0,1},{1,0},{2,3},{3,2},{4,5},{5,4},{6,7},{7,6},{8,9},{9,8},{10,11... | collective-permute-start | bytes 294920 | tf_op jit(solution)/shard_map/ppermute | solution.py:270
  53.9 5.9 %collective-permute-start.8 = (f32[3,64,128]{2,1,0:T(8,128)}, f32[3,64,128]{2,1,0:T(8,128)S(1)}, u32[]{:S(2)}, u32[]{:S(2)}) collective-permute-start(f32[3,64,128]{2,1,0:T(8,128)} %get-tuple-element.52), channel_id=1, source_target_pairs={{0,2},{1,3},{2,0},{3,1},{4,6},{5,7},{6,4},{7,5},{8,10},{9,11},{10,... | collective-permute-start | bytes 294920 | tf_op jit(solution)/shard_map/ppermute | solution.py:270
  53.9 7.7 %collective-permute-start.9 = (f32[3,64,128]{2,1,0:T(8,128)}, f32[3,64,128]{2,1,0:T(8,128)S(1)}, u32[]{:S(2)}, u32[]{:S(2)}) collective-permute-start(f32[3,64,128]{2,1,0:T(8,128)} %get-tuple-element.53), channel_id=1, source_target_pairs={{0,3},{1,2},{2,1},{3,0},{4,7},{5,6},{6,5},{7,4},{8,11},{9,10},{10,... | collective-permute-start | bytes 294920 | tf_op jit(solution)/shard_map/ppermute | solution.py:270
  55.6 7.8 %collective-permute-start.10 = (f32[3,64,128]{2,1,0:T(8,128)}, f32[3,64,128]{2,1,0:T(8,128)S(1)}, u32[]{:S(2)}, u32[]{:S(2)}) collective-permute-start(f32[3,64,128]{2,1,0:T(8,128)} %get-tuple-element.54), channel_id=1, source_target_pairs={{0,4},{1,5},{2,6},{3,7},{4,0},{5,1},{6,2},{7,3},{8,12},{9,13},{10,... | collective-permute-start | bytes 294920 | tf_op jit(solution)/shard_map/ppermute | solution.py:270
  56.9 12.7 %collective-permute-start.11 = (f32[3,64,128]{2,1,0:T(8,128)}, f32[3,64,128]{2,1,0:T(8,128)S(1)}, u32[]{:S(2)}, u32[]{:S(2)}) collective-permute-start(f32[3,64,128]{2,1,0:T(8,128)} %get-tuple-element.55), channel_id=1, source_target_pairs={{0,5},{1,4},{2,7},{3,6},{4,1},{5,0},{6,3},{7,2},{8,13},{9,12},{10,... | collective-permute-start | bytes 294920 | tf_op jit(solution)/shard_map/ppermute | solution.py:270
  58.3 17.4 %copy-start.14 = (f32[3,64,128]{2,1,0:T(8,128)}, f32[3,64,128]{2,1,0:T(8,128)S(1)}, u32[]{:S(2)}) copy-start(f32[3,64,128]{2,1,0:T(8,128)S(1)} %collective-permute-done.7.refs_1_) | copy-start | bytes 294916
  58.3 15.2 %collective-permute-start.12 = (f32[3,64,128]{2,1,0:T(8,128)}, f32[3,64,128]{2,1,0:T(8,128)S(1)}, u32[]{:S(2)}, u32[]{:S(2)}) collective-permute-start(f32[3,64,128]{2,1,0:T(8,128)} %get-tuple-element.56), channel_id=1, source_target_pairs={{0,6},{1,7},{2,4},{3,5},{4,2},{5,3},{6,0},{7,1},{8,14},{9,15},{10,... | collective-permute-start | bytes 294920 | tf_op jit(solution)/shard_map/ppermute | solution.py:270
  59.8 15.9 %copy-start.15 = (f32[3,64,128]{2,1,0:T(8,128)}, f32[3,64,128]{2,1,0:T(8,128)S(1)}, u32[]{:S(2)}) copy-start(f32[3,64,128]{2,1,0:T(8,128)S(1)} %collective-permute-done.8.refs_2_) | copy-start | bytes 294916
  59.8 15.9 %collective-permute-start.13 = (f32[3,64,128]{2,1,0:T(8,128)}, f32[3,64,128]{2,1,0:T(8,128)S(1)}, u32[]{:S(2)}, u32[]{:S(2)}) collective-permute-start(f32[3,64,128]{2,1,0:T(8,128)} %get-tuple-element.57), channel_id=1, source_target_pairs={{0,7},{1,6},{2,5},{3,4},{4,3},{5,2},{6,1},{7,0},{8,15},{9,14},{10,... | collective-permute-start | bytes 294920 | tf_op jit(solution)/shard_map/ppermute | solution.py:270
  61.6 14.1 %copy-start.16 = (f32[3,64,128]{2,1,0:T(8,128)}, f32[3,64,128]{2,1,0:T(8,128)S(1)}, u32[]{:S(2)}) copy-start(f32[3,64,128]{2,1,0:T(8,128)S(1)} %collective-permute-done.9.refs_3_) | copy-start | bytes 294916
  63.5 12.2 %copy-start.17 = (f32[3,64,128]{2,1,0:T(8,128)}, f32[3,64,128]{2,1,0:T(8,128)S(1)}, u32[]{:S(2)}) copy-start(f32[3,64,128]{2,1,0:T(8,128)S(1)} %collective-permute-done.10.refs_4_) | copy-start | bytes 294916
  69.7 6.1 %copy-start.18 = (f32[3,64,128]{2,1,0:T(8,128)}, f32[3,64,128]{2,1,0:T(8,128)S(1)}, u32[]{:S(2)}) copy-start(f32[3,64,128]{2,1,0:T(8,128)S(1)} %collective-permute-done.11.refs_5_) | copy-start | bytes 294916
  73.6 2.2 %copy-start.19 = (f32[3,64,128]{2,1,0:T(8,128)}, f32[3,64,128]{2,1,0:T(8,128)S(1)}, u32[]{:S(2)}) copy-start(f32[3,64,128]{2,1,0:T(8,128)S(1)} %collective-permute-done.12.refs_6_) | copy-start | bytes 294916
  75.7 0.6 copy-start.20
  80.4 9.4 %collective-permute-start.14 = (f32[3,64,128]{2,1,0:T(8,128)}, f32[3,64,128]{2,1,0:T(8,128)S(1)}, u32[]{:S(2)}, u32[]{:S(2)}) collective-permute-start(f32[3,64,128]{2,1,0:T(8,128)} %get-tuple-element.61), channel_id=1, source_target_pairs={{0,1},{1,0},{2,3},{3,2},{4,5},{5,4},{6,7},{7,6},{8,9},{9,8},{10,11... | collective-permute-start | bytes 294920 | tf_op jit(solution)/shard_map/ppermute | solution.py:270
  80.9 9.7 %collective-permute-start.15 = (f32[3,64,128]{2,1,0:T(8,128)}, f32[3,64,128]{2,1,0:T(8,128)S(1)}, u32[]{:S(2)}, u32[]{:S(2)}) collective-permute-start(f32[3,64,128]{2,1,0:T(8,128)} %get-tuple-element.62), channel_id=1, source_target_pairs={{0,2},{1,3},{2,0},{3,1},{4,6},{5,7},{6,4},{7,5},{8,10},{9,11},{10,... | collective-permute-start | bytes 294920 | tf_op jit(solution)/shard_map/ppermute | solution.py:270
  80.9 3.5 %collective-permute-start.23 = (f32[3,64]{1,0:T(4,128)}, f32[3,64]{1,0:T(4,128)S(1)}, u32[]{:S(2)}, u32[]{:S(2)}) collective-permute-start(f32[3,64]{1,0:T(4,128)} %get-tuple-element.68), channel_id=1, source_target_pairs={{0,24},{8,16},{16,8},{24,0},{1,25},{9,17},{17,9},{25,1},{2,26},{10... | collective-permute-start | bytes 2312 | tf_op jit(solution)/shard_map/ppermute | solution.py:277
  83.1 4.3 %collective-permute-start.22 = (f32[3,64]{1,0:T(4,128)}, f32[3,64]{1,0:T(4,128)S(1)}, u32[]{:S(2)}, u32[]{:S(2)}) collective-permute-start(f32[3,64]{1,0:T(4,128)} %get-tuple-element.68), channel_id=1, source_target_pairs={{0,16},{8,24},{16,0},{24,8},{1,17},{9,25},{17,1},{25,9},{2,18},{10... | collective-permute-start | bytes 2312 | tf_op jit(solution)/shard_map/ppermute | solution.py:277
  83.3 4.3 %collective-permute-start.21 = (f32[3,64]{1,0:T(4,128)}, f32[3,64]{1,0:T(4,128)S(1)}, u32[]{:S(2)}, u32[]{:S(2)}) collective-permute-start(f32[3,64]{1,0:T(4,128)} %get-tuple-element.68), channel_id=1, source_target_pairs={{0,8},{8,0},{16,24},{24,16},{1,9},{9,1},{17,25},{25,17},{2,10},{10... | collective-permute-start | bytes 2312 | tf_op jit(solution)/shard_map/ppermute | solution.py:277
  84.4 8.6 %collective-permute-start.16 = (f32[3,64,128]{2,1,0:T(8,128)}, f32[3,64,128]{2,1,0:T(8,128)S(1)}, u32[]{:S(2)}, u32[]{:S(2)}) collective-permute-start(f32[3,64,128]{2,1,0:T(8,128)} %get-tuple-element.63), channel_id=1, source_target_pairs={{0,3},{1,2},{2,1},{3,0},{4,7},{5,6},{6,5},{7,4},{8,11},{9,10},{10,... | collective-permute-start | bytes 294920 | tf_op jit(solution)/shard_map/ppermute | solution.py:270
  87.4 5.7 %collective-permute-start.17 = (f32[3,64,128]{2,1,0:T(8,128)}, f32[3,64,128]{2,1,0:T(8,128)S(1)}, u32[]{:S(2)}, u32[]{:S(2)}) collective-permute-start(f32[3,64,128]{2,1,0:T(8,128)} %get-tuple-element.64), channel_id=1, source_target_pairs={{0,4},{1,5},{2,6},{3,7},{4,0},{5,1},{6,2},{7,3},{8,12},{9,13},{10,... | collective-permute-start | bytes 294920 | tf_op jit(solution)/shard_map/ppermute | solution.py:270
  87.6 12.8 %collective-permute-start.18 = (f32[3,64,128]{2,1,0:T(8,128)}, f32[3,64,128]{2,1,0:T(8,128)S(1)}, u32[]{:S(2)}, u32[]{:S(2)}) collective-permute-start(f32[3,64,128]{2,1,0:T(8,128)} %get-tuple-element.65), channel_id=1, source_target_pairs={{0,5},{1,4},{2,7},{3,6},{4,1},{5,0},{6,3},{7,2},{8,13},{9,12},{10,... | collective-permute-start | bytes 294920 | tf_op jit(solution)/shard_map/ppermute | solution.py:270
  89.9 16.8 %copy-start = (f32[3,64,128]{2,1,0:T(8,128)}, f32[3,64,128]{2,1,0:T(8,128)S(1)}, u32[]{:S(2)}) copy-start(f32[3,64,128]{2,1,0:T(8,128)S(1)} %collective-permute-done.14.refs_1_) | copy-start | bytes 294916
  89.9 13.6 %collective-permute-start.19 = (f32[3,64,128]{2,1,0:T(8,128)}, f32[3,64,128]{2,1,0:T(8,128)S(1)}, u32[]{:S(2)}, u32[]{:S(2)}) collective-permute-start(f32[3,64,128]{2,1,0:T(8,128)} %get-tuple-element.66), channel_id=1, source_target_pairs={{0,6},{1,7},{2,4},{3,5},{4,2},{5,3},{6,0},{7,1},{8,14},{9,15},{10,... | collective-permute-start | bytes 294920 | tf_op jit(solution)/shard_map/ppermute | solution.py:270
  90.6 16.1 %copy-start.1 = (f32[3,64,128]{2,1,0:T(8,128)}, f32[3,64,128]{2,1,0:T(8,128)S(1)}, u32[]{:S(2)}) copy-start(f32[3,64,128]{2,1,0:T(8,128)S(1)} %collective-permute-done.15.refs_2_) | copy-start | bytes 294916
  90.6 16.1 %collective-permute-start.20 = (f32[3,64,128]{2,1,0:T(8,128)}, f32[3,64,128]{2,1,0:T(8,128)S(1)}, u32[]{:S(2)}, u32[]{:S(2)}) collective-permute-start(f32[3,64,128]{2,1,0:T(8,128)} %get-tuple-element.67), channel_id=1, source_target_pairs={{0,7},{1,6},{2,5},{3,4},{4,3},{5,2},{6,1},{7,0},{8,15},{9,14},{10,... | collective-permute-start | bytes 294920 | tf_op jit(solution)/shard_map/ppermute | solution.py:270
  93.0 13.7 %copy-start.2 = (f32[3,64,128]{2,1,0:T(8,128)}, f32[3,64,128]{2,1,0:T(8,128)S(1)}, u32[]{:S(2)}) copy-start(f32[3,64,128]{2,1,0:T(8,128)S(1)} %collective-permute-done.16.refs_3_) | copy-start | bytes 294916
  93.0 13.7 %copy-start.3 = (f32[3,64,128]{2,1,0:T(8,128)}, f32[3,64,128]{2,1,0:T(8,128)S(1)}, u32[]{:S(2)}) copy-start(f32[3,64,128]{2,1,0:T(8,128)S(1)} %collective-permute-done.17.refs_4_) | copy-start | bytes 294916
  100.4 6.4 %copy-start.4 = (f32[3,64,128]{2,1,0:T(8,128)}, f32[3,64,128]{2,1,0:T(8,128)S(1)}, u32[]{:S(2)}) copy-start(f32[3,64,128]{2,1,0:T(8,128)S(1)} %collective-permute-done.18.refs_5_) | copy-start | bytes 294916
  103.5 3.2 %copy-start.5 = (f32[3,64,128]{2,1,0:T(8,128)}, f32[3,64,128]{2,1,0:T(8,128)S(1)}, u32[]{:S(2)}) copy-start(f32[3,64,128]{2,1,0:T(8,128)S(1)} %collective-permute-done.19.refs_6_) | copy-start | bytes 294916
  106.7 0.6 copy-start.6

commit v2 on v1

--- a/solution.py
+++ b/solution.py
@@ -266,9 +266,14 @@
 
 def exchange(blocks):
     devices = len(blocks)
-    return [blocks[0]] + [
-        lax.ppermute(blocks[step], "col", [(i, i ^ step) for i in range(devices)]) for step in range(1, devices)
-    ]
+    arrived = list(blocks)
+    for step in crossing_first(devices):
+        arrived[step] = lax.ppermute(blocks[step], "col", [(i, i ^ step) for i in range(devices)])
+    return arrived
+
+
+def crossing_first(devices):
+    return sorted(range(1, devices), key=lambda step: -((step.bit_length() << 16) + (step >> 1 << 1)))
 
 
 def sum_over_groups(value):

time: 111 us -> 111 us (level)
  no operation moved by 1% of the time
where the time goes in v2:
time: 111 us; the launch traced here: 110 us
  waiting for transfers between devices  55.1 us (50%)
  starting transfers between devices  26.7 us (24%)
  Pallas kernels  24.6 us (22%)
  local copies, waits for them, and re-layouts  1.9 us (2%)
  other arithmetic  1.26 us (1%)
    ppermute x21, waiting for transfers between devices, exchange(): lax.ppermute(blocks[step], 'col', [(i, i ^ step) for i in range(devices)])  54.2 us
    ppermute x21, starting transfers between devices, exchange(): lax.ppermute(blocks[step], 'col', [(i, i ^ step) for i in range(devices)])  24.1 us
    pallas_call x1, Pallas kernels, on_device(): call(functools.partial(solve_kernel, devices), [shaped(back)] * devices +...  6.85 us
    pallas_call x1, Pallas kernels, on_device(): call(operators_kernel, [operator, operator, operator, shaped((depth, lane...  4.49 us
    pallas_call x1, Pallas kernels, on_device(): call(functools.partial(pack_kernel, devices), [shaped(sent)] * devices, [...  4.42 us
    pallas_call x1, Pallas kernels, on_device(): call(functools.partial(unpack_kernel, devices, chunk, first), [shaped(sta...  4.1 us
    pallas_call x1, Pallas kernels, on_device(): call(functools.partial(assemble_kernel, devices, first), shaped((comps, d...  3.04 us
    ppermute x3, starting transfers between devices, sum_over_groups(): lax.ppermute(value, 'grp', [(i, i ^ step) for i in range(groups)])  2.65 us
  transfers between devices with their start and end apart: 24, of which 12 were waited for; matrix products, arithmetic and copies ran while one was open for 1% of the time, Pallas kernels for 4%

profile of v2, /device:TPU:9, one launch (start us, length us, event | category | flops | bytes accessed | tf_op | source)
XLA Modules:
  0.0 110.4 jit_solution(1121918629943893899)
XLA Ops:
  0.6 1.7 %shard_map.121 = (s32[8,512]{1,0:T(8,128)}, f32[8,128]{1,0:T(8,128)}) custom-call(s32[1]{0:T(128)} %bitcast.me_ref, s32[1,512]{1,0:T(1,128)} %bitcast.3, s32[2,512]{1,0:T(2,128)} %modes_ref.5), custom_call_target="tpu_custom_call" | custom-call | flops 1000000 | bytes 100000 | tf_op jit(solution)/shard_map/pallas_call | solution.py:311
  2.4 4.4 %shard_map.123 = (f32[2,3,64,128]{3,2,1,0:T(8,128)}, f32[2,3,64,128]{3,2,1,0:T(8,128)}, f32[2,3,64,128]{3,2,1,0:T(8,128)}, f32[2,3,64,128]{3,2,1,0:T(8,128)}, f3...) custom-call(s32[8,512]{1,0:T(8,128)} %get-tuple-element.36.info_ref,, ...), custom_call_target="tpu_custom_call" | custom-call | flops 1207959552 | bytes 3932160 | tf_op jit(solution)/shard_map/pallas_call | solution.py:329
  6.8 0.7 collective-permute-start
  7.5 0.0 collective-permute-start.1
  7.5 1.6 %collective-permute-start.2 = (f32[2,3,64,128]{3,2,1,0:T(8,128)}, f32[2,3,64,128]{3,2,1,0:T(8,128)S(1)}, u32[]{:S(2)}, u32[]{:S(2)}) collective-permute-start(f32[2,3,64,128]{3,2,1,0:T(8,128)} %get-tuple-element.45), channel_id=1, source_target_pairs={{0,3},{1,2},{2,1},{3,0},{4,7},{5,6},{6,5},{7,4},{8,11},{9,10},{10,... | collective-permute-start | bytes 589832 | tf_op jit(solution)/shard_map/ppermute | solution.py:271
  9.1 2.3 %collective-permute-start.3 = (f32[2,3,64,128]{3,2,1,0:T(8,128)}, f32[2,3,64,128]{3,2,1,0:T(8,128)S(1)}, u32[]{:S(2)}, u32[]{:S(2)}) collective-permute-start(f32[2,3,64,128]{3,2,1,0:T(8,128)} %get-tuple-element.46), channel_id=1, source_target_pairs={{0,4},{1,5},{2,6},{3,7},{4,0},{5,1},{6,2},{7,3},{8,12},{9,13},{10,... | collective-permute-start | bytes 589832 | tf_op jit(solution)/shard_map/ppermute | solution.py:271
  11.4 0.4 collective-permute-start.4
  11.9 0.0 collective-permute-done.refs_1_
  11.9 1.3 %collective-permute-start.5 = (f32[2,3,64,128]{3,2,1,0:T(8,128)}, f32[2,3,64,128]{3,2,1,0:T(8,128)S(1)}, u32[]{:S(2)}, u32[]{:S(2)}) collective-permute-start(f32[2,3,64,128]{3,2,1,0:T(8,128)} %get-tuple-element.48), channel_id=1, source_target_pairs={{0,6},{1,7},{2,4},{3,5},{4,2},{5,3},{6,0},{7,1},{8,14},{9,15},{10,... | collective-permute-start | bytes 589832 | tf_op jit(solution)/shard_map/ppermute | solution.py:271
  13.2 7.1 %collective-permute-done.1.refs_2_ = f32[2,3,64,128]{3,2,1,0:T(8,128)S(1)} collective-permute-done((f32[2,3,64,128]{3,2,1,0:T(8,128)}, f32[2,3,64,128]{3,2,1,0:T(8,128)S(1)}, u32[]{:S(2)}, u32[]{:S(2)}) %collective-permute-start.1) | collective-permute-done | bytes 196640 | tf_op jit(solution)/shard_map/ppermute | solution.py:271
  20.3 1.2 %collective-permute-start.6 = (f32[2,3,64,128]{3,2,1,0:T(8,128)}, f32[2,3,64,128]{3,2,1,0:T(8,128)S(1)}, u32[]{:S(2)}, u32[]{:S(2)}) collective-permute-start(f32[2,3,64,128]{3,2,1,0:T(8,128)} %get-tuple-element.49), channel_id=1, source_target_pairs={{0,7},{1,6},{2,5},{3,4},{4,3},{5,2},{6,1},{7,0},{8,15},{9,14},{10,... | collective-permute-start | bytes 589832 | tf_op jit(solution)/shard_map/ppermute | solution.py:271
  21.5 4.5 %shard_map.122 = (bf16[512,1536]{1,0:T(8,128)(2,1)}, bf16[512,1536]{1,0:T(8,128)(2,1)}, bf16[512,1536]{1,0:T(8,128)(2,1)}, f32[512,128]{1,0:T(8,128)}) custom-call(f32[512,512]{1,0:T(8,128)} %deriv_ref.1, f32[512,512]{1,0:T(8,128)} %inverse_ref.1, f32[512,512]{1,0:T(8,128)} %basis_ref.1, f32[1,512]{1,0:T(1,128)} %bitcast.4), custom_call_target="tpu_custom_call" | custom-call | flops 1000000 | bytes 7864320 | tf_op jit(solution)/shard_map/pallas_call | solution.py:341
  26.0 0.0 collective-permute-done.2.refs_3_
  26.0 0.0 collective-permute-done.3.refs_4_
  26.0 10.9 %collective-permute-done.4.refs_5_ = f32[2,3,64,128]{3,2,1,0:T(8,128)S(1)} collective-permute-done((f32[2,3,64,128]{3,2,1,0:T(8,128)}, f32[2,3,64,128]{3,2,1,0:T(8,128)S(1)}, u32[]{:S(2)}, u32[]{:S(2)}) %collective-permute-start.4) | collective-permute-done | bytes 196640 | tf_op jit(solution)/shard_map/ppermute | solution.py:271
  36.9 4.2 %collective-permute-done.5.refs_6_ = f32[2,3,64,128]{3,2,1,0:T(8,128)S(1)} collective-permute-done((f32[2,3,64,128]{3,2,1,0:T(8,128)}, f32[2,3,64,128]{3,2,1,0:T(8,128)S(1)}, u32[]{:S(2)}, u32[]{:S(2)}) %collective-permute-start.5) | collective-permute-done | bytes 196640 | tf_op jit(solution)/shard_map/ppermute | solution.py:271
  41.2 4.2 %collective-permute-done.6.refs_7_ = f32[2,3,64,128]{3,2,1,0:T(8,128)S(1)} collective-permute-done((f32[2,3,64,128]{3,2,1,0:T(8,128)}, f32[2,3,64,128]{3,2,1,0:T(8,128)S(1)}, u32[]{:S(2)}, u32[]{:S(2)}) %collective-permute-start.6) | collective-permute-done | bytes 196640 | tf_op jit(solution)/shard_map/ppermute | solution.py:271
  45.4 0.6 copy-done.13
  46.0 6.8 %shard_map.124 = (f32[3,64,128]{2,1,0:T(8,128)}, f32[3,64,128]{2,1,0:T(8,128)}, f32[3,64,128]{2,1,0:T(8,128)}, f32[3,64,128]{2,1,0:T(8,128)}, f32[3,64,128]{2,1,...) custom-call(s32[1]{0:T(128)} %bitcast.me_ref, ...), custom_call_target="tpu_custom_call" | custom-call | flops 1811939328 | bytes 7864320 | tf_op jit(solution)/shard_map/pallas_call | solution.py:354
  52.9 1.0 collective-permute-start.7
  53.9 0.0 collective-permute-start.8
  53.9 1.7 %collective-permute-start.9 = (f32[3,64,128]{2,1,0:T(8,128)}, f32[3,64,128]{2,1,0:T(8,128)S(1)}, u32[]{:S(2)}, u32[]{:S(2)}) collective-permute-start(f32[3,64,128]{2,1,0:T(8,128)} %get-tuple-element.53), channel_id=1, source_target_pairs={{0,3},{1,2},{2,1},{3,0},{4,7},{5,6},{6,5},{7,4},{8,11},{9,10},{10,... | collective-permute-start | bytes 294920 | tf_op jit(solution)/shard_map/ppermute | solution.py:271
  55.6 1.3 %collective-permute-start.10 = (f32[3,64,128]{2,1,0:T(8,128)}, f32[3,64,128]{2,1,0:T(8,128)S(1)}, u32[]{:S(2)}, u32[]{:S(2)}) collective-permute-start(f32[3,64,128]{2,1,0:T(8,128)} %get-tuple-element.54), channel_id=1, source_target_pairs={{0,4},{1,5},{2,6},{3,7},{4,0},{5,1},{6,2},{7,3},{8,12},{9,13},{10,... | collective-permute-start | bytes 294920 | tf_op jit(solution)/shard_map/ppermute | solution.py:271
  56.9 1.4 %collective-permute-start.11 = (f32[3,64,128]{2,1,0:T(8,128)}, f32[3,64,128]{2,1,0:T(8,128)S(1)}, u32[]{:S(2)}, u32[]{:S(2)}) collective-permute-start(f32[3,64,128]{2,1,0:T(8,128)} %get-tuple-element.55), channel_id=1, source_target_pairs={{0,5},{1,4},{2,7},{3,6},{4,1},{5,0},{6,3},{7,2},{8,13},{9,12},{10,... | collective-permute-start | bytes 294920 | tf_op jit(solution)/shard_map/ppermute | solution.py:271
  58.3 1.5 %collective-permute-start.12 = (f32[3,64,128]{2,1,0:T(8,128)}, f32[3,64,128]{2,1,0:T(8,128)S(1)}, u32[]{:S(2)}, u32[]{:S(2)}) collective-permute-start(f32[3,64,128]{2,1,0:T(8,128)} %get-tuple-element.56), channel_id=1, source_target_pairs={{0,6},{1,7},{2,4},{3,5},{4,2},{5,3},{6,0},{7,1},{8,14},{9,15},{10,... | collective-permute-start | bytes 294920 | tf_op jit(solution)/shard_map/ppermute | solution.py:271
  59.8 1.8 %collective-permute-start.13 = (f32[3,64,128]{2,1,0:T(8,128)}, f32[3,64,128]{2,1,0:T(8,128)S(1)}, u32[]{:S(2)}, u32[]{:S(2)}) collective-permute-start(f32[3,64,128]{2,1,0:T(8,128)} %get-tuple-element.57), channel_id=1, source_target_pairs={{0,7},{1,6},{2,5},{3,4},{4,3},{5,2},{6,1},{7,0},{8,15},{9,14},{10,... | collective-permute-start | bytes 294920 | tf_op jit(solution)/shard_map/ppermute | solution.py:271
  61.6 1.9 %collective-permute-done.10.refs_4_ = f32[3,64,128]{2,1,0:T(8,128)S(1)} collective-permute-done((f32[3,64,128]{2,1,0:T(8,128)}, f32[3,64,128]{2,1,0:T(8,128)S(1)}, u32[]{:S(2)}, u32[]{:S(2)}) %collective-permute-start.10) | collective-permute-done | bytes 98336 | tf_op jit(solution)/shard_map/ppermute | solution.py:271
  63.5 6.2 %collective-permute-done.11.refs_5_ = f32[3,64,128]{2,1,0:T(8,128)S(1)} collective-permute-done((f32[3,64,128]{2,1,0:T(8,128)}, f32[3,64,128]{2,1,0:T(8,128)S(1)}, u32[]{:S(2)}, u32[]{:S(2)}) %collective-permute-start.11) | collective-permute-done | bytes 98336 | tf_op jit(solution)/shard_map/ppermute | solution.py:271
  69.7 3.9 %collective-permute-done.12.refs_6_ = f32[3,64,128]{2,1,0:T(8,128)S(1)} collective-permute-done((f32[3,64,128]{2,1,0:T(8,128)}, f32[3,64,128]{2,1,0:T(8,128)S(1)}, u32[]{:S(2)}, u32[]{:S(2)}) %collective-permute-start.12) | collective-permute-done | bytes 98336 | tf_op jit(solution)/shard_map/ppermute | solution.py:271
  73.6 2.1 %collective-permute-done.13.refs_7_ = f32[3,64,128]{2,1,0:T(8,128)S(1)} collective-permute-done((f32[3,64,128]{2,1,0:T(8,128)}, f32[3,64,128]{2,1,0:T(8,128)S(1)}, u32[]{:S(2)}, u32[]{:S(2)}) %collective-permute-start.13) | collective-permute-done | bytes 98336 | tf_op jit(solution)/shard_map/ppermute | solution.py:271
  75.7 0.6 copy-done.20
  76.3 4.1 %shard_map.125 = (f32[6,64,512]{2,1,0:T(8,128)}, f32[3,64]{1,0:T(4,128)}, f32[3,64,128]{2,1,0:T(8,128)}, f32[3,64,128]{2,1,0:T(8,128)}, f32[3,64,128]{2,1,0:T(8,...) custom-call(s32[8,512]{1,0:T(8,128)} %get-tuple-element.36.info_ref,, ...), custom_call_target="tpu_custom_call" | custom-call | flops 1207959552 | bytes 4718592 | tf_op jit(solution)/shard_map/pallas_call | solution.py:371
  80.4 0.4 collective-permute-start.14
  80.9 2.2 %collective-permute-start.23 = (f32[3,64]{1,0:T(4,128)}, f32[3,64]{1,0:T(4,128)S(1)}, u32[]{:S(2)}, u32[]{:S(2)}) collective-permute-start(f32[3,64]{1,0:T(4,128)} %get-tuple-element.68), channel_id=1, source_target_pairs={{0,24},{8,16},{16,8},{24,0},{1,25},{9,17},{17,9},{25,1},{2,26},{10... | collective-permute-start | bytes 2312 | tf_op jit(solution)/shard_map/ppermute | solution.py:282
  83.1 0.2 collective-permute-start.22
  83.3 0.3 collective-permute-start.21
  83.5 0.9 collective-permute-done.23
  84.4 2.9 %collective-permute-start.16 = (f32[3,64,128]{2,1,0:T(8,128)}, f32[3,64,128]{2,1,0:T(8,128)S(1)}, u32[]{:S(2)}, u32[]{:S(2)}) collective-permute-start(f32[3,64,128]{2,1,0:T(8,128)} %get-tuple-element.63), channel_id=1, source_target_pairs={{0,3},{1,2},{2,1},{3,0},{4,7},{5,6},{6,5},{7,4},{8,11},{9,10},{10,... | collective-permute-start | bytes 294920 | tf_op jit(solution)/shard_map/ppermute | solution.py:271
  87.4 0.2 collective-permute-start.17
  87.6 2.3 %collective-permute-start.18 = (f32[3,64,128]{2,1,0:T(8,128)}, f32[3,64,128]{2,1,0:T(8,128)S(1)}, u32[]{:S(2)}, u32[]{:S(2)}) collective-permute-start(f32[3,64,128]{2,1,0:T(8,128)} %get-tuple-element.65), channel_id=1, source_target_pairs={{0,5},{1,4},{2,7},{3,6},{4,1},{5,0},{6,3},{7,2},{8,13},{9,12},{10,... | collective-permute-start | bytes 294920 | tf_op jit(solution)/shard_map/ppermute | solution.py:271
  89.9 0.7 collective-permute-start.19
  90.6 1.2 %collective-permute-start.20 = (f32[3,64,128]{2,1,0:T(8,128)}, f32[3,64,128]{2,1,0:T(8,128)S(1)}, u32[]{:S(2)}, u32[]{:S(2)}) collective-permute-start(f32[3,64,128]{2,1,0:T(8,128)} %get-tuple-element.67), channel_id=1, source_target_pairs={{0,7},{1,6},{2,5},{3,4},{4,3},{5,2},{6,1},{7,0},{8,15},{9,14},{10,... | collective-permute-start | bytes 294920 | tf_op jit(solution)/shard_map/ppermute | solution.py:271
  91.8 1.3 %add_add_fusion = f32[3,64]{1,0:T(4,128)} fusion(f32[3,64]{1,0:T(4,128)S(1)} %collective-permute-done.22, f32[3,64]{1,0:T(4,128)S(1)} %collective-permute-done.23, f32[3,64]{1,0:T(4,128)} %get-tuple-element.68, f32[3,64]{1,0:T(4,128)S(1)} %collective-permute-done.21), kind=kLoop, calls=%fused_computation | loop fusion | flops 576 | bytes 3840 | tf_op jit(solution)/shard_map/add | solution.py:285
  93.1 7.3 %collective-permute-done.18.refs_5_ = f32[3,64,128]{2,1,0:T(8,128)S(1)} collective-permute-done((f32[3,64,128]{2,1,0:T(8,128)}, f32[3,64,128]{2,1,0:T(8,128)S(1)}, u32[]{:S(2)}, u32[]{:S(2)}) %collective-permute-start.18) | collective-permute-done | bytes 98336 | tf_op jit(solution)/shard_map/ppermute | solution.py:271
  100.4 3.2 %collective-permute-done.19.refs_6_ = f32[3,64,128]{2,1,0:T(8,128)S(1)} collective-permute-done((f32[3,64,128]{2,1,0:T(8,128)}, f32[3,64,128]{2,1,0:T(8,128)S(1)}, u32[]{:S(2)}, u32[]{:S(2)}) %collective-permute-start.19) | collective-permute-done | bytes 98336 | tf_op jit(solution)/shard_map/ppermute | solution.py:271
  103.5 3.2 %collective-permute-done.20.refs_7_ = f32[3,64,128]{2,1,0:T(8,128)S(1)} collective-permute-done((f32[3,64,128]{2,1,0:T(8,128)}, f32[3,64,128]{2,1,0:T(8,128)S(1)}, u32[]{:S(2)}, u32[]{:S(2)}) %collective-permute-start.20) | collective-permute-done | bytes 98336 | tf_op jit(solution)/shard_map/ppermute | solution.py:271
  106.7 0.6 copy-done.6
  107.3 3.0 %shard_map.126 = f32[6,512,128]{2,1,0:T(8,128)} custom-call(s32[1]{0:T(128)} %bitcast.me_ref, s32[8,512]{1,0:T(8,128)} %get-tuple-element.36.info_ref, f32[3,512,128]{2,1,0:T(8,128)} %get-tuple-element.59.solved_ref, f32[3,64,128]{2,1,0:T(8,128)} %get-tuple-element.60.refs_0_, f32[3,64,128]{2,1,0:T(8,128)} %copy-done, f32[3,64,128]{2,1,0:T(8,128)} %copy-done.1, ...), custom_call_target="tpu_custom_call" | custom-call | flops 1000000 | bytes 3145728 | tf_op jit(solution)/shard_map/pallas_call | solution.py:389
  (49 shorter events, 0.1 us)
Async XLA Ops:
  6.8 5.1 %collective-permute-start = (f32[2,3,64,128]{3,2,1,0:T(8,128)}, f32[2,3,64,128]{3,2,1,0:T(8,128)S(1)}, u32[]{:S(2)}, u32[]{:S(2)}) collective-permute-start(f32[2,3,64,128]{3,2,1,0:T(8,128)} %get-tuple-element.43), channel_id=1, source_target_pairs={{0,1},{1,0},{2,3},{3,2},{4,5},{5,4},{6,7},{7,6},{8,9},{9,8},{10,11... | collective-permute-start | bytes 589832 | tf_op jit(solution)/shard_map/ppermute | solution.py:271
  7.5 12.8 %collective-permute-start.1 = (f32[2,3,64,128]{3,2,1,0:T(8,128)}, f32[2,3,64,128]{3,2,1,0:T(8,128)S(1)}, u32[]{:S(2)}, u32[]{:S(2)}) collective-permute-start(f32[2,3,64,128]{3,2,1,0:T(8,128)} %get-tuple-element.44), channel_id=1, source_target_pairs={{0,2},{1,3},{2,0},{3,1},{4,6},{5,7},{6,4},{7,5},{8,10},{9,11},{10,... | collective-permute-start | bytes 589832 | tf_op jit(solution)/shard_map/ppermute | solution.py:271
  7.5 18.5 %collective-permute-start.2 = (f32[2,3,64,128]{3,2,1,0:T(8,128)}, f32[2,3,64,128]{3,2,1,0:T(8,128)S(1)}, u32[]{:S(2)}, u32[]{:S(2)}) collective-permute-start(f32[2,3,64,128]{3,2,1,0:T(8,128)} %get-tuple-element.45), channel_id=1, source_target_pairs={{0,3},{1,2},{2,1},{3,0},{4,7},{5,6},{6,5},{7,4},{8,11},{9,10},{10,... | collective-permute-start | bytes 589832 | tf_op jit(solution)/shard_map/ppermute | solution.py:271
  9.1 16.9 %collective-permute-start.3 = (f32[2,3,64,128]{3,2,1,0:T(8,128)}, f32[2,3,64,128]{3,2,1,0:T(8,128)S(1)}, u32[]{:S(2)}, u32[]{:S(2)}) collective-permute-start(f32[2,3,64,128]{3,2,1,0:T(8,128)} %get-tuple-element.46), channel_id=1, source_target_pairs={{0,4},{1,5},{2,6},{3,7},{4,0},{5,1},{6,2},{7,3},{8,12},{9,13},{10,... | collective-permute-start | bytes 589832 | tf_op jit(solution)/shard_map/ppermute | solution.py:271
  11.4 25.5 %collective-permute-start.4 = (f32[2,3,64,128]{3,2,1,0:T(8,128)}, f32[2,3,64,128]{3,2,1,0:T(8,128)S(1)}, u32[]{:S(2)}, u32[]{:S(2)}) collective-permute-start(f32[2,3,64,128]{3,2,1,0:T(8,128)} %get-tuple-element.47), channel_id=1, source_target_pairs={{0,5},{1,4},{2,7},{3,6},{4,1},{5,0},{6,3},{7,2},{8,13},{9,12},{10,... | collective-permute-start | bytes 589832 | tf_op jit(solution)/shard_map/ppermute | solution.py:271
  11.9 14.1 %copy-start.7 = (f32[2,3,64,128]{3,2,1,0:T(8,128)}, f32[2,3,64,128]{3,2,1,0:T(8,128)S(1)}, u32[]{:S(2)}) copy-start(f32[2,3,64,128]{3,2,1,0:T(8,128)S(1)} %collective-permute-done.refs_1_) | copy-start | bytes 589828
  11.9 29.3 %collective-permute-start.5 = (f32[2,3,64,128]{3,2,1,0:T(8,128)}, f32[2,3,64,128]{3,2,1,0:T(8,128)S(1)}, u32[]{:S(2)}, u32[]{:S(2)}) collective-permute-start(f32[2,3,64,128]{3,2,1,0:T(8,128)} %get-tuple-element.48), channel_id=1, source_target_pairs={{0,6},{1,7},{2,4},{3,5},{4,2},{5,3},{6,0},{7,1},{8,14},{9,15},{10,... | collective-permute-start | bytes 589832 | tf_op jit(solution)/shard_map/ppermute | solution.py:271
  20.3 5.7 %copy-start.8 = (f32[2,3,64,128]{3,2,1,0:T(8,128)}, f32[2,3,64,128]{3,2,1,0:T(8,128)S(1)}, u32[]{:S(2)}) copy-start(f32[2,3,64,128]{3,2,1,0:T(8,128)S(1)} %collective-permute-done.1.refs_2_) | copy-start | bytes 589828
  20.3 25.1 %collective-permute-start.6 = (f32[2,3,64,128]{3,2,1,0:T(8,128)}, f32[2,3,64,128]{3,2,1,0:T(8,128)S(1)}, u32[]{:S(2)}, u32[]{:S(2)}) collective-permute-start(f32[2,3,64,128]{3,2,1,0:T(8,128)} %get-tuple-element.49), channel_id=1, source_target_pairs={{0,7},{1,6},{2,5},{3,4},{4,3},{5,2},{6,1},{7,0},{8,15},{9,14},{10,... | collective-permute-start | bytes 589832 | tf_op jit(solution)/shard_map/ppermute | solution.py:271
  26.0 19.4 %copy-start.9 = (f32[2,3,64,128]{3,2,1,0:T(8,128)}, f32[2,3,64,128]{3,2,1,0:T(8,128)S(1)}, u32[]{:S(2)}) copy-start(f32[2,3,64,128]{3,2,1,0:T(8,128)S(1)} %collective-permute-done.2.refs_3_) | copy-start | bytes 589828
  26.0 19.3 %copy-start.10 = (f32[2,3,64,128]{3,2,1,0:T(8,128)}, f32[2,3,64,128]{3,2,1,0:T(8,128)S(1)}, u32[]{:S(2)}) copy-start(f32[2,3,64,128]{3,2,1,0:T(8,128)S(1)} %collective-permute-done.3.refs_4_) | copy-start | bytes 589828
  36.9 8.4 %copy-start.11 = (f32[2,3,64,128]{3,2,1,0:T(8,128)}, f32[2,3,64,128]{3,2,1,0:T(8,128)S(1)}, u32[]{:S(2)}) copy-start(f32[2,3,64,128]{3,2,1,0:T(8,128)S(1)} %collective-permute-done.4.refs_5_) | copy-start | bytes 589828
  41.2 4.2 %copy-start.12 = (f32[2,3,64,128]{3,2,1,0:T(8,128)}, f32[2,3,64,128]{3,2,1,0:T(8,128)S(1)}, u32[]{:S(2)}) copy-start(f32[2,3,64,128]{3,2,1,0:T(8,128)S(1)} %collective-permute-done.5.refs_6_) | copy-start | bytes 589828
  45.4 0.7 copy-start.13
  52.9 5.4 %collective-permute-start.7 = (f32[3,64,128]{2,1,0:T(8,128)}, f32[3,64,128]{2,1,0:T(8,128)S(1)}, u32[]{:S(2)}, u32[]{:S(2)}) collective-permute-start(f32[3,64,128]{2,1,0:T(8,128)} %get-tuple-element.51), channel_id=1, source_target_pairs={{0,1},{1,0},{2,3},{3,2},{4,5},{5,4},{6,7},{7,6},{8,9},{9,8},{10,11... | collective-permute-start | bytes 294920 | tf_op jit(solution)/shard_map/ppermute | solution.py:271
  53.9 5.9 %collective-permute-start.8 = (f32[3,64,128]{2,1,0:T(8,128)}, f32[3,64,128]{2,1,0:T(8,128)S(1)}, u32[]{:S(2)}, u32[]{:S(2)}) collective-permute-start(f32[3,64,128]{2,1,0:T(8,128)} %get-tuple-element.52), channel_id=1, source_target_pairs={{0,2},{1,3},{2,0},{3,1},{4,6},{5,7},{6,4},{7,5},{8,10},{9,11},{10,... | collective-permute-start | bytes 294920 | tf_op jit(solution)/shard_map/ppermute | solution.py:271
  53.9 7.7 %collective-permute-start.9 = (f32[3,64,128]{2,1,0:T(8,128)}, f32[3,64,128]{2,1,0:T(8,128)S(1)}, u32[]{:S(2)}, u32[]{:S(2)}) collective-permute-start(f32[3,64,128]{2,1,0:T(8,128)} %get-tuple-element.53), channel_id=1, source_target_pairs={{0,3},{1,2},{2,1},{3,0},{4,7},{5,6},{6,5},{7,4},{8,11},{9,10},{10,... | collective-permute-start | bytes 294920 | tf_op jit(solution)/shard_map/ppermute | solution.py:271
  55.6 7.8 %collective-permute-start.10 = (f32[3,64,128]{2,1,0:T(8,128)}, f32[3,64,128]{2,1,0:T(8,128)S(1)}, u32[]{:S(2)}, u32[]{:S(2)}) collective-permute-start(f32[3,64,128]{2,1,0:T(8,128)} %get-tuple-element.54), channel_id=1, source_target_pairs={{0,4},{1,5},{2,6},{3,7},{4,0},{5,1},{6,2},{7,3},{8,12},{9,13},{10,... | collective-permute-start | bytes 294920 | tf_op jit(solution)/shard_map/ppermute | solution.py:271
  56.9 12.7 %collective-permute-start.11 = (f32[3,64,128]{2,1,0:T(8,128)}, f32[3,64,128]{2,1,0:T(8,128)S(1)}, u32[]{:S(2)}, u32[]{:S(2)}) collective-permute-start(f32[3,64,128]{2,1,0:T(8,128)} %get-tuple-element.55), channel_id=1, source_target_pairs={{0,5},{1,4},{2,7},{3,6},{4,1},{5,0},{6,3},{7,2},{8,13},{9,12},{10,... | collective-permute-start | bytes 294920 | tf_op jit(solution)/shard_map/ppermute | solution.py:271
  58.3 17.4 %copy-start.14 = (f32[3,64,128]{2,1,0:T(8,128)}, f32[3,64,128]{2,1,0:T(8,128)S(1)}, u32[]{:S(2)}) copy-start(f32[3,64,128]{2,1,0:T(8,128)S(1)} %collective-permute-done.7.refs_1_) | copy-start | bytes 294916
  58.3 15.2 %collective-permute-start.12 = (f32[3,64,128]{2,1,0:T(8,128)}, f32[3,64,128]{2,1,0:T(8,128)S(1)}, u32[]{:S(2)}, u32[]{:S(2)}) collective-permute-start(f32[3,64,128]{2,1,0:T(8,128)} %get-tuple-element.56), channel_id=1, source_target_pairs={{0,6},{1,7},{2,4},{3,5},{4,2},{5,3},{6,0},{7,1},{8,14},{9,15},{10,... | collective-permute-start | bytes 294920 | tf_op jit(solution)/shard_map/ppermute | solution.py:271
  59.8 15.9 %copy-start.15 = (f32[3,64,128]{2,1,0:T(8,128)}, f32[3,64,128]{2,1,0:T(8,128)S(1)}, u32[]{:S(2)}) copy-start(f32[3,64,128]{2,1,0:T(8,128)S(1)} %collective-permute-done.8.refs_2_) | copy-start | bytes 294916
  59.8 15.9 %collective-permute-start.13 = (f32[3,64,128]{2,1,0:T(8,128)}, f32[3,64,128]{2,1,0:T(8,128)S(1)}, u32[]{:S(2)}, u32[]{:S(2)}) collective-permute-start(f32[3,64,128]{2,1,0:T(8,128)} %get-tuple-element.57), channel_id=1, source_target_pairs={{0,7},{1,6},{2,5},{3,4},{4,3},{5,2},{6,1},{7,0},{8,15},{9,14},{10,... | collective-permute-start | bytes 294920 | tf_op jit(solution)/shard_map/ppermute | solution.py:271
  61.6 14.1 %copy-start.16 = (f32[3,64,128]{2,1,0:T(8,128)}, f32[3,64,128]{2,1,0:T(8,128)S(1)}, u32[]{:S(2)}) copy-start(f32[3,64,128]{2,1,0:T(8,128)S(1)} %collective-permute-done.9.refs_3_) | copy-start | bytes 294916
  63.5 12.2 %copy-start.17 = (f32[3,64,128]{2,1,0:T(8,128)}, f32[3,64,128]{2,1,0:T(8,128)S(1)}, u32[]{:S(2)}) copy-start(f32[3,64,128]{2,1,0:T(8,128)S(1)} %collective-permute-done.10.refs_4_) | copy-start | bytes 294916
  69.7 6.1 %copy-start.18 = (f32[3,64,128]{2,1,0:T(8,128)}, f32[3,64,128]{2,1,0:T(8,128)S(1)}, u32[]{:S(2)}) copy-start(f32[3,64,128]{2,1,0:T(8,128)S(1)} %collective-permute-done.11.refs_5_) | copy-start | bytes 294916
  73.6 2.2 %copy-start.19 = (f32[3,64,128]{2,1,0:T(8,128)}, f32[3,64,128]{2,1,0:T(8,128)S(1)}, u32[]{:S(2)}) copy-start(f32[3,64,128]{2,1,0:T(8,128)S(1)} %collective-permute-done.12.refs_6_) | copy-start | bytes 294916
  75.7 0.6 copy-start.20
  80.4 9.4 %collective-permute-start.14 = (f32[3,64,128]{2,1,0:T(8,128)}, f32[3,64,128]{2,1,0:T(8,128)S(1)}, u32[]{:S(2)}, u32[]{:S(2)}) collective-permute-start(f32[3,64,128]{2,1,0:T(8,128)} %get-tuple-element.61), channel_id=1, source_target_pairs={{0,1},{1,0},{2,3},{3,2},{4,5},{5,4},{6,7},{7,6},{8,9},{9,8},{10,11... | collective-permute-start | bytes 294920 | tf_op jit(solution)/shard_map/ppermute | solution.py:271
  80.9 9.7 %collective-permute-start.15 = (f32[3,64,128]{2,1,0:T(8,128)}, f32[3,64,128]{2,1,0:T(8,128)S(1)}, u32[]{:S(2)}, u32[]{:S(2)}) collective-permute-start(f32[3,64,128]{2,1,0:T(8,128)} %get-tuple-element.62), channel_id=1, source_target_pairs={{0,2},{1,3},{2,0},{3,1},{4,6},{5,7},{6,4},{7,5},{8,10},{9,11},{10,... | collective-permute-start | bytes 294920 | tf_op jit(solution)/shard_map/ppermute | solution.py:271
  80.9 3.5 %collective-permute-start.23 = (f32[3,64]{1,0:T(4,128)}, f32[3,64]{1,0:T(4,128)S(1)}, u32[]{:S(2)}, u32[]{:S(2)}) collective-permute-start(f32[3,64]{1,0:T(4,128)} %get-tuple-element.68), channel_id=1, source_target_pairs={{0,24},{8,16},{16,8},{24,0},{1,25},{9,17},{17,9},{25,1},{2,26},{10... | collective-permute-start | bytes 2312 | tf_op jit(solution)/shard_map/ppermute | solution.py:282
  83.1 4.3 %collective-permute-start.22 = (f32[3,64]{1,0:T(4,128)}, f32[3,64]{1,0:T(4,128)S(1)}, u32[]{:S(2)}, u32[]{:S(2)}) collective-permute-start(f32[3,64]{1,0:T(4,128)} %get-tuple-element.68), channel_id=1, source_target_pairs={{0,16},{8,24},{16,0},{24,8},{1,17},{9,25},{17,1},{25,9},{2,18},{10... | collective-permute-start | bytes 2312 | tf_op jit(solution)/shard_map/ppermute | solution.py:282
  83.3 4.3 %collective-permute-start.21 = (f32[3,64]{1,0:T(4,128)}, f32[3,64]{1,0:T(4,128)S(1)}, u32[]{:S(2)}, u32[]{:S(2)}) collective-permute-start(f32[3,64]{1,0:T(4,128)} %get-tuple-element.68), channel_id=1, source_target_pairs={{0,8},{8,0},{16,24},{24,16},{1,9},{9,1},{17,25},{25,17},{2,10},{10... | collective-permute-start | bytes 2312 | tf_op jit(solution)/shard_map/ppermute | solution.py:282
  84.4 8.6 %collective-permute-start.16 = (f32[3,64,128]{2,1,0:T(8,128)}, f32[3,64,128]{2,1,0:T(8,128)S(1)}, u32[]{:S(2)}, u32[]{:S(2)}) collective-permute-start(f32[3,64,128]{2,1,0:T(8,128)} %get-tuple-element.63), channel_id=1, source_target_pairs={{0,3},{1,2},{2,1},{3,0},{4,7},{5,6},{6,5},{7,4},{8,11},{9,10},{10,... | collective-permute-start | bytes 294920 | tf_op jit(solution)/shard_map/ppermute | solution.py:271
  87.4 5.7 %collective-permute-start.17 = (f32[3,64,128]{2,1,0:T(8,128)}, f32[3,64,128]{2,1,0:T(8,128)S(1)}, u32[]{:S(2)}, u32[]{:S(2)}) collective-permute-start(f32[3,64,128]{2,1,0:T(8,128)} %get-tuple-element.64), channel_id=1, source_target_pairs={{0,4},{1,5},{2,6},{3,7},{4,0},{5,1},{6,2},{7,3},{8,12},{9,13},{10,... | collective-permute-start | bytes 294920 | tf_op jit(solution)/shard_map/ppermute | solution.py:271
  87.6 12.8 %collective-permute-start.18 = (f32[3,64,128]{2,1,0:T(8,128)}, f32[3,64,128]{2,1,0:T(8,128)S(1)}, u32[]{:S(2)}, u32[]{:S(2)}) collective-permute-start(f32[3,64,128]{2,1,0:T(8,128)} %get-tuple-element.65), channel_id=1, source_target_pairs={{0,5},{1,4},{2,7},{3,6},{4,1},{5,0},{6,3},{7,2},{8,13},{9,12},{10,... | collective-permute-start | bytes 294920 | tf_op jit(solution)/shard_map/ppermute | solution.py:271
  89.9 16.8 %copy-start = (f32[3,64,128]{2,1,0:T(8,128)}, f32[3,64,128]{2,1,0:T(8,128)S(1)}, u32[]{:S(2)}) copy-start(f32[3,64,128]{2,1,0:T(8,128)S(1)} %collective-permute-done.14.refs_1_) | copy-start | bytes 294916
  89.9 13.6 %collective-permute-start.19 = (f32[3,64,128]{2,1,0:T(8,128)}, f32[3,64,128]{2,1,0:T(8,128)S(1)}, u32[]{:S(2)}, u32[]{:S(2)}) collective-permute-start(f32[3,64,128]{2,1,0:T(8,128)} %get-tuple-element.66), channel_id=1, source_target_pairs={{0,6},{1,7},{2,4},{3,5},{4,2},{5,3},{6,0},{7,1},{8,14},{9,15},{10,... | collective-permute-start | bytes 294920 | tf_op jit(solution)/shard_map/ppermute | solution.py:271
  90.6 16.1 %copy-start.1 = (f32[3,64,128]{2,1,0:T(8,128)}, f32[3,64,128]{2,1,0:T(8,128)S(1)}, u32[]{:S(2)}) copy-start(f32[3,64,128]{2,1,0:T(8,128)S(1)} %collective-permute-done.15.refs_2_) | copy-start | bytes 294916
  90.6 16.1 %collective-permute-start.20 = (f32[3,64,128]{2,1,0:T(8,128)}, f32[3,64,128]{2,1,0:T(8,128)S(1)}, u32[]{:S(2)}, u32[]{:S(2)}) collective-permute-start(f32[3,64,128]{2,1,0:T(8,128)} %get-tuple-element.67), channel_id=1, source_target_pairs={{0,7},{1,6},{2,5},{3,4},{4,3},{5,2},{6,1},{7,0},{8,15},{9,14},{10,... | collective-permute-start | bytes 294920 | tf_op jit(solution)/shard_map/ppermute | solution.py:271
  93.0 13.7 %copy-start.2 = (f32[3,64,128]{2,1,0:T(8,128)}, f32[3,64,128]{2,1,0:T(8,128)S(1)}, u32[]{:S(2)}) copy-start(f32[3,64,128]{2,1,0:T(8,128)S(1)} %collective-permute-done.16.refs_3_) | copy-start | bytes 294916
  93.0 13.7 %copy-start.3 = (f32[3,64,128]{2,1,0:T(8,128)}, f32[3,64,128]{2,1,0:T(8,128)S(1)}, u32[]{:S(2)}) copy-start(f32[3,64,128]{2,1,0:T(8,128)S(1)} %collective-permute-done.17.refs_4_) | copy-start | bytes 294916
  100.4 6.4 %copy-start.4 = (f32[3,64,128]{2,1,0:T(8,128)}, f32[3,64,128]{2,1,0:T(8,128)S(1)}, u32[]{:S(2)}) copy-start(f32[3,64,128]{2,1,0:T(8,128)S(1)} %collective-permute-done.18.refs_5_) | copy-start | bytes 294916
  103.5 3.2 %copy-start.5 = (f32[3,64,128]{2,1,0:T(8,128)}, f32[3,64,128]{2,1,0:T(8,128)S(1)}, u32[]{:S(2)}) copy-start(f32[3,64,128]{2,1,0:T(8,128)S(1)} %collective-permute-done.19.refs_6_) | copy-start | bytes 294916
  106.7 0.6 copy-start.6

commit v3 on v1

--- a/solution.py
+++ b/solution.py
@@ -148,7 +148,7 @@
             three_parts(both), selector(info_ref[0:1, :], columns), NT, preferred_element_type=F32
         )
     )
-    for step, out in enumerate(out_refs):
+    for step, out in zip(steps_of(devices), out_refs):
         taken = placed[:, step * share : (step + 1) * share]
         for kind in range(2):
             for pair in range(comps // 2):
@@ -177,7 +177,7 @@
     out_refs, (solved_ref, state, local, after) = refs[:devices], refs[devices:]
     me = me_ref[0]
     _, pairs, points, lanes = in_refs[0].shape
-    for step, block in enumerate(in_refs):
+    for step, block in zip(steps_of(devices), in_refs):
         rows = pl.ds(pl.multiple_of((me ^ step) * points, points), points)
         for pair in range(pairs):
             state[rows, pair * lanes : (pair + 1) * lanes] = block[0, pair]
@@ -189,7 +189,7 @@
     after[...] = apply(basis_ref[...], project)
     for pair in range(pairs):
         solved_ref[pair] = after[:, pair * lanes : (pair + 1) * lanes]
-    for step, block in enumerate(out_refs):
+    for step, block in zip(steps_of(devices), out_refs):
         rows = pl.ds(pl.multiple_of((me ^ step) * points, points), points)
         for pair in range(pairs):
             block[pair] = after[rows, pair * lanes : (pair + 1) * lanes]
@@ -203,12 +203,14 @@
     pairs, points, lanes = in_refs[0].shape
     share = lanes // 2
     columns = devices * share
+    order = steps_of(devices)
+    blocks = [in_refs[order.index(step)] for step in range(devices)]
     got = []
     for pair in range(pairs):
         for half in range(2):
             got.append(
                 jnp.concatenate(
-                    [block[pair][:, half * share : (half + 1) * share] for block in in_refs], axis=1
+                    [block[pair][:, half * share : (half + 1) * share] for block in blocks], axis=1
                 )
             )
     got = jnp.concatenate(got, axis=0)
@@ -221,7 +223,7 @@
             three_parts(state), selector(info_ref[1:2, :], columns), NT, preferred_element_type=F32
         )
     )
-    for step, out in enumerate(out_refs):
+    for step, out in zip(steps_of(devices), out_refs):
         taken = extra[:, step * share : (step + 1) * share]
         for pair in range(pairs):
             real = 2 * pair * points
@@ -259,15 +261,20 @@
         for half in range(2):
             kept = jnp.where(used, solved_ref[pair][:, half * share : (half + 1) * share], 0.0)
             out_ref[2 * pair + half, :, :share] = kept
-            for step, block in enumerate(in_refs):
+            for step, block in zip(steps_of(devices), in_refs):
                 rows = pl.ds(pl.multiple_of((me ^ step) * points, points), points)
                 out_ref[2 * pair + half, rows, share:] = block[pair][:, half * share : (half + 1) * share]
 
 
+def steps_of(devices):
+    return [0] + sorted(range(1, devices), key=lambda step: -((step.bit_length() << 16) + (step >> 1 << 1)))
+
+
 def exchange(blocks):
     devices = len(blocks)
-    return [blocks[0]] + [
-        lax.ppermute(blocks[step], "col", [(i, i ^ step) for i in range(devices)]) for step in range(1, devices)
+    return [
+        block if step == 0 else lax.ppermute(block, "col", [(i, i ^ step) for i in range(devices)])
+        for step, block in zip(steps_of(devices), blocks)
     ]
 
 

time: 111 us -> 104 us (0.937)
  the two profiles are of different devices: /device:TPU:9 before, /device:TPU:0 now
where the time goes in v3:
time: 104 us
  starting transfers between devices  51.3 us (49%)
  Pallas kernels  24.7 us (24%)
  waiting for transfers between devices  23.3 us (22%)
  local copies, waits for them, and re-layouts  2.25 us (2%)
  other arithmetic  1.29 us (1%)
    ppermute x21, starting transfers between devices, exchange(): lax.ppermute(block, 'col', [(i, i ^ step) for i in range(devices)])  47.8 us
    ppermute x21, waiting for transfers between devices, exchange(): lax.ppermute(block, 'col', [(i, i ^ step) for i in range(devices)])  20.1 us
    pallas_call x1, Pallas kernels, on_device(): call(functools.partial(solve_kernel, devices), [shaped(back)] * devices +...  6.85 us
    pallas_call x1, Pallas kernels, on_device(): call(operators_kernel, [operator, operator, operator, shaped((depth, lane...  4.49 us
    pallas_call x1, Pallas kernels, on_device(): call(functools.partial(pack_kernel, devices), [shaped(sent)] * devices, [...  4.45 us
    pallas_call x1, Pallas kernels, on_device(): call(functools.partial(unpack_kernel, devices, chunk, first), [shaped(sta...  4.16 us
    ppermute x3, starting transfers between devices, sum_over_groups(): lax.ppermute(value, 'grp', [(i, i ^ step) for i in range(groups)])  3.49 us
    ppermute x3, waiting for transfers between devices, sum_over_groups(): lax.ppermute(value, 'grp', [(i, i ^ step) for i in range(groups)])  3.24 us
  transfers between devices with their start and end apart: 24, of which 12 were waited for; matrix products, arithmetic and copies ran while one was open for 1% of the time, Pallas kernels for 4%

profile of v3, /device:TPU:0, one launch (start us, length us, event | category | flops | bytes accessed | tf_op | source)
XLA Modules:
  0.0 103.7 jit_solution(18009731184124387575)
XLA Ops:
  0.6 1.7 %shard_map.121 = (s32[8,512]{1,0:T(8,128)}, f32[8,128]{1,0:T(8,128)}) custom-call(s32[1]{0:T(128)} %bitcast.me_ref, s32[1,512]{1,0:T(1,128)} %bitcast.3, s32[2,512]{1,0:T(2,128)} %modes_ref.5), custom_call_target="tpu_custom_call" | custom-call | flops 1000000 | bytes 100000 | tf_op jit(solution)/shard_map/pallas_call | solution.py:313
  2.4 4.5 %shard_map.123 = (f32[2,3,64,128]{3,2,1,0:T(8,128)}, f32[2,3,64,128]{3,2,1,0:T(8,128)}, f32[2,3,64,128]{3,2,1,0:T(8,128)}, f32[2,3,64,128]{3,2,1,0:T(8,128)}, f3...) custom-call(s32[8,512]{1,0:T(8,128)} %get-tuple-element.36.info_ref,, ...), custom_call_target="tpu_custom_call" | custom-call | flops 1207959552 | bytes 3932160 | tf_op jit(solution)/shard_map/pallas_call | solution.py:331
  6.8 5.0 %collective-permute-start = (f32[2,3,64,128]{3,2,1,0:T(8,128)}, f32[2,3,64,128]{3,2,1,0:T(8,128)S(1)}, u32[]{:S(2)}, u32[]{:S(2)}) collective-permute-start(f32[2,3,64,128]{3,2,1,0:T(8,128)} %get-tuple-element.43), channel_id=1, source_target_pairs={{0,6},{1,7},{2,4},{3,5},{4,2},{5,3},{6,0},{7,1},{8,14},{9,15},{10,... | collective-permute-start | bytes 589832 | tf_op jit(solution)/shard_map/ppermute | solution.py:276
  11.9 0.2 collective-permute-start.2
  12.0 2.2 %collective-permute-start.3 = (f32[2,3,64,128]{3,2,1,0:T(8,128)}, f32[2,3,64,128]{3,2,1,0:T(8,128)S(1)}, u32[]{:S(2)}, u32[]{:S(2)}) collective-permute-start(f32[2,3,64,128]{3,2,1,0:T(8,128)} %get-tuple-element.46), channel_id=1, source_target_pairs={{0,5},{1,4},{2,7},{3,6},{4,1},{5,0},{6,3},{7,2},{8,13},{9,12},{10,... | collective-permute-start | bytes 589832 | tf_op jit(solution)/shard_map/ppermute | solution.py:276
  14.3 1.7 %collective-permute-start.4 = (f32[2,3,64,128]{3,2,1,0:T(8,128)}, f32[2,3,64,128]{3,2,1,0:T(8,128)S(1)}, u32[]{:S(2)}, u32[]{:S(2)}) collective-permute-start(f32[2,3,64,128]{3,2,1,0:T(8,128)} %get-tuple-element.47), channel_id=1, source_target_pairs={{0,2},{1,3},{2,0},{3,1},{4,6},{5,7},{6,4},{7,5},{8,10},{9,11},{10,... | collective-permute-start | bytes 589832 | tf_op jit(solution)/shard_map/ppermute | solution.py:276
  16.0 1.5 %collective-permute-done.refs_1_ = f32[2,3,64,128]{3,2,1,0:T(8,128)S(1)} collective-permute-done((f32[2,3,64,128]{3,2,1,0:T(8,128)}, f32[2,3,64,128]{3,2,1,0:T(8,128)S(1)}, u32[]{:S(2)}, u32[]{:S(2)}) %collective-permute-start) | collective-permute-done | bytes 196640 | tf_op jit(solution)/shard_map/ppermute | solution.py:276
  17.5 14.8 %collective-permute-start.5 = (f32[2,3,64,128]{3,2,1,0:T(8,128)}, f32[2,3,64,128]{3,2,1,0:T(8,128)S(1)}, u32[]{:S(2)}, u32[]{:S(2)}) collective-permute-start(f32[2,3,64,128]{3,2,1,0:T(8,128)} %get-tuple-element.48), channel_id=1, source_target_pairs={{0,3},{1,2},{2,1},{3,0},{4,7},{5,6},{6,5},{7,4},{8,11},{9,10},{10,... | collective-permute-start | bytes 589832 | tf_op jit(solution)/shard_map/ppermute | solution.py:276
  32.3 2.3 %collective-permute-start.6 = (f32[2,3,64,128]{3,2,1,0:T(8,128)}, f32[2,3,64,128]{3,2,1,0:T(8,128)S(1)}, u32[]{:S(2)}, u32[]{:S(2)}) collective-permute-start(f32[2,3,64,128]{3,2,1,0:T(8,128)} %get-tuple-element.49), channel_id=1, source_target_pairs={{0,1},{1,0},{2,3},{3,2},{4,5},{5,4},{6,7},{7,6},{8,9},{9,8},{10,11... | collective-permute-start | bytes 589832 | tf_op jit(solution)/shard_map/ppermute | solution.py:276
  34.6 4.5 %shard_map.122 = (bf16[512,1536]{1,0:T(8,128)(2,1)}, bf16[512,1536]{1,0:T(8,128)(2,1)}, bf16[512,1536]{1,0:T(8,128)(2,1)}, f32[512,128]{1,0:T(8,128)}) custom-call(f32[512,512]{1,0:T(8,128)} %deriv_ref.1, f32[512,512]{1,0:T(8,128)} %inverse_ref.1, f32[512,512]{1,0:T(8,128)} %basis_ref.1, f32[1,512]{1,0:T(1,128)} %bitcast.4), custom_call_target="tpu_custom_call" | custom-call | flops 1000000 | bytes 7864320 | tf_op jit(solution)/shard_map/pallas_call | solution.py:343
  39.1 3.3 %collective-permute-done.2.refs_3_ = f32[2,3,64,128]{3,2,1,0:T(8,128)S(1)} collective-permute-done((f32[2,3,64,128]{3,2,1,0:T(8,128)}, f32[2,3,64,128]{3,2,1,0:T(8,128)S(1)}, u32[]{:S(2)}, u32[]{:S(2)}) %collective-permute-start.2) | collective-permute-done | bytes 196640 | tf_op jit(solution)/shard_map/ppermute | solution.py:276
  42.5 2.3 %collective-permute-done.3.refs_4_ = f32[2,3,64,128]{3,2,1,0:T(8,128)S(1)} collective-permute-done((f32[2,3,64,128]{3,2,1,0:T(8,128)}, f32[2,3,64,128]{3,2,1,0:T(8,128)S(1)}, u32[]{:S(2)}, u32[]{:S(2)}) %collective-permute-start.3) | collective-permute-done | bytes 196640 | tf_op jit(solution)/shard_map/ppermute | solution.py:276
  44.8 0.6 copy-done.10
  45.5 0.1 copy-done.11
  45.6 0.1 copy-done.12
  45.6 0.1 copy-done.13
  45.7 6.8 %shard_map.124 = (f32[3,64,128]{2,1,0:T(8,128)}, f32[3,64,128]{2,1,0:T(8,128)}, f32[3,64,128]{2,1,0:T(8,128)}, f32[3,64,128]{2,1,0:T(8,128)}, f32[3,64,128]{2,1,...) custom-call(s32[1]{0:T(128)} %bitcast.me_ref, ...), custom_call_target="tpu_custom_call" | custom-call | flops 1811939328 | bytes 7864320 | tf_op jit(solution)/shard_map/pallas_call | solution.py:356
  52.6 2.3 %collective-permute-start.7 = (f32[3,64,128]{2,1,0:T(8,128)}, f32[3,64,128]{2,1,0:T(8,128)S(1)}, u32[]{:S(2)}, u32[]{:S(2)}) collective-permute-start(f32[3,64,128]{2,1,0:T(8,128)} %get-tuple-element.51), channel_id=1, source_target_pairs={{0,6},{1,7},{2,4},{3,5},{4,2},{5,3},{6,0},{7,1},{8,14},{9,15},{10,... | collective-permute-start | bytes 294920 | tf_op jit(solution)/shard_map/ppermute | solution.py:276
  54.8 2.5 %collective-permute-start.8 = (f32[3,64,128]{2,1,0:T(8,128)}, f32[3,64,128]{2,1,0:T(8,128)S(1)}, u32[]{:S(2)}, u32[]{:S(2)}) collective-permute-start(f32[3,64,128]{2,1,0:T(8,128)} %get-tuple-element.52), channel_id=1, source_target_pairs={{0,7},{1,6},{2,5},{3,4},{4,3},{5,2},{6,1},{7,0},{8,15},{9,14},{10,... | collective-permute-start | bytes 294920 | tf_op jit(solution)/shard_map/ppermute | solution.py:276
  57.4 1.4 %collective-permute-start.10 = (f32[3,64,128]{2,1,0:T(8,128)}, f32[3,64,128]{2,1,0:T(8,128)S(1)}, u32[]{:S(2)}, u32[]{:S(2)}) collective-permute-start(f32[3,64,128]{2,1,0:T(8,128)} %get-tuple-element.54), channel_id=1, source_target_pairs={{0,5},{1,4},{2,7},{3,6},{4,1},{5,0},{6,3},{7,2},{8,13},{9,12},{10,... | collective-permute-start | bytes 294920 | tf_op jit(solution)/shard_map/ppermute | solution.py:276
  58.7 1.7 %collective-permute-start.11 = (f32[3,64,128]{2,1,0:T(8,128)}, f32[3,64,128]{2,1,0:T(8,128)S(1)}, u32[]{:S(2)}, u32[]{:S(2)}) collective-permute-start(f32[3,64,128]{2,1,0:T(8,128)} %get-tuple-element.55), channel_id=1, source_target_pairs={{0,2},{1,3},{2,0},{3,1},{4,6},{5,7},{6,4},{7,5},{8,10},{9,11},{10,... | collective-permute-start | bytes 294920 | tf_op jit(solution)/shard_map/ppermute | solution.py:276
  60.4 1.4 %collective-permute-start.12 = (f32[3,64,128]{2,1,0:T(8,128)}, f32[3,64,128]{2,1,0:T(8,128)S(1)}, u32[]{:S(2)}, u32[]{:S(2)}) collective-permute-start(f32[3,64,128]{2,1,0:T(8,128)} %get-tuple-element.56), channel_id=1, source_target_pairs={{0,3},{1,2},{2,1},{3,0},{4,7},{5,6},{6,5},{7,4},{8,11},{9,10},{10,... | collective-permute-start | bytes 294920 | tf_op jit(solution)/shard_map/ppermute | solution.py:276
  61.8 5.9 %collective-permute-start.13 = (f32[3,64,128]{2,1,0:T(8,128)}, f32[3,64,128]{2,1,0:T(8,128)S(1)}, u32[]{:S(2)}, u32[]{:S(2)}) collective-permute-start(f32[3,64,128]{2,1,0:T(8,128)} %get-tuple-element.57), channel_id=1, source_target_pairs={{0,1},{1,0},{2,3},{3,2},{4,5},{5,4},{6,7},{7,6},{8,9},{9,8},{10,11... | collective-permute-start | bytes 294920 | tf_op jit(solution)/shard_map/ppermute | solution.py:276
  67.7 3.5 %collective-permute-done.9.refs_3_ = f32[3,64,128]{2,1,0:T(8,128)S(1)} collective-permute-done((f32[3,64,128]{2,1,0:T(8,128)}, f32[3,64,128]{2,1,0:T(8,128)S(1)}, u32[]{:S(2)}, u32[]{:S(2)}) %collective-permute-start.9) | collective-permute-done | bytes 98336 | tf_op jit(solution)/shard_map/ppermute | solution.py:276
  71.2 1.9 %collective-permute-done.10.refs_4_ = f32[3,64,128]{2,1,0:T(8,128)S(1)} collective-permute-done((f32[3,64,128]{2,1,0:T(8,128)}, f32[3,64,128]{2,1,0:T(8,128)S(1)}, u32[]{:S(2)}, u32[]{:S(2)}) %collective-permute-start.10) | collective-permute-done | bytes 98336 | tf_op jit(solution)/shard_map/ppermute | solution.py:276
  73.1 0.6 copy-done.17
  73.7 0.1 copy-done.18
  73.7 0.0 copy-done.19
  73.8 0.0 copy-done.20
  73.8 4.2 %shard_map.125 = (f32[6,64,512]{2,1,0:T(8,128)}, f32[3,64]{1,0:T(4,128)}, f32[3,64,128]{2,1,0:T(8,128)}, f32[3,64,128]{2,1,0:T(8,128)}, f32[3,64,128]{2,1,0:T(8,...) custom-call(s32[8,512]{1,0:T(8,128)} %get-tuple-element.36.info_ref,, ...), custom_call_target="tpu_custom_call" | custom-call | flops 1207959552 | bytes 4718592 | tf_op jit(solution)/shard_map/pallas_call | solution.py:373
  78.0 1.5 %collective-permute-start.14 = (f32[3,64,128]{2,1,0:T(8,128)}, f32[3,64,128]{2,1,0:T(8,128)S(1)}, u32[]{:S(2)}, u32[]{:S(2)}) collective-permute-start(f32[3,64,128]{2,1,0:T(8,128)} %get-tuple-element.61), channel_id=1, source_target_pairs={{0,6},{1,7},{2,4},{3,5},{4,2},{5,3},{6,0},{7,1},{8,14},{9,15},{10,... | collective-permute-start | bytes 294920 | tf_op jit(solution)/shard_map/ppermute | solution.py:276
  79.5 2.5 %collective-permute-start.15 = (f32[3,64,128]{2,1,0:T(8,128)}, f32[3,64,128]{2,1,0:T(8,128)S(1)}, u32[]{:S(2)}, u32[]{:S(2)}) collective-permute-start(f32[3,64,128]{2,1,0:T(8,128)} %get-tuple-element.62), channel_id=1, source_target_pairs={{0,7},{1,6},{2,5},{3,4},{4,3},{5,2},{6,1},{7,0},{8,15},{9,14},{10,... | collective-permute-start | bytes 294920 | tf_op jit(solution)/shard_map/ppermute | solution.py:276
  82.0 2.4 %collective-permute-start.23 = (f32[3,64]{1,0:T(4,128)}, f32[3,64]{1,0:T(4,128)S(1)}, u32[]{:S(2)}, u32[]{:S(2)}) collective-permute-start(f32[3,64]{1,0:T(4,128)} %get-tuple-element.68), channel_id=1, source_target_pairs={{0,24},{8,16},{16,8},{24,0},{1,25},{9,17},{17,9},{25,1},{2,26},{10... | collective-permute-start | bytes 2312 | tf_op jit(solution)/shard_map/ppermute | solution.py:284
  84.4 0.5 collective-permute-start.22
  84.9 0.5 collective-permute-start.21
  85.5 1.2 %collective-permute-done.23 = f32[3,64]{1,0:T(4,128)S(1)} collective-permute-done((f32[3,64]{1,0:T(4,128)}, f32[3,64]{1,0:T(4,128)S(1)}, u32[]{:S(2)}, u32[]{:S(2)}) %collective-permute-start.23) | collective-permute-done | bytes 800 | tf_op jit(solution)/shard_map/ppermute | solution.py:284
  86.7 1.5 %collective-permute-done.22 = f32[3,64]{1,0:T(4,128)S(1)} collective-permute-done((f32[3,64]{1,0:T(4,128)}, f32[3,64]{1,0:T(4,128)S(1)}, u32[]{:S(2)}, u32[]{:S(2)}) %collective-permute-start.22) | collective-permute-done | bytes 800 | tf_op jit(solution)/shard_map/ppermute | solution.py:284
  88.2 0.5 collective-permute-done.21
  88.7 1.0 collective-permute-start.18
  89.7 1.4 %collective-permute-start.19 = (f32[3,64,128]{2,1,0:T(8,128)}, f32[3,64,128]{2,1,0:T(8,128)S(1)}, u32[]{:S(2)}, u32[]{:S(2)}) collective-permute-start(f32[3,64,128]{2,1,0:T(8,128)} %get-tuple-element.66), channel_id=1, source_target_pairs={{0,3},{1,2},{2,1},{3,0},{4,7},{5,6},{6,5},{7,4},{8,11},{9,10},{10,... | collective-permute-start | bytes 294920 | tf_op jit(solution)/shard_map/ppermute | solution.py:276
  91.1 1.3 %add_add_fusion = f32[3,64]{1,0:T(4,128)} fusion(f32[3,64]{1,0:T(4,128)S(1)} %collective-permute-done.22, f32[3,64]{1,0:T(4,128)S(1)} %collective-permute-done.23, f32[3,64]{1,0:T(4,128)} %get-tuple-element.68, f32[3,64]{1,0:T(4,128)S(1)} %collective-permute-done.21), kind=kLoop, calls=%fused_computation | loop fusion | flops 576 | bytes 3840 | tf_op jit(solution)/shard_map/add | solution.py:287
  92.4 3.9 %collective-permute-done.16.refs_3_ = f32[3,64,128]{2,1,0:T(8,128)S(1)} collective-permute-done((f32[3,64,128]{2,1,0:T(8,128)}, f32[3,64,128]{2,1,0:T(8,128)S(1)}, u32[]{:S(2)}, u32[]{:S(2)}) %collective-permute-start.16) | collective-permute-done | bytes 98336 | tf_op jit(solution)/shard_map/ppermute | solution.py:276
  96.3 0.8 collective-permute-done.17.refs_4_
  97.1 0.7 collective-permute-done.18.refs_5_
  97.8 2.1 %collective-permute-done.19.refs_6_ = f32[3,64,128]{2,1,0:T(8,128)S(1)} collective-permute-done((f32[3,64,128]{2,1,0:T(8,128)}, f32[3,64,128]{2,1,0:T(8,128)S(1)}, u32[]{:S(2)}, u32[]{:S(2)}) %collective-permute-start.19) | collective-permute-done | bytes 98336 | tf_op jit(solution)/shard_map/ppermute | solution.py:276
  100.0 0.6 copy-done.5
  100.6 0.0 copy-done.6
  100.6 3.0 %shard_map.126 = f32[6,512,128]{2,1,0:T(8,128)} custom-call(s32[1]{0:T(128)} %bitcast.me_ref, s32[8,512]{1,0:T(8,128)} %get-tuple-element.36.info_ref, f32[3,512,128]{2,1,0:T(8,128)} %get-tuple-element.59.solved_ref, f32[3,64,128]{2,1,0:T(8,128)} %get-tuple-element.60.refs_0_, f32[3,64,128]{2,1,0:T(8,128)} %copy-done, f32[3,64,128]{2,1,0:T(8,128)} %copy-done.1, ...), custom_call_target="tpu_custom_call" | custom-call | flops 1000000 | bytes 3145728 | tf_op jit(solution)/shard_map/pallas_call | solution.py:391
  (49 shorter events, 0.1 us)
Async XLA Ops:
  6.8 10.7 %collective-permute-start = (f32[2,3,64,128]{3,2,1,0:T(8,128)}, f32[2,3,64,128]{3,2,1,0:T(8,128)S(1)}, u32[]{:S(2)}, u32[]{:S(2)}) collective-permute-start(f32[2,3,64,128]{3,2,1,0:T(8,128)} %get-tuple-element.43), channel_id=1, source_target_pairs={{0,6},{1,7},{2,4},{3,5},{4,2},{5,3},{6,0},{7,1},{8,14},{9,15},{10,... | collective-permute-start | bytes 589832 | tf_op jit(solution)/shard_map/ppermute | solution.py:276
  11.9 20.4 %collective-permute-start.1 = (f32[2,3,64,128]{3,2,1,0:T(8,128)}, f32[2,3,64,128]{3,2,1,0:T(8,128)S(1)}, u32[]{:S(2)}, u32[]{:S(2)}) collective-permute-start(f32[2,3,64,128]{3,2,1,0:T(8,128)} %get-tuple-element.44), channel_id=1, source_target_pairs={{0,7},{1,6},{2,5},{3,4},{4,3},{5,2},{6,1},{7,0},{8,15},{9,14},{10,... | collective-permute-start | bytes 589832 | tf_op jit(solution)/shard_map/ppermute | solution.py:276
  11.9 30.6 %collective-permute-start.2 = (f32[2,3,64,128]{3,2,1,0:T(8,128)}, f32[2,3,64,128]{3,2,1,0:T(8,128)S(1)}, u32[]{:S(2)}, u32[]{:S(2)}) collective-permute-start(f32[2,3,64,128]{3,2,1,0:T(8,128)} %get-tuple-element.45), channel_id=1, source_target_pairs={{0,4},{1,5},{2,6},{3,7},{4,0},{5,1},{6,2},{7,3},{8,12},{9,13},{10,... | collective-permute-start | bytes 589832 | tf_op jit(solution)/shard_map/ppermute | solution.py:276
  12.0 32.7 %collective-permute-start.3 = (f32[2,3,64,128]{3,2,1,0:T(8,128)}, f32[2,3,64,128]{3,2,1,0:T(8,128)S(1)}, u32[]{:S(2)}, u32[]{:S(2)}) collective-permute-start(f32[2,3,64,128]{3,2,1,0:T(8,128)} %get-tuple-element.46), channel_id=1, source_target_pairs={{0,5},{1,4},{2,7},{3,6},{4,1},{5,0},{6,3},{7,2},{8,13},{9,12},{10,... | collective-permute-start | bytes 589832 | tf_op jit(solution)/shard_map/ppermute | solution.py:276
  14.3 30.5 %collective-permute-start.4 = (f32[2,3,64,128]{3,2,1,0:T(8,128)}, f32[2,3,64,128]{3,2,1,0:T(8,128)S(1)}, u32[]{:S(2)}, u32[]{:S(2)}) collective-permute-start(f32[2,3,64,128]{3,2,1,0:T(8,128)} %get-tuple-element.47), channel_id=1, source_target_pairs={{0,2},{1,3},{2,0},{3,1},{4,6},{5,7},{6,4},{7,5},{8,10},{9,11},{10,... | collective-permute-start | bytes 589832 | tf_op jit(solution)/shard_map/ppermute | solution.py:276
  17.5 21.6 %copy-start.7 = (f32[2,3,64,128]{3,2,1,0:T(8,128)}, f32[2,3,64,128]{3,2,1,0:T(8,128)S(1)}, u32[]{:S(2)}) copy-start(f32[2,3,64,128]{3,2,1,0:T(8,128)S(1)} %collective-permute-done.refs_1_) | copy-start | bytes 589828
  17.5 27.3 %collective-permute-start.5 = (f32[2,3,64,128]{3,2,1,0:T(8,128)}, f32[2,3,64,128]{3,2,1,0:T(8,128)S(1)}, u32[]{:S(2)}, u32[]{:S(2)}) collective-permute-start(f32[2,3,64,128]{3,2,1,0:T(8,128)} %get-tuple-element.48), channel_id=1, source_target_pairs={{0,3},{1,2},{2,1},{3,0},{4,7},{5,6},{6,5},{7,4},{8,11},{9,10},{10,... | collective-permute-start | bytes 589832 | tf_op jit(solution)/shard_map/ppermute | solution.py:276
  32.3 6.8 %copy-start.8 = (f32[2,3,64,128]{3,2,1,0:T(8,128)}, f32[2,3,64,128]{3,2,1,0:T(8,128)S(1)}, u32[]{:S(2)}) copy-start(f32[2,3,64,128]{3,2,1,0:T(8,128)S(1)} %collective-permute-done.1.refs_2_) | copy-start | bytes 589828
  32.3 12.5 %collective-permute-start.6 = (f32[2,3,64,128]{3,2,1,0:T(8,128)}, f32[2,3,64,128]{3,2,1,0:T(8,128)S(1)}, u32[]{:S(2)}, u32[]{:S(2)}) collective-permute-start(f32[2,3,64,128]{3,2,1,0:T(8,128)} %get-tuple-element.49), channel_id=1, source_target_pairs={{0,1},{1,0},{2,3},{3,2},{4,5},{5,4},{6,7},{7,6},{8,9},{9,8},{10,11... | collective-permute-start | bytes 589832 | tf_op jit(solution)/shard_map/ppermute | solution.py:276
  42.5 2.3 %copy-start.9 = (f32[2,3,64,128]{3,2,1,0:T(8,128)}, f32[2,3,64,128]{3,2,1,0:T(8,128)S(1)}, u32[]{:S(2)}) copy-start(f32[2,3,64,128]{3,2,1,0:T(8,128)S(1)} %collective-permute-done.2.refs_3_) | copy-start | bytes 589828
  44.8 0.7 copy-start.10
  44.8 0.8 copy-start.11
  44.8 0.8 copy-start.12
  44.8 0.9 copy-start.13
  52.6 7.9 %collective-permute-start.7 = (f32[3,64,128]{2,1,0:T(8,128)}, f32[3,64,128]{2,1,0:T(8,128)S(1)}, u32[]{:S(2)}, u32[]{:S(2)}) collective-permute-start(f32[3,64,128]{2,1,0:T(8,128)} %get-tuple-element.51), channel_id=1, source_target_pairs={{0,6},{1,7},{2,4},{3,5},{4,2},{5,3},{6,0},{7,1},{8,14},{9,15},{10,... | collective-permute-start | bytes 294920 | tf_op jit(solution)/shard_map/ppermute | solution.py:276
  54.8 6.9 %collective-permute-start.8 = (f32[3,64,128]{2,1,0:T(8,128)}, f32[3,64,128]{2,1,0:T(8,128)S(1)}, u32[]{:S(2)}, u32[]{:S(2)}) collective-permute-start(f32[3,64,128]{2,1,0:T(8,128)} %get-tuple-element.52), channel_id=1, source_target_pairs={{0,7},{1,6},{2,5},{3,4},{4,3},{5,2},{6,1},{7,0},{8,15},{9,14},{10,... | collective-permute-start | bytes 294920 | tf_op jit(solution)/shard_map/ppermute | solution.py:276
  57.4 13.8 %collective-permute-start.9 = (f32[3,64,128]{2,1,0:T(8,128)}, f32[3,64,128]{2,1,0:T(8,128)S(1)}, u32[]{:S(2)}, u32[]{:S(2)}) collective-permute-start(f32[3,64,128]{2,1,0:T(8,128)} %get-tuple-element.53), channel_id=1, source_target_pairs={{0,4},{1,5},{2,6},{3,7},{4,0},{5,1},{6,2},{7,3},{8,12},{9,13},{10,... | collective-permute-start | bytes 294920 | tf_op jit(solution)/shard_map/ppermute | solution.py:276
  57.4 15.7 %collective-permute-start.10 = (f32[3,64,128]{2,1,0:T(8,128)}, f32[3,64,128]{2,1,0:T(8,128)S(1)}, u32[]{:S(2)}, u32[]{:S(2)}) collective-permute-start(f32[3,64,128]{2,1,0:T(8,128)} %get-tuple-element.54), channel_id=1, source_target_pairs={{0,5},{1,4},{2,7},{3,6},{4,1},{5,0},{6,3},{7,2},{8,13},{9,12},{10,... | collective-permute-start | bytes 294920 | tf_op jit(solution)/shard_map/ppermute | solution.py:276
  58.7 14.3 %collective-permute-start.11 = (f32[3,64,128]{2,1,0:T(8,128)}, f32[3,64,128]{2,1,0:T(8,128)S(1)}, u32[]{:S(2)}, u32[]{:S(2)}) collective-permute-start(f32[3,64,128]{2,1,0:T(8,128)} %get-tuple-element.55), channel_id=1, source_target_pairs={{0,2},{1,3},{2,0},{3,1},{4,6},{5,7},{6,4},{7,5},{8,10},{9,11},{10,... | collective-permute-start | bytes 294920 | tf_op jit(solution)/shard_map/ppermute | solution.py:276
  60.4 12.7 %copy-start.14 = (f32[3,64,128]{2,1,0:T(8,128)}, f32[3,64,128]{2,1,0:T(8,128)S(1)}, u32[]{:S(2)}) copy-start(f32[3,64,128]{2,1,0:T(8,128)S(1)} %collective-permute-done.7.refs_1_) | copy-start | bytes 294916
  60.4 12.7 %collective-permute-start.12 = (f32[3,64,128]{2,1,0:T(8,128)}, f32[3,64,128]{2,1,0:T(8,128)S(1)}, u32[]{:S(2)}, u32[]{:S(2)}) collective-permute-start(f32[3,64,128]{2,1,0:T(8,128)} %get-tuple-element.56), channel_id=1, source_target_pairs={{0,3},{1,2},{2,1},{3,0},{4,7},{5,6},{6,5},{7,4},{8,11},{9,10},{10,... | collective-permute-start | bytes 294920 | tf_op jit(solution)/shard_map/ppermute | solution.py:276
  61.8 11.3 %copy-start.15 = (f32[3,64,128]{2,1,0:T(8,128)}, f32[3,64,128]{2,1,0:T(8,128)S(1)}, u32[]{:S(2)}) copy-start(f32[3,64,128]{2,1,0:T(8,128)S(1)} %collective-permute-done.8.refs_2_) | copy-start | bytes 294916
  61.8 11.3 %collective-permute-start.13 = (f32[3,64,128]{2,1,0:T(8,128)}, f32[3,64,128]{2,1,0:T(8,128)S(1)}, u32[]{:S(2)}, u32[]{:S(2)}) collective-permute-start(f32[3,64,128]{2,1,0:T(8,128)} %get-tuple-element.57), channel_id=1, source_target_pairs={{0,1},{1,0},{2,3},{3,2},{4,5},{5,4},{6,7},{7,6},{8,9},{9,8},{10,11... | collective-permute-start | bytes 294920 | tf_op jit(solution)/shard_map/ppermute | solution.py:276
  71.2 2.0 %copy-start.16 = (f32[3,64,128]{2,1,0:T(8,128)}, f32[3,64,128]{2,1,0:T(8,128)S(1)}, u32[]{:S(2)}) copy-start(f32[3,64,128]{2,1,0:T(8,128)S(1)} %collective-permute-done.9.refs_3_) | copy-start | bytes 294916
  73.1 0.6 copy-start.17
  73.1 0.7 copy-start.18
  73.1 0.7 copy-start.19
  73.1 0.7 copy-start.20
  78.0 11.7 %collective-permute-start.14 = (f32[3,64,128]{2,1,0:T(8,128)}, f32[3,64,128]{2,1,0:T(8,128)S(1)}, u32[]{:S(2)}, u32[]{:S(2)}) collective-permute-start(f32[3,64,128]{2,1,0:T(8,128)} %get-tuple-element.61), channel_id=1, source_target_pairs={{0,6},{1,7},{2,4},{3,5},{4,2},{5,3},{6,0},{7,1},{8,14},{9,15},{10,... | collective-permute-start | bytes 294920 | tf_op jit(solution)/shard_map/ppermute | solution.py:276
  79.5 11.6 %collective-permute-start.15 = (f32[3,64,128]{2,1,0:T(8,128)}, f32[3,64,128]{2,1,0:T(8,128)S(1)}, u32[]{:S(2)}, u32[]{:S(2)}) collective-permute-start(f32[3,64,128]{2,1,0:T(8,128)} %get-tuple-element.62), channel_id=1, source_target_pairs={{0,7},{1,6},{2,5},{3,4},{4,3},{5,2},{6,1},{7,0},{8,15},{9,14},{10,... | collective-permute-start | bytes 294920 | tf_op jit(solution)/shard_map/ppermute | solution.py:276
  82.0 4.7 %collective-permute-start.23 = (f32[3,64]{1,0:T(4,128)}, f32[3,64]{1,0:T(4,128)S(1)}, u32[]{:S(2)}, u32[]{:S(2)}) collective-permute-start(f32[3,64]{1,0:T(4,128)} %get-tuple-element.68), channel_id=1, source_target_pairs={{0,24},{8,16},{16,8},{24,0},{1,25},{9,17},{17,9},{25,1},{2,26},{10... | collective-permute-start | bytes 2312 | tf_op jit(solution)/shard_map/ppermute | solution.py:284
  84.4 3.8 %collective-permute-start.22 = (f32[3,64]{1,0:T(4,128)}, f32[3,64]{1,0:T(4,128)S(1)}, u32[]{:S(2)}, u32[]{:S(2)}) collective-permute-start(f32[3,64]{1,0:T(4,128)} %get-tuple-element.68), channel_id=1, source_target_pairs={{0,16},{8,24},{16,0},{24,8},{1,17},{9,25},{17,1},{25,9},{2,18},{10... | collective-permute-start | bytes 2312 | tf_op jit(solution)/shard_map/ppermute | solution.py:284
  84.9 3.8 %collective-permute-start.21 = (f32[3,64]{1,0:T(4,128)}, f32[3,64]{1,0:T(4,128)S(1)}, u32[]{:S(2)}, u32[]{:S(2)}) collective-permute-start(f32[3,64]{1,0:T(4,128)} %get-tuple-element.68), channel_id=1, source_target_pairs={{0,8},{8,0},{16,24},{24,16},{1,9},{9,1},{17,25},{25,17},{2,10},{10... | collective-permute-start | bytes 2312 | tf_op jit(solution)/shard_map/ppermute | solution.py:284
  86.7 9.6 %collective-permute-start.16 = (f32[3,64,128]{2,1,0:T(8,128)}, f32[3,64,128]{2,1,0:T(8,128)S(1)}, u32[]{:S(2)}, u32[]{:S(2)}) collective-permute-start(f32[3,64,128]{2,1,0:T(8,128)} %get-tuple-element.63), channel_id=1, source_target_pairs={{0,4},{1,5},{2,6},{3,7},{4,0},{5,1},{6,2},{7,3},{8,12},{9,13},{10,... | collective-permute-start | bytes 294920 | tf_op jit(solution)/shard_map/ppermute | solution.py:276
  88.2 8.9 %collective-permute-start.17 = (f32[3,64,128]{2,1,0:T(8,128)}, f32[3,64,128]{2,1,0:T(8,128)S(1)}, u32[]{:S(2)}, u32[]{:S(2)}) collective-permute-start(f32[3,64,128]{2,1,0:T(8,128)} %get-tuple-element.64), channel_id=1, source_target_pairs={{0,5},{1,4},{2,7},{3,6},{4,1},{5,0},{6,3},{7,2},{8,13},{9,12},{10,... | collective-permute-start | bytes 294920 | tf_op jit(solution)/shard_map/ppermute | solution.py:276
  88.7 9.1 %collective-permute-start.18 = (f32[3,64,128]{2,1,0:T(8,128)}, f32[3,64,128]{2,1,0:T(8,128)S(1)}, u32[]{:S(2)}, u32[]{:S(2)}) collective-permute-start(f32[3,64,128]{2,1,0:T(8,128)} %get-tuple-element.65), channel_id=1, source_target_pairs={{0,2},{1,3},{2,0},{3,1},{4,6},{5,7},{6,4},{7,5},{8,10},{9,11},{10,... | collective-permute-start | bytes 294920 | tf_op jit(solution)/shard_map/ppermute | solution.py:276
  89.7 10.3 %copy-start = (f32[3,64,128]{2,1,0:T(8,128)}, f32[3,64,128]{2,1,0:T(8,128)S(1)}, u32[]{:S(2)}) copy-start(f32[3,64,128]{2,1,0:T(8,128)S(1)} %collective-permute-done.14.refs_1_) | copy-start | bytes 294916
  89.7 10.3 %collective-permute-start.19 = (f32[3,64,128]{2,1,0:T(8,128)}, f32[3,64,128]{2,1,0:T(8,128)S(1)}, u32[]{:S(2)}, u32[]{:S(2)}) collective-permute-start(f32[3,64,128]{2,1,0:T(8,128)} %get-tuple-element.66), channel_id=1, source_target_pairs={{0,3},{1,2},{2,1},{3,0},{4,7},{5,6},{6,5},{7,4},{8,11},{9,10},{10,... | collective-permute-start | bytes 294920 | tf_op jit(solution)/shard_map/ppermute | solution.py:276
  91.1 8.9 %copy-start.1 = (f32[3,64,128]{2,1,0:T(8,128)}, f32[3,64,128]{2,1,0:T(8,128)S(1)}, u32[]{:S(2)}) copy-start(f32[3,64,128]{2,1,0:T(8,128)S(1)} %collective-permute-done.15.refs_2_) | copy-start | bytes 294916
  91.1 8.9 %collective-permute-start.20 = (f32[3,64,128]{2,1,0:T(8,128)}, f32[3,64,128]{2,1,0:T(8,128)S(1)}, u32[]{:S(2)}, u32[]{:S(2)}) collective-permute-start(f32[3,64,128]{2,1,0:T(8,128)} %get-tuple-element.67), channel_id=1, source_target_pairs={{0,1},{1,0},{2,3},{3,2},{4,5},{5,4},{6,7},{7,6},{8,9},{9,8},{10,11... | collective-permute-start | bytes 294920 | tf_op jit(solution)/shard_map/ppermute | solution.py:276
  96.3 3.7 %copy-start.2 = (f32[3,64,128]{2,1,0:T(8,128)}, f32[3,64,128]{2,1,0:T(8,128)S(1)}, u32[]{:S(2)}) copy-start(f32[3,64,128]{2,1,0:T(8,128)S(1)} %collective-permute-done.16.refs_3_) | copy-start | bytes 294916
  97.1 2.9 %copy-start.3 = (f32[3,64,128]{2,1,0:T(8,128)}, f32[3,64,128]{2,1,0:T(8,128)S(1)}, u32[]{:S(2)}) copy-start(f32[3,64,128]{2,1,0:T(8,128)S(1)} %collective-permute-done.17.refs_4_) | copy-start | bytes 294916
  97.8 2.2 %copy-start.4 = (f32[3,64,128]{2,1,0:T(8,128)}, f32[3,64,128]{2,1,0:T(8,128)S(1)}, u32[]{:S(2)}) copy-start(f32[3,64,128]{2,1,0:T(8,128)S(1)} %collective-permute-done.18.refs_5_) | copy-start | bytes 294916
  99.9 0.6 copy-start.5
  100.0 0.7 copy-start.6

commit v4 on v3

--- a/solution.py
+++ b/solution.py
@@ -15,7 +15,7 @@
 RK_ZETA = -17.0 / 60.0
 WAVE_SCALE = 8.0
 VMEM_LIMIT = 56 * 1024 * 1024
-GROUPS = 3
+GROUPS = 1
 LANES = 128
 
 F32 = jnp.float32

time: 104 us -> 140 us (1.35)
  starting transfers between devices: 51.3 us -> 79.8 us
  Pallas kernels: 24.7 us -> 46.1 us
  waiting for transfers between devices: 23.3 us -> 9.2 us
    ppermute x21 -> x63, starting transfers between devices: 47.8 us -> 76.3 us  [exchange(): lax.ppermute(block, 'col', [(i, i ^ step) for i in range(devices)])]
    ppermute x21 -> x63, waiting for transfers between devices: 20.1 us -> 7.74 us  [exchange(): lax.ppermute(block, 'col', [(i, i ^ step) for i in range(devices)])]
    pallas_call x1 -> x3, Pallas kernels: 6.85 us -> 17.1 us  [on_device(): call(functools.partial(solve_kernel, devices), [shaped(back)] * devices +...]
    pallas_call x1 -> x3, Pallas kernels: 4.16 us -> 8.66 us  [on_device(): call(functools.partial(unpack_kernel, devices, chunk, first), [shaped(sta...]
    pallas_call x1 -> x3, Pallas kernels: 4.45 us -> 8.02 us  [on_device(): call(functools.partial(pack_kernel, devices), [shaped(sent)] * devices, [...]
    pallas_call x1 -> x3, Pallas kernels: 3.04 us -> 5.96 us  [on_device(): call(functools.partial(assemble_kernel, devices, first), shaped((comps, d...]
    ppermute x3, waiting for transfers between devices: 3.24 us -> 1.46 us  [sum_over_groups(): lax.ppermute(value, 'grp', [(i, i ^ step) for i in range(groups)])]
  transfers between devices with their start and end apart: 24 -> 66, of which waited for: 12 -> 10; matrix products, arithmetic and copies ran while one was open for 1% -> 1% of each run, Pallas kernels for 4% -> 26%
where the time goes in v4:
time: 140 us; the launch traced here: 139 us
  starting transfers between devices  79.8 us (57%)
  Pallas kernels  46.1 us (33%)
  waiting for transfers between devices  9.2 us (7%)
  between operations  1.55 us (1%)
  local copies, waits for them, and re-layouts  1.5 us (1%)
    ppermute x63, starting transfers between devices, exchange(): lax.ppermute(block, 'col', [(i, i ^ step) for i in range(devices)])  76.3 us
    pallas_call x3, Pallas kernels, on_device(): call(functools.partial(solve_kernel, devices), [shaped(back)] * devices +...  17.1 us
    pallas_call x3, Pallas kernels, on_device(): call(functools.partial(unpack_kernel, devices, chunk, first), [shaped(sta...  8.66 us
    pallas_call x3, Pallas kernels, on_device(): call(functools.partial(pack_kernel, devices), [shaped(sent)] * devices, [...  8.02 us
    ppermute x63, waiting for transfers between devices, exchange(): lax.ppermute(block, 'col', [(i, i ^ step) for i in range(devices)])  7.74 us
    pallas_call x3, Pallas kernels, on_device(): call(functools.partial(assemble_kernel, devices, first), shaped((comps, d...  5.96 us
    pallas_call x1, Pallas kernels, on_device(): call(operators_kernel, [operator, operator, operator, shaped((depth, lane...  4.61 us
    ppermute x3, starting transfers between devices, sum_over_groups(): lax.ppermute(value, 'grp', [(i, i ^ step) for i in range(groups)])  3.49 us
  transfers between devices with their start and end apart: 66, of which 10 were waited for; matrix products, arithmetic and copies ran while one was open for 1% of the time, Pallas kernels for 26%

profile of v4, /device:TPU:0, one launch (start us, length us, event | category | flops | bytes accessed | tf_op | source)
XLA Modules:
  0.0 139.4 jit_solution(13317406899516332193)
XLA Ops:
  0.6 1.7 %shard_map.121 = (s32[8,512]{1,0:T(8,128)}, f32[8,128]{1,0:T(8,128)}) custom-call(s32[1]{0:T(128)} %bitcast.me_ref, s32[1,512]{1,0:T(1,128)} %bitcast.3, s32[2,512]{1,0:T(2,128)} %modes_ref.13), custom_call_target="tpu_custom_call" | custom-call | flops 1000000 | bytes 100000 | tf_op jit(solution)/shard_map/pallas_call | solution.py:313
  2.4 2.7 %shard_map.127 = (f32[2,1,64,128]{3,2,1,0:T(8,128)}, f32[2,1,64,128]{3,2,1,0:T(8,128)}, f32[2,1,64,128]{3,2,1,0:T(8,128)}, f32[2,1,64,128]{3,2,1,0:T(8,128)}, f3...) custom-call(s32[8,512]{1,0:T(8,128)} %get-tuple-element.90.info_ref,, ...), custom_call_target="tpu_custom_call" | custom-call | flops 402653184 | bytes 1310720 | tf_op jit(solution)/shard_map/pallas_call | solution.py:331
  5.0 5.0 %collective-permute-start.28 = (f32[2,1,64,128]{3,2,1,0:T(8,128)}, f32[2,1,64,128]{3,2,1,0:T(8,128)S(1)}, u32[]{:S(2)}, u32[]{:S(2)}) collective-permute-start(f32[2,1,64,128]{3,2,1,0:T(8,128)} %get-tuple-element.129), channel_id=1, source_target_pairs={{0,6},{1,7},{2,4},{3,5},{4,2},{5,3},{6,0},{7,1},{8,14},{9,15},{10,... | collective-permute-start | bytes 196616 | tf_op jit(solution)/shard_map/ppermute | solution.py:276
  10.3 2.2 %collective-permute-start.31 = (f32[2,1,64,128]{3,2,1,0:T(8,128)}, f32[2,1,64,128]{3,2,1,0:T(8,128)S(1)}, u32[]{:S(2)}, u32[]{:S(2)}) collective-permute-start(f32[2,1,64,128]{3,2,1,0:T(8,128)} %get-tuple-element.132), channel_id=1, source_target_pairs={{0,5},{1,4},{2,7},{3,6},{4,1},{5,0},{6,3},{7,2},{8,13},{9,12},{10,... | collective-permute-start | bytes 196616 | tf_op jit(solution)/shard_map/ppermute | solution.py:276
  12.5 1.7 %collective-permute-start.32 = (f32[2,1,64,128]{3,2,1,0:T(8,128)}, f32[2,1,64,128]{3,2,1,0:T(8,128)S(1)}, u32[]{:S(2)}, u32[]{:S(2)}) collective-permute-start(f32[2,1,64,128]{3,2,1,0:T(8,128)} %get-tuple-element.133), channel_id=1, source_target_pairs={{0,2},{1,3},{2,0},{3,1},{4,6},{5,7},{6,4},{7,5},{8,10},{9,11},{10,... | collective-permute-start | bytes 196616 | tf_op jit(solution)/shard_map/ppermute | solution.py:276
  14.5 2.1 %collective-permute-done.29.refs_2_ = f32[2,1,64,128]{3,2,1,0:T(8,128)S(1)} collective-permute-done((f32[2,1,64,128]{3,2,1,0:T(8,128)}, f32[2,1,64,128]{3,2,1,0:T(8,128)S(1)}, u32[]{:S(2)}, u32[]{:S(2)}) %collective-permute-start.29) | collective-permute-done | bytes 65568 | tf_op jit(solution)/shard_map/ppermute | solution.py:276
  17.7 2.7 %shard_map.125 = (f32[2,1,64,128]{3,2,1,0:T(8,128)}, f32[2,1,64,128]{3,2,1,0:T(8,128)}, f32[2,1,64,128]{3,2,1,0:T(8,128)}, f32[2,1,64,128]{3,2,1,0:T(8,128)}, f3...) custom-call(s32[8,512]{1,0:T(8,128)} %get-tuple-element.90.info_ref,, ...), custom_call_target="tpu_custom_call" | custom-call | flops 402653184 | bytes 1310720 | tf_op jit(solution)/shard_map/pallas_call | solution.py:331
  20.7 3.4 %collective-permute-start.14 = (f32[2,1,64,128]{3,2,1,0:T(8,128)}, f32[2,1,64,128]{3,2,1,0:T(8,128)S(1)}, u32[]{:S(2)}, u32[]{:S(2)}) collective-permute-start(f32[2,1,64,128]{3,2,1,0:T(8,128)} %get-tuple-element.113), channel_id=1, source_target_pairs={{0,6},{1,7},{2,4},{3,5},{4,2},{5,3},{6,0},{7,1},{8,14},{9,15},{10,... | collective-permute-start | bytes 196616 | tf_op jit(solution)/shard_map/ppermute | solution.py:276
  24.1 1.2 collective-permute-start.16
  25.3 1.6 %collective-permute-start.17 = (f32[2,1,64,128]{3,2,1,0:T(8,128)}, f32[2,1,64,128]{3,2,1,0:T(8,128)S(1)}, u32[]{:S(2)}, u32[]{:S(2)}) collective-permute-start(f32[2,1,64,128]{3,2,1,0:T(8,128)} %get-tuple-element.116), channel_id=1, source_target_pairs={{0,5},{1,4},{2,7},{3,6},{4,1},{5,0},{6,3},{7,2},{8,13},{9,12},{10,... | collective-permute-start | bytes 196616 | tf_op jit(solution)/shard_map/ppermute | solution.py:276
  26.9 1.4 collective-permute-start.18
  28.3 2.7 %shard_map.123 = (f32[2,1,64,128]{3,2,1,0:T(8,128)}, f32[2,1,64,128]{3,2,1,0:T(8,128)}, f32[2,1,64,128]{3,2,1,0:T(8,128)}, f32[2,1,64,128]{3,2,1,0:T(8,128)}, f3...) custom-call(s32[8,512]{1,0:T(8,128)} %get-tuple-element.90.info_ref,, ...), custom_call_target="tpu_custom_call" | custom-call | flops 402653184 | bytes 1310720 | tf_op jit(solution)/shard_map/pallas_call | solution.py:331
  31.4 1.5 %collective-permute-start.20 = (f32[2,1,64,128]{3,2,1,0:T(8,128)S(1)}, f32[2,1,64,128]{3,2,1,0:T(8,128)S(1)}, u32[]{:S(2)}, u32[]{:S(2)}) collective-permute-start(f32[2,1,64,128]{3,2,1,0:T(8,128)S(1)} %copy-done.60), channel_id=1, source_target_pairs={{0,1},{1,0},{2,3},{3,2},{4,5},{5,4},{6,7},{7,6},{8,9},{9,8},{10,11... | collective-permute-start | bytes 196616 | tf_op jit(solution)/shard_map/ppermute | solution.py:276
  32.9 2.3 %collective-permute-done.16.refs_3_ = f32[2,1,64,128]{3,2,1,0:T(8,128)S(1)} collective-permute-done((f32[2,1,64,128]{3,2,1,0:T(8,128)}, f32[2,1,64,128]{3,2,1,0:T(8,128)S(1)}, u32[]{:S(2)}, u32[]{:S(2)}) %collective-permute-start.16) | collective-permute-done | bytes 65568 | tf_op jit(solution)/shard_map/ppermute | solution.py:276
  35.2 3.1 %collective-permute-start = (f32[2,1,64,128]{3,2,1,0:T(8,128)}, f32[2,1,64,128]{3,2,1,0:T(8,128)S(1)}, u32[]{:S(2)}, u32[]{:S(2)}) collective-permute-start(f32[2,1,64,128]{3,2,1,0:T(8,128)} %get-tuple-element.97), channel_id=1, source_target_pairs={{0,6},{1,7},{2,4},{3,5},{4,2},{5,3},{6,0},{7,1},{8,14},{9,15},{10,... | collective-permute-start | bytes 196616 | tf_op jit(solution)/shard_map/ppermute | solution.py:276
  38.5 4.6 %shard_map.122 = (bf16[512,1536]{1,0:T(8,128)(2,1)}, bf16[512,1536]{1,0:T(8,128)(2,1)}, bf16[512,1536]{1,0:T(8,128)(2,1)}, f32[512,128]{1,0:T(8,128)}) custom-call(f32[512,512]{1,0:T(8,128)} %deriv_ref.1, f32[512,512]{1,0:T(8,128)} %inverse_ref.1, f32[512,512]{1,0:T(8,128)} %basis_ref.1, f32[1,512]{1,0:T(1,128)} %bitcast.4), custom_call_target="tpu_custom_call" | custom-call | flops 1000000 | bytes 7864320 | tf_op jit(solution)/shard_map/pallas_call | solution.py:343
  43.2 3.0 %collective-permute-start.3 = (f32[2,1,64,128]{3,2,1,0:T(8,128)S(1)}, f32[2,1,64,128]{3,2,1,0:T(8,128)S(1)}, u32[]{:S(2)}, u32[]{:S(2)}) collective-permute-start(f32[2,1,64,128]{3,2,1,0:T(8,128)S(1)} %copy-done.59), channel_id=1, source_target_pairs={{0,5},{1,4},{2,7},{3,6},{4,1},{5,0},{6,3},{7,2},{8,13},{9,12},{10,... | collective-permute-start | bytes 196616 | tf_op jit(solution)/shard_map/ppermute | solution.py:276
  46.2 1.1 collective-permute-start.4
  48.5 5.7 %shard_map.126 = (f32[1,64,128]{2,1,0:T(8,128)}, f32[1,64,128]{2,1,0:T(8,128)}, f32[1,64,128]{2,1,0:T(8,128)}, f32[1,64,128]{2,1,0:T(8,128)}, f32[1,64,128]{2,1,...) custom-call(s32[1]{0:T(128)} %bitcast.me_ref, ...), custom_call_target="tpu_custom_call" | custom-call | flops 603979776 | bytes 5767168 | tf_op jit(solution)/shard_map/pallas_call | solution.py:356
  54.3 3.1 %collective-permute-start.21 = (f32[1,64,128]{2,1,0:T(8,128)}, f32[1,64,128]{2,1,0:T(8,128)S(1)}, u32[]{:S(2)}, u32[]{:S(2)}) collective-permute-start(f32[1,64,128]{2,1,0:T(8,128)} %get-tuple-element.121), channel_id=1, source_target_pairs={{0,6},{1,7},{2,4},{3,5},{4,2},{5,3},{6,0},{7,1},{8,14},{9,15},{10,... | collective-permute-start | bytes 98312 | tf_op jit(solution)/shard_map/ppermute | solution.py:276
  57.4 5.7 %shard_map.128 = (f32[1,64,128]{2,1,0:T(8,128)}, f32[1,64,128]{2,1,0:T(8,128)}, f32[1,64,128]{2,1,0:T(8,128)}, f32[1,64,128]{2,1,0:T(8,128)}, f32[1,64,128]{2,1,...) custom-call(s32[1]{0:T(128)} %bitcast.me_ref, ...), custom_call_target="tpu_custom_call" | custom-call | flops 603979776 | bytes 5767168 | tf_op jit(solution)/shard_map/pallas_call | solution.py:356
  63.7 2.8 %collective-permute-start.24 = (f32[1,64,128]{2,1,0:T(8,128)S(1)}, f32[1,64,128]{2,1,0:T(8,128)S(1)}, u32[]{:S(2)}, u32[]{:S(2)}) collective-permute-start(f32[1,64,128]{2,1,0:T(8,128)S(1)} %copy-done.83), channel_id=1, source_target_pairs={{0,5},{1,4},{2,7},{3,6},{4,1},{5,0},{6,3},{7,2},{8,13},{9,12},{10,... | collective-permute-start | bytes 98312 | tf_op jit(solution)/shard_map/ppermute | solution.py:276
  66.5 3.1 %collective-permute-start.35 = (f32[1,64,128]{2,1,0:T(8,128)}, f32[1,64,128]{2,1,0:T(8,128)S(1)}, u32[]{:S(2)}, u32[]{:S(2)}) collective-permute-start(f32[1,64,128]{2,1,0:T(8,128)} %get-tuple-element.137), channel_id=1, source_target_pairs={{0,6},{1,7},{2,4},{3,5},{4,2},{5,3},{6,0},{7,1},{8,14},{9,15},{10,... | collective-permute-start | bytes 98312 | tf_op jit(solution)/shard_map/ppermute | solution.py:276
  70.0 2.7 %collective-permute-start.38 = (f32[1,64,128]{2,1,0:T(8,128)}, f32[1,64,128]{2,1,0:T(8,128)S(1)}, u32[]{:S(2)}, u32[]{:S(2)}) collective-permute-start(f32[1,64,128]{2,1,0:T(8,128)} %get-tuple-element.140), channel_id=1, source_target_pairs={{0,5},{1,4},{2,7},{3,6},{4,1},{5,0},{6,3},{7,2},{8,13},{9,12},{10,... | collective-permute-start | bytes 98312 | tf_op jit(solution)/shard_map/ppermute | solution.py:276
  74.1 1.2 collective-permute-done.36.refs_2_
  75.4 5.7 %shard_map.124 = (f32[1,64,128]{2,1,0:T(8,128)}, f32[1,64,128]{2,1,0:T(8,128)}, f32[1,64,128]{2,1,0:T(8,128)}, f32[1,64,128]{2,1,0:T(8,128)}, f32[1,64,128]{2,1,...) custom-call(s32[1]{0:T(128)} %bitcast.me_ref, ...), custom_call_target="tpu_custom_call" | custom-call | flops 603979776 | bytes 5767168 | tf_op jit(solution)/shard_map/pallas_call | solution.py:356
  81.8 1.4 collective-permute-start.26
  83.6 2.5 %collective-permute-start.7 = (f32[1,64,128]{2,1,0:T(8,128)}, f32[1,64,128]{2,1,0:T(8,128)S(1)}, u32[]{:S(2)}, u32[]{:S(2)}) collective-permute-start(f32[1,64,128]{2,1,0:T(8,128)} %get-tuple-element.105), channel_id=1, source_target_pairs={{0,6},{1,7},{2,4},{3,5},{4,2},{5,3},{6,0},{7,1},{8,14},{9,15},{10,... | collective-permute-start | bytes 98312 | tf_op jit(solution)/shard_map/ppermute | solution.py:276
  87.0 2.8 %shard_map.129 = (f32[6,64,512]{2,1,0:T(8,128)}, f32[3,64]{1,0:T(4,128)}, f32[1,64,128]{2,1,0:T(8,128)}, f32[1,64,128]{2,1,0:T(8,128)}, f32[1,64,128]{2,1,0:T(8,...) custom-call(s32[8,512]{1,0:T(8,128)} %get-tuple-element.90.info_ref,, ...), custom_call_target="tpu_custom_call" | custom-call | flops 402653184 | bytes 1572864 | tf_op jit(solution)/shard_map/pallas_call | solution.py:373
  89.9 2.8 %collective-permute-start.10 = (f32[1,64,128]{2,1,0:T(8,128)}, f32[1,64,128]{2,1,0:T(8,128)S(1)}, u32[]{:S(2)}, u32[]{:S(2)}) collective-permute-start(f32[1,64,128]{2,1,0:T(8,128)} %get-tuple-element.108), channel_id=1, source_target_pairs={{0,5},{1,4},{2,7},{3,6},{4,1},{5,0},{6,3},{7,2},{8,13},{9,12},{10,... | collective-permute-start | bytes 98312 | tf_op jit(solution)/shard_map/ppermute | solution.py:276
  95.0 2.8 %shard_map.130 = (f32[6,64,512]{2,1,0:T(8,128)}, f32[3,64]{1,0:T(4,128)}, f32[1,64,128]{2,1,0:T(8,128)}, f32[1,64,128]{2,1,0:T(8,128)}, f32[1,64,128]{2,1,0:T(8,...) custom-call(s32[8,512]{1,0:T(8,128)} %get-tuple-element.90.info_ref,, ...), custom_call_target="tpu_custom_call", output_to_operand_aliasing={{0}: (11, {})} | custom-call | flops 402653184 | bytes 1572864 | tf_op jit(solution)/shard_map/pallas_call | solution.py:373
  98.6 3.0 %shard_map.131 = (f32[6,64,512]{2,1,0:T(8,128)}, f32[3,64]{1,0:T(4,128)}, f32[1,64,128]{2,1,0:T(8,128)}, f32[1,64,128]{2,1,0:T(8,128)}, f32[1,64,128]{2,1,0:T(8,...) custom-call(s32[8,512]{1,0:T(8,128)} %get-tuple-element.90.info_ref,, ...), custom_call_target="tpu_custom_call", output_to_operand_aliasing={{0}: (11, {})} | custom-call | flops 402653184 | bytes 1572864 | tf_op jit(solution)/shard_map/pallas_call | solution.py:373
  101.6 2.6 %collective-permute-start.42 = (f32[1,64,128]{2,1,0:T(8,128)}, f32[1,64,128]{2,1,0:T(8,128)S(1)}, u32[]{:S(2)}, u32[]{:S(2)}) collective-permute-start(f32[1,64,128]{2,1,0:T(8,128)} %get-tuple-element.151), channel_id=1, source_target_pairs={{0,6},{1,7},{2,4},{3,5},{4,2},{5,3},{6,0},{7,1},{8,14},{9,15},{10,... | collective-permute-start | bytes 98312 | tf_op jit(solution)/shard_map/ppermute | solution.py:276
  104.2 2.4 %collective-permute-start.65 = (f32[3,64]{1,0:T(4,128)}, f32[3,64]{1,0:T(4,128)S(1)}, u32[]{:S(2)}, u32[]{:S(2)}) collective-permute-start(f32[3,64]{1,0:T(4,128)} %get-tuple-element.176), channel_id=1, source_target_pairs={{0,24},{8,16},{16,8},{24,0},{1,25},{9,17},{17,9},{25,1},{2,26},{10... | collective-permute-start | bytes 2312 | tf_op jit(solution)/shard_map/ppermute | solution.py:284
  107.7 1.2 collective-permute-done.65
  108.9 1.3 collective-permute-start.49
  110.4 1.8 %collective-permute-start.50 = (f32[1,64,128]{2,1,0:T(8,128)S(1)}, f32[1,64,128]{2,1,0:T(8,128)S(1)}, u32[]{:S(2)}, u32[]{:S(2)}) collective-permute-start(f32[1,64,128]{2,1,0:T(8,128)S(1)} %copy-done.78), channel_id=1, source_target_pairs={{0,7},{1,6},{2,5},{3,4},{4,3},{5,2},{6,1},{7,0},{8,15},{9,14},{10,... | collective-permute-start | bytes 98312 | tf_op jit(solution)/shard_map/ppermute | solution.py:276
  112.3 2.9 %collective-permute-start.52 = (f32[1,64,128]{2,1,0:T(8,128)S(1)}, f32[1,64,128]{2,1,0:T(8,128)S(1)}, u32[]{:S(2)}, u32[]{:S(2)}) collective-permute-start(f32[1,64,128]{2,1,0:T(8,128)S(1)} %copy-done.75), channel_id=1, source_target_pairs={{0,5},{1,4},{2,7},{3,6},{4,1},{5,0},{6,3},{7,2},{8,13},{9,12},{10,... | collective-permute-start | bytes 98312 | tf_op jit(solution)/shard_map/ppermute | solution.py:276
  115.5 1.3 collective-permute-start.54
  117.7 2.2 %collective-permute-start.56 = (f32[1,64,128]{2,1,0:T(8,128)S(1)}, f32[1,64,128]{2,1,0:T(8,128)S(1)}, u32[]{:S(2)}, u32[]{:S(2)}) collective-permute-start(f32[1,64,128]{2,1,0:T(8,128)S(1)} %copy-done.68), channel_id=1, source_target_pairs={{0,6},{1,7},{2,4},{3,5},{4,2},{5,3},{6,0},{7,1},{8,14},{9,15},{10,... | collective-permute-start | bytes 98312 | tf_op jit(solution)/shard_map/ppermute | solution.py:276
  121.1 3.0 %collective-permute-start.59 = (f32[1,64,128]{2,1,0:T(8,128)S(1)}, f32[1,64,128]{2,1,0:T(8,128)S(1)}, u32[]{:S(2)}, u32[]{:S(2)}) collective-permute-start(f32[1,64,128]{2,1,0:T(8,128)S(1)} %copy-done.65), channel_id=1, source_target_pairs={{0,5},{1,4},{2,7},{3,6},{4,1},{5,0},{6,3},{7,2},{8,13},{9,12},{10,... | collective-permute-start | bytes 98312 | tf_op jit(solution)/shard_map/ppermute | solution.py:276
  124.4 1.3 collective-permute-start.61
  128.0 1.2 collective-permute-start.45
  129.9 1.4 %collective-permute-start.47 = (f32[1,64,128]{2,1,0:T(8,128)}, f32[1,64,128]{2,1,0:T(8,128)S(1)}, u32[]{:S(2)}, u32[]{:S(2)}) collective-permute-start(f32[1,64,128]{2,1,0:T(8,128)} %get-tuple-element.156), channel_id=1, source_target_pairs={{0,3},{1,2},{2,1},{3,0},{4,7},{5,6},{6,5},{7,4},{8,11},{9,10},{10,... | collective-permute-start | bytes 98312 | tf_op jit(solution)/shard_map/ppermute | solution.py:276
  131.4 1.3 add_add_fusion
  132.7 2.0 %shard_map.132.refs_8_ = f32[6,512,128]{2,1,0:T(8,128)} custom-call(s32[1]{0:T(128)} %bitcast.me_ref, s32[8,512]{1,0:T(8,128)} %get-tuple-element.90.info_ref, f32[1,512,128]{2,1,0:T(8,128)} %get-tuple-element.167.solved_ref, f32[1,64,128]{2,1,0:T(8,128)} %get-tuple-element.168.refs_0_, f32[1,64,128]{2,1,0:T(8,128)} %copy-done.38, f32[1,64,128]{2,1,0:T(8,128)} %copy-done.40, ...), custom_call_target="tpu_custom_call" | custom-call | flops 1000000 | bytes 1048576 | tf_op jit(solution)/shard_map/pallas_call | solution.py:391
  134.7 2.0 %shard_map.133.refs_8_ = f32[6,512,128]{2,1,0:T(8,128)} custom-call(s32[1]{0:T(128)} %bitcast.me_ref, s32[8,512]{1,0:T(8,128)} %get-tuple-element.90.info_ref, f32[1,512,128]{2,1,0:T(8,128)} %get-tuple-element.158.solved_ref, f32[1,64,128]{2,1,0:T(8,128)} %get-tuple-element.159.refs_0_, f32[1,64,128]{2,1,0:T(8,128)} %copy-done.27, ...), custom_call_target="tpu_custom_call", output_to_operand_aliasing={{}: (11, {})} | custom-call | flops 1000000 | bytes 1048576 | tf_op jit(solution)/shard_map/pallas_call | solution.py:391
  137.4 2.0 %shard_map.134 = f32[6,512,128]{2,1,0:T(8,128)} custom-call(s32[1]{0:T(128)} %bitcast.me_ref, s32[8,512]{1,0:T(8,128)} %get-tuple-element.90.info_ref, f32[1,512,128]{2,1,0:T(8,128)} %get-tuple-element.149.solved_ref, f32[1,64,128]{2,1,0:T(8,128)} %get-tuple-element.150.refs_0_, f32[1,64,128]{2,1,0:T(8,128)} %copy-done.22, ...), custom_call_target="tpu_custom_call", output_to_operand_aliasing={{}: (11, {})} | custom-call | flops 1000000 | bytes 1048576 | tf_op jit(solution)/shard_map/pallas_call | solution.py:391
  (277 shorter events, 18.4 us)
Async XLA Ops:
  5.0 9.2 %collective-permute-start.28 = (f32[2,1,64,128]{3,2,1,0:T(8,128)}, f32[2,1,64,128]{3,2,1,0:T(8,128)S(1)}, u32[]{:S(2)}, u32[]{:S(2)}) collective-permute-start(f32[2,1,64,128]{3,2,1,0:T(8,128)} %get-tuple-element.129), channel_id=1, source_target_pairs={{0,6},{1,7},{2,4},{3,5},{4,2},{5,3},{6,0},{7,1},{8,14},{9,15},{10,... | collective-permute-start | bytes 196616 | tf_op jit(solution)/shard_map/ppermute | solution.py:276
  10.1 10.6 %collective-permute-start.30 = (f32[2,1,64,128]{3,2,1,0:T(8,128)}, f32[2,1,64,128]{3,2,1,0:T(8,128)S(1)}, u32[]{:S(2)}, u32[]{:S(2)}) collective-permute-start(f32[2,1,64,128]{3,2,1,0:T(8,128)} %get-tuple-element.131), channel_id=1, source_target_pairs={{0,4},{1,5},{2,6},{3,7},{4,0},{5,1},{6,2},{7,3},{8,12},{9,13},{10,... | collective-permute-start | bytes 196616 | tf_op jit(solution)/shard_map/ppermute | solution.py:276
  10.3 13.8 %collective-permute-start.31 = (f32[2,1,64,128]{3,2,1,0:T(8,128)}, f32[2,1,64,128]{3,2,1,0:T(8,128)S(1)}, u32[]{:S(2)}, u32[]{:S(2)}) collective-permute-start(f32[2,1,64,128]{3,2,1,0:T(8,128)} %get-tuple-element.132), channel_id=1, source_target_pairs={{0,5},{1,4},{2,7},{3,6},{4,1},{5,0},{6,3},{7,2},{8,13},{9,12},{10,... | collective-permute-start | bytes 196616 | tf_op jit(solution)/shard_map/ppermute | solution.py:276
  12.5 11.6 %collective-permute-start.32 = (f32[2,1,64,128]{3,2,1,0:T(8,128)}, f32[2,1,64,128]{3,2,1,0:T(8,128)S(1)}, u32[]{:S(2)}, u32[]{:S(2)}) collective-permute-start(f32[2,1,64,128]{3,2,1,0:T(8,128)} %get-tuple-element.133), channel_id=1, source_target_pairs={{0,2},{1,3},{2,0},{3,1},{4,6},{5,7},{6,4},{7,5},{8,10},{9,11},{10,... | collective-permute-start | bytes 196616 | tf_op jit(solution)/shard_map/ppermute | solution.py:276
  14.2 11.1 %collective-permute-start.33 = (f32[2,1,64,128]{3,2,1,0:T(8,128)}, f32[2,1,64,128]{3,2,1,0:T(8,128)S(1)}, u32[]{:S(2)}, u32[]{:S(2)}) collective-permute-start(f32[2,1,64,128]{3,2,1,0:T(8,128)} %get-tuple-element.134), channel_id=1, source_target_pairs={{0,3},{1,2},{2,1},{3,0},{4,7},{5,6},{6,5},{7,4},{8,11},{9,10},{10,... | collective-permute-start | bytes 196616 | tf_op jit(solution)/shard_map/ppermute | solution.py:276
  16.6 10.3 %collective-permute-start.34 = (f32[2,1,64,128]{3,2,1,0:T(8,128)}, f32[2,1,64,128]{3,2,1,0:T(8,128)S(1)}, u32[]{:S(2)}, u32[]{:S(2)}) collective-permute-start(f32[2,1,64,128]{3,2,1,0:T(8,128)} %get-tuple-element.135), channel_id=1, source_target_pairs={{0,1},{1,0},{2,3},{3,2},{4,5},{5,4},{6,7},{7,6},{8,9},{9,8},{10,11... | collective-permute-start | bytes 196616 | tf_op jit(solution)/shard_map/ppermute | solution.py:276
  20.7 10.3 %collective-permute-start.14 = (f32[2,1,64,128]{3,2,1,0:T(8,128)}, f32[2,1,64,128]{3,2,1,0:T(8,128)S(1)}, u32[]{:S(2)}, u32[]{:S(2)}) collective-permute-start(f32[2,1,64,128]{3,2,1,0:T(8,128)} %get-tuple-element.113), channel_id=1, source_target_pairs={{0,6},{1,7},{2,4},{3,5},{4,2},{5,3},{6,0},{7,1},{8,14},{9,15},{10,... | collective-permute-start | bytes 196616 | tf_op jit(solution)/shard_map/ppermute | solution.py:276
  24.1 7.3 %collective-permute-start.15 = (f32[2,1,64,128]{3,2,1,0:T(8,128)}, f32[2,1,64,128]{3,2,1,0:T(8,128)S(1)}, u32[]{:S(2)}, u32[]{:S(2)}) collective-permute-start(f32[2,1,64,128]{3,2,1,0:T(8,128)} %get-tuple-element.114), channel_id=1, source_target_pairs={{0,7},{1,6},{2,5},{3,4},{4,3},{5,2},{6,1},{7,0},{8,15},{9,14},{10,... | collective-permute-start | bytes 196616 | tf_op jit(solution)/shard_map/ppermute | solution.py:276
  24.1 11.1 %collective-permute-start.16 = (f32[2,1,64,128]{3,2,1,0:T(8,128)}, f32[2,1,64,128]{3,2,1,0:T(8,128)S(1)}, u32[]{:S(2)}, u32[]{:S(2)}) collective-permute-start(f32[2,1,64,128]{3,2,1,0:T(8,128)} %get-tuple-element.115), channel_id=1, source_target_pairs={{0,4},{1,5},{2,6},{3,7},{4,0},{5,1},{6,2},{7,3},{8,12},{9,13},{10,... | collective-permute-start | bytes 196616 | tf_op jit(solution)/shard_map/ppermute | solution.py:276
  25.3 13.0 %collective-permute-start.17 = (f32[2,1,64,128]{3,2,1,0:T(8,128)}, f32[2,1,64,128]{3,2,1,0:T(8,128)S(1)}, u32[]{:S(2)}, u32[]{:S(2)}) collective-permute-start(f32[2,1,64,128]{3,2,1,0:T(8,128)} %get-tuple-element.116), channel_id=1, source_target_pairs={{0,5},{1,4},{2,7},{3,6},{4,1},{5,0},{6,3},{7,2},{8,13},{9,12},{10,... | collective-permute-start | bytes 196616 | tf_op jit(solution)/shard_map/ppermute | solution.py:276
  26.9 11.5 %collective-permute-start.18 = (f32[2,1,64,128]{3,2,1,0:T(8,128)}, f32[2,1,64,128]{3,2,1,0:T(8,128)S(1)}, u32[]{:S(2)}, u32[]{:S(2)}) collective-permute-start(f32[2,1,64,128]{3,2,1,0:T(8,128)} %get-tuple-element.117), channel_id=1, source_target_pairs={{0,2},{1,3},{2,0},{3,1},{4,6},{5,7},{6,4},{7,5},{8,10},{9,11},{10,... | collective-permute-start | bytes 196616 | tf_op jit(solution)/shard_map/ppermute | solution.py:276
  31.0 12.1 %collective-permute-start.19 = (f32[2,1,64,128]{3,2,1,0:T(8,128)S(1)}, f32[2,1,64,128]{3,2,1,0:T(8,128)S(1)}, u32[]{:S(2)}, u32[]{:S(2)}) collective-permute-start(f32[2,1,64,128]{3,2,1,0:T(8,128)S(1)} %copy-done.61), channel_id=1, source_target_pairs={{0,3},{1,2},{2,1},{3,0},{4,7},{5,6},{6,5},{7,4},{8,11},{9,10},{10,... | collective-permute-start | bytes 196616 | tf_op jit(solution)/shard_map/ppermute | solution.py:276
  31.4 14.8 %collective-permute-start.20 = (f32[2,1,64,128]{3,2,1,0:T(8,128)S(1)}, f32[2,1,64,128]{3,2,1,0:T(8,128)S(1)}, u32[]{:S(2)}, u32[]{:S(2)}) collective-permute-start(f32[2,1,64,128]{3,2,1,0:T(8,128)S(1)} %copy-done.60), channel_id=1, source_target_pairs={{0,1},{1,0},{2,3},{3,2},{4,5},{5,4},{6,7},{7,6},{8,9},{9,8},{10,11... | collective-permute-start | bytes 196616 | tf_op jit(solution)/shard_map/ppermute | solution.py:276
  35.2 12.1 %collective-permute-start = (f32[2,1,64,128]{3,2,1,0:T(8,128)}, f32[2,1,64,128]{3,2,1,0:T(8,128)S(1)}, u32[]{:S(2)}, u32[]{:S(2)}) collective-permute-start(f32[2,1,64,128]{3,2,1,0:T(8,128)} %get-tuple-element.97), channel_id=1, source_target_pairs={{0,6},{1,7},{2,4},{3,5},{4,2},{5,3},{6,0},{7,1},{8,14},{9,15},{10,... | collective-permute-start | bytes 196616 | tf_op jit(solution)/shard_map/ppermute | solution.py:276
  38.3 9.4 %collective-permute-start.1 = (f32[2,1,64,128]{3,2,1,0:T(8,128)}, f32[2,1,64,128]{3,2,1,0:T(8,128)S(1)}, u32[]{:S(2)}, u32[]{:S(2)}) collective-permute-start(f32[2,1,64,128]{3,2,1,0:T(8,128)} %get-tuple-element.98), channel_id=1, source_target_pairs={{0,7},{1,6},{2,5},{3,4},{4,3},{5,2},{6,1},{7,0},{8,15},{9,14},{10,... | collective-permute-start | bytes 196616 | tf_op jit(solution)/shard_map/ppermute | solution.py:276
  38.4 15.8 %collective-permute-start.2 = (f32[2,1,64,128]{3,2,1,0:T(8,128)}, f32[2,1,64,128]{3,2,1,0:T(8,128)S(1)}, u32[]{:S(2)}, u32[]{:S(2)}) collective-permute-start(f32[2,1,64,128]{3,2,1,0:T(8,128)} %get-tuple-element.99), channel_id=1, source_target_pairs={{0,4},{1,5},{2,6},{3,7},{4,0},{5,1},{6,2},{7,3},{8,12},{9,13},{10,... | collective-permute-start | bytes 196616 | tf_op jit(solution)/shard_map/ppermute | solution.py:276
  43.2 20.0 %collective-permute-start.3 = (f32[2,1,64,128]{3,2,1,0:T(8,128)S(1)}, f32[2,1,64,128]{3,2,1,0:T(8,128)S(1)}, u32[]{:S(2)}, u32[]{:S(2)}) collective-permute-start(f32[2,1,64,128]{3,2,1,0:T(8,128)S(1)} %copy-done.59), channel_id=1, source_target_pairs={{0,5},{1,4},{2,7},{3,6},{4,1},{5,0},{6,3},{7,2},{8,13},{9,12},{10,... | collective-permute-start | bytes 196616 | tf_op jit(solution)/shard_map/ppermute | solution.py:276
  46.2 17.2 %collective-permute-start.4 = (f32[2,1,64,128]{3,2,1,0:T(8,128)S(1)}, f32[2,1,64,128]{3,2,1,0:T(8,128)S(1)}, u32[]{:S(2)}, u32[]{:S(2)}) collective-permute-start(f32[2,1,64,128]{3,2,1,0:T(8,128)S(1)} %copy-done.58), channel_id=1, source_target_pairs={{0,2},{1,3},{2,0},{3,1},{4,6},{5,7},{6,4},{7,5},{8,10},{9,11},{10,... | collective-permute-start | bytes 196616 | tf_op jit(solution)/shard_map/ppermute | solution.py:276
  47.3 16.4 %collective-permute-start.5 = (f32[2,1,64,128]{3,2,1,0:T(8,128)S(1)}, f32[2,1,64,128]{3,2,1,0:T(8,128)S(1)}, u32[]{:S(2)}, u32[]{:S(2)}) collective-permute-start(f32[2,1,64,128]{3,2,1,0:T(8,128)S(1)} %copy-done.57), channel_id=1, source_target_pairs={{0,3},{1,2},{2,1},{3,0},{4,7},{5,6},{6,5},{7,4},{8,11},{9,10},{10,... | collective-permute-start | bytes 196616 | tf_op jit(solution)/shard_map/ppermute | solution.py:276
  47.7 18.8 %collective-permute-start.6 = (f32[2,1,64,128]{3,2,1,0:T(8,128)S(1)}, f32[2,1,64,128]{3,2,1,0:T(8,128)S(1)}, u32[]{:S(2)}, u32[]{:S(2)}) collective-permute-start(f32[2,1,64,128]{3,2,1,0:T(8,128)S(1)} %copy-done.56), channel_id=1, source_target_pairs={{0,1},{1,0},{2,3},{3,2},{4,5},{5,4},{6,7},{7,6},{8,9},{9,8},{10,11... | collective-permute-start | bytes 196616 | tf_op jit(solution)/shard_map/ppermute | solution.py:276
  54.3 15.3 %collective-permute-start.21 = (f32[1,64,128]{2,1,0:T(8,128)}, f32[1,64,128]{2,1,0:T(8,128)S(1)}, u32[]{:S(2)}, u32[]{:S(2)}) collective-permute-start(f32[1,64,128]{2,1,0:T(8,128)} %get-tuple-element.121), channel_id=1, source_target_pairs={{0,6},{1,7},{2,4},{3,5},{4,2},{5,3},{6,0},{7,1},{8,14},{9,15},{10,... | collective-permute-start | bytes 98312 | tf_op jit(solution)/shard_map/ppermute | solution.py:276
  63.2 6.5 %collective-permute-start.22 = (f32[1,64,128]{2,1,0:T(8,128)S(1)}, f32[1,64,128]{2,1,0:T(8,128)S(1)}, u32[]{:S(2)}, u32[]{:S(2)}) collective-permute-start(f32[1,64,128]{2,1,0:T(8,128)S(1)} %copy-done.87), channel_id=1, source_target_pairs={{0,7},{1,6},{2,5},{3,4},{4,3},{5,2},{6,1},{7,0},{8,15},{9,14},{10,... | collective-permute-start | bytes 98312 | tf_op jit(solution)/shard_map/ppermute | solution.py:276
  63.4 6.6 %collective-permute-start.23 = (f32[1,64,128]{2,1,0:T(8,128)S(1)}, f32[1,64,128]{2,1,0:T(8,128)S(1)}, u32[]{:S(2)}, u32[]{:S(2)}) collective-permute-start(f32[1,64,128]{2,1,0:T(8,128)S(1)} %copy-done.85), channel_id=1, source_target_pairs={{0,4},{1,5},{2,6},{3,7},{4,0},{5,1},{6,2},{7,3},{8,12},{9,13},{10,... | collective-permute-start | bytes 98312 | tf_op jit(solution)/shard_map/ppermute | solution.py:276
  63.7 9.0 %collective-permute-start.24 = (f32[1,64,128]{2,1,0:T(8,128)S(1)}, f32[1,64,128]{2,1,0:T(8,128)S(1)}, u32[]{:S(2)}, u32[]{:S(2)}) collective-permute-start(f32[1,64,128]{2,1,0:T(8,128)S(1)} %copy-done.83), channel_id=1, source_target_pairs={{0,5},{1,4},{2,7},{3,6},{4,1},{5,0},{6,3},{7,2},{8,13},{9,12},{10,... | collective-permute-start | bytes 98312 | tf_op jit(solution)/shard_map/ppermute | solution.py:276
  66.5 7.3 %collective-permute-start.35 = (f32[1,64,128]{2,1,0:T(8,128)}, f32[1,64,128]{2,1,0:T(8,128)S(1)}, u32[]{:S(2)}, u32[]{:S(2)}) collective-permute-start(f32[1,64,128]{2,1,0:T(8,128)} %get-tuple-element.137), channel_id=1, source_target_pairs={{0,6},{1,7},{2,4},{3,5},{4,2},{5,3},{6,0},{7,1},{8,14},{9,15},{10,... | collective-permute-start | bytes 98312 | tf_op jit(solution)/shard_map/ppermute | solution.py:276
  69.7 11.5 %collective-permute-start.37 = (f32[1,64,128]{2,1,0:T(8,128)}, f32[1,64,128]{2,1,0:T(8,128)S(1)}, u32[]{:S(2)}, u32[]{:S(2)}) collective-permute-start(f32[1,64,128]{2,1,0:T(8,128)} %get-tuple-element.139), channel_id=1, source_target_pairs={{0,4},{1,5},{2,6},{3,7},{4,0},{5,1},{6,2},{7,3},{8,12},{9,13},{10,... | collective-permute-start | bytes 98312 | tf_op jit(solution)/shard_map/ppermute | solution.py:276
  70.0 11.8 %collective-permute-start.38 = (f32[1,64,128]{2,1,0:T(8,128)}, f32[1,64,128]{2,1,0:T(8,128)S(1)}, u32[]{:S(2)}, u32[]{:S(2)}) collective-permute-start(f32[1,64,128]{2,1,0:T(8,128)} %get-tuple-element.140), channel_id=1, source_target_pairs={{0,5},{1,4},{2,7},{3,6},{4,1},{5,0},{6,3},{7,2},{8,13},{9,12},{10,... | collective-permute-start | bytes 98312 | tf_op jit(solution)/shard_map/ppermute | solution.py:276
  72.7 10.5 %collective-permute-start.39 = (f32[1,64,128]{2,1,0:T(8,128)}, f32[1,64,128]{2,1,0:T(8,128)S(1)}, u32[]{:S(2)}, u32[]{:S(2)}) collective-permute-start(f32[1,64,128]{2,1,0:T(8,128)} %get-tuple-element.141), channel_id=1, source_target_pairs={{0,2},{1,3},{2,0},{3,1},{4,6},{5,7},{6,4},{7,5},{8,10},{9,11},{10,... | collective-permute-start | bytes 98312 | tf_op jit(solution)/shard_map/ppermute | solution.py:276
  73.8 9.8 %collective-permute-start.40 = (f32[1,64,128]{2,1,0:T(8,128)}, f32[1,64,128]{2,1,0:T(8,128)S(1)}, u32[]{:S(2)}, u32[]{:S(2)}) collective-permute-start(f32[1,64,128]{2,1,0:T(8,128)} %get-tuple-element.142), channel_id=1, source_target_pairs={{0,3},{1,2},{2,1},{3,0},{4,7},{5,6},{6,5},{7,4},{8,11},{9,10},{10,... | collective-permute-start | bytes 98312 | tf_op jit(solution)/shard_map/ppermute | solution.py:276
  75.4 10.8 %collective-permute-start.41 = (f32[1,64,128]{2,1,0:T(8,128)}, f32[1,64,128]{2,1,0:T(8,128)S(1)}, u32[]{:S(2)}, u32[]{:S(2)}) collective-permute-start(f32[1,64,128]{2,1,0:T(8,128)} %get-tuple-element.143), channel_id=1, source_target_pairs={{0,1},{1,0},{2,3},{3,2},{4,5},{5,4},{6,7},{7,6},{8,9},{9,8},{10,11... | collective-permute-start | bytes 98312 | tf_op jit(solution)/shard_map/ppermute | solution.py:276
  81.2 8.6 %collective-permute-start.25 = (f32[1,64,128]{2,1,0:T(8,128)S(1)}, f32[1,64,128]{2,1,0:T(8,128)S(1)}, u32[]{:S(2)}, u32[]{:S(2)}) collective-permute-start(f32[1,64,128]{2,1,0:T(8,128)S(1)} %copy-done.71), channel_id=1, source_target_pairs={{0,2},{1,3},{2,0},{3,1},{4,6},{5,7},{6,4},{7,5},{8,10},{9,11},{10,... | collective-permute-start | bytes 98312 | tf_op jit(solution)/shard_map/ppermute | solution.py:276
  81.8 8.1 %collective-permute-start.26 = (f32[1,64,128]{2,1,0:T(8,128)S(1)}, f32[1,64,128]{2,1,0:T(8,128)S(1)}, u32[]{:S(2)}, u32[]{:S(2)}) collective-permute-start(f32[1,64,128]{2,1,0:T(8,128)S(1)} %copy-done.70), channel_id=1, source_target_pairs={{0,3},{1,2},{2,1},{3,0},{4,7},{5,6},{6,5},{7,4},{8,11},{9,10},{10,... | collective-permute-start | bytes 98312 | tf_op jit(solution)/shard_map/ppermute | solution.py:276
  83.2 9.5 %collective-permute-start.27 = (f32[1,64,128]{2,1,0:T(8,128)S(1)}, f32[1,64,128]{2,1,0:T(8,128)S(1)}, u32[]{:S(2)}, u32[]{:S(2)}) collective-permute-start(f32[1,64,128]{2,1,0:T(8,128)S(1)} %copy-done.69), channel_id=1, source_target_pairs={{0,1},{1,0},{2,3},{3,2},{4,5},{5,4},{6,7},{7,6},{8,9},{9,8},{10,11... | collective-permute-start | bytes 98312 | tf_op jit(solution)/shard_map/ppermute | solution.py:276
  83.6 9.7 %collective-permute-start.7 = (f32[1,64,128]{2,1,0:T(8,128)}, f32[1,64,128]{2,1,0:T(8,128)S(1)}, u32[]{:S(2)}, u32[]{:S(2)}) collective-permute-start(f32[1,64,128]{2,1,0:T(8,128)} %get-tuple-element.105), channel_id=1, source_target_pairs={{0,6},{1,7},{2,4},{3,5},{4,2},{5,3},{6,0},{7,1},{8,14},{9,15},{10,... | collective-permute-start | bytes 98312 | tf_op jit(solution)/shard_map/ppermute | solution.py:276
  86.1 8.2 %collective-permute-start.8 = (f32[1,64,128]{2,1,0:T(8,128)}, f32[1,64,128]{2,1,0:T(8,128)S(1)}, u32[]{:S(2)}, u32[]{:S(2)}) collective-permute-start(f32[1,64,128]{2,1,0:T(8,128)} %get-tuple-element.106), channel_id=1, source_target_pairs={{0,7},{1,6},{2,5},{3,4},{4,3},{5,2},{6,1},{7,0},{8,15},{9,14},{10,... | collective-permute-start | bytes 98312 | tf_op jit(solution)/shard_map/ppermute | solution.py:276
  89.8 8.1 %collective-permute-start.9 = (f32[1,64,128]{2,1,0:T(8,128)}, f32[1,64,128]{2,1,0:T(8,128)S(1)}, u32[]{:S(2)}, u32[]{:S(2)}) collective-permute-start(f32[1,64,128]{2,1,0:T(8,128)} %get-tuple-element.107), channel_id=1, source_target_pairs={{0,4},{1,5},{2,6},{3,7},{4,0},{5,1},{6,2},{7,3},{8,12},{9,13},{10,... | collective-permute-start | bytes 98312 | tf_op jit(solution)/shard_map/ppermute | solution.py:276
  89.9 8.0 %collective-permute-start.10 = (f32[1,64,128]{2,1,0:T(8,128)}, f32[1,64,128]{2,1,0:T(8,128)S(1)}, u32[]{:S(2)}, u32[]{:S(2)}) collective-permute-start(f32[1,64,128]{2,1,0:T(8,128)} %get-tuple-element.108), channel_id=1, source_target_pairs={{0,5},{1,4},{2,7},{3,6},{4,1},{5,0},{6,3},{7,2},{8,13},{9,12},{10,... | collective-permute-start | bytes 98312 | tf_op jit(solution)/shard_map/ppermute | solution.py:276
  101.6 10.7 %collective-permute-start.42 = (f32[1,64,128]{2,1,0:T(8,128)}, f32[1,64,128]{2,1,0:T(8,128)S(1)}, u32[]{:S(2)}, u32[]{:S(2)}) collective-permute-start(f32[1,64,128]{2,1,0:T(8,128)} %get-tuple-element.151), channel_id=1, source_target_pairs={{0,6},{1,7},{2,4},{3,5},{4,2},{5,3},{6,0},{7,1},{8,14},{9,15},{10,... | collective-permute-start | bytes 98312 | tf_op jit(solution)/shard_map/ppermute | solution.py:276
  107.6 7.5 %collective-permute-start.43 = (f32[1,64,128]{2,1,0:T(8,128)}, f32[1,64,128]{2,1,0:T(8,128)S(1)}, u32[]{:S(2)}, u32[]{:S(2)}) collective-permute-start(f32[1,64,128]{2,1,0:T(8,128)} %get-tuple-element.152), channel_id=1, source_target_pairs={{0,7},{1,6},{2,5},{3,4},{4,3},{5,2},{6,1},{7,0},{8,15},{9,14},{10,... | collective-permute-start | bytes 98312 | tf_op jit(solution)/shard_map/ppermute | solution.py:276
  108.9 6.6 %collective-permute-start.49 = (f32[1,64,128]{2,1,0:T(8,128)S(1)}, f32[1,64,128]{2,1,0:T(8,128)S(1)}, u32[]{:S(2)}, u32[]{:S(2)}) collective-permute-start(f32[1,64,128]{2,1,0:T(8,128)S(1)} %copy-done.80), channel_id=1, source_target_pairs={{0,6},{1,7},{2,4},{3,5},{4,2},{5,3},{6,0},{7,1},{8,14},{9,15},{10,... | collective-permute-start | bytes 98312 | tf_op jit(solution)/shard_map/ppermute | solution.py:276
  112.3 7.7 %collective-permute-start.52 = (f32[1,64,128]{2,1,0:T(8,128)S(1)}, f32[1,64,128]{2,1,0:T(8,128)S(1)}, u32[]{:S(2)}, u32[]{:S(2)}) collective-permute-start(f32[1,64,128]{2,1,0:T(8,128)S(1)} %copy-done.75), channel_id=1, source_target_pairs={{0,5},{1,4},{2,7},{3,6},{4,1},{5,0},{6,3},{7,2},{8,13},{9,12},{10,... | collective-permute-start | bytes 98312 | tf_op jit(solution)/shard_map/ppermute | solution.py:276
  116.8 7.3 %collective-permute-start.55 = (f32[1,64,128]{2,1,0:T(8,128)S(1)}, f32[1,64,128]{2,1,0:T(8,128)S(1)}, u32[]{:S(2)}, u32[]{:S(2)}) collective-permute-start(f32[1,64,128]{2,1,0:T(8,128)S(1)} %copy-done.72), channel_id=1, source_target_pairs={{0,1},{1,0},{2,3},{3,2},{4,5},{5,4},{6,7},{7,6},{8,9},{9,8},{10,11... | collective-permute-start | bytes 98312 | tf_op jit(solution)/shard_map/ppermute | solution.py:276
  117.7 6.6 %collective-permute-start.56 = (f32[1,64,128]{2,1,0:T(8,128)S(1)}, f32[1,64,128]{2,1,0:T(8,128)S(1)}, u32[]{:S(2)}, u32[]{:S(2)}) collective-permute-start(f32[1,64,128]{2,1,0:T(8,128)S(1)} %copy-done.68), channel_id=1, source_target_pairs={{0,6},{1,7},{2,4},{3,5},{4,2},{5,3},{6,0},{7,1},{8,14},{9,15},{10,... | collective-permute-start | bytes 98312 | tf_op jit(solution)/shard_map/ppermute | solution.py:276
  121.1 6.9 %collective-permute-start.59 = (f32[1,64,128]{2,1,0:T(8,128)S(1)}, f32[1,64,128]{2,1,0:T(8,128)S(1)}, u32[]{:S(2)}, u32[]{:S(2)}) collective-permute-start(f32[1,64,128]{2,1,0:T(8,128)S(1)} %copy-done.65), channel_id=1, source_target_pairs={{0,5},{1,4},{2,7},{3,6},{4,1},{5,0},{6,3},{7,2},{8,13},{9,12},{10,... | collective-permute-start | bytes 98312 | tf_op jit(solution)/shard_map/ppermute | solution.py:276
  126.9 9.9 %collective-permute-start.44 = (f32[1,64,128]{2,1,0:T(8,128)}, f32[1,64,128]{2,1,0:T(8,128)S(1)}, u32[]{:S(2)}, u32[]{:S(2)}) collective-permute-start(f32[1,64,128]{2,1,0:T(8,128)} %get-tuple-element.153), channel_id=1, source_target_pairs={{0,4},{1,5},{2,6},{3,7},{4,0},{5,1},{6,2},{7,3},{8,12},{9,13},{10,... | collective-permute-start | bytes 98312 | tf_op jit(solution)/shard_map/ppermute | solution.py:276
  128.0 8.8 %collective-permute-start.45 = (f32[1,64,128]{2,1,0:T(8,128)}, f32[1,64,128]{2,1,0:T(8,128)S(1)}, u32[]{:S(2)}, u32[]{:S(2)}) collective-permute-start(f32[1,64,128]{2,1,0:T(8,128)} %get-tuple-element.154), channel_id=1, source_target_pairs={{0,5},{1,4},{2,7},{3,6},{4,1},{5,0},{6,3},{7,2},{8,13},{9,12},{10,... | collective-permute-start | bytes 98312 | tf_op jit(solution)/shard_map/ppermute | solution.py:276
  129.2 7.6 %collective-permute-start.46 = (f32[1,64,128]{2,1,0:T(8,128)}, f32[1,64,128]{2,1,0:T(8,128)S(1)}, u32[]{:S(2)}, u32[]{:S(2)}) collective-permute-start(f32[1,64,128]{2,1,0:T(8,128)} %get-tuple-element.155), channel_id=1, source_target_pairs={{0,2},{1,3},{2,0},{3,1},{4,6},{5,7},{6,4},{7,5},{8,10},{9,11},{10,... | collective-permute-start | bytes 98312 | tf_op jit(solution)/shard_map/ppermute | solution.py:276
  129.9 6.9 %collective-permute-start.47 = (f32[1,64,128]{2,1,0:T(8,128)}, f32[1,64,128]{2,1,0:T(8,128)S(1)}, u32[]{:S(2)}, u32[]{:S(2)}) collective-permute-start(f32[1,64,128]{2,1,0:T(8,128)} %get-tuple-element.156), channel_id=1, source_target_pairs={{0,3},{1,2},{2,1},{3,0},{4,7},{5,6},{6,5},{7,4},{8,11},{9,10},{10,... | collective-permute-start | bytes 98312 | tf_op jit(solution)/shard_map/ppermute | solution.py:276
  (107 other events, 1011.5 us)

commit v5 on v1

--- a/solution.py
+++ b/solution.py
@@ -15,7 +15,7 @@
 RK_ZETA = -17.0 / 60.0
 WAVE_SCALE = 8.0
 VMEM_LIMIT = 56 * 1024 * 1024
-GROUPS = 3
+GROUPS = 1
 LANES = 128
 
 F32 = jnp.float32
@@ -134,7 +134,8 @@
     wave_ref[...] = jnp.concatenate([picked, picked], axis=1)[:8]
 
 
-def pack_kernel(devices, info_ref, modes_ref, state_ref, now_ref, old_ref, *out_refs):
+def pack_kernel(devices, me_ref, info_ref, modes_ref, state_ref, now_ref, old_ref, out_ref):
+    me = me_ref[0]
     comps, points, columns = state_ref.shape
     share = columns // devices
     wave = wave_row(modes_ref[...]).reshape(1, 1, columns)
@@ -148,13 +149,13 @@
             three_parts(both), selector(info_ref[0:1, :], columns), NT, preferred_element_type=F32
         )
     )
-    for step, out in enumerate(out_refs):
+    for step in range(devices):
         taken = placed[:, step * share : (step + 1) * share]
         for kind in range(2):
             for pair in range(comps // 2):
                 real = (kind * comps + 2 * pair) * points
                 imag = real + points
-                out[kind, pair] = jnp.concatenate(
+                out_ref[me ^ step, kind, pair] = jnp.concatenate(
                     [taken[real : real + points], taken[imag : imag + points]], axis=1
                 )
 
@@ -172,35 +173,31 @@
     return jnp.dot(operator, jnp.concatenate([high, low, high], axis=0), preferred_element_type=F32)
 
 
-def solve_kernel(devices, me_ref, wave_ref, values_ref, deriv_ref, inverse_ref, basis_ref, *refs):
-    in_refs, refs = refs[:devices], refs[devices:]
-    out_refs, (solved_ref, state, local, after) = refs[:devices], refs[devices:]
-    me = me_ref[0]
-    _, pairs, points, lanes = in_refs[0].shape
-    for step, block in enumerate(in_refs):
-        rows = pl.ds(pl.multiple_of((me ^ step) * points, points), points)
+def solve_kernel(devices, wave_ref, values_ref, deriv_ref, inverse_ref, basis_ref, in_ref, out_ref, solved_ref, state, local):
+    _, _, pairs, points, lanes = in_ref.shape
+    for device in range(devices):
+        rows = slice(device * points, (device + 1) * points)
         for pair in range(pairs):
-            state[rows, pair * lanes : (pair + 1) * lanes] = block[0, pair]
-            local[rows, pair * lanes : (pair + 1) * lanes] = block[1, pair]
+            state[rows, pair * lanes : (pair + 1) * lanes] = in_ref[device, 0, pair]
+            local[rows, pair * lanes : (pair + 1) * lanes] = in_ref[device, 1, pair]
     rhs = local[...] + (TIME_STEP * RK_ALPHA) * apply(deriv_ref[...], state[...])
     project = apply(inverse_ref[...], rhs)
     damping = 1.0 + TIME_STEP * RK_BETA * (values_ref[...] + wave_ref[0:1, :])
     project = project / jnp.concatenate([damping] * pairs, axis=1)
-    after[...] = apply(basis_ref[...], project)
+    after = apply(basis_ref[...], project)
     for pair in range(pairs):
-        solved_ref[pair] = after[:, pair * lanes : (pair + 1) * lanes]
-    for step, block in enumerate(out_refs):
-        rows = pl.ds(pl.multiple_of((me ^ step) * points, points), points)
-        for pair in range(pairs):
-            block[pair] = after[rows, pair * lanes : (pair + 1) * lanes]
-
-
-def unpack_kernel(devices, chunk, first, info_ref, modes_ref, velocity_ref, *refs):
-    in_refs, refs = refs[:devices], refs[devices:]
+        solved = after[:, pair * lanes : (pair + 1) * lanes]
+        solved_ref[pair] = solved
+        for device in range(devices):
+            out_ref[device, pair] = solved[device * points : (device + 1) * points]
+
+
+def unpack_kernel(devices, chunk, first, me_ref, info_ref, modes_ref, velocity_ref, in_ref, *refs):
+    me = me_ref[0]
     if not first:
         (_, emf_in), refs = refs[:2], refs[2:]
-    (state_ref, emf_ref), out_refs = refs[:2], refs[2:]
-    pairs, points, lanes = in_refs[0].shape
+    state_ref, emf_ref, out_ref = refs
+    _, pairs, points, lanes = in_ref.shape
     share = lanes // 2
     columns = devices * share
     got = []
@@ -208,7 +205,7 @@
         for half in range(2):
             got.append(
                 jnp.concatenate(
-                    [block[pair][:, half * share : (half + 1) * share] for block in in_refs], axis=1
+                    [in_ref[me ^ step, pair][:, half * share : (half + 1) * share] for step in range(devices)], axis=1
                 )
             )
     got = jnp.concatenate(got, axis=0)
@@ -221,12 +218,12 @@
             three_parts(state), selector(info_ref[1:2, :], columns), NT, preferred_element_type=F32
         )
     )
-    for step, out in enumerate(out_refs):
+    for step in range(devices):
         taken = extra[:, step * share : (step + 1) * share]
         for pair in range(pairs):
             real = 2 * pair * points
             imag = real + points
-            out[pair] = jnp.concatenate([taken[real : real + points], taken[imag : imag + points]], axis=1)
+            out_ref[me ^ step, pair] = jnp.concatenate([taken[real : real + points], taken[imag : imag + points]], axis=1)
     weight = jnp.where(modes_ref[0:1, :] > 0, 2.0, 1.0).astype(F32)
     totals = [jnp.zeros((points, columns), F32)] * 3
     for pair in range(pairs):
@@ -245,13 +242,9 @@
     emf_ref[...] = rows if first else rows + emf_in[...]
 
 
-def assemble_kernel(devices, first, me_ref, info_ref, solved_ref, *refs):
-    in_refs, refs = refs[:devices], refs[devices:]
-    if not first:
-        refs = refs[1:]
-    (out_ref,) = refs
-    me = me_ref[0]
-    pairs, points, lanes = in_refs[0].shape
+def assemble_kernel(devices, first, info_ref, solved_ref, in_ref, *refs):
+    out_ref = refs[-1]
+    _, pairs, points, lanes = in_ref.shape
     share = lanes // 2
     depth = solved_ref.shape[1]
     used = lax.broadcasted_iota(jnp.int32, (depth, share), 1) < info_ref[2:3, :share]
@@ -259,16 +252,13 @@
         for half in range(2):
             kept = jnp.where(used, solved_ref[pair][:, half * share : (half + 1) * share], 0.0)
             out_ref[2 * pair + half, :, :share] = kept
-            for step, block in enumerate(in_refs):
-                rows = pl.ds(pl.multiple_of((me ^ step) * points, points), points)
-                out_ref[2 * pair + half, rows, share:] = block[pair][:, half * share : (half + 1) * share]
+            for device in range(devices):
+                rows = slice(device * points, (device + 1) * points)
+                out_ref[2 * pair + half, rows, share:] = in_ref[device, pair][:, half * share : (half + 1) * share]
 
 
 def exchange(blocks):
-    devices = len(blocks)
-    return [blocks[0]] + [
-        lax.ppermute(blocks[step], "col", [(i, i ^ step) for i in range(devices)]) for step in range(1, devices)
-    ]
+    return lax.all_to_all(blocks, "col", split_axis=0, concat_axis=0, tiled=True)
 
 
 def sum_over_groups(value):
@@ -313,8 +303,8 @@
     )(me, owner, kept_modes)
 
     field = (2 * pairs, points, columns)
-    sent = (2, pairs, points, lanes)
-    back = (pairs, points, lanes)
+    sent = (devices, 2, pairs, points, lanes)
+    back = (devices, pairs, points, lanes)
     moved = 4 * 2 * pairs * points * columns
 
     forward = []
@@ -323,12 +313,12 @@
             exchange(
                 call(
                     functools.partial(pack_kernel, devices),
-                    [shaped(sent)] * devices,
-                    [whole((8, columns)), whole((2, columns))] + [part(field, chunk)] * 3,
-                    [whole(sent)] * devices,
+                    shaped(sent),
+                    [scalar(), whole((8, columns)), whole((2, columns))] + [part(field, chunk)] * 3,
+                    whole(sent),
                     12 * 2 * pairs * points * columns * columns,
                     5 * moved,
-                )(info, kept_modes, state_now, force_now, force_old)
+                )(me, info, kept_modes, state_now, force_now, force_old)
             )
         )
 
@@ -348,34 +338,31 @@
         width = pairs * lanes
         outs = call(
             functools.partial(solve_kernel, devices),
-            [shaped(back)] * devices + [shaped((pairs, depth, lanes))],
-            [scalar(), whole((8, lanes)), whole((depth, lanes))]
-            + [whole((depth, 3 * depth))] * 3
-            + [whole(sent)] * devices,
-            [whole(back)] * devices + [whole((pairs, depth, lanes))],
+            [shaped(back), shaped((pairs, depth, lanes))],
+            [whole((8, lanes)), whole((depth, lanes))] + [whole((depth, 3 * depth))] * 3 + [whole(sent)],
+            [whole(back), whole((pairs, depth, lanes))],
             18 * depth * depth * width,
             18 * depth * depth + 16 * depth * width,
-            [pltpu.VMEM((depth, width), F32)] * 3,
-        )(me, wave, values, *operators[:3], *forward[chunk])
-        solved.append(outs[devices])
-        returned.append(exchange(outs[:devices]))
+            [pltpu.VMEM((depth, width), F32)] * 2,
+        )(wave, values, *operators[:3], forward[chunk])
+        solved.append(outs[1])
+        returned.append(exchange(outs[0]))
 
     state_next, emf, extra = None, None, []
     for chunk in range(chunks):
         first = chunk == 0
         outs = call(
             functools.partial(unpack_kernel, devices, chunk, first),
-            [shaped(state_now.shape), shaped((3, points))] + [shaped(back)] * devices,
-            [whole((8, columns)), whole((2, columns)), whole(velocity.shape)]
-            + [whole(back)] * devices
+            [shaped(state_now.shape), shaped((3, points)), shaped(back)],
+            [scalar(), whole((8, columns)), whole((2, columns)), whole(velocity.shape), whole(back)]
             + ([] if first else [untouched(), whole((3, points))]),
-            [part(field, chunk), whole((3, points))] + [whole(back)] * devices,
+            [part(field, chunk), whole((3, points)), whole(back)],
             12 * 2 * pairs * points * columns * columns,
             6 * moved,
-            aliases={} if first else {3 + devices: 0},
-        )(info, kept_modes, velocity, *returned[chunk], *([] if first else [state_next, emf]))
+            aliases={} if first else {5: 0},
+        )(me, info, kept_modes, velocity, returned[chunk], *([] if first else [state_next, emf]))
         state_next, emf = outs[:2]
-        extra.append(exchange(outs[2:]))
+        extra.append(exchange(outs[2]))
     mean_emf = sum_over_groups(emf)
 
     owned = None
@@ -384,14 +371,12 @@
         owned = call(
             functools.partial(assemble_kernel, devices, first),
             shaped((comps, depth, lanes)),
-            [scalar(), whole((8, columns)), whole((pairs, depth, lanes))]
-            + [whole(back)] * devices
-            + ([] if first else [untouched()]),
+            [whole((8, columns)), whole((pairs, depth, lanes)), whole(back)] + ([] if first else [untouched()]),
             part((2 * pairs, depth, lanes), chunk),
             1000000,
             16 * pairs * depth * lanes,
-            aliases={} if first else {3 + devices: 0},
-        )(me, info, solved[chunk], *extra[chunk], *([] if first else [owned]))
+            aliases={} if first else {3: 0},
+        )(info, solved[chunk], extra[chunk], *([] if first else [owned]))
     return (state_next, owned, mean_emf)
 
 

time: 111 us -> 150 us (1.35)
  the two profiles are of different devices: /device:TPU:9 before, /device:TPU:0 now
where the time goes in v5:
time: 150 us; the launch traced here: 149 us
  waiting for transfers between devices  52.4 us (35%)
  Pallas kernels  45.9 us (31%)
  starting transfers between devices  33.9 us (23%)
  blocking collectives  13.8 us (9%)
    all_to_all x8, waiting for transfers between devices, exchange(): lax.all_to_all(blocks, 'col', split_axis=0, concat_axis=0, tiled=True)  49.2 us
    all_to_all x8, starting transfers between devices, exchange(): lax.all_to_all(blocks, 'col', split_axis=0, concat_axis=0, tiled=True)  30.4 us
    pallas_call x3, Pallas kernels, on_device(): call(functools.partial(solve_kernel, devices), [shaped(back), shaped((pai...  17 us
    all_to_all x1, blocking collectives, exchange(): lax.all_to_all(blocks, 'col', split_axis=0, concat_axis=0, tiled=True)  13.8 us
    pallas_call x3, Pallas kernels, on_device(): call(functools.partial(unpack_kernel, devices, chunk, first), [shaped(sta...  8.5 us
    pallas_call x3, Pallas kernels, on_device(): call(functools.partial(pack_kernel, devices), shaped(sent), [scalar(), wh...  8.11 us
    pallas_call x3, Pallas kernels, on_device(): call(functools.partial(assemble_kernel, devices, first), shaped((comps, d...  6.12 us
    pallas_call x1, Pallas kernels, on_device(): call(operators_kernel, [operator, operator, operator, shaped((depth, lane...  4.5 us
  transfers between devices with their start and end apart: 11, of which 10 were waited for; matrix products, arithmetic and copies ran while one was open for 1% of the time, Pallas kernels for 27%

profile of v5, /device:TPU:0, one launch (start us, length us, event | category | flops | bytes accessed | tf_op | source)
XLA Modules:
  0.0 148.8 jit_solution(15737257195258975949)
XLA Ops:
  0.6 1.7 %shard_map.121 = (s32[8,512]{1,0:T(8,128)}, f32[8,128]{1,0:T(8,128)}) custom-call(s32[1]{0:T(128)} %bitcast.me_ref, s32[1,512]{1,0:T(1,128)} %bitcast.3, s32[2,512]{1,0:T(2,128)} %modes_ref.13), custom_call_target="tpu_custom_call" | custom-call | flops 1000000 | bytes 100000 | tf_op jit(solution)/shard_map/pallas_call | solution.py:296
  2.4 2.7 %shard_map.127 = f32[8,2,1,64,128]{4,3,2,1,0:T(8,128)} custom-call(s32[1]{0:T(128)} %bitcast.me_ref, s32[8,512]{1,0:T(8,128)} %get-tuple-element.24.info_ref, s32[2,512]{1,0:T(2,128)} %modes_ref.13, f32[6,64,512]{2,1,0:T(8,128)} %state_ref.5, f32[6,64,512]{2,1,0:T(8,128)} %now_ref.5, f32[6,64,512]{2,1,0:T(8,128)} %old_ref.5), custom_call_target="tpu_custom_call" | custom-call | flops 402653184 | bytes 1310720 | tf_op jit(solution)/shard_map/pallas_call | solution.py:314
  5.1 6.3 %all-to-all-start.4 = ((f32[8,2,1,64,128]{4,3,2,1,0:T(8,128)}), f32[8,2,1,64,128]{4,3,2,1,0:T(8,128)S(1)}, u32[]{:S(2)}, u32[]{:S(2)}) async-start(f32[8,2,1,64,128]{4,3,2,1,0:T(8,128)} %shard_map.127), calls=%async_computation.4 | async-start | bytes 1048576 | tf_op jit(solution)/shard_map/all_to_all | solution.py:261
  11.4 2.7 %shard_map.125 = f32[8,2,1,64,128]{4,3,2,1,0:T(8,128)} custom-call(s32[1]{0:T(128)} %bitcast.me_ref, s32[8,512]{1,0:T(8,128)} %get-tuple-element.24.info_ref, s32[2,512]{1,0:T(2,128)} %modes_ref.13, f32[6,64,512]{2,1,0:T(8,128)} %state_ref.5, f32[6,64,512]{2,1,0:T(8,128)} %now_ref.5, f32[6,64,512]{2,1,0:T(8,128)} %old_ref.5), custom_call_target="tpu_custom_call" | custom-call | flops 402653184 | bytes 1310720 | tf_op jit(solution)/shard_map/pallas_call | solution.py:314
  14.1 12.7 %all-to-all-done.4.in_ref = f32[8,2,1,64,128]{4,3,2,1,0:T(8,128)S(1)} async-done(((f32[8,2,1,64,128]{4,3,2,1,0:T(8,128)}), f32[8,2,1,64,128]{4,3,2,1,0:T(8,128)S(1)}, u32[]{:S(2)}, u32[]{:S(2)}) %all-to-all-start.4) | async-done | bytes 524320 | tf_op jit(solution)/shard_map/all_to_all | solution.py:261
  26.8 0.0 copy-start
  26.8 3.5 %all-to-all-start.2 = ((f32[8,2,1,64,128]{4,3,2,1,0:T(8,128)}), f32[8,2,1,64,128]{4,3,2,1,0:T(8,128)S(1)}, u32[]{:S(2)}, u32[]{:S(2)}) async-start(f32[8,2,1,64,128]{4,3,2,1,0:T(8,128)} %shard_map.125), calls=%async_computation.2 | async-start | bytes 1048576 | tf_op jit(solution)/shard_map/all_to_all | solution.py:261
  30.3 2.7 %shard_map.123 = f32[8,2,1,64,128]{4,3,2,1,0:T(8,128)} custom-call(s32[1]{0:T(128)} %bitcast.me_ref, s32[8,512]{1,0:T(8,128)} %get-tuple-element.24.info_ref, s32[2,512]{1,0:T(2,128)} %modes_ref.13, f32[6,64,512]{2,1,0:T(8,128)} %state_ref.5, f32[6,64,512]{2,1,0:T(8,128)} %now_ref.5, f32[6,64,512]{2,1,0:T(8,128)} %old_ref.5), custom_call_target="tpu_custom_call" | custom-call | flops 402653184 | bytes 1310720 | tf_op jit(solution)/shard_map/pallas_call | solution.py:314
  33.0 0.0 copy-done
  33.0 12.6 %all-to-all-done.2.in_ref = f32[8,2,1,64,128]{4,3,2,1,0:T(8,128)S(1)} async-done(((f32[8,2,1,64,128]{4,3,2,1,0:T(8,128)}), f32[8,2,1,64,128]{4,3,2,1,0:T(8,128)S(1)}, u32[]{:S(2)}, u32[]{:S(2)}) %all-to-all-start.2) | async-done | bytes 524320 | tf_op jit(solution)/shard_map/all_to_all | solution.py:261
  45.6 0.0 copy-start.2
  45.6 3.5 %all-to-all-start = ((f32[8,2,1,64,128]{4,3,2,1,0:T(8,128)}), f32[8,2,1,64,128]{4,3,2,1,0:T(8,128)S(1)}, u32[]{:S(2)}, u32[]{:S(2)}) async-start(f32[8,2,1,64,128]{4,3,2,1,0:T(8,128)} %shard_map.123), calls=%async_computation | async-start | bytes 1048576 | tf_op jit(solution)/shard_map/all_to_all | solution.py:261
  49.1 4.5 %shard_map.122 = (bf16[512,1536]{1,0:T(8,128)(2,1)}, bf16[512,1536]{1,0:T(8,128)(2,1)}, bf16[512,1536]{1,0:T(8,128)(2,1)}, f32[512,128]{1,0:T(8,128)}) custom-call(f32[512,512]{1,0:T(8,128)} %deriv_ref.1, f32[512,512]{1,0:T(8,128)} %inverse_ref.1, f32[512,512]{1,0:T(8,128)} %basis_ref.1, f32[1,512]{1,0:T(1,128)} %bitcast.4), custom_call_target="tpu_custom_call" | custom-call | flops 1000000 | bytes 7864320 | tf_op jit(solution)/shard_map/pallas_call | solution.py:326
  53.6 0.0 copy-done.2
  53.6 5.7 %shard_map.126 = (f32[8,1,64,128]{3,2,1,0:T(8,128)}, f32[1,512,128]{2,1,0:T(8,128)}) custom-call(f32[8,128]{1,0:T(8,128)} %get-tuple-element.25.wave_ref, f32[512,128]{1,0:T(8,128)} %get-tuple-element.26.values_ref, bf16[512,1536]{1,0:T(8,128)(2,1)} %get-tuple-element.27.deriv_ref, bf16[512,1536]{1,0:T(8,128)(2,1)} %get-tuple-element.28.inverse_ref, ...), custom_call_target="tpu_custom_call" | custom-call | flops 603979776 | bytes 5767168 | tf_op jit(solution)/shard_map/pallas_call | solution.py:339
  59.3 5.1 %all-to-all-done.in_ref = f32[8,2,1,64,128]{4,3,2,1,0:T(8,128)S(1)} async-done(((f32[8,2,1,64,128]{4,3,2,1,0:T(8,128)}), f32[8,2,1,64,128]{4,3,2,1,0:T(8,128)S(1)}, u32[]{:S(2)}, u32[]{:S(2)}) %all-to-all-start) | async-done | bytes 524320 | tf_op jit(solution)/shard_map/all_to_all | solution.py:261
  64.3 3.4 %all-to-all-start.3 = ((f32[8,1,64,128]{3,2,1,0:T(8,128)}), f32[8,1,64,128]{3,2,1,0:T(8,128)S(1)}, u32[]{:S(2)}, u32[]{:S(2)}) async-start(f32[8,1,64,128]{3,2,1,0:T(8,128)} %get-tuple-element.31), calls=%async_computation.3 | async-start | bytes 524288 | tf_op jit(solution)/shard_map/all_to_all | solution.py:261
  67.8 5.7 %shard_map.128 = (f32[8,1,64,128]{3,2,1,0:T(8,128)}, f32[1,512,128]{2,1,0:T(8,128)}) custom-call(f32[8,128]{1,0:T(8,128)} %get-tuple-element.25.wave_ref, f32[512,128]{1,0:T(8,128)} %get-tuple-element.26.values_ref, bf16[512,1536]{1,0:T(8,128)(2,1)} %get-tuple-element.27.deriv_ref, bf16[512,1536]{1,0:T(8,128)(2,1)} %get-tuple-element.28.inverse_ref, ...), custom_call_target="tpu_custom_call" | custom-call | flops 603979776 | bytes 5767168 | tf_op jit(solution)/shard_map/pallas_call | solution.py:339
  73.4 0.0 copy-done.1
  73.4 4.0 %all-to-all-done.3.in_ref = f32[8,1,64,128]{3,2,1,0:T(8,128)S(1)} async-done(((f32[8,1,64,128]{3,2,1,0:T(8,128)}), f32[8,1,64,128]{3,2,1,0:T(8,128)S(1)}, u32[]{:S(2)}, u32[]{:S(2)}) %all-to-all-start.3) | async-done | bytes 262176 | tf_op jit(solution)/shard_map/all_to_all | solution.py:261
  77.4 3.4 %all-to-all-start.5 = ((f32[8,1,64,128]{3,2,1,0:T(8,128)}), f32[8,1,64,128]{3,2,1,0:T(8,128)S(1)}, u32[]{:S(2)}, u32[]{:S(2)}) async-start(f32[8,1,64,128]{3,2,1,0:T(8,128)} %get-tuple-element.32), calls=%async_computation.5 | async-start | bytes 524288 | tf_op jit(solution)/shard_map/all_to_all | solution.py:261
  80.8 5.6 %shard_map.124 = (f32[8,1,64,128]{3,2,1,0:T(8,128)}, f32[1,512,128]{2,1,0:T(8,128)}) custom-call(f32[8,128]{1,0:T(8,128)} %get-tuple-element.25.wave_ref, f32[512,128]{1,0:T(8,128)} %get-tuple-element.26.values_ref, bf16[512,1536]{1,0:T(8,128)(2,1)} %get-tuple-element.27.deriv_ref, bf16[512,1536]{1,0:T(8,128)(2,1)} %get-tuple-element.28.inverse_ref, ...), custom_call_target="tpu_custom_call" | custom-call | flops 603979776 | bytes 5767168 | tf_op jit(solution)/shard_map/pallas_call | solution.py:339
  86.5 0.0 copy-done.4
  86.5 4.0 %all-to-all-done.5.in_ref = f32[8,1,64,128]{3,2,1,0:T(8,128)S(1)} async-done(((f32[8,1,64,128]{3,2,1,0:T(8,128)}), f32[8,1,64,128]{3,2,1,0:T(8,128)S(1)}, u32[]{:S(2)}, u32[]{:S(2)}) %all-to-all-start.5) | async-done | bytes 262176 | tf_op jit(solution)/shard_map/all_to_all | solution.py:261
  90.5 3.4 %all-to-all-start.1 = ((f32[8,1,64,128]{3,2,1,0:T(8,128)}), f32[8,1,64,128]{3,2,1,0:T(8,128)S(1)}, u32[]{:S(2)}, u32[]{:S(2)}) async-start(f32[8,1,64,128]{3,2,1,0:T(8,128)} %get-tuple-element.30), calls=%async_computation.1 | async-start | bytes 524288 | tf_op jit(solution)/shard_map/all_to_all | solution.py:261
  93.9 0.0 copy-done.7
  93.9 2.8 %shard_map.129 = (f32[6,64,512]{2,1,0:T(8,128)}, f32[3,64]{1,0:T(4,128)}, f32[8,1,64,128]{3,2,1,0:T(8,128)}) custom-call(s32[1]{0:T(128)} %bitcast.me_ref, s32[8,512]{1,0:T(8,128)} %get-tuple-element.24.info_ref, s32[2,512]{1,0:T(2,128)} %modes_ref.13, f32[6,64,512]{2,1,0:T(8,128)} %velocity_ref.5, f32[8,1,64,128]{3,2,1,0:T(8,128)} %copy-done.7), custom_call_target="tpu_custom_call" | custom-call | flops 402653184 | bytes 1572864 | tf_op jit(solution)/shard_map/pallas_call | solution.py:354
  96.7 2.8 %shard_map.130 = (f32[6,64,512]{2,1,0:T(8,128)}, f32[3,64]{1,0:T(4,128)}, f32[8,1,64,128]{3,2,1,0:T(8,128)}) custom-call(s32[1]{0:T(128)} %bitcast.me_ref, s32[8,512]{1,0:T(8,128)} %get-tuple-element.24.info_ref, s32[2,512]{1,0:T(2,128)} %modes_ref.13, f32[6,64,512]{2,1,0:T(8,128)} %velocity_ref.5, ...), custom_call_target="tpu_custom_call", output_to_operand_aliasing={{0}: (5, {})} | custom-call | flops 402653184 | bytes 1572864 | tf_op jit(solution)/shard_map/pallas_call | solution.py:354
  99.6 4.0 %all-to-all-done.1.in_ref = f32[8,1,64,128]{3,2,1,0:T(8,128)S(1)} async-done(((f32[8,1,64,128]{3,2,1,0:T(8,128)}), f32[8,1,64,128]{3,2,1,0:T(8,128)S(1)}, u32[]{:S(2)}, u32[]{:S(2)}) %all-to-all-start.1) | async-done | bytes 262176 | tf_op jit(solution)/shard_map/all_to_all | solution.py:261
  103.6 13.8 %all_to_all.45.in_ref = f32[8,1,64,128]{3,2,1,0:T(8,128)} all-to-all(f32[8,1,64,128]{3,2,1,0:T(8,128)} %get-tuple-element.41), channel_id=1, replica_groups=mesh['grp'=4,'col'=8] {'col'}, dimensions={0} | all-to-all | bytes 524288 | tf_op jit(solution)/shard_map/all_to_all | solution.py:261
  117.4 3.4 %all-to-all-start.8 = ((f32[8,1,64,128]{3,2,1,0:T(8,128)}), f32[8,1,64,128]{3,2,1,0:T(8,128)S(1)}, u32[]{:S(2)}, u32[]{:S(2)}) async-start(f32[8,1,64,128]{3,2,1,0:T(8,128)} %get-tuple-element.43), calls=%async_computation.8 | async-start | bytes 524288 | tf_op jit(solution)/shard_map/all_to_all | solution.py:261
  120.8 0.0 copy-done.5
  120.8 2.9 %shard_map.131 = (f32[6,64,512]{2,1,0:T(8,128)}, f32[3,64]{1,0:T(4,128)}, f32[8,1,64,128]{3,2,1,0:T(8,128)}) custom-call(s32[1]{0:T(128)} %bitcast.me_ref, s32[8,512]{1,0:T(8,128)} %get-tuple-element.24.info_ref, s32[2,512]{1,0:T(2,128)} %modes_ref.13, f32[6,64,512]{2,1,0:T(8,128)} %velocity_ref.5, ...), custom_call_target="tpu_custom_call", output_to_operand_aliasing={{0}: (5, {})} | custom-call | flops 402653184 | bytes 1572864 | tf_op jit(solution)/shard_map/pallas_call | solution.py:354
  123.6 6.8 %all-to-all-done.8.in_ref = f32[8,1,64,128]{3,2,1,0:T(8,128)S(1)} async-done(((f32[8,1,64,128]{3,2,1,0:T(8,128)}), f32[8,1,64,128]{3,2,1,0:T(8,128)S(1)}, u32[]{:S(2)}, u32[]{:S(2)}) %all-to-all-start.8) | async-done | bytes 262176 | tf_op jit(solution)/shard_map/all_to_all | solution.py:261
  130.4 3.4 %all-to-all-start.6 = ((f32[8,1,64,128]{3,2,1,0:T(8,128)}), f32[8,1,64,128]{3,2,1,0:T(8,128)S(1)}, u32[]{:S(2)}, u32[]{:S(2)}) async-start(f32[8,1,64,128]{3,2,1,0:T(8,128)} %get-tuple-element.39), calls=%async_computation.6 | async-start | bytes 524288 | tf_op jit(solution)/shard_map/all_to_all | solution.py:261
  133.9 2.5 %collective-permute-start.2 = (f32[3,64]{1,0:T(4,128)}, f32[3,64]{1,0:T(4,128)S(1)}, u32[]{:S(2)}, u32[]{:S(2)}) collective-permute-start(f32[3,64]{1,0:T(4,128)} %get-tuple-element.44), channel_id=1, source_target_pairs={{0,24},{8,16},{16,8},{24,0},{1,25},{9,17},{17,9},{25,1},{2,26},{10... | collective-permute-start | bytes 2312 | tf_op jit(solution)/shard_map/ppermute | solution.py:267
  136.4 0.5 collective-permute-start.1
  136.9 0.5 collective-permute-start
  137.4 1.2 collective-permute-done.2
  138.6 1.5 %collective-permute-done.1 = f32[3,64]{1,0:T(4,128)S(1)} collective-permute-done((f32[3,64]{1,0:T(4,128)}, f32[3,64]{1,0:T(4,128)S(1)}, u32[]{:S(2)}, u32[]{:S(2)}) %collective-permute-start.1) | collective-permute-done | bytes 800 | tf_op jit(solution)/shard_map/ppermute | solution.py:267
  140.2 0.5 collective-permute-done
  140.7 1.3 add_add_fusion
  141.9 0.0 copy-done.6
  141.9 2.0 %shard_map.132.refs_0_ = f32[6,512,128]{2,1,0:T(8,128)} custom-call(s32[8,512]{1,0:T(8,128)} %get-tuple-element.24.info_ref, f32[1,512,128]{2,1,0:T(8,128)} %get-tuple-element.42.solved_ref, f32[8,1,64,128]{3,2,1,0:T(8,128)} %copy-done.6), custom_call_target="tpu_custom_call" | custom-call | flops 1000000 | bytes 1048576 | tf_op jit(solution)/shard_map/pallas_call | solution.py:371
  144.0 2.0 %shard_map.133.refs_0_ = f32[6,512,128]{2,1,0:T(8,128)} custom-call(s32[8,512]{1,0:T(8,128)} %get-tuple-element.24.info_ref, f32[1,512,128]{2,1,0:T(8,128)} %get-tuple-element.40.solved_ref, f32[8,1,64,128]{3,2,1,0:T(8,128)} %all_to_all.45.in_ref, f32[6,512,128]{2,1,0:T(8,128)} %shard_map.132.refs_0_), custom_call_target="tpu_custom_call", output_to_operand_aliasing={{}: (3, {})} | custom-call | flops 1000000 | bytes 1048576 | tf_op jit(solution)/shard_map/pallas_call | solution.py:371
  146.0 0.0 all-to-all-done.6.in_ref
  146.0 0.7 copy-done.3
  146.7 2.0 %shard_map.134 = f32[6,512,128]{2,1,0:T(8,128)} custom-call(s32[8,512]{1,0:T(8,128)} %get-tuple-element.24.info_ref, f32[1,512,128]{2,1,0:T(8,128)} %get-tuple-element.38.solved_ref, f32[8,1,64,128]{3,2,1,0:T(8,128)} %copy-done.3, f32[6,512,128]{2,1,0:T(8,128)} %shard_map.133.refs_0_), custom_call_target="tpu_custom_call", output_to_operand_aliasing={{}: (3, {})} | custom-call | flops 1000000 | bytes 1048576 | tf_op jit(solution)/shard_map/pallas_call | solution.py:371
  (6 shorter events, 0.0 us)
Async XLA Ops:
  5.1 21.7 %all-to-all-start.4 = ((f32[8,2,1,64,128]{4,3,2,1,0:T(8,128)}), f32[8,2,1,64,128]{4,3,2,1,0:T(8,128)S(1)}, u32[]{:S(2)}, u32[]{:S(2)}) async-start(f32[8,2,1,64,128]{4,3,2,1,0:T(8,128)} %shard_map.127), calls=%async_computation.4 | async-start | bytes 1048576 | tf_op jit(solution)/shard_map/all_to_all | solution.py:261
  26.8 6.2 %copy-start = (f32[8,2,1,64,128]{4,3,2,1,0:T(8,128)}, f32[8,2,1,64,128]{4,3,2,1,0:T(8,128)S(1)}, u32[]{:S(2)}) copy-start(f32[8,2,1,64,128]{4,3,2,1,0:T(8,128)S(1)} %all-to-all-done.4.in_ref) | copy-start | bytes 1572868
  26.8 18.8 %all-to-all-start.2 = ((f32[8,2,1,64,128]{4,3,2,1,0:T(8,128)}), f32[8,2,1,64,128]{4,3,2,1,0:T(8,128)S(1)}, u32[]{:S(2)}, u32[]{:S(2)}) async-start(f32[8,2,1,64,128]{4,3,2,1,0:T(8,128)} %shard_map.125), calls=%async_computation.2 | async-start | bytes 1048576 | tf_op jit(solution)/shard_map/all_to_all | solution.py:261
  45.6 8.0 %copy-start.2 = (f32[8,2,1,64,128]{4,3,2,1,0:T(8,128)}, f32[8,2,1,64,128]{4,3,2,1,0:T(8,128)S(1)}, u32[]{:S(2)}) copy-start(f32[8,2,1,64,128]{4,3,2,1,0:T(8,128)S(1)} %all-to-all-done.2.in_ref) | copy-start | bytes 1572868
  45.6 18.8 %all-to-all-start = ((f32[8,2,1,64,128]{4,3,2,1,0:T(8,128)}), f32[8,2,1,64,128]{4,3,2,1,0:T(8,128)S(1)}, u32[]{:S(2)}, u32[]{:S(2)}) async-start(f32[8,2,1,64,128]{4,3,2,1,0:T(8,128)} %shard_map.123), calls=%async_computation | async-start | bytes 1048576 | tf_op jit(solution)/shard_map/all_to_all | solution.py:261
  64.3 9.1 %copy-start.1 = (f32[8,2,1,64,128]{4,3,2,1,0:T(8,128)}, f32[8,2,1,64,128]{4,3,2,1,0:T(8,128)S(1)}, u32[]{:S(2)}) copy-start(f32[8,2,1,64,128]{4,3,2,1,0:T(8,128)S(1)} %all-to-all-done.in_ref) | copy-start | bytes 1572868
  64.3 13.1 %all-to-all-start.3 = ((f32[8,1,64,128]{3,2,1,0:T(8,128)}), f32[8,1,64,128]{3,2,1,0:T(8,128)S(1)}, u32[]{:S(2)}, u32[]{:S(2)}) async-start(f32[8,1,64,128]{3,2,1,0:T(8,128)} %get-tuple-element.31), calls=%async_computation.3 | async-start | bytes 524288 | tf_op jit(solution)/shard_map/all_to_all | solution.py:261
  77.4 9.1 %copy-start.4 = (f32[8,1,64,128]{3,2,1,0:T(8,128)}, f32[8,1,64,128]{3,2,1,0:T(8,128)S(1)}, u32[]{:S(2)}) copy-start(f32[8,1,64,128]{3,2,1,0:T(8,128)S(1)} %all-to-all-done.3.in_ref) | copy-start | bytes 786436
  77.4 13.1 %all-to-all-start.5 = ((f32[8,1,64,128]{3,2,1,0:T(8,128)}), f32[8,1,64,128]{3,2,1,0:T(8,128)S(1)}, u32[]{:S(2)}, u32[]{:S(2)}) async-start(f32[8,1,64,128]{3,2,1,0:T(8,128)} %get-tuple-element.32), calls=%async_computation.5 | async-start | bytes 524288 | tf_op jit(solution)/shard_map/all_to_all | solution.py:261
  90.5 3.4 %copy-start.7 = (f32[8,1,64,128]{3,2,1,0:T(8,128)}, f32[8,1,64,128]{3,2,1,0:T(8,128)S(1)}, u32[]{:S(2)}) copy-start(f32[8,1,64,128]{3,2,1,0:T(8,128)S(1)} %all-to-all-done.5.in_ref) | copy-start | bytes 786436
  90.5 13.1 %all-to-all-start.1 = ((f32[8,1,64,128]{3,2,1,0:T(8,128)}), f32[8,1,64,128]{3,2,1,0:T(8,128)S(1)}, u32[]{:S(2)}, u32[]{:S(2)}) async-start(f32[8,1,64,128]{3,2,1,0:T(8,128)} %get-tuple-element.30), calls=%async_computation.1 | async-start | bytes 524288 | tf_op jit(solution)/shard_map/all_to_all | solution.py:261
  103.6 17.2 %copy-start.5 = (f32[8,1,64,128]{3,2,1,0:T(8,128)}, f32[8,1,64,128]{3,2,1,0:T(8,128)S(1)}, u32[]{:S(2)}) copy-start(f32[8,1,64,128]{3,2,1,0:T(8,128)S(1)} %all-to-all-done.1.in_ref) | copy-start | bytes 786436
  117.4 13.1 %all-to-all-start.8 = ((f32[8,1,64,128]{3,2,1,0:T(8,128)}), f32[8,1,64,128]{3,2,1,0:T(8,128)S(1)}, u32[]{:S(2)}, u32[]{:S(2)}) async-start(f32[8,1,64,128]{3,2,1,0:T(8,128)} %get-tuple-element.43), calls=%async_computation.8 | async-start | bytes 524288 | tf_op jit(solution)/shard_map/all_to_all | solution.py:261
  130.4 11.5 %copy-start.6 = (f32[8,1,64,128]{3,2,1,0:T(8,128)}, f32[8,1,64,128]{3,2,1,0:T(8,128)S(1)}, u32[]{:S(2)}) copy-start(f32[8,1,64,128]{3,2,1,0:T(8,128)S(1)} %all-to-all-done.8.in_ref) | copy-start | bytes 786436
  130.4 15.6 %all-to-all-start.6 = ((f32[8,1,64,128]{3,2,1,0:T(8,128)}), f32[8,1,64,128]{3,2,1,0:T(8,128)S(1)}, u32[]{:S(2)}, u32[]{:S(2)}) async-start(f32[8,1,64,128]{3,2,1,0:T(8,128)} %get-tuple-element.39), calls=%async_computation.6 | async-start | bytes 524288 | tf_op jit(solution)/shard_map/all_to_all | solution.py:261
  133.9 4.8 %collective-permute-start.2 = (f32[3,64]{1,0:T(4,128)}, f32[3,64]{1,0:T(4,128)S(1)}, u32[]{:S(2)}, u32[]{:S(2)}) collective-permute-start(f32[3,64]{1,0:T(4,128)} %get-tuple-element.44), channel_id=1, source_target_pairs={{0,24},{8,16},{16,8},{24,0},{1,25},{9,17},{17,9},{25,1},{2,26},{10... | collective-permute-start | bytes 2312 | tf_op jit(solution)/shard_map/ppermute | solution.py:267
  136.4 3.8 %collective-permute-start.1 = (f32[3,64]{1,0:T(4,128)}, f32[3,64]{1,0:T(4,128)S(1)}, u32[]{:S(2)}, u32[]{:S(2)}) collective-permute-start(f32[3,64]{1,0:T(4,128)} %get-tuple-element.44), channel_id=1, source_target_pairs={{0,16},{8,24},{16,0},{24,8},{1,17},{9,25},{17,1},{25,9},{2,18},{10... | collective-permute-start | bytes 2312 | tf_op jit(solution)/shard_map/ppermute | solution.py:267
  136.9 3.8 %collective-permute-start = (f32[3,64]{1,0:T(4,128)}, f32[3,64]{1,0:T(4,128)S(1)}, u32[]{:S(2)}, u32[]{:S(2)}) collective-permute-start(f32[3,64]{1,0:T(4,128)} %get-tuple-element.44), channel_id=1, source_target_pairs={{0,8},{8,0},{16,24},{24,16},{1,9},{9,1},{17,25},{25,17},{2,10},{10... | collective-permute-start | bytes 2312 | tf_op jit(solution)/shard_map/ppermute | solution.py:267
  146.0 0.7 copy-start.3

commit v6 on v3

--- a/solution.py
+++ b/solution.py
@@ -14,7 +14,7 @@
 RK_GAMMA = 5.0 / 12.0
 RK_ZETA = -17.0 / 60.0
 WAVE_SCALE = 8.0
-VMEM_LIMIT = 56 * 1024 * 1024
+VMEM_LIMIT = 24 * 1024 * 1024
 GROUPS = 3
 LANES = 128
 
@@ -195,11 +195,11 @@
             block[pair] = after[rows, pair * lanes : (pair + 1) * lanes]
 
 
-def unpack_kernel(devices, chunk, first, info_ref, modes_ref, velocity_ref, *refs):
+def unpack_kernel(devices, first, info_ref, *refs):
     in_refs, refs = refs[:devices], refs[devices:]
     if not first:
-        (_, emf_in), refs = refs[:2], refs[2:]
-    (state_ref, emf_ref), out_refs = refs[:2], refs[2:]
+        refs = refs[1:]
+    state_ref, out_refs = refs[0], refs[1:]
     pairs, points, lanes = in_refs[0].shape
     share = lanes // 2
     columns = devices * share
@@ -229,12 +229,15 @@
             real = 2 * pair * points
             imag = real + points
             out[pair] = jnp.concatenate([taken[real : real + points], taken[imag : imag + points]], axis=1)
+
+
+def emf_kernel(modes_ref, velocity_ref, state_ref, later_ref, emf_ref):
+    _, points, columns = state_ref.shape
     weight = jnp.where(modes_ref[0:1, :] > 0, 2.0, 1.0).astype(F32)
     totals = [jnp.zeros((points, columns), F32)] * 3
-    for pair in range(pairs):
-        field = chunk * pairs + pair
-        real = weight * state[2 * pair * points : (2 * pair + 1) * points]
-        imag = weight * state[(2 * pair + 1) * points : (2 * pair + 2) * points]
+    for field in range(3):
+        real = weight * state_ref[2 * field]
+        imag = weight * state_ref[2 * field + 1]
         for sign, i, j in ((1.0, (field + 1) % 3, (field + 2) % 3), (-1.0, (field + 2) % 3, (field + 1) % 3)):
             totals[i] = totals[i] + sign * (velocity_ref[2 * j] * real + velocity_ref[2 * j + 1] * imag)
     rows = []
@@ -243,8 +246,7 @@
         for at in range(1, columns // LANES):
             folded = folded + total[:, at * LANES : (at + 1) * LANES]
         rows.append(jnp.sum(jnp.transpose(folded), axis=0, keepdims=True))
-    rows = jnp.concatenate(rows, axis=0)
-    emf_ref[...] = rows if first else rows + emf_in[...]
+    emf_ref[...] = jnp.concatenate(rows, axis=0)
 
 
 def assemble_kernel(devices, first, me_ref, info_ref, solved_ref, *refs):
@@ -367,22 +369,28 @@
         solved.append(outs[devices])
         returned.append(exchange(outs[:devices]))
 
-    state_next, emf, extra = None, None, []
+    state_next, extra = None, []
     for chunk in range(chunks):
         first = chunk == 0
         outs = call(
-            functools.partial(unpack_kernel, devices, chunk, first),
-            [shaped(state_now.shape), shaped((3, points))] + [shaped(back)] * devices,
-            [whole((8, columns)), whole((2, columns)), whole(velocity.shape)]
-            + [whole(back)] * devices
-            + ([] if first else [untouched(), whole((3, points))]),
-            [part(field, chunk), whole((3, points))] + [whole(back)] * devices,
+            functools.partial(unpack_kernel, devices, first),
+            [shaped(state_now.shape)] + [shaped(back)] * devices,
+            [whole((8, columns))] + [whole(back)] * devices + ([] if first else [untouched()]),
+            [part(field, chunk)] + [whole(back)] * devices,
             12 * 2 * pairs * points * columns * columns,
             6 * moved,
-            aliases={} if first else {3 + devices: 0},
-        )(info, kept_modes, velocity, *returned[chunk], *([] if first else [state_next, emf]))
-        state_next, emf = outs[:2]
-        extra.append(exchange(outs[2:]))
+            aliases={} if first else {1 + devices: 0},
+        )(info, *returned[chunk], *([] if first else [state_next]))
+        state_next = outs[0]
+        extra.append(exchange(outs[1:]))
+    emf = call(
+        emf_kernel,
+        shaped((3, points)),
+        [whole((2, columns)), whole(velocity.shape), whole(velocity.shape), untouched()],
+        whole((3, points)),
+        30 * comps * points * columns,
+        8 * comps * points * columns,
+    )(kept_modes, velocity, state_next, extra[-1][1 + devices // 2])
     mean_emf = sum_over_groups(emf)
 
     owned = None

time: 104 us -> 95.4 us (0.917)
  Pallas kernels: 24.7 us -> 10.4 us
  local copies, waits for them, and re-layouts: 2.25 us -> 5.95 us
  starting transfers between devices: 51.3 us -> 53 us
    pallas_call x1, Pallas kernels: 6.85 us -> 2.88 us  [on_device(): call(functools.partial(solve_kernel, devices), [shaped(back)] * devices +...]
    ppermute x21, waiting for transfers between devices: 20.1 us -> 23.9 us  [exchange(): lax.ppermute(block, 'col', [(i, i ^ step) for i in range(devices)])]
    unnamed x42 -> x24, local copies, waits for them, and re-layouts: 2.25 us -> 5.95 us
    pallas_call x1, Pallas kernels: 4.49 us -> 0.99 us  [on_device(): call(operators_kernel, [operator, operator, operator, shaped((depth, lane...]
    ppermute x3, waiting for transfers between devices: 3.24 us -> 0.4 us  [sum_over_groups(): lax.ppermute(value, 'grp', [(i, i ^ step) for i in range(groups)])]
    pallas_call x1, Pallas kernels: 4.45 us -> 1.7 us  [on_device(): call(functools.partial(pack_kernel, devices), [shaped(sent)] * devices, [...]
    ppermute x3, starting transfers between devices: 3.49 us -> 5.42 us  [sum_over_groups(): lax.ppermute(value, 'grp', [(i, i ^ step) for i in range(groups)])]
    pallas_call x1 -> x2, Pallas kernels: 4.16 us -> 2.73 us  [the longest x1 2.46 us: on_device(): call(functools.partial(unpack_kernel, devices, first), [shaped(state_now....]
  transfers between devices with their start and end apart: 24 -> 24, of which waited for: 12 -> 11; matrix products, arithmetic and copies ran while one was open for 1% -> 0% of each run, Pallas kernels for 4% -> 3%
where the time goes in v6:
time: 95.4 us; the launch traced here: 95 us
  starting transfers between devices  53 us (56%)
  waiting for transfers between devices  24.3 us (25%)
  Pallas kernels  10.4 us (11%)
  local copies, waits for them, and re-layouts  5.95 us (6%)
    ppermute x21, starting transfers between devices, exchange(): lax.ppermute(block, 'col', [(i, i ^ step) for i in range(devices)])  47.6 us
    ppermute x21, waiting for transfers between devices, exchange(): lax.ppermute(block, 'col', [(i, i ^ step) for i in range(devices)])  23.9 us
    unnamed x24, local copies, waits for them, and re-layouts  5.95 us
    ppermute x3, starting transfers between devices, sum_over_groups(): lax.ppermute(value, 'grp', [(i, i ^ step) for i in range(groups)])  5.42 us
    pallas_call x1, Pallas kernels, on_device(): call(functools.partial(solve_kernel, devices), [shaped(back)] * devices +...  2.88 us
    pallas_call x1, Pallas kernels, on_device(): call(functools.partial(unpack_kernel, devices, first), [shaped(state_now....  2.46 us
  transfers between devices with their start and end apart: 24, of which 11 were waited for; matrix products, arithmetic and copies ran while one was open for 0% of the time, Pallas kernels for 3%

profile of v6, /device:TPU:0, one launch (start us, length us, event | category | flops | bytes accessed | tf_op | source)
XLA Modules:
  0.0 95.0 jit_solution(5147122340549886660)
XLA Ops:
  0.6 0.0 copy-start.5
  0.6 0.7 copy-done.5
  1.3 0.7 copy-done.7
  2.0 0.4 shard_map.121
  2.4 1.2 %copy-done.9 = f32[6,64,512]{2,1,0:T(8,128)S(1)} copy-done((f32[6,64,512]{2,1,0:T(8,128)S(1)}, f32[6,64,512]{2,1,0:T(8,128)}, u32[]{:S(2)}) %copy-start.9) | copy-done | bytes 786456
  3.6 1.1 %copy-done.10 = f32[6,64,512]{2,1,0:T(8,128)S(1)} copy-done((f32[6,64,512]{2,1,0:T(8,128)S(1)}, f32[6,64,512]{2,1,0:T(8,128)}, u32[]{:S(2)}) %copy-start.10) | copy-done | bytes 786456
  4.7 1.1 %copy-done.11 = f32[6,64,512]{2,1,0:T(8,128)S(1)} copy-done((f32[6,64,512]{2,1,0:T(8,128)S(1)}, f32[6,64,512]{2,1,0:T(8,128)}, u32[]{:S(2)}) %copy-start.11) | copy-done | bytes 786456
  5.9 1.7 %shard_map.123 = (f32[2,3,64,128]{3,2,1,0:T(8,128)S(1)}, f32[2,3,64,128]{3,2,1,0:T(8,128)S(1)}, f32[2,3,64,128]{3,2,1,0:T(8,128)S(1)}, f32[2,3,64,128]{3,2,1,0:T...) custom-call(s32[8,512]{1,0:T(8,128)S(1)} %get-tuple-element.35.info_, ...), custom_call_target="tpu_custom_call" | custom-call | flops 1207959552 | bytes 3932160 | tf_op jit(solution)/shard_map/pallas_call | solution.py:333
  7.6 5.1 %collective-permute-start = (f32[2,3,64,128]{3,2,1,0:T(8,128)S(1)}, f32[2,3,64,128]{3,2,1,0:T(8,128)S(1)}, u32[]{:S(2)}, u32[]{:S(2)}) collective-permute-start(f32[2,3,64,128]{3,2,1,0:T(8,128)S(1)} %get-tuple-element.42), channel_id=1, source_target_pairs={{0,6},{1,7},{2,4},{3,5},{4,2},{5,3},{6,0},{7,1},{8,14},{9,15},{10,... | collective-permute-start | bytes 589832 | tf_op jit(solution)/shard_map/ppermute | solution.py:278
  12.7 0.2 collective-permute-start.2
  12.9 2.3 %collective-permute-start.3 = (f32[2,3,64,128]{3,2,1,0:T(8,128)S(1)}, f32[2,3,64,128]{3,2,1,0:T(8,128)S(1)}, u32[]{:S(2)}, u32[]{:S(2)}) collective-permute-start(f32[2,3,64,128]{3,2,1,0:T(8,128)S(1)} %get-tuple-element.45), channel_id=1, source_target_pairs={{0,5},{1,4},{2,7},{3,6},{4,1},{5,0},{6,3},{7,2},{8,13},{9,12},{10,... | collective-permute-start | bytes 589832 | tf_op jit(solution)/shard_map/ppermute | solution.py:278
  15.1 1.7 %collective-permute-start.4 = (f32[2,3,64,128]{3,2,1,0:T(8,128)S(1)}, f32[2,3,64,128]{3,2,1,0:T(8,128)S(1)}, u32[]{:S(2)}, u32[]{:S(2)}) collective-permute-start(f32[2,3,64,128]{3,2,1,0:T(8,128)S(1)} %get-tuple-element.46), channel_id=1, source_target_pairs={{0,2},{1,3},{2,0},{3,1},{4,6},{5,7},{6,4},{7,5},{8,10},{9,11},{10,... | collective-permute-start | bytes 589832 | tf_op jit(solution)/shard_map/ppermute | solution.py:278
  16.8 1.2 %collective-permute-done.refs_1_ = f32[2,3,64,128]{3,2,1,0:T(8,128)S(1)} collective-permute-done((f32[2,3,64,128]{3,2,1,0:T(8,128)S(1)}, f32[2,3,64,128]{3,2,1,0:T(8,128)S(1)}, u32[]{:S(2)}, u32[]{:S(2)}) %collective-permute-start) | collective-permute-done | bytes 196640 | tf_op jit(solution)/shard_map/ppermute | solution.py:278
  18.0 14.9 %collective-permute-start.5 = (f32[2,3,64,128]{3,2,1,0:T(8,128)S(1)}, f32[2,3,64,128]{3,2,1,0:T(8,128)S(1)}, u32[]{:S(2)}, u32[]{:S(2)}) collective-permute-start(f32[2,3,64,128]{3,2,1,0:T(8,128)S(1)} %get-tuple-element.47), channel_id=1, source_target_pairs={{0,3},{1,2},{2,1},{3,0},{4,7},{5,6},{6,5},{7,4},{8,11},{9,10},{10,... | collective-permute-start | bytes 589832 | tf_op jit(solution)/shard_map/ppermute | solution.py:278
  32.9 2.3 %collective-permute-start.6 = (f32[2,3,64,128]{3,2,1,0:T(8,128)S(1)}, f32[2,3,64,128]{3,2,1,0:T(8,128)S(1)}, u32[]{:S(2)}, u32[]{:S(2)}) collective-permute-start(f32[2,3,64,128]{3,2,1,0:T(8,128)S(1)} %get-tuple-element.48), channel_id=1, source_target_pairs={{0,1},{1,0},{2,3},{3,2},{4,5},{5,4},{6,7},{7,6},{8,9},{9,8},{10,11... | collective-permute-start | bytes 589832 | tf_op jit(solution)/shard_map/ppermute | solution.py:278
  35.3 1.0 %shard_map.122 = (bf16[512,1536]{1,0:T(8,128)(2,1)S(1)}, bf16[512,1536]{1,0:T(8,128)(2,1)S(1)}, bf16[512,1536]{1,0:T(8,128)(2,1)S(1)}, f32[512,128]{1,0:T(8,128)S(1)}) custom-call(f32[512,512]{1,0:T(8,128)S(1)} %copy-done, f32[512,512]{1,0:T(8,128)S(1)} %copy-done.1, f32[512,512]{1,0:T(8,128)S(1)} %copy-done.2, f32[1,512]{1,0:T(1,128)S(1)} %bitcast.4), custom_call_target="tpu_custom_call" | custom-call | flops 1000000 | bytes 7864320 | tf_op jit(solution)/shard_map/pallas_call | solution.py:345
  36.2 6.8 %collective-permute-done.2.refs_3_ = f32[2,3,64,128]{3,2,1,0:T(8,128)S(1)} collective-permute-done((f32[2,3,64,128]{3,2,1,0:T(8,128)S(1)}, f32[2,3,64,128]{3,2,1,0:T(8,128)S(1)}, u32[]{:S(2)}, u32[]{:S(2)}) %collective-permute-start.2) | collective-permute-done | bytes 196640 | tf_op jit(solution)/shard_map/ppermute | solution.py:278
  43.1 2.3 %collective-permute-done.3.refs_4_ = f32[2,3,64,128]{3,2,1,0:T(8,128)S(1)} collective-permute-done((f32[2,3,64,128]{3,2,1,0:T(8,128)S(1)}, f32[2,3,64,128]{3,2,1,0:T(8,128)S(1)}, u32[]{:S(2)}, u32[]{:S(2)}) %collective-permute-start.3) | collective-permute-done | bytes 196640 | tf_op jit(solution)/shard_map/ppermute | solution.py:278
  45.4 2.9 %shard_map.124 = (f32[3,64,128]{2,1,0:T(8,128)S(1)}, f32[3,64,128]{2,1,0:T(8,128)S(1)}, f32[3,64,128]{2,1,0:T(8,128)S(1)}, f32[3,64,128]{2,1,0:T(8,128)S(1)}, f3...) custom-call(s32[1]{0:T(128)} %bitcast.me_ref, ...), custom_call_target="tpu_custom_call" | custom-call | flops 1811939328 | bytes 7864320 | tf_op jit(solution)/shard_map/pallas_call | solution.py:358
  48.3 2.4 %collective-permute-start.7 = (f32[3,64,128]{2,1,0:T(8,128)S(1)}, f32[3,64,128]{2,1,0:T(8,128)S(1)}, u32[]{:S(2)}, u32[]{:S(2)}) collective-permute-start(f32[3,64,128]{2,1,0:T(8,128)S(1)} %get-tuple-element.50), channel_id=1, source_target_pairs={{0,6},{1,7},{2,4},{3,5},{4,2},{5,3},{6,0},{7,1},{8,14},{9,15},{10,... | collective-permute-start | bytes 294920 | tf_op jit(solution)/shard_map/ppermute | solution.py:278
  50.6 2.5 %collective-permute-start.8 = (f32[3,64,128]{2,1,0:T(8,128)S(1)}, f32[3,64,128]{2,1,0:T(8,128)S(1)}, u32[]{:S(2)}, u32[]{:S(2)}) collective-permute-start(f32[3,64,128]{2,1,0:T(8,128)S(1)} %get-tuple-element.51), channel_id=1, source_target_pairs={{0,7},{1,6},{2,5},{3,4},{4,3},{5,2},{6,1},{7,0},{8,15},{9,14},{10,... | collective-permute-start | bytes 294920 | tf_op jit(solution)/shard_map/ppermute | solution.py:278
  53.1 1.4 %collective-permute-start.10 = (f32[3,64,128]{2,1,0:T(8,128)S(1)}, f32[3,64,128]{2,1,0:T(8,128)S(1)}, u32[]{:S(2)}, u32[]{:S(2)}) collective-permute-start(f32[3,64,128]{2,1,0:T(8,128)S(1)} %get-tuple-element.53), channel_id=1, source_target_pairs={{0,5},{1,4},{2,7},{3,6},{4,1},{5,0},{6,3},{7,2},{8,13},{9,12},{10,... | collective-permute-start | bytes 294920 | tf_op jit(solution)/shard_map/ppermute | solution.py:278
  54.5 1.7 %collective-permute-start.11 = (f32[3,64,128]{2,1,0:T(8,128)S(1)}, f32[3,64,128]{2,1,0:T(8,128)S(1)}, u32[]{:S(2)}, u32[]{:S(2)}) collective-permute-start(f32[3,64,128]{2,1,0:T(8,128)S(1)} %get-tuple-element.54), channel_id=1, source_target_pairs={{0,2},{1,3},{2,0},{3,1},{4,6},{5,7},{6,4},{7,5},{8,10},{9,11},{10,... | collective-permute-start | bytes 294920 | tf_op jit(solution)/shard_map/ppermute | solution.py:278
  56.2 1.3 %collective-permute-start.12 = (f32[3,64,128]{2,1,0:T(8,128)S(1)}, f32[3,64,128]{2,1,0:T(8,128)S(1)}, u32[]{:S(2)}, u32[]{:S(2)}) collective-permute-start(f32[3,64,128]{2,1,0:T(8,128)S(1)} %get-tuple-element.55), channel_id=1, source_target_pairs={{0,3},{1,2},{2,1},{3,0},{4,7},{5,6},{6,5},{7,4},{8,11},{9,10},{10,... | collective-permute-start | bytes 294920 | tf_op jit(solution)/shard_map/ppermute | solution.py:278
  57.5 5.6 %collective-permute-start.13 = (f32[3,64,128]{2,1,0:T(8,128)S(1)}, f32[3,64,128]{2,1,0:T(8,128)S(1)}, u32[]{:S(2)}, u32[]{:S(2)}) collective-permute-start(f32[3,64,128]{2,1,0:T(8,128)S(1)} %get-tuple-element.56), channel_id=1, source_target_pairs={{0,1},{1,0},{2,3},{3,2},{4,5},{5,4},{6,7},{7,6},{8,9},{9,8},{10,11... | collective-permute-start | bytes 294920 | tf_op jit(solution)/shard_map/ppermute | solution.py:278
  63.1 3.4 %collective-permute-done.9.refs_3_ = f32[3,64,128]{2,1,0:T(8,128)S(1)} collective-permute-done((f32[3,64,128]{2,1,0:T(8,128)S(1)}, f32[3,64,128]{2,1,0:T(8,128)S(1)}, u32[]{:S(2)}, u32[]{:S(2)}) %collective-permute-start.9) | collective-permute-done | bytes 98336 | tf_op jit(solution)/shard_map/ppermute | solution.py:278
  66.4 2.1 %collective-permute-done.10.refs_4_ = f32[3,64,128]{2,1,0:T(8,128)S(1)} collective-permute-done((f32[3,64,128]{2,1,0:T(8,128)S(1)}, f32[3,64,128]{2,1,0:T(8,128)S(1)}, u32[]{:S(2)}, u32[]{:S(2)}) %collective-permute-start.10) | collective-permute-done | bytes 98336 | tf_op jit(solution)/shard_map/ppermute | solution.py:278
  68.6 0.0 copy-start.6
  68.6 2.5 %shard_map.125 = (f32[6,64,512]{2,1,0:T(8,128)}, f32[3,64,128]{2,1,0:T(8,128)S(1)}, f32[3,64,128]{2,1,0:T(8,128)S(1)}, f32[3,64,128]{2,1,0:T(8,128)S(1)}, f32[3,...) custom-call(s32[8,512]{1,0:T(8,128)S(1)} %get-tuple-element.35.info_, ...), custom_call_target="tpu_custom_call" | custom-call | flops 1207959552 | bytes 4718592 | tf_op jit(solution)/shard_map/pallas_call | solution.py:375
  71.1 1.3 %collective-permute-start.14 = (f32[3,64,128]{2,1,0:T(8,128)S(1)}, f32[3,64,128]{2,1,0:T(8,128)S(1)}, u32[]{:S(2)}, u32[]{:S(2)}) collective-permute-start(f32[3,64,128]{2,1,0:T(8,128)S(1)} %get-tuple-element.60), channel_id=1, source_target_pairs={{0,6},{1,7},{2,4},{3,5},{4,2},{5,3},{6,0},{7,1},{8,14},{9,15},{10,... | collective-permute-start | bytes 294920 | tf_op jit(solution)/shard_map/ppermute | solution.py:278
  72.4 0.6 collective-permute-start.18
  73.0 2.0 %collective-permute-start.15 = (f32[3,64,128]{2,1,0:T(8,128)S(1)}, f32[3,64,128]{2,1,0:T(8,128)S(1)}, u32[]{:S(2)}, u32[]{:S(2)}) collective-permute-start(f32[3,64,128]{2,1,0:T(8,128)S(1)} %get-tuple-element.61), channel_id=1, source_target_pairs={{0,7},{1,6},{2,5},{3,4},{4,3},{5,2},{6,1},{7,0},{8,15},{9,14},{10,... | collective-permute-start | bytes 294920 | tf_op jit(solution)/shard_map/ppermute | solution.py:278
  75.0 1.7 %collective-permute-start.16 = (f32[3,64,128]{2,1,0:T(8,128)S(1)}, f32[3,64,128]{2,1,0:T(8,128)S(1)}, u32[]{:S(2)}, u32[]{:S(2)}) collective-permute-start(f32[3,64,128]{2,1,0:T(8,128)S(1)} %get-tuple-element.62), channel_id=1, source_target_pairs={{0,4},{1,5},{2,6},{3,7},{4,0},{5,1},{6,2},{7,3},{8,12},{9,13},{10,... | collective-permute-start | bytes 294920 | tf_op jit(solution)/shard_map/ppermute | solution.py:278
  76.7 0.6 collective-permute-start.17
  77.3 1.3 %collective-permute-done.14.refs_1_ = f32[3,64,128]{2,1,0:T(8,128)S(1)} collective-permute-done((f32[3,64,128]{2,1,0:T(8,128)S(1)}, f32[3,64,128]{2,1,0:T(8,128)S(1)}, u32[]{:S(2)}, u32[]{:S(2)}) %collective-permute-start.14) | collective-permute-done | bytes 98336 | tf_op jit(solution)/shard_map/ppermute | solution.py:278
  78.6 1.3 %collective-permute-done.18.refs_5_.later_ref = f32[3,64,128]{2,1,0:T(8,128)S(1)} collective-permute-done((f32[3,64,128]{2,1,0:T(8,128)S(1)}, f32[3,64,128]{2,1,0:T(8,128)S(1)}, u32[]{:S(2)}, u32[]{:S(2)}) %collective-permute-start.18) | collective-permute-done | bytes 98336 | tf_op jit(solution)/shard_map/ppermute | solution.py:278
  79.9 0.1 collective-permute-start.20
  80.0 1.1 %copy-done.4 = f32[6,64,512]{2,1,0:T(8,128)S(1)} copy-done((f32[6,64,512]{2,1,0:T(8,128)S(1)}, f32[6,64,512]{2,1,0:T(8,128)}, u32[]{:S(2)}) %copy-start.4) | copy-done | bytes 786456
  81.1 0.3 shard_map.127
  81.4 1.1 %collective-permute-done.15.refs_2_ = f32[3,64,128]{2,1,0:T(8,128)S(1)} collective-permute-done((f32[3,64,128]{2,1,0:T(8,128)S(1)}, f32[3,64,128]{2,1,0:T(8,128)S(1)}, u32[]{:S(2)}, u32[]{:S(2)}) %collective-permute-start.15) | collective-permute-done | bytes 98336 | tf_op jit(solution)/shard_map/ppermute | solution.py:278
  82.5 2.4 %collective-permute-start.23 = (f32[3,64]{1,0:T(4,128)S(1)}, f32[3,64]{1,0:T(4,128)S(1)}, u32[]{:S(2)}, u32[]{:S(2)}) collective-permute-start(f32[3,64]{1,0:T(4,128)S(1)} %shard_map.127), channel_id=1, source_target_pairs={{0,24},{8,16},{16,8},{24,0},{1,25},{9,17},{17,9},{25,1},{2,26},{10... | collective-permute-start | bytes 2312 | tf_op jit(solution)/shard_map/ppermute | solution.py:286
  84.9 4.0 %collective-permute-done.16.refs_3_ = f32[3,64,128]{2,1,0:T(8,128)S(1)} collective-permute-done((f32[3,64,128]{2,1,0:T(8,128)S(1)}, f32[3,64,128]{2,1,0:T(8,128)S(1)}, u32[]{:S(2)}, u32[]{:S(2)}) %collective-permute-start.16) | collective-permute-done | bytes 98336 | tf_op jit(solution)/shard_map/ppermute | solution.py:278
  89.0 1.5 %collective-permute-start.22 = (f32[3,64]{1,0:T(4,128)S(1)}, f32[3,64]{1,0:T(4,128)S(1)}, u32[]{:S(2)}, u32[]{:S(2)}) collective-permute-start(f32[3,64]{1,0:T(4,128)S(1)} %shard_map.127), channel_id=1, source_target_pairs={{0,16},{8,24},{16,0},{24,8},{1,17},{9,25},{17,1},{25,9},{2,18},{10... | collective-permute-start | bytes 2312 | tf_op jit(solution)/shard_map/ppermute | solution.py:286
  90.5 0.4 collective-permute-done.17.refs_4_
  90.9 1.5 %collective-permute-start.21 = (f32[3,64]{1,0:T(4,128)S(1)}, f32[3,64]{1,0:T(4,128)S(1)}, u32[]{:S(2)}, u32[]{:S(2)}) collective-permute-start(f32[3,64]{1,0:T(4,128)S(1)} %shard_map.127), channel_id=1, source_target_pairs={{0,8},{8,0},{16,24},{24,16},{1,9},{9,1},{17,25},{25,17},{2,10},{10... | collective-permute-start | bytes 2312 | tf_op jit(solution)/shard_map/ppermute | solution.py:286
  92.3 1.7 %shard_map.126 = f32[6,512,128]{2,1,0:T(8,128)} custom-call(s32[1]{0:T(128)} %bitcast.me_ref, s32[8,512]{1,0:T(8,128)S(1)} %get-tuple-element.35.info_ref, f32[3,512,128]{2,1,0:T(8,128)S(1)} %get-tuple-element.58.solved_ref, f32[3,64,128]{2,1,0:T(8,128)S(1)} %get-tuple-element.59.refs_0_, f32[3,64,128]{2,1,0:T(8,128)S(1)} %collective-permute-done.14.refs_1_, ...), custom_call_target="tpu_custom_call" | custom-call | flops 1000000 | bytes 3145728 | tf_op jit(solution)/shard_map/pallas_call | solution.py:399
  94.0 0.4 collective-permute-done.21
  94.4 0.6 add_add_fusion
  (32 shorter events, 0.1 us)
Async XLA Ops:
  0.6 0.7 copy-start.5
  1.3 0.7 copy-start.7
  2.4 1.2 %copy-start.9 = (f32[6,64,512]{2,1,0:T(8,128)S(1)}, f32[6,64,512]{2,1,0:T(8,128)}, u32[]{:S(2)}) copy-start(f32[6,64,512]{2,1,0:T(8,128)} %state_ref.1) | copy-start | bytes 2359300
  3.6 1.1 %copy-start.10 = (f32[6,64,512]{2,1,0:T(8,128)S(1)}, f32[6,64,512]{2,1,0:T(8,128)}, u32[]{:S(2)}) copy-start(f32[6,64,512]{2,1,0:T(8,128)} %now_ref.1) | copy-start | bytes 2359300
  4.7 1.1 %copy-start.11 = (f32[6,64,512]{2,1,0:T(8,128)S(1)}, f32[6,64,512]{2,1,0:T(8,128)}, u32[]{:S(2)}) copy-start(f32[6,64,512]{2,1,0:T(8,128)} %old_ref.1) | copy-start | bytes 2359300
  5.8 29.4 %copy-start = (f32[512,512]{1,0:T(8,128)S(1)}, f32[512,512]{1,0:T(8,128)}, u32[]{:S(2)}) copy-start(f32[512,512]{1,0:T(8,128)} %deriv_ref.1) | copy-start | bytes 3145732
  5.8 29.4 %copy-start.1 = (f32[512,512]{1,0:T(8,128)S(1)}, f32[512,512]{1,0:T(8,128)}, u32[]{:S(2)}) copy-start(f32[512,512]{1,0:T(8,128)} %inverse_ref.1) | copy-start | bytes 3145732
  5.9 29.4 %copy-start.2 = (f32[512,512]{1,0:T(8,128)S(1)}, f32[512,512]{1,0:T(8,128)}, u32[]{:S(2)}) copy-start(f32[512,512]{1,0:T(8,128)} %basis_ref.1) | copy-start | bytes 3145732
  5.9 29.4 %copy-start.8 = (f32[512]{0:T(512)S(1)}, f32[512]{0:T(512)}, u32[]{:S(2)}) copy-start(f32[512]{0:T(512)} %param.17) | copy-start | bytes 6148
  7.6 10.4 %collective-permute-start = (f32[2,3,64,128]{3,2,1,0:T(8,128)S(1)}, f32[2,3,64,128]{3,2,1,0:T(8,128)S(1)}, u32[]{:S(2)}, u32[]{:S(2)}) collective-permute-start(f32[2,3,64,128]{3,2,1,0:T(8,128)S(1)} %get-tuple-element.42), channel_id=1, source_target_pairs={{0,6},{1,7},{2,4},{3,5},{4,2},{5,3},{6,0},{7,1},{8,14},{9,15},{10,... | collective-permute-start | bytes 589832 | tf_op jit(solution)/shard_map/ppermute | solution.py:278
  12.7 20.2 %collective-permute-start.1 = (f32[2,3,64,128]{3,2,1,0:T(8,128)S(1)}, f32[2,3,64,128]{3,2,1,0:T(8,128)S(1)}, u32[]{:S(2)}, u32[]{:S(2)}) collective-permute-start(f32[2,3,64,128]{3,2,1,0:T(8,128)S(1)} %get-tuple-element.43), channel_id=1, source_target_pairs={{0,7},{1,6},{2,5},{3,4},{4,3},{5,2},{6,1},{7,0},{8,15},{9,14},{10,... | collective-permute-start | bytes 589832 | tf_op jit(solution)/shard_map/ppermute | solution.py:278
  12.7 30.4 %collective-permute-start.2 = (f32[2,3,64,128]{3,2,1,0:T(8,128)S(1)}, f32[2,3,64,128]{3,2,1,0:T(8,128)S(1)}, u32[]{:S(2)}, u32[]{:S(2)}) collective-permute-start(f32[2,3,64,128]{3,2,1,0:T(8,128)S(1)} %get-tuple-element.44), channel_id=1, source_target_pairs={{0,4},{1,5},{2,6},{3,7},{4,0},{5,1},{6,2},{7,3},{8,12},{9,13},{10,... | collective-permute-start | bytes 589832 | tf_op jit(solution)/shard_map/ppermute | solution.py:278
  12.9 32.5 %collective-permute-start.3 = (f32[2,3,64,128]{3,2,1,0:T(8,128)S(1)}, f32[2,3,64,128]{3,2,1,0:T(8,128)S(1)}, u32[]{:S(2)}, u32[]{:S(2)}) collective-permute-start(f32[2,3,64,128]{3,2,1,0:T(8,128)S(1)} %get-tuple-element.45), channel_id=1, source_target_pairs={{0,5},{1,4},{2,7},{3,6},{4,1},{5,0},{6,3},{7,2},{8,13},{9,12},{10,... | collective-permute-start | bytes 589832 | tf_op jit(solution)/shard_map/ppermute | solution.py:278
  15.1 30.2 %collective-permute-start.4 = (f32[2,3,64,128]{3,2,1,0:T(8,128)S(1)}, f32[2,3,64,128]{3,2,1,0:T(8,128)S(1)}, u32[]{:S(2)}, u32[]{:S(2)}) collective-permute-start(f32[2,3,64,128]{3,2,1,0:T(8,128)S(1)} %get-tuple-element.46), channel_id=1, source_target_pairs={{0,2},{1,3},{2,0},{3,1},{4,6},{5,7},{6,4},{7,5},{8,10},{9,11},{10,... | collective-permute-start | bytes 589832 | tf_op jit(solution)/shard_map/ppermute | solution.py:278
  18.0 27.4 %collective-permute-start.5 = (f32[2,3,64,128]{3,2,1,0:T(8,128)S(1)}, f32[2,3,64,128]{3,2,1,0:T(8,128)S(1)}, u32[]{:S(2)}, u32[]{:S(2)}) collective-permute-start(f32[2,3,64,128]{3,2,1,0:T(8,128)S(1)} %get-tuple-element.47), channel_id=1, source_target_pairs={{0,3},{1,2},{2,1},{3,0},{4,7},{5,6},{6,5},{7,4},{8,11},{9,10},{10,... | collective-permute-start | bytes 589832 | tf_op jit(solution)/shard_map/ppermute | solution.py:278
  32.9 12.5 %collective-permute-start.6 = (f32[2,3,64,128]{3,2,1,0:T(8,128)S(1)}, f32[2,3,64,128]{3,2,1,0:T(8,128)S(1)}, u32[]{:S(2)}, u32[]{:S(2)}) collective-permute-start(f32[2,3,64,128]{3,2,1,0:T(8,128)S(1)} %get-tuple-element.48), channel_id=1, source_target_pairs={{0,1},{1,0},{2,3},{3,2},{4,5},{5,4},{6,7},{7,6},{8,9},{9,8},{10,11... | collective-permute-start | bytes 589832 | tf_op jit(solution)/shard_map/ppermute | solution.py:278
  48.3 8.0 %collective-permute-start.7 = (f32[3,64,128]{2,1,0:T(8,128)S(1)}, f32[3,64,128]{2,1,0:T(8,128)S(1)}, u32[]{:S(2)}, u32[]{:S(2)}) collective-permute-start(f32[3,64,128]{2,1,0:T(8,128)S(1)} %get-tuple-element.50), channel_id=1, source_target_pairs={{0,6},{1,7},{2,4},{3,5},{4,2},{5,3},{6,0},{7,1},{8,14},{9,15},{10,... | collective-permute-start | bytes 294920 | tf_op jit(solution)/shard_map/ppermute | solution.py:278
  50.6 6.9 %collective-permute-start.8 = (f32[3,64,128]{2,1,0:T(8,128)S(1)}, f32[3,64,128]{2,1,0:T(8,128)S(1)}, u32[]{:S(2)}, u32[]{:S(2)}) collective-permute-start(f32[3,64,128]{2,1,0:T(8,128)S(1)} %get-tuple-element.51), channel_id=1, source_target_pairs={{0,7},{1,6},{2,5},{3,4},{4,3},{5,2},{6,1},{7,0},{8,15},{9,14},{10,... | collective-permute-start | bytes 294920 | tf_op jit(solution)/shard_map/ppermute | solution.py:278
  53.1 13.3 %collective-permute-start.9 = (f32[3,64,128]{2,1,0:T(8,128)S(1)}, f32[3,64,128]{2,1,0:T(8,128)S(1)}, u32[]{:S(2)}, u32[]{:S(2)}) collective-permute-start(f32[3,64,128]{2,1,0:T(8,128)S(1)} %get-tuple-element.52), channel_id=1, source_target_pairs={{0,4},{1,5},{2,6},{3,7},{4,0},{5,1},{6,2},{7,3},{8,12},{9,13},{10,... | collective-permute-start | bytes 294920 | tf_op jit(solution)/shard_map/ppermute | solution.py:278
  53.1 15.5 %collective-permute-start.10 = (f32[3,64,128]{2,1,0:T(8,128)S(1)}, f32[3,64,128]{2,1,0:T(8,128)S(1)}, u32[]{:S(2)}, u32[]{:S(2)}) collective-permute-start(f32[3,64,128]{2,1,0:T(8,128)S(1)} %get-tuple-element.53), channel_id=1, source_target_pairs={{0,5},{1,4},{2,7},{3,6},{4,1},{5,0},{6,3},{7,2},{8,13},{9,12},{10,... | collective-permute-start | bytes 294920 | tf_op jit(solution)/shard_map/ppermute | solution.py:278
  54.5 14.1 %collective-permute-start.11 = (f32[3,64,128]{2,1,0:T(8,128)S(1)}, f32[3,64,128]{2,1,0:T(8,128)S(1)}, u32[]{:S(2)}, u32[]{:S(2)}) collective-permute-start(f32[3,64,128]{2,1,0:T(8,128)S(1)} %get-tuple-element.54), channel_id=1, source_target_pairs={{0,2},{1,3},{2,0},{3,1},{4,6},{5,7},{6,4},{7,5},{8,10},{9,11},{10,... | collective-permute-start | bytes 294920 | tf_op jit(solution)/shard_map/ppermute | solution.py:278
  56.2 12.4 %collective-permute-start.12 = (f32[3,64,128]{2,1,0:T(8,128)S(1)}, f32[3,64,128]{2,1,0:T(8,128)S(1)}, u32[]{:S(2)}, u32[]{:S(2)}) collective-permute-start(f32[3,64,128]{2,1,0:T(8,128)S(1)} %get-tuple-element.55), channel_id=1, source_target_pairs={{0,3},{1,2},{2,1},{3,0},{4,7},{5,6},{6,5},{7,4},{8,11},{9,10},{10,... | collective-permute-start | bytes 294920 | tf_op jit(solution)/shard_map/ppermute | solution.py:278
  57.5 11.1 %collective-permute-start.13 = (f32[3,64,128]{2,1,0:T(8,128)S(1)}, f32[3,64,128]{2,1,0:T(8,128)S(1)}, u32[]{:S(2)}, u32[]{:S(2)}) collective-permute-start(f32[3,64,128]{2,1,0:T(8,128)S(1)} %get-tuple-element.56), channel_id=1, source_target_pairs={{0,1},{1,0},{2,3},{3,2},{4,5},{5,4},{6,7},{7,6},{8,9},{9,8},{10,11... | collective-permute-start | bytes 294920 | tf_op jit(solution)/shard_map/ppermute | solution.py:278
  68.6 11.4 %copy-start.3 = (f32[6,64,512]{2,1,0:T(8,128)S(1)}, f32[6,64,512]{2,1,0:T(8,128)}, u32[]{:S(2)}) copy-start(f32[6,64,512]{2,1,0:T(8,128)} %velocity_ref.1) | copy-start | bytes 2359300
  68.6 11.4 %copy-start.6 = (s32[2,512]{1,0:T(2,128)S(1)}, s32[2,512]{1,0:T(2,128)}, u32[]{:S(2)}) copy-start(s32[2,512]{1,0:T(2,128)} %modes_ref.5) | copy-start | bytes 12292
  71.1 7.5 %collective-permute-start.14 = (f32[3,64,128]{2,1,0:T(8,128)S(1)}, f32[3,64,128]{2,1,0:T(8,128)S(1)}, u32[]{:S(2)}, u32[]{:S(2)}) collective-permute-start(f32[3,64,128]{2,1,0:T(8,128)S(1)} %get-tuple-element.60), channel_id=1, source_target_pairs={{0,6},{1,7},{2,4},{3,5},{4,2},{5,3},{6,0},{7,1},{8,14},{9,15},{10,... | collective-permute-start | bytes 294920 | tf_op jit(solution)/shard_map/ppermute | solution.py:278
  72.4 7.5 %collective-permute-start.18 = (f32[3,64,128]{2,1,0:T(8,128)S(1)}, f32[3,64,128]{2,1,0:T(8,128)S(1)}, u32[]{:S(2)}, u32[]{:S(2)}) collective-permute-start(f32[3,64,128]{2,1,0:T(8,128)S(1)} %get-tuple-element.64), channel_id=1, source_target_pairs={{0,2},{1,3},{2,0},{3,1},{4,6},{5,7},{6,4},{7,5},{8,10},{9,11},{10,... | collective-permute-start | bytes 294920 | tf_op jit(solution)/shard_map/ppermute | solution.py:278
  73.0 9.5 %collective-permute-start.15 = (f32[3,64,128]{2,1,0:T(8,128)S(1)}, f32[3,64,128]{2,1,0:T(8,128)S(1)}, u32[]{:S(2)}, u32[]{:S(2)}) collective-permute-start(f32[3,64,128]{2,1,0:T(8,128)S(1)} %get-tuple-element.61), channel_id=1, source_target_pairs={{0,7},{1,6},{2,5},{3,4},{4,3},{5,2},{6,1},{7,0},{8,15},{9,14},{10,... | collective-permute-start | bytes 294920 | tf_op jit(solution)/shard_map/ppermute | solution.py:278
  75.0 14.0 %collective-permute-start.16 = (f32[3,64,128]{2,1,0:T(8,128)S(1)}, f32[3,64,128]{2,1,0:T(8,128)S(1)}, u32[]{:S(2)}, u32[]{:S(2)}) collective-permute-start(f32[3,64,128]{2,1,0:T(8,128)S(1)} %get-tuple-element.62), channel_id=1, source_target_pairs={{0,4},{1,5},{2,6},{3,7},{4,0},{5,1},{6,2},{7,3},{8,12},{9,13},{10,... | collective-permute-start | bytes 294920 | tf_op jit(solution)/shard_map/ppermute | solution.py:278
  76.7 14.1 %collective-permute-start.17 = (f32[3,64,128]{2,1,0:T(8,128)S(1)}, f32[3,64,128]{2,1,0:T(8,128)S(1)}, u32[]{:S(2)}, u32[]{:S(2)}) collective-permute-start(f32[3,64,128]{2,1,0:T(8,128)S(1)} %get-tuple-element.63), channel_id=1, source_target_pairs={{0,5},{1,4},{2,7},{3,6},{4,1},{5,0},{6,3},{7,2},{8,13},{9,12},{10,... | collective-permute-start | bytes 294920 | tf_op jit(solution)/shard_map/ppermute | solution.py:278
  78.6 13.8 %collective-permute-start.19 = (f32[3,64,128]{2,1,0:T(8,128)S(1)}, f32[3,64,128]{2,1,0:T(8,128)S(1)}, u32[]{:S(2)}, u32[]{:S(2)}) collective-permute-start(f32[3,64,128]{2,1,0:T(8,128)S(1)} %get-tuple-element.65), channel_id=1, source_target_pairs={{0,3},{1,2},{2,1},{3,0},{4,7},{5,6},{6,5},{7,4},{8,11},{9,10},{10,... | collective-permute-start | bytes 294920 | tf_op jit(solution)/shard_map/ppermute | solution.py:278
  79.9 12.5 %collective-permute-start.20 = (f32[3,64,128]{2,1,0:T(8,128)S(1)}, f32[3,64,128]{2,1,0:T(8,128)S(1)}, u32[]{:S(2)}, u32[]{:S(2)}) collective-permute-start(f32[3,64,128]{2,1,0:T(8,128)S(1)} %get-tuple-element.66), channel_id=1, source_target_pairs={{0,1},{1,0},{2,3},{3,2},{4,5},{5,4},{6,7},{7,6},{8,9},{9,8},{10,11... | collective-permute-start | bytes 294920 | tf_op jit(solution)/shard_map/ppermute | solution.py:278
  80.0 1.1 %copy-start.4 = (f32[6,64,512]{2,1,0:T(8,128)S(1)}, f32[6,64,512]{2,1,0:T(8,128)}, u32[]{:S(2)}) copy-start(f32[6,64,512]{2,1,0:T(8,128)} %get-tuple-element.32.state_ref) | copy-start | bytes 2359300
  82.5 11.5 %collective-permute-start.23 = (f32[3,64]{1,0:T(4,128)S(1)}, f32[3,64]{1,0:T(4,128)S(1)}, u32[]{:S(2)}, u32[]{:S(2)}) collective-permute-start(f32[3,64]{1,0:T(4,128)S(1)} %shard_map.127), channel_id=1, source_target_pairs={{0,24},{8,16},{16,8},{24,0},{1,25},{9,17},{17,9},{25,1},{2,26},{10... | collective-permute-start | bytes 2312 | tf_op jit(solution)/shard_map/ppermute | solution.py:286
  89.0 5.1 %collective-permute-start.22 = (f32[3,64]{1,0:T(4,128)S(1)}, f32[3,64]{1,0:T(4,128)S(1)}, u32[]{:S(2)}, u32[]{:S(2)}) collective-permute-start(f32[3,64]{1,0:T(4,128)S(1)} %shard_map.127), channel_id=1, source_target_pairs={{0,16},{8,24},{16,0},{24,8},{1,17},{9,25},{17,1},{25,9},{2,18},{10... | collective-permute-start | bytes 2312 | tf_op jit(solution)/shard_map/ppermute | solution.py:286
  90.9 3.6 %collective-permute-start.21 = (f32[3,64]{1,0:T(4,128)S(1)}, f32[3,64]{1,0:T(4,128)S(1)}, u32[]{:S(2)}, u32[]{:S(2)}) collective-permute-start(f32[3,64]{1,0:T(4,128)S(1)} %shard_map.127), channel_id=1, source_target_pairs={{0,8},{8,0},{16,24},{24,16},{1,9},{9,1},{17,25},{25,17},{2,10},{10... | collective-permute-start | bytes 2312 | tf_op jit(solution)/shard_map/ppermute | solution.py:286

commit v7 on v6

--- a/solution.py
+++ b/solution.py
@@ -15,41 +15,31 @@
 RK_ZETA = -17.0 / 60.0
 WAVE_SCALE = 8.0
 VMEM_LIMIT = 24 * 1024 * 1024
-GROUPS = 3
+CHUNKS = (2, 1)
 LANES = 128
+HEAVY = 10
 
 F32 = jnp.float32
 BF16 = jnp.bfloat16
 
 
-def call(body, out_shape, in_specs, out_specs, flops, nbytes, scratch=(), aliases=None):
+def call(body, out_shape, in_specs, out_specs, weight, scratch=(), aliases=None):
     return pl.pallas_call(
         body,
-        grid=(1,),
         out_shape=out_shape,
         in_specs=in_specs,
         out_specs=out_specs,
         scratch_shapes=list(scratch),
         input_output_aliases=aliases or {},
-        cost_estimate=pl.CostEstimate(flops=flops, bytes_accessed=nbytes, transcendentals=0),
+        cost_estimate=pl.CostEstimate(flops=weight * 10**9, bytes_accessed=weight * 10**6, transcendentals=0),
         compiler_params=pltpu.CompilerParams(vmem_limit_bytes=VMEM_LIMIT),
     )
 
 
-def whole(shape):
-    return pl.BlockSpec(shape, lambda i: (0,) * len(shape))
-
-
-def part(shape, at):
-    return pl.BlockSpec(shape, lambda i: (at,) + (0,) * (len(shape) - 1))
-
-
-def scalar():
-    return pl.BlockSpec(memory_space=pltpu.SMEM)
-
-
-def untouched():
-    return pl.BlockSpec(memory_space=pl.ANY)
+LOCAL = pl.BlockSpec(memory_space=pltpu.VMEM)
+SCALAR = pl.BlockSpec(memory_space=pltpu.SMEM)
+FAR = pl.BlockSpec(memory_space=pltpu.HBM)
+ANYWHERE = pl.BlockSpec(memory_space=pl.ANY)
 
 
 def shaped(shape, dtype=F32):
@@ -89,12 +79,10 @@
 NT = (((1,), (1,)), ((), ()))
 
 
-def plan_kernel(devices, me_ref, owner_ref, modes_ref, info_ref, wave_ref):
-    columns = owner_ref.shape[1]
+def plan(devices, me, owner, modes):
+    columns = owner.shape[1]
     share = columns // devices
     rows = -(-devices // 8) * 8
-    me = me_ref[0]
-    owner = owner_ref[...]
     owned = (lax.broadcasted_iota(jnp.int32, (rows, columns), 0) == owner).astype(F32)
     before = (
         lax.broadcasted_iota(jnp.int32, (LANES, LANES), 0) < lax.broadcasted_iota(jnp.int32, (LANES, LANES), 1)
@@ -124,29 +112,26 @@
     place = (solver ^ me) * share + slot.astype(jnp.int32)
     extra = jnp.where(beyond, (owner ^ me) * share + rank.astype(jnp.int32) - share, -1)
     mine = jnp.sum((owner == me).astype(F32), axis=1, keepdims=True).astype(jnp.int32)
-    info_ref[...] = jnp.concatenate(
+    info = jnp.concatenate(
         [place, extra, jnp.broadcast_to(mine, (1, columns)), jnp.zeros((5, columns), jnp.int32)], axis=0
     )
-    wave = jnp.broadcast_to(wave_row(modes_ref[...]), (16, columns))
+    wave = jnp.broadcast_to(wave_row(modes), (16, columns))
     picked = sum_parts(
         lax.dot_general(three_parts(wave), selector(place, share), NT, preferred_element_type=F32)
     )
-    wave_ref[...] = jnp.concatenate([picked, picked], axis=1)[:8]
-
-
-def pack_kernel(devices, info_ref, modes_ref, state_ref, now_ref, old_ref, *out_refs):
-    comps, points, columns = state_ref.shape
+    return info, jnp.concatenate([picked, picked], axis=1)[:8]
+
+
+def pack(devices, points, wave, place, state, now, old, out_refs):
+    comps, _, columns = state.shape
     share = columns // devices
-    wave = wave_row(modes_ref[...]).reshape(1, 1, columns)
-    state = state_ref[...]
-    forcing = RK_GAMMA * now_ref[...] + RK_ZETA * old_ref[...]
+    wave = wave.reshape(1, 1, columns)
+    forcing = RK_GAMMA * now + RK_ZETA * old
     local = state + TIME_STEP * (forcing - RK_ALPHA * (wave * state))
     rows = comps * points
     both = jnp.concatenate([state.reshape(rows, columns), local.reshape(rows, columns)], axis=0)
     placed = sum_parts(
-        lax.dot_general(
-            three_parts(both), selector(info_ref[0:1, :], columns), NT, preferred_element_type=F32
-        )
+        lax.dot_general(three_parts(both), selector(place, columns), NT, preferred_element_type=F32)
     )
     for step, out in zip(steps_of(devices), out_refs):
         taken = placed[:, step * share : (step + 1) * share]
@@ -159,6 +144,53 @@
                 )
 
 
+def first_kernel(
+    devices, me_ref, owner_hbm, modes_hbm, state_hbm, now_hbm, old_hbm, info_ref, wave_ref, *refs
+):
+    out_refs, (owner_ref, modes_ref, state_ref, now_ref, old_ref, sems) = refs[:devices], refs[devices:]
+    comps, points, _ = state_ref.shape
+    copies = [
+        pltpu.make_async_copy(source, target, sems.at[at])
+        for at, (source, target) in enumerate(
+            (
+                (owner_hbm, owner_ref),
+                (modes_hbm, modes_ref),
+                (state_hbm.at[:comps], state_ref),
+                (now_hbm.at[:comps], now_ref),
+                (old_hbm.at[:comps], old_ref),
+            )
+        )
+    ]
+    for copy in copies:
+        copy.start()
+    copies[0].wait()
+    copies[1].wait()
+    info, wave = plan(devices, me_ref[0], owner_ref[...], modes_ref[...])
+    info_ref[...] = info
+    wave_ref[...] = wave
+    for copy in copies[2:]:
+        copy.wait()
+    wave = wave_row(modes_ref[...])
+    pack(devices, points, wave, info[0:1], state_ref[...], now_ref[...], old_ref[...], out_refs)
+
+
+def pack_kernel(devices, done, info_ref, modes_ref, state_hbm, now_hbm, old_hbm, after_ref, *refs):
+    out_refs, (state_ref, now_ref, old_ref, sems) = refs[:devices], refs[devices:]
+    comps, points, _ = state_ref.shape
+    copies = [
+        pltpu.make_async_copy(source.at[done : done + comps], target, sems.at[at])
+        for at, (source, target) in enumerate(
+            ((state_hbm, state_ref), (now_hbm, now_ref), (old_hbm, old_ref))
+        )
+    ]
+    for copy in copies:
+        copy.start()
+    for copy in copies:
+        copy.wait()
+    wave = wave_row(modes_ref[...])
+    pack(devices, points, wave, info_ref[0:1, :], state_ref[...], now_ref[...], old_ref[...], out_refs)
+
+
 def operators_kernel(deriv_ref, inverse_ref, basis_ref, values_ref, deriv_out, inverse_out, basis_out, values_out):
     for source, target in ((deriv_ref, deriv_out), (inverse_ref, inverse_out), (basis_ref, basis_out)):
         high, low = two_parts(source[...])
@@ -174,7 +206,7 @@
 
 def solve_kernel(devices, me_ref, wave_ref, values_ref, deriv_ref, inverse_ref, basis_ref, *refs):
     in_refs, refs = refs[:devices], refs[devices:]
-    out_refs, (solved_ref, state, local, after) = refs[:devices], refs[devices:]
+    out_refs, (solved_ref, state, local, after) = refs[-devices - 4 : -4], refs[-4:]
     me = me_ref[0]
     _, pairs, points, lanes = in_refs[0].shape
     for step, block in zip(steps_of(devices), in_refs):
@@ -195,11 +227,11 @@
             block[pair] = after[rows, pair * lanes : (pair + 1) * lanes]
 
 
-def unpack_kernel(devices, first, info_ref, *refs):
+def unpack_kernel(devices, done, info_ref, *refs):
     in_refs, refs = refs[:devices], refs[devices:]
-    if not first:
-        refs = refs[1:]
-    state_ref, out_refs = refs[0], refs[1:]
+    if done:
+        refs = refs[2:]
+    state_hbm, out_refs, (state_ref, sem) = refs[0], refs[1:-2], refs[-2:]
     pairs, points, lanes = in_refs[0].shape
     share = lanes // 2
     columns = devices * share
@@ -218,6 +250,8 @@
         jnp.dot(three_parts(got), selector(info_ref[0:1, :], columns), preferred_element_type=F32)
     )
     state_ref[...] = state.reshape(2 * pairs, points, columns)
+    copy = pltpu.make_async_copy(state_ref, state_hbm.at[done : done + 2 * pairs], sem)
+    copy.start()
     extra = sum_parts(
         lax.dot_general(
             three_parts(state), selector(info_ref[1:2, :], columns), NT, preferred_element_type=F32
@@ -229,6 +263,7 @@
             real = 2 * pair * points
             imag = real + points
             out[pair] = jnp.concatenate([taken[real : real + points], taken[imag : imag + points]], axis=1)
+    copy.wait()
 
 
 def emf_kernel(modes_ref, velocity_ref, state_ref, later_ref, emf_ref):
@@ -249,23 +284,29 @@
     emf_ref[...] = jnp.concatenate(rows, axis=0)
 
 
-def assemble_kernel(devices, first, me_ref, info_ref, solved_ref, *refs):
+def assemble_kernel(devices, done, me_ref, info_ref, solved_ref, *refs):
     in_refs, refs = refs[:devices], refs[devices:]
-    if not first:
+    if done:
         refs = refs[1:]
-    (out_ref,) = refs
+    out_hbm, whole, sems = refs
     me = me_ref[0]
     pairs, points, lanes = in_refs[0].shape
     share = lanes // 2
     depth = solved_ref.shape[1]
     used = lax.broadcasted_iota(jnp.int32, (depth, share), 1) < info_ref[2:3, :share]
+    copies = []
     for pair in range(pairs):
         for half in range(2):
+            comp = 2 * pair + half
             kept = jnp.where(used, solved_ref[pair][:, half * share : (half + 1) * share], 0.0)
-            out_ref[2 * pair + half, :, :share] = kept
+            whole[comp, :, :share] = kept
             for step, block in zip(steps_of(devices), in_refs):
                 rows = pl.ds(pl.multiple_of((me ^ step) * points, points), points)
-                out_ref[2 * pair + half, rows, share:] = block[pair][:, half * share : (half + 1) * share]
+                whole[comp, rows, share:] = block[pair][:, half * share : (half + 1) * share]
+            copies.append(pltpu.make_async_copy(whole.at[comp], out_hbm.at[done + comp], sems.at[comp]))
+            copies[-1].start()
+    for copy in copies:
+        copy.wait()
 
 
 def steps_of(devices):
@@ -307,106 +348,95 @@
     depth = devices * points
     share = columns // devices
     lanes = 2 * share
-    pairs = GROUPS
-    chunks = comps // (2 * pairs)
+    starts = [2 * sum(CHUNKS[:at]) for at in range(len(CHUNKS))]
     me = lax.axis_index("col").astype(jnp.int32).reshape(1)
     owner = col_owner.reshape(1, columns)
-
-    info, wave = call(
-        functools.partial(plan_kernel, devices),
-        [shaped((8, columns), jnp.int32), shaped((8, lanes))],
-        [scalar(), whole((1, columns)), whole((2, columns))],
-        [whole((8, columns)), whole((8, lanes))],
-        1000000,
-        100000,
-    )(me, owner, kept_modes)
-
-    field = (2 * pairs, points, columns)
-    sent = (2, pairs, points, lanes)
-    back = (pairs, points, lanes)
-    moved = 4 * 2 * pairs * points * columns
+    state_far, now_far, old_far, modes_far, owner_far = (
+        pltpu.with_memory_space_constraint(array, pltpu.HBM)
+        for array in (state_now, force_now, force_old, kept_modes, owner)
+    )
+    fields = (state_far, now_far, old_far)
 
     forward = []
-    for chunk in range(chunks):
-        forward.append(
-            exchange(
-                call(
-                    functools.partial(pack_kernel, devices),
-                    [shaped(sent)] * devices,
-                    [whole((8, columns)), whole((2, columns))] + [part(field, chunk)] * 3,
-                    [whole(sent)] * devices,
-                    12 * 2 * pairs * points * columns * columns,
-                    5 * moved,
-                )(info, kept_modes, state_now, force_now, force_old)
-            )
-        )
+    for pairs, done in zip(CHUNKS, starts):
+        sent = [shaped((2, pairs, points, lanes))] * devices
+        loaded = [pltpu.VMEM((2 * pairs, points, columns), F32)] * 3
+        if done == 0:
+            outs = call(
+                functools.partial(first_kernel, devices),
+                [shaped((8, columns), jnp.int32), shaped((8, lanes))] + sent,
+                [SCALAR] + [FAR] * 5,
+                [LOCAL] * (2 + devices),
+                1,
+                [pltpu.VMEM((1, columns), jnp.int32), pltpu.VMEM((2, columns), jnp.int32)]
+                + loaded
+                + [pltpu.SemaphoreType.DMA((5,))],
+            )(me, owner_far, modes_far, *fields)
+            info, wave = outs[:2]
+            blocks = outs[2:]
+        else:
+            blocks = call(
+                functools.partial(pack_kernel, devices, done),
+                sent,
+                [LOCAL] * 2 + [FAR] * 3 + [ANYWHERE],
+                [LOCAL] * devices,
+                HEAVY,
+                loaded + [pltpu.SemaphoreType.DMA((3,))],
+            )(info, kept_modes, *fields, forward[-1][3])
+        forward.append(exchange(blocks))
 
     operator = shaped((depth, 3 * depth), BF16)
     operators = call(
         operators_kernel,
         [operator, operator, operator, shaped((depth, lanes))],
-        [whole((depth, depth))] * 3 + [whole((1, depth))],
-        [whole((depth, 3 * depth))] * 3 + [whole((depth, lanes))],
-        1000000,
-        30 * depth * depth,
+        [LOCAL] * 4,
+        [LOCAL] * 4,
+        HEAVY,
     )(second_deriv, eig_inverse, eig_basis, eig_values.reshape(1, depth))
-    values = operators[3]
 
     solved, returned = [], []
-    for chunk in range(chunks):
+    for pairs, blocks in zip(CHUNKS, forward):
         width = pairs * lanes
         outs = call(
             functools.partial(solve_kernel, devices),
-            [shaped(back)] * devices + [shaped((pairs, depth, lanes))],
-            [scalar(), whole((8, lanes)), whole((depth, lanes))]
-            + [whole((depth, 3 * depth))] * 3
-            + [whole(sent)] * devices,
-            [whole(back)] * devices + [whole((pairs, depth, lanes))],
-            18 * depth * depth * width,
-            18 * depth * depth + 16 * depth * width,
+            [shaped((pairs, points, lanes))] * devices + [shaped((pairs, depth, lanes))],
+            [SCALAR] + [LOCAL] * (5 + devices) + [ANYWHERE] * len(returned[-1:]),
+            [LOCAL] * (devices + 1),
+            HEAVY,
             [pltpu.VMEM((depth, width), F32)] * 3,
-        )(me, wave, values, *operators[:3], *forward[chunk])
+        )(me, wave, operators[3], *operators[:3], *blocks, *[sent[1] for sent in returned[-1:]])
         solved.append(outs[devices])
         returned.append(exchange(outs[:devices]))
 
     state_next, extra = None, []
-    for chunk in range(chunks):
-        first = chunk == 0
+    for pairs, done, blocks in zip(CHUNKS, starts, returned):
         outs = call(
-            functools.partial(unpack_kernel, devices, first),
-            [shaped(state_now.shape)] + [shaped(back)] * devices,
-            [whole((8, columns))] + [whole(back)] * devices + ([] if first else [untouched()]),
-            [part(field, chunk)] + [whole(back)] * devices,
-            12 * 2 * pairs * points * columns * columns,
-            6 * moved,
-            aliases={} if first else {1 + devices: 0},
-        )(info, *returned[chunk], *([] if first else [state_next]))
+            functools.partial(unpack_kernel, devices, done),
+            [shaped(state_now.shape)] + [shaped((pairs, points, lanes))] * devices,
+            [LOCAL] * (1 + devices) + ([FAR, ANYWHERE] if done else []),
+            [FAR] + [LOCAL] * devices,
+            HEAVY,
+            [pltpu.VMEM((2 * pairs, points, columns), F32), pltpu.SemaphoreType.DMA],
+            aliases={1 + devices: 0} if done else {},
+        )(info, *blocks, *([state_next, extra[-1][1]] if done else []))
         state_next = outs[0]
         extra.append(exchange(outs[1:]))
     emf = call(
-        emf_kernel,
-        shaped((3, points)),
-        [whole((2, columns)), whole(velocity.shape), whole(velocity.shape), untouched()],
-        whole((3, points)),
-        30 * comps * points * columns,
-        8 * comps * points * columns,
-    )(kept_modes, velocity, state_next, extra[-1][1 + devices // 2])
+        emf_kernel, shaped((3, points)), [LOCAL] * 3 + [ANYWHERE], LOCAL, 1
+    )(kept_modes, velocity, state_next, extra[-1][1])
     mean_emf = sum_over_groups(emf)
 
     owned = None
-    for chunk in range(chunks):
-        first = chunk == 0
+    for pairs, done, column, blocks in zip(CHUNKS, starts, solved, extra):
         owned = call(
-            functools.partial(assemble_kernel, devices, first),
+            functools.partial(assemble_kernel, devices, done),
             shaped((comps, depth, lanes)),
-            [scalar(), whole((8, columns)), whole((pairs, depth, lanes))]
-            + [whole(back)] * devices
-            + ([] if first else [untouched()]),
-            part((2 * pairs, depth, lanes), chunk),
-            1000000,
-            16 * pairs * depth * lanes,
-            aliases={} if first else {3 + devices: 0},
-        )(me, info, solved[chunk], *extra[chunk], *([] if first else [owned]))
+            [SCALAR] + [LOCAL] * (2 + devices) + ([FAR] if done else []),
+            FAR,
+            1,
+            [pltpu.VMEM((2 * pairs, depth, lanes), F32), pltpu.SemaphoreType.DMA((2 * pairs,))],
+            aliases={3 + devices: 0} if done else {},
+        )(me, info, column, *blocks, *([owned] if done else []))
     return (state_next, owned, mean_emf)
 
 

time: 95.4 us -> 95.8 us (level)
  local copies, waits for them, and re-layouts: 5.95 us -> 0.03 us
  starting transfers between devices: 53 us -> 58.8 us
  Pallas kernels: 10.4 us -> 15.4 us
  waiting for transfers between devices: 24.3 us -> 20 us
    ppermute x21 -> x42, starting transfers between devices: 47.6 us -> 55.3 us  [exchange(): lax.ppermute(block, 'col', [(i, i ^ step) for i in range(devices)])]
    ppermute x21 -> x42, waiting for transfers between devices: 23.9 us -> 17.9 us  [exchange(): lax.ppermute(block, 'col', [(i, i ^ step) for i in range(devices)])]
    unnamed x24 -> x14, local copies, waits for them, and re-layouts: 5.95 us -> 0.03 us
    pallas_call x6 -> x9, Pallas kernels: 9.42 us -> 14.4 us  [the longest x2 4.73 us: on_device(): call(functools.partial(solve_kernel, devices), [shaped((pairs, points, la...]
    ppermute x3, starting transfers between devices: 5.42 us -> 3.55 us  [sum_over_groups(): lax.ppermute(value, 'grp', [(i, i ^ step) for i in range(groups)])]
    ppermute x3, waiting for transfers between devices: 0.4 us -> 2.09 us  [sum_over_groups(): lax.ppermute(value, 'grp', [(i, i ^ step) for i in range(groups)])]
  transfers between devices with their start and end apart: 24 -> 45, of which waited for: 11 -> 10; matrix products, arithmetic and copies ran while one was open for 0% -> 0% of each run, Pallas kernels for 3% -> 13%
where the time goes in v7:
time: 95.8 us; the launch traced here: 95.6 us
  starting transfers between devices  58.8 us (61%)
  waiting for transfers between devices  20 us (21%)
  Pallas kernels  15.4 us (16%)
    ppermute x42, starting transfers between devices, exchange(): lax.ppermute(block, 'col', [(i, i ^ step) for i in range(devices)])  55.3 us
    ppermute x42, waiting for transfers between devices, exchange(): lax.ppermute(block, 'col', [(i, i ^ step) for i in range(devices)])  17.9 us
    pallas_call x2, Pallas kernels, on_device(): call(functools.partial(solve_kernel, devices), [shaped((pairs, points, la...  4.73 us
    ppermute x3, starting transfers between devices, sum_over_groups(): lax.ppermute(value, 'grp', [(i, i ^ step) for i in range(groups)])  3.55 us
    pallas_call x1, Pallas kernels, on_device(): call(functools.partial(first_kernel, devices), [shaped((8, columns), jnp....  2.8 us
    pallas_call x2, Pallas kernels, on_device(): call(functools.partial(unpack_kernel, devices, done), [shaped(state_now.s...  2.63 us
    ppermute x3, waiting for transfers between devices, sum_over_groups(): lax.ppermute(value, 'grp', [(i, i ^ step) for i in range(groups)])  2.09 us
    pallas_call x2, Pallas kernels, on_device(): call(functools.partial(assemble_kernel, devices, done), shaped((comps, de...  2.07 us
  transfers between devices with their start and end apart: 45, of which 10 were waited for; matrix products, arithmetic and copies ran while one was open for 0% of the time, Pallas kernels for 13%

profile of v7, /device:TPU:0, one launch (start us, length us, event | category | flops | bytes accessed | tf_op | source)
XLA Modules:
  0.0 95.6 jit_solution(778013688380678085)
XLA Ops:
  0.7 2.8 %shard_map.121 = (s32[8,512]{1,0:T(8,128)S(1)}, f32[8,128]{1,0:T(8,128)S(1)}, f32[2,2,64,128]{3,2,1,0:T(8,128)S(1)}, f32[2,2,64,128]{3,2,1,0:T(8,128)S(1)}, f32[...) custom-call(s32[1]{0:T(128)} %bitcast.me_ref, ...), custom_call_target="tpu_custom_call" | custom-call | flops 1000000000 | bytes 1000000 | tf_op jit(solution)/shard_map/pallas_call | solution.py:365
  3.5 4.1 %collective-permute-start = (f32[2,2,64,128]{3,2,1,0:T(8,128)S(1)}, f32[2,2,64,128]{3,2,1,0:T(8,128)S(1)}, u32[]{:S(2)}, u32[]{:S(2)}) collective-permute-start(f32[2,2,64,128]{3,2,1,0:T(8,128)S(1)} %get-tuple-element.67), channel_id=1, source_target_pairs={{0,4},{1,5},{2,6},{3,7},{4,0},{5,1},{6,2},{7,3},{8,12},{9,13},{10,... | collective-permute-start | bytes 393224 | tf_op jit(solution)/shard_map/ppermute | solution.py:319
  7.6 1.3 %collective-permute-start.8 = (f32[2,2,64,128]{3,2,1,0:T(8,128)S(1)}, f32[2,2,64,128]{3,2,1,0:T(8,128)S(1)}, u32[]{:S(2)}, u32[]{:S(2)}) collective-permute-start(f32[2,2,64,128]{3,2,1,0:T(8,128)S(1)} %get-tuple-element.77), channel_id=1, source_target_pairs={{0,6},{1,7},{2,4},{3,5},{4,2},{5,3},{6,0},{7,1},{8,14},{9,15},{10,... | collective-permute-start | bytes 393224 | tf_op jit(solution)/shard_map/ppermute | solution.py:319
  8.9 1.4 %collective-permute-start.9 = (f32[2,2,64,128]{3,2,1,0:T(8,128)S(1)}, f32[2,2,64,128]{3,2,1,0:T(8,128)S(1)}, u32[]{:S(2)}, u32[]{:S(2)}) collective-permute-start(f32[2,2,64,128]{3,2,1,0:T(8,128)S(1)} %get-tuple-element.78), channel_id=1, source_target_pairs={{0,7},{1,6},{2,5},{3,4},{4,3},{5,2},{6,1},{7,0},{8,15},{9,14},{10,... | collective-permute-start | bytes 393224 | tf_op jit(solution)/shard_map/ppermute | solution.py:319
  10.4 2.7 %collective-permute-start.11 = (f32[2,2,64,128]{3,2,1,0:T(8,128)S(1)}, f32[2,2,64,128]{3,2,1,0:T(8,128)S(1)}, u32[]{:S(2)}, u32[]{:S(2)}) collective-permute-start(f32[2,2,64,128]{3,2,1,0:T(8,128)S(1)} %get-tuple-element.80), channel_id=1, source_target_pairs={{0,2},{1,3},{2,0},{3,1},{4,6},{5,7},{6,4},{7,5},{8,10},{9,11},{10,... | collective-permute-start | bytes 393224 | tf_op jit(solution)/shard_map/ppermute | solution.py:319
  13.1 1.0 %shard_map.122 = (bf16[512,1536]{1,0:T(8,128)(2,1)S(1)}, bf16[512,1536]{1,0:T(8,128)(2,1)S(1)}, bf16[512,1536]{1,0:T(8,128)(2,1)S(1)}, f32[512,128]{1,0:T(8,128)S(1)}) custom-call(f32[512,512]{1,0:T(8,128)S(1)} %copy-done, f32[512,512]{1,0:T(8,128)S(1)} %copy-done.1, f32[512,512]{1,0:T(8,128)S(1)} %copy-done.2, f32[1,512]{1,0:T(1,128)S(1)} %bitcast.3), custom_call_target="tpu_custom_call" | custom-call | flops 10000000000 | bytes 10000000 | tf_op jit(solution)/shard_map/pallas_call | solution.py:389
  14.1 9.1 %collective-permute-done.after_ref.refs_3_ = f32[2,2,64,128]{3,2,1,0:T(8,128)S(1)} collective-permute-done((f32[2,2,64,128]{3,2,1,0:T(8,128)S(1)}, f32[2,2,64,128]{3,2,1,0:T(8,128)S(1)}, u32[]{:S(2)}, u32[]{:S(2)}) %collective-permute-start) | collective-permute-done | bytes 131104 | tf_op jit(solution)/shard_map/ppermute | solution.py:319
  23.3 1.9 %shard_map.123 = (f32[2,1,64,128]{3,2,1,0:T(8,128)S(1)}, f32[2,1,64,128]{3,2,1,0:T(8,128)S(1)}, f32[2,1,64,128]{3,2,1,0:T(8,128)S(1)}, f32[2,1,64,128]{3,2,1,0:T...) custom-call(s32[8,512]{1,0:T(8,128)S(1)} %get-tuple-element.61.info_, ...), custom_call_target="tpu_custom_call" | custom-call | flops 10000000000 | bytes 10000000 | tf_op jit(solution)/shard_map/pallas_call | solution.py:378
  25.2 2.8 %collective-permute-start.1 = (f32[2,1,64,128]{3,2,1,0:T(8,128)S(1)}, f32[2,1,64,128]{3,2,1,0:T(8,128)S(1)}, u32[]{:S(2)}, u32[]{:S(2)}) collective-permute-start(f32[2,1,64,128]{3,2,1,0:T(8,128)S(1)} %get-tuple-element.69), channel_id=1, source_target_pairs={{0,6},{1,7},{2,4},{3,5},{4,2},{5,3},{6,0},{7,1},{8,14},{9,15},{10,... | collective-permute-start | bytes 196616 | tf_op jit(solution)/shard_map/ppermute | solution.py:319
  28.0 1.9 %collective-permute-done.10.refs_4_ = f32[2,2,64,128]{3,2,1,0:T(8,128)S(1)} collective-permute-done((f32[2,2,64,128]{3,2,1,0:T(8,128)S(1)}, f32[2,2,64,128]{3,2,1,0:T(8,128)S(1)}, u32[]{:S(2)}, u32[]{:S(2)}) %collective-permute-start.10) | collective-permute-done | bytes 131104 | tf_op jit(solution)/shard_map/ppermute | solution.py:319
  30.0 5.4 %collective-permute-start.2 = (f32[2,1,64,128]{3,2,1,0:T(8,128)S(1)}, f32[2,1,64,128]{3,2,1,0:T(8,128)S(1)}, u32[]{:S(2)}, u32[]{:S(2)}) collective-permute-start(f32[2,1,64,128]{3,2,1,0:T(8,128)S(1)} %get-tuple-element.70), channel_id=1, source_target_pairs={{0,7},{1,6},{2,5},{3,4},{4,3},{5,2},{6,1},{7,0},{8,15},{9,14},{10,... | collective-permute-start | bytes 196616 | tf_op jit(solution)/shard_map/ppermute | solution.py:319
  35.4 2.7 %collective-permute-start.4 = (f32[2,1,64,128]{3,2,1,0:T(8,128)S(1)}, f32[2,1,64,128]{3,2,1,0:T(8,128)S(1)}, u32[]{:S(2)}, u32[]{:S(2)}) collective-permute-start(f32[2,1,64,128]{3,2,1,0:T(8,128)S(1)} %get-tuple-element.72), channel_id=1, source_target_pairs={{0,5},{1,4},{2,7},{3,6},{4,1},{5,0},{6,3},{7,2},{8,13},{9,12},{10,... | collective-permute-start | bytes 196616 | tf_op jit(solution)/shard_map/ppermute | solution.py:319
  38.1 2.4 %shard_map.124 = (f32[2,64,128]{2,1,0:T(8,128)S(1)}, f32[2,64,128]{2,1,0:T(8,128)S(1)}, f32[2,64,128]{2,1,0:T(8,128)S(1)}, f32[2,64,128]{2,1,0:T(8,128)S(1)}, f3...) custom-call(s32[1]{0:T(128)} %bitcast.me_ref, ...), custom_call_target="tpu_custom_call" | custom-call | flops 10000000000 | bytes 10000000 | tf_op jit(solution)/shard_map/pallas_call | solution.py:400
  40.5 1.8 %collective-permute-start.6 = (f32[2,1,64,128]{3,2,1,0:T(8,128)S(1)}, f32[2,1,64,128]{3,2,1,0:T(8,128)S(1)}, u32[]{:S(2)}, u32[]{:S(2)}) collective-permute-start(f32[2,1,64,128]{3,2,1,0:T(8,128)S(1)} %get-tuple-element.74), channel_id=1, source_target_pairs={{0,3},{1,2},{2,1},{3,0},{4,7},{5,6},{6,5},{7,4},{8,11},{9,10},{10,... | collective-permute-start | bytes 196616 | tf_op jit(solution)/shard_map/ppermute | solution.py:319
  42.3 0.5 collective-permute-start.7
  42.7 2.9 %collective-permute-start.14 = (f32[2,64,128]{2,1,0:T(8,128)S(1)}, f32[2,64,128]{2,1,0:T(8,128)S(1)}, u32[]{:S(2)}, u32[]{:S(2)}) collective-permute-start(f32[2,64,128]{2,1,0:T(8,128)S(1)} %get-tuple-element.83), channel_id=1, source_target_pairs={{0,6},{1,7},{2,4},{3,5},{4,2},{5,3},{6,0},{7,1},{8,14},{9,15},{10,... | collective-permute-start | bytes 196616 | tf_op jit(solution)/shard_map/ppermute | solution.py:319
  46.0 0.5 collective-permute-done.6.refs_6_
  46.5 2.5 %collective-permute-start.24 = (f32[2,64,128]{2,1,0:T(8,128)S(1)}, f32[2,64,128]{2,1,0:T(8,128)S(1)}, u32[]{:S(2)}, u32[]{:S(2)}) collective-permute-start(f32[2,64,128]{2,1,0:T(8,128)S(1)} %get-tuple-element.95), channel_id=1, source_target_pairs={{0,5},{1,4},{2,7},{3,6},{4,1},{5,0},{6,3},{7,2},{8,13},{9,12},{10,... | collective-permute-start | bytes 196616 | tf_op jit(solution)/shard_map/ppermute | solution.py:319
  48.9 0.9 collective-permute-start.25
  49.8 0.5 collective-permute-start.26
  50.4 0.8 collective-permute-done.22.refs_2_
  51.1 2.3 %shard_map.125 = (f32[1,64,128]{2,1,0:T(8,128)S(1)}, f32[1,64,128]{2,1,0:T(8,128)S(1)}, f32[1,64,128]{2,1,0:T(8,128)S(1)}, f32[1,64,128]{2,1,0:T(8,128)S(1)}, f3...) custom-call(s32[1]{0:T(128)} %bitcast.me_ref, ...), custom_call_target="tpu_custom_call" | custom-call | flops 10000000000 | bytes 10000000 | tf_op jit(solution)/shard_map/pallas_call | solution.py:400
  53.5 2.1 %collective-permute-done.23.refs_3_ = f32[2,64,128]{2,1,0:T(8,128)S(1)} collective-permute-done((f32[2,64,128]{2,1,0:T(8,128)S(1)}, f32[2,64,128]{2,1,0:T(8,128)S(1)}, u32[]{:S(2)}, u32[]{:S(2)}) %collective-permute-start.23) | collective-permute-done | bytes 65568 | tf_op jit(solution)/shard_map/ppermute | solution.py:319
  55.6 1.7 %collective-permute-start.15 = (f32[1,64,128]{2,1,0:T(8,128)S(1)}, f32[1,64,128]{2,1,0:T(8,128)S(1)}, u32[]{:S(2)}, u32[]{:S(2)}) collective-permute-start(f32[1,64,128]{2,1,0:T(8,128)S(1)} %get-tuple-element.85), channel_id=1, source_target_pairs={{0,6},{1,7},{2,4},{3,5},{4,2},{5,3},{6,0},{7,1},{8,14},{9,15},{10,... | collective-permute-start | bytes 98312 | tf_op jit(solution)/shard_map/ppermute | solution.py:319
  57.3 1.1 %collective-permute-start.16 = (f32[1,64,128]{2,1,0:T(8,128)S(1)}, f32[1,64,128]{2,1,0:T(8,128)S(1)}, u32[]{:S(2)}, u32[]{:S(2)}) collective-permute-start(f32[1,64,128]{2,1,0:T(8,128)S(1)} %get-tuple-element.86), channel_id=1, source_target_pairs={{0,7},{1,6},{2,5},{3,4},{4,3},{5,2},{6,1},{7,0},{8,15},{9,14},{10,... | collective-permute-start | bytes 98312 | tf_op jit(solution)/shard_map/ppermute | solution.py:319
  58.4 3.4 %collective-permute-start.18 = (f32[1,64,128]{2,1,0:T(8,128)S(1)}, f32[1,64,128]{2,1,0:T(8,128)S(1)}, u32[]{:S(2)}, u32[]{:S(2)}) collective-permute-start(f32[1,64,128]{2,1,0:T(8,128)S(1)} %get-tuple-element.88), channel_id=1, source_target_pairs={{0,5},{1,4},{2,7},{3,6},{4,1},{5,0},{6,3},{7,2},{8,13},{9,12},{10,... | collective-permute-start | bytes 98312 | tf_op jit(solution)/shard_map/ppermute | solution.py:319
  61.8 1.5 %shard_map.126 = (f32[6,64,512]{2,1,0:T(8,128)}, f32[2,64,128]{2,1,0:T(8,128)S(1)}, f32[2,64,128]{2,1,0:T(8,128)S(1)}, f32[2,64,128]{2,1,0:T(8,128)S(1)}, f32[2,...) custom-call(s32[8,512]{1,0:T(8,128)S(1)} %get-tuple-element.61.info_, ...), custom_call_target="tpu_custom_call" | custom-call | flops 10000000000 | bytes 10000000 | tf_op jit(solution)/shard_map/pallas_call | solution.py:413
  63.3 1.8 %collective-permute-start.28 = (f32[2,64,128]{2,1,0:T(8,128)S(1)}, f32[2,64,128]{2,1,0:T(8,128)S(1)}, u32[]{:S(2)}, u32[]{:S(2)}) collective-permute-start(f32[2,64,128]{2,1,0:T(8,128)S(1)} %get-tuple-element.100), channel_id=1, source_target_pairs={{0,6},{1,7},{2,4},{3,5},{4,2},{5,3},{6,0},{7,1},{8,14},{9,15},{10,... | collective-permute-start | bytes 196616 | tf_op jit(solution)/shard_map/ppermute | solution.py:319
  65.1 1.1 %collective-permute-start.36 = (f32[2,64,128]{2,1,0:T(8,128)S(1)}, f32[2,64,128]{2,1,0:T(8,128)S(1)}, u32[]{:S(2)}, u32[]{:S(2)}) collective-permute-start(f32[2,64,128]{2,1,0:T(8,128)S(1)} %get-tuple-element.113), channel_id=1, source_target_pairs={{0,7},{1,6},{2,5},{3,4},{4,3},{5,2},{6,1},{7,0},{8,15},{9,14},{10,... | collective-permute-start | bytes 196616 | tf_op jit(solution)/shard_map/ppermute | solution.py:319
  66.2 2.5 %collective-permute-start.20 = (f32[1,64,128]{2,1,0:T(8,128)S(1)}, f32[1,64,128]{2,1,0:T(8,128)S(1)}, u32[]{:S(2)}, u32[]{:S(2)}) collective-permute-start(f32[1,64,128]{2,1,0:T(8,128)S(1)} %get-tuple-element.90), channel_id=1, source_target_pairs={{0,3},{1,2},{2,1},{3,0},{4,7},{5,6},{6,5},{7,4},{8,11},{9,10},{10,... | collective-permute-start | bytes 98312 | tf_op jit(solution)/shard_map/ppermute | solution.py:319
  68.6 3.0 %collective-permute-done.19.refs_5_ = f32[1,64,128]{2,1,0:T(8,128)S(1)} collective-permute-done((f32[1,64,128]{2,1,0:T(8,128)S(1)}, f32[1,64,128]{2,1,0:T(8,128)S(1)}, u32[]{:S(2)}, u32[]{:S(2)}) %collective-permute-start.19) | collective-permute-done | bytes 32800 | tf_op jit(solution)/shard_map/ppermute | solution.py:319
  71.7 0.7 collective-permute-start.37
  72.5 1.5 %collective-permute-start.38 = (f32[2,64,128]{2,1,0:T(8,128)S(1)}, f32[2,64,128]{2,1,0:T(8,128)S(1)}, u32[]{:S(2)}, u32[]{:S(2)}) collective-permute-start(f32[2,64,128]{2,1,0:T(8,128)S(1)} %get-tuple-element.115), channel_id=1, source_target_pairs={{0,5},{1,4},{2,7},{3,6},{4,1},{5,0},{6,3},{7,2},{8,13},{9,12},{10,... | collective-permute-start | bytes 196616 | tf_op jit(solution)/shard_map/ppermute | solution.py:319
  74.0 0.6 collective-permute-start.39
  74.6 1.5 %collective-permute-start.40 = (f32[2,64,128]{2,1,0:T(8,128)S(1)}, f32[2,64,128]{2,1,0:T(8,128)S(1)}, u32[]{:S(2)}, u32[]{:S(2)}) collective-permute-start(f32[2,64,128]{2,1,0:T(8,128)S(1)} %get-tuple-element.117), channel_id=1, source_target_pairs={{0,3},{1,2},{2,1},{3,0},{4,7},{5,6},{6,5},{7,4},{8,11},{9,10},{10,... | collective-permute-start | bytes 196616 | tf_op jit(solution)/shard_map/ppermute | solution.py:319
  76.2 1.2 %shard_map.127 = (f32[6,64,512]{2,1,0:T(8,128)}, f32[1,64,128]{2,1,0:T(8,128)S(1)}, f32[1,64,128]{2,1,0:T(8,128)S(1)}, f32[1,64,128]{2,1,0:T(8,128)S(1)}, f32[1,...) custom-call(s32[8,512]{1,0:T(8,128)S(1)} %get-tuple-element.61.info_, ...), custom_call_target="tpu_custom_call", output_to_operand_aliasing={{0}: (9, {})} | custom-call | flops 10000000000 | bytes 10000000 | tf_op jit(solution)/shard_map/pallas_call | solution.py:413
  77.6 3.7 %collective-permute-start.29 = (f32[1,64,128]{2,1,0:T(8,128)S(1)}, f32[1,64,128]{2,1,0:T(8,128)S(1)}, u32[]{:S(2)}, u32[]{:S(2)}) collective-permute-start(f32[1,64,128]{2,1,0:T(8,128)S(1)} %get-tuple-element.104), channel_id=1, source_target_pairs={{0,6},{1,7},{2,4},{3,5},{4,2},{5,3},{6,0},{7,1},{8,14},{9,15},{10,... | collective-permute-start | bytes 98312 | tf_op jit(solution)/shard_map/ppermute | solution.py:319
  81.3 0.8 collective-permute-start.30
  82.1 2.7 %collective-permute-start.32 = (f32[1,64,128]{2,1,0:T(8,128)S(1)}, f32[1,64,128]{2,1,0:T(8,128)S(1)}, u32[]{:S(2)}, u32[]{:S(2)}) collective-permute-start(f32[1,64,128]{2,1,0:T(8,128)S(1)} %get-tuple-element.107), channel_id=1, source_target_pairs={{0,5},{1,4},{2,7},{3,6},{4,1},{5,0},{6,3},{7,2},{8,13},{9,12},{10,... | collective-permute-start | bytes 98312 | tf_op jit(solution)/shard_map/ppermute | solution.py:319
  84.8 0.7 collective-permute-start.33
  85.5 1.1 %shard_map.128.refs_8_ = f32[6,512,128]{2,1,0:T(8,128)} custom-call(s32[1]{0:T(128)} %bitcast.me_ref, s32[8,512]{1,0:T(8,128)S(1)} %get-tuple-element.61.info_ref, f32[2,512,128]{2,1,0:T(8,128)S(1)} %get-tuple-element.111.solved_ref, f32[2,64,128]{2,1,0:T(8,128)S(1)} %get-tuple-element.112.refs_0_, ...), custom_call_target="tpu_custom_call" | custom-call | flops 1000000000 | bytes 1000000 | tf_op jit(solution)/shard_map/pallas_call | solution.py:431
  86.7 1.0 %collective-permute-start.34 = (f32[1,64,128]{2,1,0:T(8,128)S(1)}, f32[1,64,128]{2,1,0:T(8,128)S(1)}, u32[]{:S(2)}, u32[]{:S(2)}) collective-permute-start(f32[1,64,128]{2,1,0:T(8,128)S(1)} %get-tuple-element.109), channel_id=1, source_target_pairs={{0,3},{1,2},{2,1},{3,0},{4,7},{5,6},{6,5},{7,4},{8,11},{9,10},{10,... | collective-permute-start | bytes 98312 | tf_op jit(solution)/shard_map/ppermute | solution.py:319
  87.7 0.4 collective-permute-start.35
  88.4 2.8 %collective-permute-start.44 = (f32[3,64]{1,0:T(4,128)S(1)}, f32[3,64]{1,0:T(4,128)S(1)}, u32[]{:S(2)}, u32[]{:S(2)}) collective-permute-start(f32[3,64]{1,0:T(4,128)S(1)} %shard_map.130), channel_id=1, source_target_pairs={{0,24},{8,16},{16,8},{24,0},{1,25},{9,17},{17,9},{25,1},{2,26},{10... | collective-permute-start | bytes 2312 | tf_op jit(solution)/shard_map/ppermute | solution.py:327
  91.5 0.5 collective-permute-start.42
  92.0 0.9 shard_map.129
  93.0 1.8 %collective-permute-done.43 = f32[3,64]{1,0:T(4,128)S(1)} collective-permute-done((f32[3,64]{1,0:T(4,128)S(1)}, f32[3,64]{1,0:T(4,128)S(1)}, u32[]{:S(2)}, u32[]{:S(2)}) %collective-permute-start.43) | collective-permute-done | bytes 800 | tf_op jit(solution)/shard_map/ppermute | solution.py:327
  95.0 0.6 add_add_fusion
  (67 shorter events, 1.9 us)
Async XLA Ops:
  0.6 12.4 %copy-start = (f32[512,512]{1,0:T(8,128)S(1)}, f32[512,512]{1,0:T(8,128)}, u32[]{:S(2)}) copy-start(f32[512,512]{1,0:T(8,128)} %deriv_ref.1) | copy-start | bytes 3145732
  0.6 12.4 %copy-start.1 = (f32[512,512]{1,0:T(8,128)S(1)}, f32[512,512]{1,0:T(8,128)}, u32[]{:S(2)}) copy-start(f32[512,512]{1,0:T(8,128)} %inverse_ref.1) | copy-start | bytes 3145732
  0.7 12.4 %copy-start.2 = (f32[512,512]{1,0:T(8,128)S(1)}, f32[512,512]{1,0:T(8,128)}, u32[]{:S(2)}) copy-start(f32[512,512]{1,0:T(8,128)} %basis_ref.1) | copy-start | bytes 3145732
  3.5 19.7 %collective-permute-start = (f32[2,2,64,128]{3,2,1,0:T(8,128)S(1)}, f32[2,2,64,128]{3,2,1,0:T(8,128)S(1)}, u32[]{:S(2)}, u32[]{:S(2)}) collective-permute-start(f32[2,2,64,128]{3,2,1,0:T(8,128)S(1)} %get-tuple-element.67), channel_id=1, source_target_pairs={{0,4},{1,5},{2,6},{3,7},{4,0},{5,1},{6,2},{7,3},{8,12},{9,13},{10,... | collective-permute-start | bytes 393224 | tf_op jit(solution)/shard_map/ppermute | solution.py:319
  7.6 15.6 %collective-permute-start.8 = (f32[2,2,64,128]{3,2,1,0:T(8,128)S(1)}, f32[2,2,64,128]{3,2,1,0:T(8,128)S(1)}, u32[]{:S(2)}, u32[]{:S(2)}) collective-permute-start(f32[2,2,64,128]{3,2,1,0:T(8,128)S(1)} %get-tuple-element.77), channel_id=1, source_target_pairs={{0,6},{1,7},{2,4},{3,5},{4,2},{5,3},{6,0},{7,1},{8,14},{9,15},{10,... | collective-permute-start | bytes 393224 | tf_op jit(solution)/shard_map/ppermute | solution.py:319
  8.9 16.3 %collective-permute-start.9 = (f32[2,2,64,128]{3,2,1,0:T(8,128)S(1)}, f32[2,2,64,128]{3,2,1,0:T(8,128)S(1)}, u32[]{:S(2)}, u32[]{:S(2)}) collective-permute-start(f32[2,2,64,128]{3,2,1,0:T(8,128)S(1)} %get-tuple-element.78), channel_id=1, source_target_pairs={{0,7},{1,6},{2,5},{3,4},{4,3},{5,2},{6,1},{7,0},{8,15},{9,14},{10,... | collective-permute-start | bytes 393224 | tf_op jit(solution)/shard_map/ppermute | solution.py:319
  10.3 19.7 %collective-permute-start.10 = (f32[2,2,64,128]{3,2,1,0:T(8,128)S(1)}, f32[2,2,64,128]{3,2,1,0:T(8,128)S(1)}, u32[]{:S(2)}, u32[]{:S(2)}) collective-permute-start(f32[2,2,64,128]{3,2,1,0:T(8,128)S(1)} %get-tuple-element.79), channel_id=1, source_target_pairs={{0,5},{1,4},{2,7},{3,6},{4,1},{5,0},{6,3},{7,2},{8,13},{9,12},{10,... | collective-permute-start | bytes 393224 | tf_op jit(solution)/shard_map/ppermute | solution.py:319
  10.4 25.0 %collective-permute-start.11 = (f32[2,2,64,128]{3,2,1,0:T(8,128)S(1)}, f32[2,2,64,128]{3,2,1,0:T(8,128)S(1)}, u32[]{:S(2)}, u32[]{:S(2)}) collective-permute-start(f32[2,2,64,128]{3,2,1,0:T(8,128)S(1)} %get-tuple-element.80), channel_id=1, source_target_pairs={{0,2},{1,3},{2,0},{3,1},{4,6},{5,7},{6,4},{7,5},{8,10},{9,11},{10,... | collective-permute-start | bytes 393224 | tf_op jit(solution)/shard_map/ppermute | solution.py:319
  23.2 12.2 %collective-permute-start.12 = (f32[2,2,64,128]{3,2,1,0:T(8,128)S(1)}, f32[2,2,64,128]{3,2,1,0:T(8,128)S(1)}, u32[]{:S(2)}, u32[]{:S(2)}) collective-permute-start(f32[2,2,64,128]{3,2,1,0:T(8,128)S(1)} %get-tuple-element.81), channel_id=1, source_target_pairs={{0,3},{1,2},{2,1},{3,0},{4,7},{5,6},{6,5},{7,4},{8,11},{9,10},{10,... | collective-permute-start | bytes 393224 | tf_op jit(solution)/shard_map/ppermute | solution.py:319
  23.2 14.9 %collective-permute-start.13 = (f32[2,2,64,128]{3,2,1,0:T(8,128)S(1)}, f32[2,2,64,128]{3,2,1,0:T(8,128)S(1)}, u32[]{:S(2)}, u32[]{:S(2)}) collective-permute-start(f32[2,2,64,128]{3,2,1,0:T(8,128)S(1)} %get-tuple-element.82), channel_id=1, source_target_pairs={{0,1},{1,0},{2,3},{3,2},{4,5},{5,4},{6,7},{7,6},{8,9},{9,8},{10,11... | collective-permute-start | bytes 393224 | tf_op jit(solution)/shard_map/ppermute | solution.py:319
  25.2 15.3 %collective-permute-start.1 = (f32[2,1,64,128]{3,2,1,0:T(8,128)S(1)}, f32[2,1,64,128]{3,2,1,0:T(8,128)S(1)}, u32[]{:S(2)}, u32[]{:S(2)}) collective-permute-start(f32[2,1,64,128]{3,2,1,0:T(8,128)S(1)} %get-tuple-element.69), channel_id=1, source_target_pairs={{0,6},{1,7},{2,4},{3,5},{4,2},{5,3},{6,0},{7,1},{8,14},{9,15},{10,... | collective-permute-start | bytes 196616 | tf_op jit(solution)/shard_map/ppermute | solution.py:319
  30.0 12.3 %collective-permute-start.2 = (f32[2,1,64,128]{3,2,1,0:T(8,128)S(1)}, f32[2,1,64,128]{3,2,1,0:T(8,128)S(1)}, u32[]{:S(2)}, u32[]{:S(2)}) collective-permute-start(f32[2,1,64,128]{3,2,1,0:T(8,128)S(1)} %get-tuple-element.70), channel_id=1, source_target_pairs={{0,7},{1,6},{2,5},{3,4},{4,3},{5,2},{6,1},{7,0},{8,15},{9,14},{10,... | collective-permute-start | bytes 196616 | tf_op jit(solution)/shard_map/ppermute | solution.py:319
  35.4 7.3 %collective-permute-start.3 = (f32[2,1,64,128]{3,2,1,0:T(8,128)S(1)}, f32[2,1,64,128]{3,2,1,0:T(8,128)S(1)}, u32[]{:S(2)}, u32[]{:S(2)}) collective-permute-start(f32[2,1,64,128]{3,2,1,0:T(8,128)S(1)} %get-tuple-element.71), channel_id=1, source_target_pairs={{0,4},{1,5},{2,6},{3,7},{4,0},{5,1},{6,2},{7,3},{8,12},{9,13},{10,... | collective-permute-start | bytes 196616 | tf_op jit(solution)/shard_map/ppermute | solution.py:319
  35.4 10.2 %collective-permute-start.4 = (f32[2,1,64,128]{3,2,1,0:T(8,128)S(1)}, f32[2,1,64,128]{3,2,1,0:T(8,128)S(1)}, u32[]{:S(2)}, u32[]{:S(2)}) collective-permute-start(f32[2,1,64,128]{3,2,1,0:T(8,128)S(1)} %get-tuple-element.72), channel_id=1, source_target_pairs={{0,5},{1,4},{2,7},{3,6},{4,1},{5,0},{6,3},{7,2},{8,13},{9,12},{10,... | collective-permute-start | bytes 196616 | tf_op jit(solution)/shard_map/ppermute | solution.py:319
  38.1 7.8 %collective-permute-start.5 = (f32[2,1,64,128]{3,2,1,0:T(8,128)S(1)}, f32[2,1,64,128]{3,2,1,0:T(8,128)S(1)}, u32[]{:S(2)}, u32[]{:S(2)}) collective-permute-start(f32[2,1,64,128]{3,2,1,0:T(8,128)S(1)} %get-tuple-element.73), channel_id=1, source_target_pairs={{0,2},{1,3},{2,0},{3,1},{4,6},{5,7},{6,4},{7,5},{8,10},{9,11},{10,... | collective-permute-start | bytes 196616 | tf_op jit(solution)/shard_map/ppermute | solution.py:319
  40.5 5.9 %collective-permute-start.6 = (f32[2,1,64,128]{3,2,1,0:T(8,128)S(1)}, f32[2,1,64,128]{3,2,1,0:T(8,128)S(1)}, u32[]{:S(2)}, u32[]{:S(2)}) collective-permute-start(f32[2,1,64,128]{3,2,1,0:T(8,128)S(1)} %get-tuple-element.74), channel_id=1, source_target_pairs={{0,3},{1,2},{2,1},{3,0},{4,7},{5,6},{6,5},{7,4},{8,11},{9,10},{10,... | collective-permute-start | bytes 196616 | tf_op jit(solution)/shard_map/ppermute | solution.py:319
  42.3 6.7 %collective-permute-start.7 = (f32[2,1,64,128]{3,2,1,0:T(8,128)S(1)}, f32[2,1,64,128]{3,2,1,0:T(8,128)S(1)}, u32[]{:S(2)}, u32[]{:S(2)}) collective-permute-start(f32[2,1,64,128]{3,2,1,0:T(8,128)S(1)} %get-tuple-element.75), channel_id=1, source_target_pairs={{0,1},{1,0},{2,3},{3,2},{4,5},{5,4},{6,7},{7,6},{8,9},{9,8},{10,11... | collective-permute-start | bytes 196616 | tf_op jit(solution)/shard_map/ppermute | solution.py:319
  42.7 7.1 %collective-permute-start.14 = (f32[2,64,128]{2,1,0:T(8,128)S(1)}, f32[2,64,128]{2,1,0:T(8,128)S(1)}, u32[]{:S(2)}, u32[]{:S(2)}) collective-permute-start(f32[2,64,128]{2,1,0:T(8,128)S(1)} %get-tuple-element.83), channel_id=1, source_target_pairs={{0,6},{1,7},{2,4},{3,5},{4,2},{5,3},{6,0},{7,1},{8,14},{9,15},{10,... | collective-permute-start | bytes 196616 | tf_op jit(solution)/shard_map/ppermute | solution.py:319
  45.6 5.5 %collective-permute-start.22 = (f32[2,64,128]{2,1,0:T(8,128)S(1)}, f32[2,64,128]{2,1,0:T(8,128)S(1)}, u32[]{:S(2)}, u32[]{:S(2)}) collective-permute-start(f32[2,64,128]{2,1,0:T(8,128)S(1)} %get-tuple-element.93), channel_id=1, source_target_pairs={{0,7},{1,6},{2,5},{3,4},{4,3},{5,2},{6,1},{7,0},{8,15},{9,14},{10,... | collective-permute-start | bytes 196616 | tf_op jit(solution)/shard_map/ppermute | solution.py:319
  46.0 9.6 %collective-permute-start.23 = (f32[2,64,128]{2,1,0:T(8,128)S(1)}, f32[2,64,128]{2,1,0:T(8,128)S(1)}, u32[]{:S(2)}, u32[]{:S(2)}) collective-permute-start(f32[2,64,128]{2,1,0:T(8,128)S(1)} %get-tuple-element.94), channel_id=1, source_target_pairs={{0,4},{1,5},{2,6},{3,7},{4,0},{5,1},{6,2},{7,3},{8,12},{9,13},{10,... | collective-permute-start | bytes 196616 | tf_op jit(solution)/shard_map/ppermute | solution.py:319
  46.5 10.9 %collective-permute-start.24 = (f32[2,64,128]{2,1,0:T(8,128)S(1)}, f32[2,64,128]{2,1,0:T(8,128)S(1)}, u32[]{:S(2)}, u32[]{:S(2)}) collective-permute-start(f32[2,64,128]{2,1,0:T(8,128)S(1)} %get-tuple-element.95), channel_id=1, source_target_pairs={{0,5},{1,4},{2,7},{3,6},{4,1},{5,0},{6,3},{7,2},{8,13},{9,12},{10,... | collective-permute-start | bytes 196616 | tf_op jit(solution)/shard_map/ppermute | solution.py:319
  48.9 9.5 %collective-permute-start.25 = (f32[2,64,128]{2,1,0:T(8,128)S(1)}, f32[2,64,128]{2,1,0:T(8,128)S(1)}, u32[]{:S(2)}, u32[]{:S(2)}) collective-permute-start(f32[2,64,128]{2,1,0:T(8,128)S(1)} %get-tuple-element.96), channel_id=1, source_target_pairs={{0,2},{1,3},{2,0},{3,1},{4,6},{5,7},{6,4},{7,5},{8,10},{9,11},{10,... | collective-permute-start | bytes 196616 | tf_op jit(solution)/shard_map/ppermute | solution.py:319
  49.8 8.6 %collective-permute-start.26 = (f32[2,64,128]{2,1,0:T(8,128)S(1)}, f32[2,64,128]{2,1,0:T(8,128)S(1)}, u32[]{:S(2)}, u32[]{:S(2)}) collective-permute-start(f32[2,64,128]{2,1,0:T(8,128)S(1)} %get-tuple-element.97), channel_id=1, source_target_pairs={{0,3},{1,2},{2,1},{3,0},{4,7},{5,6},{6,5},{7,4},{8,11},{9,10},{10,... | collective-permute-start | bytes 196616 | tf_op jit(solution)/shard_map/ppermute | solution.py:319
  51.1 10.7 %collective-permute-start.27 = (f32[2,64,128]{2,1,0:T(8,128)S(1)}, f32[2,64,128]{2,1,0:T(8,128)S(1)}, u32[]{:S(2)}, u32[]{:S(2)}) collective-permute-start(f32[2,64,128]{2,1,0:T(8,128)S(1)} %get-tuple-element.98), channel_id=1, source_target_pairs={{0,1},{1,0},{2,3},{3,2},{4,5},{5,4},{6,7},{7,6},{8,9},{9,8},{10,11... | collective-permute-start | bytes 196616 | tf_op jit(solution)/shard_map/ppermute | solution.py:319
  55.6 9.5 %collective-permute-start.15 = (f32[1,64,128]{2,1,0:T(8,128)S(1)}, f32[1,64,128]{2,1,0:T(8,128)S(1)}, u32[]{:S(2)}, u32[]{:S(2)}) collective-permute-start(f32[1,64,128]{2,1,0:T(8,128)S(1)} %get-tuple-element.85), channel_id=1, source_target_pairs={{0,6},{1,7},{2,4},{3,5},{4,2},{5,3},{6,0},{7,1},{8,14},{9,15},{10,... | collective-permute-start | bytes 98312 | tf_op jit(solution)/shard_map/ppermute | solution.py:319
  57.3 8.8 %collective-permute-start.16 = (f32[1,64,128]{2,1,0:T(8,128)S(1)}, f32[1,64,128]{2,1,0:T(8,128)S(1)}, u32[]{:S(2)}, u32[]{:S(2)}) collective-permute-start(f32[1,64,128]{2,1,0:T(8,128)S(1)} %get-tuple-element.86), channel_id=1, source_target_pairs={{0,7},{1,6},{2,5},{3,4},{4,3},{5,2},{6,1},{7,0},{8,15},{9,14},{10,... | collective-permute-start | bytes 98312 | tf_op jit(solution)/shard_map/ppermute | solution.py:319
  58.4 7.7 %collective-permute-start.17 = (f32[1,64,128]{2,1,0:T(8,128)S(1)}, f32[1,64,128]{2,1,0:T(8,128)S(1)}, u32[]{:S(2)}, u32[]{:S(2)}) collective-permute-start(f32[1,64,128]{2,1,0:T(8,128)S(1)} %get-tuple-element.87), channel_id=1, source_target_pairs={{0,4},{1,5},{2,6},{3,7},{4,0},{5,1},{6,2},{7,3},{8,12},{9,13},{10,... | collective-permute-start | bytes 98312 | tf_op jit(solution)/shard_map/ppermute | solution.py:319
  58.4 10.2 %collective-permute-start.18 = (f32[1,64,128]{2,1,0:T(8,128)S(1)}, f32[1,64,128]{2,1,0:T(8,128)S(1)}, u32[]{:S(2)}, u32[]{:S(2)}) collective-permute-start(f32[1,64,128]{2,1,0:T(8,128)S(1)} %get-tuple-element.88), channel_id=1, source_target_pairs={{0,5},{1,4},{2,7},{3,6},{4,1},{5,0},{6,3},{7,2},{8,13},{9,12},{10,... | collective-permute-start | bytes 98312 | tf_op jit(solution)/shard_map/ppermute | solution.py:319
  63.3 11.3 %collective-permute-start.28 = (f32[2,64,128]{2,1,0:T(8,128)S(1)}, f32[2,64,128]{2,1,0:T(8,128)S(1)}, u32[]{:S(2)}, u32[]{:S(2)}) collective-permute-start(f32[2,64,128]{2,1,0:T(8,128)S(1)} %get-tuple-element.100), channel_id=1, source_target_pairs={{0,6},{1,7},{2,4},{3,5},{4,2},{5,3},{6,0},{7,1},{8,14},{9,15},{10,... | collective-permute-start | bytes 196616 | tf_op jit(solution)/shard_map/ppermute | solution.py:319
  65.1 11.0 %collective-permute-start.36 = (f32[2,64,128]{2,1,0:T(8,128)S(1)}, f32[2,64,128]{2,1,0:T(8,128)S(1)}, u32[]{:S(2)}, u32[]{:S(2)}) collective-permute-start(f32[2,64,128]{2,1,0:T(8,128)S(1)} %get-tuple-element.113), channel_id=1, source_target_pairs={{0,7},{1,6},{2,5},{3,4},{4,3},{5,2},{6,1},{7,0},{8,15},{9,14},{10,... | collective-permute-start | bytes 196616 | tf_op jit(solution)/shard_map/ppermute | solution.py:319
  66.1 5.5 %collective-permute-start.19 = (f32[1,64,128]{2,1,0:T(8,128)S(1)}, f32[1,64,128]{2,1,0:T(8,128)S(1)}, u32[]{:S(2)}, u32[]{:S(2)}) collective-permute-start(f32[1,64,128]{2,1,0:T(8,128)S(1)} %get-tuple-element.89), channel_id=1, source_target_pairs={{0,2},{1,3},{2,0},{3,1},{4,6},{5,7},{6,4},{7,5},{8,10},{9,11},{10,... | collective-permute-start | bytes 98312 | tf_op jit(solution)/shard_map/ppermute | solution.py:319
  66.2 6.4 %collective-permute-start.20 = (f32[1,64,128]{2,1,0:T(8,128)S(1)}, f32[1,64,128]{2,1,0:T(8,128)S(1)}, u32[]{:S(2)}, u32[]{:S(2)}) collective-permute-start(f32[1,64,128]{2,1,0:T(8,128)S(1)} %get-tuple-element.90), channel_id=1, source_target_pairs={{0,3},{1,2},{2,1},{3,0},{4,7},{5,6},{6,5},{7,4},{8,11},{9,10},{10,... | collective-permute-start | bytes 98312 | tf_op jit(solution)/shard_map/ppermute | solution.py:319
  68.6 5.4 %collective-permute-start.21 = (f32[1,64,128]{2,1,0:T(8,128)S(1)}, f32[1,64,128]{2,1,0:T(8,128)S(1)}, u32[]{:S(2)}, u32[]{:S(2)}) collective-permute-start(f32[1,64,128]{2,1,0:T(8,128)S(1)} %get-tuple-element.91), channel_id=1, source_target_pairs={{0,1},{1,0},{2,3},{3,2},{4,5},{5,4},{6,7},{7,6},{8,9},{9,8},{10,11... | collective-permute-start | bytes 98312 | tf_op jit(solution)/shard_map/ppermute | solution.py:319
  71.7 5.9 %collective-permute-start.37 = (f32[2,64,128]{2,1,0:T(8,128)S(1)}, f32[2,64,128]{2,1,0:T(8,128)S(1)}, u32[]{:S(2)}, u32[]{:S(2)}) collective-permute-start(f32[2,64,128]{2,1,0:T(8,128)S(1)} %get-tuple-element.114), channel_id=1, source_target_pairs={{0,4},{1,5},{2,6},{3,7},{4,0},{5,1},{6,2},{7,3},{8,12},{9,13},{10,... | collective-permute-start | bytes 196616 | tf_op jit(solution)/shard_map/ppermute | solution.py:319
  72.5 8.8 %collective-permute-start.38 = (f32[2,64,128]{2,1,0:T(8,128)S(1)}, f32[2,64,128]{2,1,0:T(8,128)S(1)}, u32[]{:S(2)}, u32[]{:S(2)}) collective-permute-start(f32[2,64,128]{2,1,0:T(8,128)S(1)} %get-tuple-element.115), channel_id=1, source_target_pairs={{0,5},{1,4},{2,7},{3,6},{4,1},{5,0},{6,3},{7,2},{8,13},{9,12},{10,... | collective-permute-start | bytes 196616 | tf_op jit(solution)/shard_map/ppermute | solution.py:319
  74.0 8.1 %collective-permute-start.39 = (f32[2,64,128]{2,1,0:T(8,128)S(1)}, f32[2,64,128]{2,1,0:T(8,128)S(1)}, u32[]{:S(2)}, u32[]{:S(2)}) collective-permute-start(f32[2,64,128]{2,1,0:T(8,128)S(1)} %get-tuple-element.116), channel_id=1, source_target_pairs={{0,2},{1,3},{2,0},{3,1},{4,6},{5,7},{6,4},{7,5},{8,10},{9,11},{10,... | collective-permute-start | bytes 196616 | tf_op jit(solution)/shard_map/ppermute | solution.py:319
  74.6 7.5 %collective-permute-start.40 = (f32[2,64,128]{2,1,0:T(8,128)S(1)}, f32[2,64,128]{2,1,0:T(8,128)S(1)}, u32[]{:S(2)}, u32[]{:S(2)}) collective-permute-start(f32[2,64,128]{2,1,0:T(8,128)S(1)} %get-tuple-element.117), channel_id=1, source_target_pairs={{0,3},{1,2},{2,1},{3,0},{4,7},{5,6},{6,5},{7,4},{8,11},{9,10},{10,... | collective-permute-start | bytes 196616 | tf_op jit(solution)/shard_map/ppermute | solution.py:319
  76.1 8.7 %collective-permute-start.41 = (f32[2,64,128]{2,1,0:T(8,128)S(1)}, f32[2,64,128]{2,1,0:T(8,128)S(1)}, u32[]{:S(2)}, u32[]{:S(2)}) collective-permute-start(f32[2,64,128]{2,1,0:T(8,128)S(1)} %get-tuple-element.118), channel_id=1, source_target_pairs={{0,1},{1,0},{2,3},{3,2},{4,5},{5,4},{6,7},{7,6},{8,9},{9,8},{10,11... | collective-permute-start | bytes 196616 | tf_op jit(solution)/shard_map/ppermute | solution.py:319
  77.6 9.1 %collective-permute-start.29 = (f32[1,64,128]{2,1,0:T(8,128)S(1)}, f32[1,64,128]{2,1,0:T(8,128)S(1)}, u32[]{:S(2)}, u32[]{:S(2)}) collective-permute-start(f32[1,64,128]{2,1,0:T(8,128)S(1)} %get-tuple-element.104), channel_id=1, source_target_pairs={{0,6},{1,7},{2,4},{3,5},{4,2},{5,3},{6,0},{7,1},{8,14},{9,15},{10,... | collective-permute-start | bytes 98312 | tf_op jit(solution)/shard_map/ppermute | solution.py:319
  81.3 6.4 %collective-permute-start.30 = (f32[1,64,128]{2,1,0:T(8,128)S(1)}, f32[1,64,128]{2,1,0:T(8,128)S(1)}, u32[]{:S(2)}, u32[]{:S(2)}) collective-permute-start(f32[1,64,128]{2,1,0:T(8,128)S(1)} %get-tuple-element.105), channel_id=1, source_target_pairs={{0,7},{1,6},{2,5},{3,4},{4,3},{5,2},{6,1},{7,0},{8,15},{9,14},{10,... | collective-permute-start | bytes 98312 | tf_op jit(solution)/shard_map/ppermute | solution.py:319
  82.1 6.3 %collective-permute-start.31 = (f32[1,64,128]{2,1,0:T(8,128)S(1)}, f32[1,64,128]{2,1,0:T(8,128)S(1)}, u32[]{:S(2)}, u32[]{:S(2)}) collective-permute-start(f32[1,64,128]{2,1,0:T(8,128)S(1)} %get-tuple-element.106), channel_id=1, source_target_pairs={{0,4},{1,5},{2,6},{3,7},{4,0},{5,1},{6,2},{7,3},{8,12},{9,13},{10,... | collective-permute-start | bytes 98312 | tf_op jit(solution)/shard_map/ppermute | solution.py:319
  82.1 9.1 %collective-permute-start.32 = (f32[1,64,128]{2,1,0:T(8,128)S(1)}, f32[1,64,128]{2,1,0:T(8,128)S(1)}, u32[]{:S(2)}, u32[]{:S(2)}) collective-permute-start(f32[1,64,128]{2,1,0:T(8,128)S(1)} %get-tuple-element.107), channel_id=1, source_target_pairs={{0,5},{1,4},{2,7},{3,6},{4,1},{5,0},{6,3},{7,2},{8,13},{9,12},{10,... | collective-permute-start | bytes 98312 | tf_op jit(solution)/shard_map/ppermute | solution.py:319
  84.8 6.7 %collective-permute-start.33 = (f32[1,64,128]{2,1,0:T(8,128)S(1)}, f32[1,64,128]{2,1,0:T(8,128)S(1)}, u32[]{:S(2)}, u32[]{:S(2)}) collective-permute-start(f32[1,64,128]{2,1,0:T(8,128)S(1)} %get-tuple-element.108), channel_id=1, source_target_pairs={{0,2},{1,3},{2,0},{3,1},{4,6},{5,7},{6,4},{7,5},{8,10},{9,11},{10,... | collective-permute-start | bytes 98312 | tf_op jit(solution)/shard_map/ppermute | solution.py:319
  86.7 5.3 %collective-permute-start.34 = (f32[1,64,128]{2,1,0:T(8,128)S(1)}, f32[1,64,128]{2,1,0:T(8,128)S(1)}, u32[]{:S(2)}, u32[]{:S(2)}) collective-permute-start(f32[1,64,128]{2,1,0:T(8,128)S(1)} %get-tuple-element.109), channel_id=1, source_target_pairs={{0,3},{1,2},{2,1},{3,0},{4,7},{5,6},{6,5},{7,4},{8,11},{9,10},{10,... | collective-permute-start | bytes 98312 | tf_op jit(solution)/shard_map/ppermute | solution.py:319
  87.7 4.3 %collective-permute-start.35 = (f32[1,64,128]{2,1,0:T(8,128)S(1)}, f32[1,64,128]{2,1,0:T(8,128)S(1)}, u32[]{:S(2)}, u32[]{:S(2)}) collective-permute-start(f32[1,64,128]{2,1,0:T(8,128)S(1)} %get-tuple-element.110), channel_id=1, source_target_pairs={{0,1},{1,0},{2,3},{3,2},{4,5},{5,4},{6,7},{7,6},{8,9},{9,8},{10,11... | collective-permute-start | bytes 98312 | tf_op jit(solution)/shard_map/ppermute | solution.py:319
  88.4 4.5 %collective-permute-start.44 = (f32[3,64]{1,0:T(4,128)S(1)}, f32[3,64]{1,0:T(4,128)S(1)}, u32[]{:S(2)}, u32[]{:S(2)}) collective-permute-start(f32[3,64]{1,0:T(4,128)S(1)} %shard_map.130), channel_id=1, source_target_pairs={{0,24},{8,16},{16,8},{24,0},{1,25},{9,17},{17,9},{25,1},{2,26},{10... | collective-permute-start | bytes 2312 | tf_op jit(solution)/shard_map/ppermute | solution.py:327
  91.2 3.6 %collective-permute-start.43 = (f32[3,64]{1,0:T(4,128)S(1)}, f32[3,64]{1,0:T(4,128)S(1)}, u32[]{:S(2)}, u32[]{:S(2)}) collective-permute-start(f32[3,64]{1,0:T(4,128)S(1)} %shard_map.130), channel_id=1, source_target_pairs={{0,16},{8,24},{16,0},{24,8},{1,17},{9,25},{17,1},{25,9},{2,18},{10... | collective-permute-start | bytes 2312 | tf_op jit(solution)/shard_map/ppermute | solution.py:327
  91.5 3.6 %collective-permute-start.42 = (f32[3,64]{1,0:T(4,128)S(1)}, f32[3,64]{1,0:T(4,128)S(1)}, u32[]{:S(2)}, u32[]{:S(2)}) collective-permute-start(f32[3,64]{1,0:T(4,128)S(1)} %shard_map.130), channel_id=1, source_target_pairs={{0,8},{8,0},{16,24},{24,16},{1,9},{9,1},{17,25},{25,17},{2,10},{10... | collective-permute-start | bytes 2312 | tf_op jit(solution)/shard_map/ppermute | solution.py:327
  (4 other events, 27.9 us)

commit v8 on v7

v8 whole, which is shorter than its diff:
```python
import functools

import jax
import jax.numpy as jnp
from jax import lax
from jax.experimental import pallas as pl
from jax.experimental.pallas import tpu as pltpu
from jax.sharding import PartitionSpec as P

KMAX = 2048
TIME_STEP = 2.0
RK_ALPHA = -3.0 / 40.0
RK_BETA = 5.0 / 24.0
RK_GAMMA = 5.0 / 12.0
RK_ZETA = -17.0 / 60.0
WAVE_SCALE = 8.0
VMEM_LIMIT = 24 * 1024 * 1024
PAIRS = 3
LANES = 128
HEAVY = 10

F32 = jnp.float32
BF16 = jnp.bfloat16


def call(body, out_shape, in_specs, out_specs, weight, scratch=(), aliases=None):
    return pl.pallas_call(
        body,
        out_shape=out_shape,
        in_specs=in_specs,
        out_specs=out_specs,
        scratch_shapes=list(scratch),
        input_output_aliases=aliases or {},
        cost_estimate=pl.CostEstimate(flops=weight * 10**9, bytes_accessed=weight * 10**6, transcendentals=0),
        compiler_params=pltpu.CompilerParams(vmem_limit_bytes=VMEM_LIMIT),
    )


LOCAL = pl.BlockSpec(memory_space=pltpu.VMEM)
SCALAR = pl.BlockSpec(memory_space=pltpu.SMEM)
FAR = pl.BlockSpec(memory_space=pltpu.HBM)
ANYWHERE = pl.BlockSpec(memory_space=pl.ANY)


def shaped(shape, dtype=F32):
    return jax.ShapeDtypeStruct(shape, dtype)


def three_parts(x):
    high = x.astype(BF16)
    rest = x - high.astype(F32)
    middle = rest.astype(BF16)
    low = (rest - middle.astype(F32)).astype(BF16)
    return jnp.concatenate([high, middle, low], axis=0)


def sum_parts(x):
    rows = x.shape[0] // 3
    return x[:rows] + x[rows : 2 * rows] + x[2 * rows :]


def two_parts(x):
    high = x.astype(BF16)
    low = (x - high.astype(F32)).astype(BF16)
    return high, low


def selector(places, rows):
    columns = places.shape[1]
    return (lax.broadcasted_iota(jnp.int32, (rows, columns), 0) == places).astype(F32).astype(BF16)


def wave_row(modes):
    wave_x = modes[0:1, :].astype(F32)
    wave_z = modes[1:2, :].astype(F32)
    return (wave_x * wave_x + wave_z * wave_z) * (WAVE_SCALE / (KMAX * KMAX))


NT = (((1,), (1,)), ((), ()))


def plan(devices, me, owner, modes):
    columns = owner.shape[1]
    share = columns // devices
    rows = -(-devices // 8) * 8
    owned = (lax.broadcasted_iota(jnp.int32, (rows, columns), 0) == owner).astype(F32)
    before = (
        lax.broadcasted_iota(jnp.int32, (LANES, LANES), 0) < lax.broadcasted_iota(jnp.int32, (LANES, LANES), 1)
    ).astype(F32)
    carry = jnp.zeros((rows, 1), F32)
    earlier = []
    for at in range(columns // LANES):
        block = owned[:, at * LANES : (at + 1) * LANES]
        earlier.append(jnp.dot(block, before, preferred_element_type=F32) + carry)
        carry = carry + jnp.sum(block, axis=1, keepdims=True)
    counts = carry
    rank = jnp.sum(owned * jnp.concatenate(earlier, axis=1), axis=0, keepdims=True)
    surplus = jnp.maximum(counts - share, 0.0)
    lower = (lax.broadcasted_iota(jnp.int32, (rows, columns), 0) < owner).astype(F32)
    number = jnp.sum(lower * surplus, axis=0, keepdims=True) + (rank - share)
    free = share - jnp.minimum(counts, share)
    start = jnp.zeros((1, 1), F32)
    solver = owner
    slot = rank
    beyond = rank >= share
    for device in range(devices):
        here = free[device : device + 1, :]
        inside = beyond & (number >= start) & (number < start + here)
        solver = jnp.where(inside, device, solver)
        slot = jnp.where(inside, share - here + number - start, slot)
        start = start + here
    place = (solver ^ me) * share + slot.astype(jnp.int32)
    extra = jnp.where(beyond, (owner ^ me) * share + rank.astype(jnp.int32) - share, -1)
    mine = jnp.sum((owner == me).astype(F32), axis=1, keepdims=True).astype(jnp.int32)
    info = jnp.concatenate(
        [place, extra, jnp.broadcast_to(mine, (1, columns)), jnp.zeros((5, columns), jnp.int32)], axis=0
    )
    wave = jnp.broadcast_to(wave_row(modes), (16, columns))
    picked = sum_parts(
        lax.dot_general(three_parts(wave), selector(place, share), NT, preferred_element_type=F32)
    )
    return info, jnp.concatenate([picked, picked], axis=1)[:8]


def pack(devices, wave, chosen, state, now, old, out_refs, pair):
    comps, points, columns = state.shape
    share = columns // devices
    wave = wave.reshape(1, 1, columns)
    forcing = RK_GAMMA * now + RK_ZETA * old
    local = state + TIME_STEP * (forcing - RK_ALPHA * (wave * state))
    rows = comps * points
    both = jnp.concatenate([state.reshape(rows, columns), local.reshape(rows, columns)], axis=0)
    placed = sum_parts(lax.dot_general(three_parts(both), chosen, NT, preferred_element_type=F32))
    for step, out in zip(steps_of(devices, points), out_refs):
        taken = placed[:, step * share : (step + 1) * share]
        for kind in range(2):
            real = 2 * kind * points
            imag = real + points
            out[kind, pair] = jnp.concatenate([taken[real : real + points], taken[imag : imag + points]], axis=1)


def first_kernel(
    devices, me_ref, owner_hbm, modes_hbm, state_hbm, now_hbm, old_hbm, info_ref, wave_ref, *refs
):
    out_refs, (owner_ref, modes_ref, state_ref, now_ref, old_ref, sems) = refs[:devices], refs[devices:]
    columns = owner_ref.shape[1]
    copies = [
        pltpu.make_async_copy(owner_hbm, owner_ref, sems.at[0]),
        pltpu.make_async_copy(modes_hbm, modes_ref, sems.at[1]),
    ]
    for pair in range(PAIRS):
        comps = slice(2 * pair, 2 * pair + 2)
        for at, (source, target) in enumerate(((state_hbm, state_ref), (now_hbm, now_ref), (old_hbm, old_ref))):
            copies.append(
                pltpu.make_async_copy(source.at[comps], target.at[comps], sems.at[2 + 3 * pair + at])
            )
    for copy in copies:
        copy.start()
    copies[0].wait()
    copies[1].wait()
    info, wave = plan(devices, me_ref[0], owner_ref[...], modes_ref[...])
    info_ref[...] = info
    wave_ref[...] = wave
    wave = wave_row(modes_ref[...])
    chosen = selector(info[0:1], columns)
    for pair in range(PAIRS):
        for copy in copies[2 + 3 * pair : 5 + 3 * pair]:
            copy.wait()
        comps = slice(2 * pair, 2 * pair + 2)
        pack(devices, wave, chosen, state_ref[comps], now_ref[comps], old_ref[comps], out_refs, pair)


def operators_kernel(
    deriv_ref, inverse_ref, basis_ref, values_ref, high_out, low_out, both_high_out, both_low_out, basis_out, values_out
):
    high, low = two_parts(inverse_ref[...])
    high_out[...] = high
    low_out[...] = low
    both = (TIME_STEP * RK_ALPHA) * apply(jnp.concatenate([high, high, low], axis=1), deriv_ref[...])
    high, low = two_parts(both)
    both_high_out[...] = high
    both_low_out[...] = low
    high, low = two_parts(basis_ref[...])
    basis_out[...] = jnp.concatenate([high, high, low], axis=1)
    lanes = values_out.shape[1]
    values_out[...] = jnp.transpose(jnp.broadcast_to(values_ref[...], (lanes, values_ref.shape[1])))


def apply(operator, x):
    high, low = two_parts(x)
    return jnp.dot(operator, jnp.concatenate([high, low, high], axis=0), preferred_element_type=F32)


def projected(me, operators, steps, blocks, state, local):
    _, pairs, points, lanes = blocks[0].shape
    fill = LANES // points
    for at, (step, block) in enumerate(zip(steps, blocks)):
        first = at // fill * LANES
        rows = pl.ds(pl.multiple_of(first + ((me ^ step) % fill) * points, points), points)
        for pair in range(pairs):
            state[rows, pair * lanes : (pair + 1) * lanes] = block[0, pair]
            local[rows, pair * lanes : (pair + 1) * lanes] = block[1, pair]
    high, low, both_high, both_low = operators
    matrix, values = [], []
    for first in range(0, len(steps), fill):
        depth = pl.ds(pl.multiple_of((me ^ steps[first]) // fill * LANES, LANES), LANES)
        rows = slice(first // fill * LANES, (first // fill + 1) * LANES)
        for upper, lower, x in ((high, low, local), (both_high, both_low, state)):
            x_high, x_low = two_parts(x[rows, :])
            matrix += [upper[:, depth], upper[:, depth], lower[:, depth]]
            values += [x_high, x_low, x_high]
    return jnp.dot(
        jnp.concatenate(matrix, axis=1), jnp.concatenate(values, axis=0), preferred_element_type=F32
    )


def solve_early_kernel(steps, me_ref, *refs):
    operators, in_refs, (out_ref, state, local) = refs[:4], refs[4:-3], refs[-3:]
    out_ref[...] = projected(me_ref[0], operators, steps, in_refs, state, local)


def solve_late_kernel(steps, order, me_ref, wave_ref, values_ref, basis_ref, early_ref, *refs):
    operators, refs = refs[:4], refs[4:]
    in_refs, refs = refs[: len(steps)], refs[len(steps) :]
    out_refs, (solved_ref, state, local, after) = refs[:-4], refs[-4:]
    me = me_ref[0]
    pairs, points, lanes = out_refs[0].shape
    project = early_ref[...] + projected(me, operators, steps, in_refs, state, local)
    damping = 1.0 + TIME_STEP * RK_BETA * (values_ref[...] + wave_ref[0:1, :])
    project = project / jnp.concatenate([damping] * pairs, axis=1)
    after[...] = apply(basis_ref[...], project)
    for pair in range(pairs):
        solved_ref[pair] = after[:, pair * lanes : (pair + 1) * lanes]
    for step, block in zip(order, out_refs):
        rows = pl.ds(pl.multiple_of((me ^ step) * points, points), points)
        for pair in range(pairs):
            block[pair] = after[rows, pair * lanes : (pair + 1) * lanes]


def side_by_side(steps, blocks):
    pairs, _, lanes = blocks[0].shape
    share = lanes // 2
    sorted_blocks = [blocks[steps.index(step)] for step in sorted(steps)]
    rows = []
    for pair in range(pairs):
        for half in range(2):
            rows.append(
                jnp.concatenate(
                    [block[pair][:, half * share : (half + 1) * share] for block in sorted_blocks], axis=1
                )
            )
    return jnp.concatenate(rows, axis=0)


def surplus_early_kernel(steps, info_ref, *refs):
    in_refs, (out_ref, late_ref) = refs[:-2], refs[-2:]
    columns = info_ref.shape[1]
    share = in_refs[0].shape[2] // 2
    chosen = lax.dot_general(
        selector(info_ref[0:1, :], columns), selector(info_ref[1:2, :], columns), NT, preferred_element_type=F32
    ).astype(BF16)
    devices = columns // share
    late = [step for step in range(devices) if step not in steps]
    first, last = late[0] * share, (late[-1] + 1) * share
    late_ref[...] = chosen[first:last]
    kept = jnp.concatenate([chosen[:first], chosen[last:]], axis=0)
    out_ref[...] = sum_parts(
        jnp.dot(three_parts(side_by_side(steps, in_refs)), kept, preferred_element_type=F32)
    )


def surplus_late_kernel(steps, order, early_ref, chosen_ref, *refs):
    in_refs, out_refs = refs[: len(steps)], refs[len(steps) :]
    pairs, points, lanes = in_refs[0].shape
    share = lanes // 2
    extra = early_ref[...] + sum_parts(
        jnp.dot(three_parts(side_by_side(steps, in_refs)), chosen_ref[...], preferred_element_type=F32)
    )
    for step, out in zip(order, out_refs):
        taken = extra[:, step * share : (step + 1) * share]
        for pair in range(pairs):
            real = 2 * pair * points
            imag = real + points
            out[pair] = jnp.concatenate([taken[real : real + points], taken[imag : imag + points]], axis=1)


def state_kernel(order, info_ref, modes_ref, velocity_ref, *refs):
    in_refs, (_, state_hbm, emf_ref, state_ref, sem) = refs[: len(order)], refs[len(order) :]
    comps, points, columns = state_ref.shape
    state = sum_parts(
        jnp.dot(
            three_parts(side_by_side(order, in_refs)),
            selector(info_ref[0:1, :], columns),
            preferred_element_type=F32,
        )
    )
    state_ref[...] = state.reshape(comps, points, columns)
    copy = pltpu.make_async_copy(state_ref, state_hbm, sem)
    copy.start()
    emf_ref[...] = emf_of(modes_ref[...], velocity_ref, state_ref)
    copy.wait()


def emf_of(modes, velocity_ref, state_ref):
    _, points, columns = state_ref.shape
    weight = jnp.where(modes[0:1, :] > 0, 2.0, 1.0).astype(F32)
    totals = [jnp.zeros((points, columns), F32)] * 3
    for field in range(3):
        real = weight * state_ref[2 * field]
        imag = weight * state_ref[2 * field + 1]
        for sign, i, j in ((1.0, (field + 1) % 3, (field + 2) % 3), (-1.0, (field + 2) % 3, (field + 1) % 3)):
            totals[i] = totals[i] + sign * (velocity_ref[2 * j] * real + velocity_ref[2 * j + 1] * imag)
    rows = []
    for total in totals:
        folded = total[:, :LANES]
        for at in range(1, columns // LANES):
            folded = folded + total[:, at * LANES : (at + 1) * LANES]
        rows.append(jnp.sum(jnp.transpose(folded), axis=0, keepdims=True))
    return jnp.concatenate(rows, axis=0)


def assemble(me, steps, used, solved_ref, in_refs, out_hbm, rows_ref, sems):
    pairs, points, lanes = in_refs[0].shape
    share = lanes // 2
    fill = LANES // points
    copies = []
    for first in range(0, len(steps), fill):
        depth = pl.ds(pl.multiple_of((me ^ steps[first]) // fill * LANES, LANES), LANES)
        rows = slice(first // fill * LANES, (first // fill + 1) * LANES)
        for pair in range(pairs):
            solved = solved_ref[pair, depth, :]
            for half in range(2):
                comp = 2 * pair + half
                kept = solved[:, half * share : (half + 1) * share]
                rows_ref[comp, rows, :share] = jnp.where(used < 0, 0.0, kept)
                for at in range(first, first + fill):
                    place = pl.ds(
                        pl.multiple_of(first // fill * LANES + ((me ^ steps[at]) % fill) * points, points), points
                    )
                    rows_ref[comp, place, share:] = in_refs[at][pair][:, half * share : (half + 1) * share]
                copies.append(
                    pltpu.make_async_copy(
                        rows_ref.at[comp, rows], out_hbm.at[comp, depth], sems.at[first // fill * 2 * pairs + comp]
                    )
                )
                copies[-1].start()
    for copy in copies:
        copy.wait()


def unused(info_ref, share):
    lane = lax.broadcasted_iota(jnp.int32, (LANES, share), 1)
    return jnp.where(lane < info_ref[2:3, :share], 0, -1)


def assemble_early_kernel(steps, me_ref, info_ref, solved_ref, *refs):
    in_refs, (out_hbm, rows_ref, sems) = refs[: len(steps)], refs[len(steps) :]
    share = in_refs[0].shape[2] // 2
    assemble(me_ref[0], steps, unused(info_ref, share), solved_ref, in_refs, out_hbm, rows_ref, sems)


def assemble_late_kernel(steps, terms, me_ref, info_ref, solved_ref, *refs):
    in_refs, refs = refs[: len(steps)], refs[len(steps) :]
    parts, (_, out_hbm, emf_ref, rows_ref, sems) = refs[:terms], refs[terms:]
    parts = [ref[...] for ref in parts]
    while len(parts) > 1:
        parts = [parts[at] + parts[at + 1] for at in range(0, len(parts), 2)]
    emf_ref[...] = parts[0]
    share = in_refs[0].shape[2] // 2
    assemble(me_ref[0], steps, unused(info_ref, share), solved_ref, in_refs, out_hbm, rows_ref, sems)


def late_steps(devices, points):
    return list(range(devices // 2, devices // 2 + LANES // points))


def early_steps(devices, points):
    half = devices // 2
    return list(range(half + LANES // points, devices)) + list(range(half))


def steps_of(devices, points):
    return early_steps(devices, points) + late_steps(devices, points)


def exchange(blocks, steps):
    devices = len(blocks)
    return [
        block if step == 0 else lax.ppermute(block, "col", [(i, i ^ step) for i in range(devices)])
        for step, block in zip(steps, blocks)
    ]


def from_groups(value):
    groups = lax.axis_size("grp")
    return [value] + [
        lax.ppermute(value, "grp", [(i, i ^ step) for i in range(groups)]) for step in range(1, groups)
    ]


def on_device(
    state_now,
    force_now,
    force_old,
    velocity,
    second_deriv,
    eig_basis,
    eig_inverse,
    eig_values,
    kept_modes,
    col_owner,
):
    comps, points, columns = state_now.shape
    devices = lax.axis_size("col")
    depth = devices * points
    share = columns // devices
    lanes = 2 * share
    width = PAIRS * lanes
    steps = steps_of(devices, points)
    early, late = early_steps(devices, points), late_steps(devices, points)
    split = len(early)
    early_rows, late_rows = split * points, len(late) * points
    back = [shaped((PAIRS, points, lanes))] * devices
    me = lax.axis_index("col").astype(jnp.int32).reshape(1)
    far = [
        pltpu.with_memory_space_constraint(array, pltpu.HBM)
        for array in (col_owner.reshape(1, columns), kept_modes, state_now, force_now, force_old)
    ]

    outs = call(
        functools.partial(first_kernel, devices),
        [shaped((8, columns), jnp.int32), shaped((8, lanes))] + [shaped((2, PAIRS, points, lanes))] * devices,
        [SCALAR] + [FAR] * 5,
        [LOCAL] * (2 + devices),
        1,
        [pltpu.VMEM((1, columns), jnp.int32), pltpu.VMEM((2, columns), jnp.int32)]
        + [pltpu.VMEM((comps, points, columns), F32)] * 3
        + [pltpu.SemaphoreType.DMA((2 + 3 * PAIRS,))],
    )(me, *far)
    info, wave = outs[:2]
    forward = exchange(outs[2:], steps)

    square = shaped((depth, depth), BF16)
    operators = call(
        operators_kernel,
        [square] * 4 + [shaped((depth, 3 * depth), BF16), shaped((depth, lanes))],
        [LOCAL] * 4,
        [LOCAL] * 6,
        HEAVY,
    )(second_deriv, eig_inverse, eig_basis, eig_values.reshape(1, depth))
    basis, values = operators[4:]

    begun = call(
        functools.partial(solve_early_kernel, early),
        shaped((depth, width)),
        [SCALAR] + [LOCAL] * (4 + split),
        LOCAL,
        HEAVY,
        [pltpu.VMEM((early_rows, width), F32)] * 2,
    )(me, *operators[:4], *forward[:split])
    outs = call(
        functools.partial(solve_late_kernel, late, steps),
        back + [shaped((PAIRS, depth, lanes))],
        [SCALAR] + [LOCAL] * (8 + len(late)),
        [LOCAL] * (devices + 1),
        1,
        [pltpu.VMEM((late_rows, width), F32)] * 2 + [pltpu.VMEM((depth, width), F32)],
    )(me, wave, values, basis, begun, *operators[:4], *forward[split:])
    solved = outs[devices]
    returned = exchange(outs[:devices], steps)

    begun, chosen = call(
        functools.partial(surplus_early_kernel, early),
        [shaped((comps * points, columns)), shaped((len(late) * share, columns), BF16)],
        [LOCAL] * (1 + split),
        [LOCAL] * 2,
        HEAVY,
    )(info, *returned[:split])
    outs = call(
        functools.partial(surplus_late_kernel, late, steps),
        back,
        [LOCAL] * (2 + len(late)),
        [LOCAL] * devices,
        1,
    )(begun, chosen, *returned[split:])
    extra = exchange(outs, steps)

    state_next, emf = call(
        functools.partial(state_kernel, steps),
        [shaped(state_now.shape), shaped((3, points))],
        [LOCAL] * (3 + devices) + [ANYWHERE],
        [FAR, LOCAL],
        HEAVY,
        [pltpu.VMEM(state_now.shape, F32), pltpu.SemaphoreType.DMA],
    )(info, kept_modes, velocity, *returned, extra[split])
    terms = from_groups(emf)

    owned = call(
        functools.partial(assemble_early_kernel, early),
        shaped((comps, depth, lanes)),
        [SCALAR] + [LOCAL] * (2 + split),
        FAR,
        HEAVY,
        [
            pltpu.VMEM((comps, early_rows, lanes), F32),
            pltpu.SemaphoreType.DMA((comps * early_rows // LANES,)),
        ],
    )(me, info, solved, *extra[:split])
    owned, mean_emf = call(
        functools.partial(assemble_late_kernel, late, len(terms)),
        [shaped((comps, depth, lanes)), shaped((3, points))],
        [SCALAR] + [LOCAL] * (2 + len(late) + len(terms)) + [FAR],
        [FAR, LOCAL],
        1,
        [pltpu.VMEM((comps, late_rows, lanes), F32), pltpu.SemaphoreType.DMA((comps,))],
        aliases={3 + len(late) + len(terms): 0},
    )(me, info, solved, *extra[split:], *terms, owned)
    return (state_next, owned, mean_emf)


def solution(mesh):
    return jax.shard_map(
        on_device,
        mesh=mesh,
        in_specs=(
            P(None, "col", "grp"),
            P(None, "col", "grp"),
            P(None, "col", "grp"),
            P(None, "col", "grp"),
            P(),
            P(),
            P(),
            P(),
            P(None, "grp"),
            P("grp", None),
        ),
        out_specs=(P(None, "col", "grp"), P(None, None, ("grp", "col")), P(None, "col")),
        check_vma=False,
    )
```

time: 95.8 us -> 88.1 us (0.920)
  starting transfers between devices: 58.8 us -> 41.5 us
  waiting for transfers between devices: 20 us -> 31.2 us
  Pallas kernels: 15.4 us -> 14.4 us
    ppermute x42 -> x21, starting transfers between devices: 55.3 us -> 38 us  [exchange(): lax.ppermute(block, 'col', [(i, i ^ step) for i in range(devices)])]
    ppermute x42 -> x21, waiting for transfers between devices: 17.9 us -> 30.3 us  [exchange(): lax.ppermute(block, 'col', [(i, i ^ step) for i in range(devices)])]
    pallas_call x9 -> x8, Pallas kernels: 12.6 us -> 10.7 us  [the longest x1 1.83 us: on_device(): call(functools.partial(state_kernel, steps), [shaped(state_now.shape), sh...]
    ppermute x3, waiting for transfers between devices: 2.09 us -> 0.88 us  [from_groups(): lax.ppermute(value, 'grp', [(i, i ^ step) for i in range(groups)])]
  transfers between devices with their start and end apart: 45 -> 24, of which waited for: 10 -> 11; matrix products, arithmetic and copies ran while one was open for 0% -> 0% of each run, Pallas kernels for 13% -> 8%
where the time goes in v8:
time: 88.1 us; the launch traced here: 87.9 us
  starting transfers between devices  41.5 us (47%)
  waiting for transfers between devices  31.2 us (35%)
  Pallas kernels  14.4 us (16%)
    ppermute x21, starting transfers between devices, exchange(): lax.ppermute(block, 'col', [(i, i ^ step) for i in range(devices)])  38 us
    ppermute x21, waiting for transfers between devices, exchange(): lax.ppermute(block, 'col', [(i, i ^ step) for i in range(devices)])  30.3 us
    pallas_call x1, Pallas kernels, on_device(): call(functools.partial(first_kernel, devices), [shaped((8, columns), jnp....  3.76 us
    ppermute x3, starting transfers between devices, from_groups(): lax.ppermute(value, 'grp', [(i, i ^ step) for i in range(groups)])  3.49 us
    pallas_call x1, Pallas kernels, on_device(): call(functools.partial(state_kernel, steps), [shaped(state_now.shape), sh...  1.83 us
  transfers between devices with their start and end apart: 24, of which 11 were waited for; matrix products, arithmetic and copies ran while one was open for 0% of the time, Pallas kernels for 8%

profile of v8, /device:TPU:0, one launch (start us, length us, event | category | flops | bytes accessed | tf_op | source)
XLA Modules:
  0.0 87.9 jit_solution(12602568279490198677)
XLA Ops:
  0.7 3.8 %shard_map.121 = (s32[8,512]{1,0:T(8,128)S(1)}, f32[8,128]{1,0:T(8,128)S(1)}, f32[2,3,64,128]{3,2,1,0:T(8,128)S(1)}, f32[2,3,64,128]{3,2,1,0:T(8,128)S(1)}, f32[...) custom-call(s32[1]{0:T(128)} %bitcast.me_ref, ...), custom_call_target="tpu_custom_call" | custom-call | flops 1000000000 | bytes 1000000 | tf_op jit(solution)/shard_map/pallas_call | solution.py:430
  4.4 5.1 %collective-permute-start = (f32[2,3,64,128]{3,2,1,0:T(8,128)S(1)}, f32[2,3,64,128]{3,2,1,0:T(8,128)S(1)}, u32[]{:S(2)}, u32[]{:S(2)}) collective-permute-start(f32[2,3,64,128]{3,2,1,0:T(8,128)S(1)} %get-tuple-element.50), channel_id=1, source_target_pairs={{0,6},{1,7},{2,4},{3,5},{4,2},{5,3},{6,0},{7,1},{8,14},{9,15},{10,... | collective-permute-start | bytes 589832 | tf_op jit(solution)/shard_map/ppermute | solution.py:389
  9.6 0.0 collective-permute-start.1
  9.6 0.2 collective-permute-start.2
  9.8 0.0 collective-permute-start.3
  9.8 1.7 %collective-permute-start.4 = (f32[2,3,64,128]{3,2,1,0:T(8,128)S(1)}, f32[2,3,64,128]{3,2,1,0:T(8,128)S(1)}, u32[]{:S(2)}, u32[]{:S(2)}) collective-permute-start(f32[2,3,64,128]{3,2,1,0:T(8,128)S(1)} %get-tuple-element.55), channel_id=1, source_target_pairs={{0,3},{1,2},{2,1},{3,0},{4,7},{5,6},{6,5},{7,4},{8,11},{9,10},{10,... | collective-permute-start | bytes 589832 | tf_op jit(solution)/shard_map/ppermute | solution.py:389
  11.4 1.4 %shard_map.122 = (bf16[512,512]{1,0:T(8,128)(2,1)S(1)}, bf16[512,512]{1,0:T(8,128)(2,1)S(1)}, bf16[512,512]{1,0:T(8,128)(2,1)S(1)}, bf16[512,512]{1,0:T(8,128)(2...) custom-call(f32[512,512]{1,0:T(8,128)S(1)} %copy-done, f32[512,512]{1,0:T(8,128)S(1)} %copy-done.1, ...), custom_call_target="tpu_custom_call" | custom-call | flops 10000000000 | bytes 10000000 | tf_op jit(solution)/shard_map/pallas_call | solution.py:444
  12.8 2.1 %collective-permute-done.refs_4_ = f32[2,3,64,128]{3,2,1,0:T(8,128)S(1)} collective-permute-done((f32[2,3,64,128]{3,2,1,0:T(8,128)S(1)}, f32[2,3,64,128]{3,2,1,0:T(8,128)S(1)}, u32[]{:S(2)}, u32[]{:S(2)}) %collective-permute-start) | collective-permute-done | bytes 196640 | tf_op jit(solution)/shard_map/ppermute | solution.py:389
  14.9 9.8 %collective-permute-start.5 = (f32[2,3,64,128]{3,2,1,0:T(8,128)S(1)}, f32[2,3,64,128]{3,2,1,0:T(8,128)S(1)}, u32[]{:S(2)}, u32[]{:S(2)}) collective-permute-start(f32[2,3,64,128]{3,2,1,0:T(8,128)S(1)} %get-tuple-element.56), channel_id=1, source_target_pairs={{0,4},{1,5},{2,6},{3,7},{4,0},{5,1},{6,2},{7,3},{8,12},{9,13},{10,... | collective-permute-start | bytes 589832 | tf_op jit(solution)/shard_map/ppermute | solution.py:389
  24.8 0.0 collective-permute-done.1.refs_5_
  24.8 3.9 %collective-permute-start.6 = (f32[2,3,64,128]{3,2,1,0:T(8,128)S(1)}, f32[2,3,64,128]{3,2,1,0:T(8,128)S(1)}, u32[]{:S(2)}, u32[]{:S(2)}) collective-permute-start(f32[2,3,64,128]{3,2,1,0:T(8,128)S(1)} %get-tuple-element.57), channel_id=1, source_target_pairs={{0,5},{1,4},{2,7},{3,6},{4,1},{5,0},{6,3},{7,2},{8,13},{9,12},{10,... | collective-permute-start | bytes 589832 | tf_op jit(solution)/shard_map/ppermute | solution.py:389
  28.7 0.0 collective-permute-done.4.refs_9_
  28.7 1.4 %shard_map.123.early_ref = f32[512,384]{1,0:T(8,128)S(1)} custom-call(s32[1]{0:T(128)} %bitcast.me_ref, bf16[512,512]{1,0:T(8,128)(2,1)S(1)} %get-tuple-element.46.refs_0_, bf16[512,512]{1,0:T(8,128)(2,1)S(1)} %get-tuple-element.47.refs_1_, bf16[512,512]{1,0:T(8,128)(2,1)S(1)} %get-tuple-element.48.refs_2_, bf16[512,512]{1,0:T(8,128)(2,1)S(1)} %get-tuple-element.49.refs_3_, ...), custom_call_target="tpu_custom_call" | custom-call | flops 10000000000 | bytes 10000000 | tf_op jit(solution)/shard_map/pallas_call | solution.py:453
  30.1 9.7 %collective-permute-done.5.refs_4_ = f32[2,3,64,128]{3,2,1,0:T(8,128)S(1)} collective-permute-done((f32[2,3,64,128]{3,2,1,0:T(8,128)S(1)}, f32[2,3,64,128]{3,2,1,0:T(8,128)S(1)}, u32[]{:S(2)}, u32[]{:S(2)}) %collective-permute-start.5) | collective-permute-done | bytes 196640 | tf_op jit(solution)/shard_map/ppermute | solution.py:389
  39.9 2.3 %collective-permute-done.6.refs_5_ = f32[2,3,64,128]{3,2,1,0:T(8,128)S(1)} collective-permute-done((f32[2,3,64,128]{3,2,1,0:T(8,128)S(1)}, f32[2,3,64,128]{3,2,1,0:T(8,128)S(1)}, u32[]{:S(2)}, u32[]{:S(2)}) %collective-permute-start.6) | collective-permute-done | bytes 196640 | tf_op jit(solution)/shard_map/ppermute | solution.py:389
  42.1 1.6 %shard_map.124 = (f32[3,64,128]{2,1,0:T(8,128)S(1)}, f32[3,64,128]{2,1,0:T(8,128)S(1)}, f32[3,64,128]{2,1,0:T(8,128)S(1)}, f32[3,64,128]{2,1,0:T(8,128)S(1)}, f3...) custom-call(s32[1]{0:T(128)} %bitcast.me_ref, ...), custom_call_target="tpu_custom_call" | custom-call | flops 1000000000 | bytes 1000000 | tf_op jit(solution)/shard_map/pallas_call | solution.py:461
  43.7 2.3 %collective-permute-start.7 = (f32[3,64,128]{2,1,0:T(8,128)S(1)}, f32[3,64,128]{2,1,0:T(8,128)S(1)}, u32[]{:S(2)}, u32[]{:S(2)}) collective-permute-start(f32[3,64,128]{2,1,0:T(8,128)S(1)} %get-tuple-element.58), channel_id=1, source_target_pairs={{0,6},{1,7},{2,4},{3,5},{4,2},{5,3},{6,0},{7,1},{8,14},{9,15},{10,... | collective-permute-start | bytes 294920 | tf_op jit(solution)/shard_map/ppermute | solution.py:389
  46.0 1.7 %collective-permute-start.8 = (f32[3,64,128]{2,1,0:T(8,128)S(1)}, f32[3,64,128]{2,1,0:T(8,128)S(1)}, u32[]{:S(2)}, u32[]{:S(2)}) collective-permute-start(f32[3,64,128]{2,1,0:T(8,128)S(1)} %get-tuple-element.59), channel_id=1, source_target_pairs={{0,7},{1,6},{2,5},{3,4},{4,3},{5,2},{6,1},{7,0},{8,15},{9,14},{10,... | collective-permute-start | bytes 294920 | tf_op jit(solution)/shard_map/ppermute | solution.py:389
  47.7 1.9 %collective-permute-start.11 = (f32[3,64,128]{2,1,0:T(8,128)S(1)}, f32[3,64,128]{2,1,0:T(8,128)S(1)}, u32[]{:S(2)}, u32[]{:S(2)}) collective-permute-start(f32[3,64,128]{2,1,0:T(8,128)S(1)} %get-tuple-element.63), channel_id=1, source_target_pairs={{0,3},{1,2},{2,1},{3,0},{4,7},{5,6},{6,5},{7,4},{8,11},{9,10},{10,... | collective-permute-start | bytes 294920 | tf_op jit(solution)/shard_map/ppermute | solution.py:389
  49.6 1.8 %collective-permute-done.7.refs_0_ = f32[3,64,128]{2,1,0:T(8,128)S(1)} collective-permute-done((f32[3,64,128]{2,1,0:T(8,128)S(1)}, f32[3,64,128]{2,1,0:T(8,128)S(1)}, u32[]{:S(2)}, u32[]{:S(2)}) %collective-permute-start.7) | collective-permute-done | bytes 98336 | tf_op jit(solution)/shard_map/ppermute | solution.py:389
  51.4 1.3 %collective-permute-start.12 = (f32[3,64,128]{2,1,0:T(8,128)S(1)}, f32[3,64,128]{2,1,0:T(8,128)S(1)}, u32[]{:S(2)}, u32[]{:S(2)}) collective-permute-start(f32[3,64,128]{2,1,0:T(8,128)S(1)} %get-tuple-element.64), channel_id=1, source_target_pairs={{0,4},{1,5},{2,6},{3,7},{4,0},{5,1},{6,2},{7,3},{8,12},{9,13},{10,... | collective-permute-start | bytes 294920 | tf_op jit(solution)/shard_map/ppermute | solution.py:389
  52.7 2.2 %collective-permute-start.13 = (f32[3,64,128]{2,1,0:T(8,128)S(1)}, f32[3,64,128]{2,1,0:T(8,128)S(1)}, u32[]{:S(2)}, u32[]{:S(2)}) collective-permute-start(f32[3,64,128]{2,1,0:T(8,128)S(1)} %get-tuple-element.65), channel_id=1, source_target_pairs={{0,5},{1,4},{2,7},{3,6},{4,1},{5,0},{6,3},{7,2},{8,13},{9,12},{10,... | collective-permute-start | bytes 294920 | tf_op jit(solution)/shard_map/ppermute | solution.py:389
  54.9 3.0 %collective-permute-done.10.refs_4_ = f32[3,64,128]{2,1,0:T(8,128)S(1)} collective-permute-done((f32[3,64,128]{2,1,0:T(8,128)S(1)}, f32[3,64,128]{2,1,0:T(8,128)S(1)}, u32[]{:S(2)}, u32[]{:S(2)}) %collective-permute-start.10) | collective-permute-done | bytes 98336 | tf_op jit(solution)/shard_map/ppermute | solution.py:389
  58.0 2.2 %collective-permute-done.11.refs_5_ = f32[3,64,128]{2,1,0:T(8,128)S(1)} collective-permute-done((f32[3,64,128]{2,1,0:T(8,128)S(1)}, f32[3,64,128]{2,1,0:T(8,128)S(1)}, u32[]{:S(2)}, u32[]{:S(2)}) %collective-permute-start.11) | collective-permute-done | bytes 98336 | tf_op jit(solution)/shard_map/ppermute | solution.py:389
  60.2 1.2 %shard_map.125 = (f32[384,512]{1,0:T(8,128)S(1)}, bf16[128,512]{1,0:T(8,128)(2,1)S(1)}) custom-call(s32[8,512]{1,0:T(8,128)S(1)} %get-tuple-element.42.info_ref, f32[3,64,128]{2,1,0:T(8,128)S(1)} %collective-permute-done.7.refs_0_, f32[3,64,128]{2,1,0:T(8,128)S(1)} %collective-permute-done.8.refs_1_, f32[3,64,128]{2,1,0:T(8,128)S(1)} %get-tuple-element.60.refs_2_, ...), custom_call_target="tpu_custom_call" | custom-call | flops 10000000000 | bytes 10000000 | tf_op jit(solution)/shard_map/pallas_call | solution.py:472
  61.3 0.0 collective-permute-done.12.refs_0_.refs_6_
  61.3 1.5 %collective-permute-done.13.refs_1_.refs_7_ = f32[3,64,128]{2,1,0:T(8,128)S(1)} collective-permute-done((f32[3,64,128]{2,1,0:T(8,128)S(1)}, f32[3,64,128]{2,1,0:T(8,128)S(1)}, u32[]{:S(2)}, u32[]{:S(2)}) %collective-permute-start.13) | collective-permute-done | bytes 98336 | tf_op jit(solution)/shard_map/ppermute | solution.py:389
  62.9 0.7 shard_map.126
  63.5 0.5 collective-permute-start.14
  64.0 2.9 %collective-permute-start.19 = (f32[3,64,128]{2,1,0:T(8,128)S(1)}, f32[3,64,128]{2,1,0:T(8,128)S(1)}, u32[]{:S(2)}, u32[]{:S(2)}) collective-permute-start(f32[3,64,128]{2,1,0:T(8,128)S(1)} %get-tuple-element.73), channel_id=1, source_target_pairs={{0,6},{1,7},{2,4},{3,5},{4,2},{5,3},{6,0},{7,1},{8,14},{9,15},{10,... | collective-permute-start | bytes 294920 | tf_op jit(solution)/shard_map/ppermute | solution.py:389
  67.0 0.1 collective-permute-start.20
  67.0 0.9 %collective-permute-start.21 = (f32[3,64,128]{2,1,0:T(8,128)S(1)}, f32[3,64,128]{2,1,0:T(8,128)S(1)}, u32[]{:S(2)}, u32[]{:S(2)}) collective-permute-start(f32[3,64,128]{2,1,0:T(8,128)S(1)} %get-tuple-element.76), channel_id=1, source_target_pairs={{0,1},{1,0},{2,3},{3,2},{4,5},{5,4},{6,7},{7,6},{8,9},{9,8},{10,11... | collective-permute-start | bytes 294920 | tf_op jit(solution)/shard_map/ppermute | solution.py:389
  68.0 1.6 %collective-permute-start.22 = (f32[3,64,128]{2,1,0:T(8,128)S(1)}, f32[3,64,128]{2,1,0:T(8,128)S(1)}, u32[]{:S(2)}, u32[]{:S(2)}) collective-permute-start(f32[3,64,128]{2,1,0:T(8,128)S(1)} %get-tuple-element.77), channel_id=1, source_target_pairs={{0,2},{1,3},{2,0},{3,1},{4,6},{5,7},{6,4},{7,5},{8,10},{9,11},{10,... | collective-permute-start | bytes 294920 | tf_op jit(solution)/shard_map/ppermute | solution.py:389
  69.6 6.6 %collective-permute-done.14.refs_8_.refs_0_ = f32[3,64,128]{2,1,0:T(8,128)S(1)} collective-permute-done((f32[3,64,128]{2,1,0:T(8,128)S(1)}, f32[3,64,128]{2,1,0:T(8,128)S(1)}, u32[]{:S(2)}, u32[]{:S(2)}) %collective-permute-start.14) | collective-permute-done | bytes 98336 | tf_op jit(solution)/shard_map/ppermute | solution.py:389
  76.3 1.8 %shard_map.127 = (f32[6,64,512]{2,1,0:T(8,128)}, f32[3,64]{1,0:T(4,128)S(1)}) custom-call(s32[8,512]{1,0:T(8,128)S(1)} %get-tuple-element.42.info_ref, s32[2,512]{1,0:T(2,128)S(1)} %copy-done.4, f32[6,64,512]{2,1,0:T(8,128)S(1)} %copy-done.3, f32[3,64,128]{2,1,0:T(8,128)S(1)} %collective-permute-done.7.refs_0_, ...), custom_call_target="tpu_custom_call" | custom-call | flops 10000000000 | bytes 10000000 | tf_op jit(solution)/shard_map/pallas_call | solution.py:488
  78.1 0.0 collective-permute-done.19.refs_0_
  78.1 1.8 %collective-permute-start.15 = (f32[3,64,128]{2,1,0:T(8,128)S(1)}, f32[3,64,128]{2,1,0:T(8,128)S(1)}, u32[]{:S(2)}, u32[]{:S(2)}) collective-permute-start(f32[3,64,128]{2,1,0:T(8,128)S(1)} %get-tuple-element.71), channel_id=1, source_target_pairs={{0,5},{1,4},{2,7},{3,6},{4,1},{5,0},{6,3},{7,2},{8,13},{9,12},{10,... | collective-permute-start | bytes 294920 | tf_op jit(solution)/shard_map/ppermute | solution.py:389
  79.9 2.5 %collective-permute-start.18 = (f32[3,64]{1,0:T(4,128)S(1)}, f32[3,64]{1,0:T(4,128)S(1)}, u32[]{:S(2)}, u32[]{:S(2)}) collective-permute-start(f32[3,64]{1,0:T(4,128)S(1)} %get-tuple-element.72.refs_2_), channel_id=1, source_target_pairs={{0,24},{8,16},{16,8},{24,0},{1,25},{9,17},{17,9},{25,1},{2,26},{10... | collective-permute-start | bytes 2312 | tf_op jit(solution)/shard_map/ppermute | solution.py:397
  82.4 0.0 collective-permute-done.21.refs_3_
  82.4 0.5 collective-permute-start.17
  82.9 0.0 collective-permute-done.22.refs_4_
  82.9 0.5 collective-permute-start.16
  83.4 0.0 collective-permute-done.23.refs_5_
  83.4 1.2 %shard_map.128.refs_6_ = f32[6,512,128]{2,1,0:T(8,128)} custom-call(s32[1]{0:T(128)} %bitcast.me_ref, s32[8,512]{1,0:T(8,128)S(1)} %get-tuple-element.42.info_ref, f32[3,512,128]{2,1,0:T(8,128)S(1)} %get-tuple-element.70.solved_ref, f32[3,64,128]{2,1,0:T(8,128)S(1)} %collective-permute-done.19.refs_0_, f32[3,64,128]{2,1,0:T(8,128)S(1)} %collective-permute-done.20.refs_1_, ...), custom_call_target="tpu_custom_call" | custom-call | flops 10000000000 | bytes 10000000 | tf_op jit(solution)/shard_map/pallas_call | solution.py:498
  84.7 0.9 %collective-permute-done.15.refs_1_ = f32[3,64,128]{2,1,0:T(8,128)S(1)} collective-permute-done((f32[3,64,128]{2,1,0:T(8,128)S(1)}, f32[3,64,128]{2,1,0:T(8,128)S(1)}, u32[]{:S(2)}, u32[]{:S(2)}) %collective-permute-start.15) | collective-permute-done | bytes 98336 | tf_op jit(solution)/shard_map/ppermute | solution.py:389
  85.6 0.4 collective-permute-done.17.refs_4_
  86.0 0.5 collective-permute-done.16.refs_3_
  86.5 1.4 %shard_map.129 = (f32[6,512,128]{2,1,0:T(8,128)}, f32[3,64]{1,0:T(4,128)}) custom-call(s32[1]{0:T(128)} %bitcast.me_ref, s32[8,512]{1,0:T(8,128)S(1)} %get-tuple-element.42.info_ref, f32[3,512,128]{2,1,0:T(8,128)S(1)} %get-tuple-element.70.solved_ref, f32[3,64,128]{2,1,0:T(8,128)S(1)} %collective-permute-done.14.refs_8_.refs_0_, ...), custom_call_target="tpu_custom_call", output_to_operand_aliasing={{0}: (9, {})} | custom-call | flops 1000000000 | bytes 1000000 | tf_op jit(solution)/shard_map/pallas_call | solution.py:509
  (21 shorter events, 0.0 us)
Async XLA Ops:
  0.6 10.8 %copy-start = (f32[512,512]{1,0:T(8,128)S(1)}, f32[512,512]{1,0:T(8,128)}, u32[]{:S(2)}) copy-start(f32[512,512]{1,0:T(8,128)} %deriv_ref.1) | copy-start | bytes 3145732
  0.6 10.8 %copy-start.1 = (f32[512,512]{1,0:T(8,128)S(1)}, f32[512,512]{1,0:T(8,128)}, u32[]{:S(2)}) copy-start(f32[512,512]{1,0:T(8,128)} %inverse_ref.1) | copy-start | bytes 3145732
  0.7 10.8 %copy-start.2 = (f32[512,512]{1,0:T(8,128)S(1)}, f32[512,512]{1,0:T(8,128)}, u32[]{:S(2)}) copy-start(f32[512,512]{1,0:T(8,128)} %basis_ref.1) | copy-start | bytes 3145732
  0.7 10.8 %copy-start.5 = (f32[512]{0:T(512)S(1)}, f32[512]{0:T(512)}, u32[]{:S(2)}) copy-start(f32[512]{0:T(512)} %param.17) | copy-start | bytes 6148
  4.4 10.5 %collective-permute-start = (f32[2,3,64,128]{3,2,1,0:T(8,128)S(1)}, f32[2,3,64,128]{3,2,1,0:T(8,128)S(1)}, u32[]{:S(2)}, u32[]{:S(2)}) collective-permute-start(f32[2,3,64,128]{3,2,1,0:T(8,128)S(1)} %get-tuple-element.50), channel_id=1, source_target_pairs={{0,6},{1,7},{2,4},{3,5},{4,2},{5,3},{6,0},{7,1},{8,14},{9,15},{10,... | collective-permute-start | bytes 589832 | tf_op jit(solution)/shard_map/ppermute | solution.py:389
  9.6 15.2 %collective-permute-start.1 = (f32[2,3,64,128]{3,2,1,0:T(8,128)S(1)}, f32[2,3,64,128]{3,2,1,0:T(8,128)S(1)}, u32[]{:S(2)}, u32[]{:S(2)}) collective-permute-start(f32[2,3,64,128]{3,2,1,0:T(8,128)S(1)} %get-tuple-element.51), channel_id=1, source_target_pairs={{0,7},{1,6},{2,5},{3,4},{4,3},{5,2},{6,1},{7,0},{8,15},{9,14},{10,... | collective-permute-start | bytes 589832 | tf_op jit(solution)/shard_map/ppermute | solution.py:389
  9.6 19.1 %collective-permute-start.2 = (f32[2,3,64,128]{3,2,1,0:T(8,128)S(1)}, f32[2,3,64,128]{3,2,1,0:T(8,128)S(1)}, u32[]{:S(2)}, u32[]{:S(2)}) collective-permute-start(f32[2,3,64,128]{3,2,1,0:T(8,128)S(1)} %get-tuple-element.53), channel_id=1, source_target_pairs={{0,1},{1,0},{2,3},{3,2},{4,5},{5,4},{6,7},{7,6},{8,9},{9,8},{10,11... | collective-permute-start | bytes 589832 | tf_op jit(solution)/shard_map/ppermute | solution.py:389
  9.8 18.9 %collective-permute-start.3 = (f32[2,3,64,128]{3,2,1,0:T(8,128)S(1)}, f32[2,3,64,128]{3,2,1,0:T(8,128)S(1)}, u32[]{:S(2)}, u32[]{:S(2)}) collective-permute-start(f32[2,3,64,128]{3,2,1,0:T(8,128)S(1)} %get-tuple-element.54), channel_id=1, source_target_pairs={{0,2},{1,3},{2,0},{3,1},{4,6},{5,7},{6,4},{7,5},{8,10},{9,11},{10,... | collective-permute-start | bytes 589832 | tf_op jit(solution)/shard_map/ppermute | solution.py:389
  9.8 18.9 %collective-permute-start.4 = (f32[2,3,64,128]{3,2,1,0:T(8,128)S(1)}, f32[2,3,64,128]{3,2,1,0:T(8,128)S(1)}, u32[]{:S(2)}, u32[]{:S(2)}) collective-permute-start(f32[2,3,64,128]{3,2,1,0:T(8,128)S(1)} %get-tuple-element.55), channel_id=1, source_target_pairs={{0,3},{1,2},{2,1},{3,0},{4,7},{5,6},{6,5},{7,4},{8,11},{9,10},{10,... | collective-permute-start | bytes 589832 | tf_op jit(solution)/shard_map/ppermute | solution.py:389
  14.9 24.9 %collective-permute-start.5 = (f32[2,3,64,128]{3,2,1,0:T(8,128)S(1)}, f32[2,3,64,128]{3,2,1,0:T(8,128)S(1)}, u32[]{:S(2)}, u32[]{:S(2)}) collective-permute-start(f32[2,3,64,128]{3,2,1,0:T(8,128)S(1)} %get-tuple-element.56), channel_id=1, source_target_pairs={{0,4},{1,5},{2,6},{3,7},{4,0},{5,1},{6,2},{7,3},{8,12},{9,13},{10,... | collective-permute-start | bytes 589832 | tf_op jit(solution)/shard_map/ppermute | solution.py:389
  24.8 17.4 %collective-permute-start.6 = (f32[2,3,64,128]{3,2,1,0:T(8,128)S(1)}, f32[2,3,64,128]{3,2,1,0:T(8,128)S(1)}, u32[]{:S(2)}, u32[]{:S(2)}) collective-permute-start(f32[2,3,64,128]{3,2,1,0:T(8,128)S(1)} %get-tuple-element.57), channel_id=1, source_target_pairs={{0,5},{1,4},{2,7},{3,6},{4,1},{5,0},{6,3},{7,2},{8,13},{9,12},{10,... | collective-permute-start | bytes 589832 | tf_op jit(solution)/shard_map/ppermute | solution.py:389
  43.7 7.7 %collective-permute-start.7 = (f32[3,64,128]{2,1,0:T(8,128)S(1)}, f32[3,64,128]{2,1,0:T(8,128)S(1)}, u32[]{:S(2)}, u32[]{:S(2)}) collective-permute-start(f32[3,64,128]{2,1,0:T(8,128)S(1)} %get-tuple-element.58), channel_id=1, source_target_pairs={{0,6},{1,7},{2,4},{3,5},{4,2},{5,3},{6,0},{7,1},{8,14},{9,15},{10,... | collective-permute-start | bytes 294920 | tf_op jit(solution)/shard_map/ppermute | solution.py:389
  46.0 6.7 %collective-permute-start.8 = (f32[3,64,128]{2,1,0:T(8,128)S(1)}, f32[3,64,128]{2,1,0:T(8,128)S(1)}, u32[]{:S(2)}, u32[]{:S(2)}) collective-permute-start(f32[3,64,128]{2,1,0:T(8,128)S(1)} %get-tuple-element.59), channel_id=1, source_target_pairs={{0,7},{1,6},{2,5},{3,4},{4,3},{5,2},{6,1},{7,0},{8,15},{9,14},{10,... | collective-permute-start | bytes 294920 | tf_op jit(solution)/shard_map/ppermute | solution.py:389
  47.7 7.2 %collective-permute-start.9 = (f32[3,64,128]{2,1,0:T(8,128)S(1)}, f32[3,64,128]{2,1,0:T(8,128)S(1)}, u32[]{:S(2)}, u32[]{:S(2)}) collective-permute-start(f32[3,64,128]{2,1,0:T(8,128)S(1)} %get-tuple-element.61), channel_id=1, source_target_pairs={{0,1},{1,0},{2,3},{3,2},{4,5},{5,4},{6,7},{7,6},{8,9},{9,8},{10,11... | collective-permute-start | bytes 294920 | tf_op jit(solution)/shard_map/ppermute | solution.py:389
  47.7 10.3 %collective-permute-start.10 = (f32[3,64,128]{2,1,0:T(8,128)S(1)}, f32[3,64,128]{2,1,0:T(8,128)S(1)}, u32[]{:S(2)}, u32[]{:S(2)}) collective-permute-start(f32[3,64,128]{2,1,0:T(8,128)S(1)} %get-tuple-element.62), channel_id=1, source_target_pairs={{0,2},{1,3},{2,0},{3,1},{4,6},{5,7},{6,4},{7,5},{8,10},{9,11},{10,... | collective-permute-start | bytes 294920 | tf_op jit(solution)/shard_map/ppermute | solution.py:389
  47.7 12.4 %collective-permute-start.11 = (f32[3,64,128]{2,1,0:T(8,128)S(1)}, f32[3,64,128]{2,1,0:T(8,128)S(1)}, u32[]{:S(2)}, u32[]{:S(2)}) collective-permute-start(f32[3,64,128]{2,1,0:T(8,128)S(1)} %get-tuple-element.63), channel_id=1, source_target_pairs={{0,3},{1,2},{2,1},{3,0},{4,7},{5,6},{6,5},{7,4},{8,11},{9,10},{10,... | collective-permute-start | bytes 294920 | tf_op jit(solution)/shard_map/ppermute | solution.py:389
  51.4 9.9 %collective-permute-start.12 = (f32[3,64,128]{2,1,0:T(8,128)S(1)}, f32[3,64,128]{2,1,0:T(8,128)S(1)}, u32[]{:S(2)}, u32[]{:S(2)}) collective-permute-start(f32[3,64,128]{2,1,0:T(8,128)S(1)} %get-tuple-element.64), channel_id=1, source_target_pairs={{0,4},{1,5},{2,6},{3,7},{4,0},{5,1},{6,2},{7,3},{8,12},{9,13},{10,... | collective-permute-start | bytes 294920 | tf_op jit(solution)/shard_map/ppermute | solution.py:389
  52.7 10.1 %collective-permute-start.13 = (f32[3,64,128]{2,1,0:T(8,128)S(1)}, f32[3,64,128]{2,1,0:T(8,128)S(1)}, u32[]{:S(2)}, u32[]{:S(2)}) collective-permute-start(f32[3,64,128]{2,1,0:T(8,128)S(1)} %get-tuple-element.65), channel_id=1, source_target_pairs={{0,5},{1,4},{2,7},{3,6},{4,1},{5,0},{6,3},{7,2},{8,13},{9,12},{10,... | collective-permute-start | bytes 294920 | tf_op jit(solution)/shard_map/ppermute | solution.py:389
  62.9 13.4 %copy-start.3 = (f32[6,64,512]{2,1,0:T(8,128)S(1)}, f32[6,64,512]{2,1,0:T(8,128)}, u32[]{:S(2)}) copy-start(f32[6,64,512]{2,1,0:T(8,128)} %velocity_ref.1) | copy-start | bytes 2359300
  62.9 13.4 %copy-start.4 = (s32[2,512]{1,0:T(2,128)S(1)}, s32[2,512]{1,0:T(2,128)}, u32[]{:S(2)}) copy-start(s32[2,512]{1,0:T(2,128)} %modes_ref.1) | copy-start | bytes 12292
  63.5 12.7 %collective-permute-start.14 = (f32[3,64,128]{2,1,0:T(8,128)S(1)}, f32[3,64,128]{2,1,0:T(8,128)S(1)}, u32[]{:S(2)}, u32[]{:S(2)}) collective-permute-start(f32[3,64,128]{2,1,0:T(8,128)S(1)} %get-tuple-element.68), channel_id=1, source_target_pairs={{0,4},{1,5},{2,6},{3,7},{4,0},{5,1},{6,2},{7,3},{8,12},{9,13},{10,... | collective-permute-start | bytes 294920 | tf_op jit(solution)/shard_map/ppermute | solution.py:389
  64.0 14.1 %collective-permute-start.19 = (f32[3,64,128]{2,1,0:T(8,128)S(1)}, f32[3,64,128]{2,1,0:T(8,128)S(1)}, u32[]{:S(2)}, u32[]{:S(2)}) collective-permute-start(f32[3,64,128]{2,1,0:T(8,128)S(1)} %get-tuple-element.73), channel_id=1, source_target_pairs={{0,6},{1,7},{2,4},{3,5},{4,2},{5,3},{6,0},{7,1},{8,14},{9,15},{10,... | collective-permute-start | bytes 294920 | tf_op jit(solution)/shard_map/ppermute | solution.py:389
  67.0 12.9 %collective-permute-start.20 = (f32[3,64,128]{2,1,0:T(8,128)S(1)}, f32[3,64,128]{2,1,0:T(8,128)S(1)}, u32[]{:S(2)}, u32[]{:S(2)}) collective-permute-start(f32[3,64,128]{2,1,0:T(8,128)S(1)} %get-tuple-element.74), channel_id=1, source_target_pairs={{0,7},{1,6},{2,5},{3,4},{4,3},{5,2},{6,1},{7,0},{8,15},{9,14},{10,... | collective-permute-start | bytes 294920 | tf_op jit(solution)/shard_map/ppermute | solution.py:389
  67.0 15.3 %collective-permute-start.21 = (f32[3,64,128]{2,1,0:T(8,128)S(1)}, f32[3,64,128]{2,1,0:T(8,128)S(1)}, u32[]{:S(2)}, u32[]{:S(2)}) collective-permute-start(f32[3,64,128]{2,1,0:T(8,128)S(1)} %get-tuple-element.76), channel_id=1, source_target_pairs={{0,1},{1,0},{2,3},{3,2},{4,5},{5,4},{6,7},{7,6},{8,9},{9,8},{10,11... | collective-permute-start | bytes 294920 | tf_op jit(solution)/shard_map/ppermute | solution.py:389
  68.0 14.9 %collective-permute-start.22 = (f32[3,64,128]{2,1,0:T(8,128)S(1)}, f32[3,64,128]{2,1,0:T(8,128)S(1)}, u32[]{:S(2)}, u32[]{:S(2)}) collective-permute-start(f32[3,64,128]{2,1,0:T(8,128)S(1)} %get-tuple-element.77), channel_id=1, source_target_pairs={{0,2},{1,3},{2,0},{3,1},{4,6},{5,7},{6,4},{7,5},{8,10},{9,11},{10,... | collective-permute-start | bytes 294920 | tf_op jit(solution)/shard_map/ppermute | solution.py:389
  76.3 7.2 %collective-permute-start.23 = (f32[3,64,128]{2,1,0:T(8,128)S(1)}, f32[3,64,128]{2,1,0:T(8,128)S(1)}, u32[]{:S(2)}, u32[]{:S(2)}) collective-permute-start(f32[3,64,128]{2,1,0:T(8,128)S(1)} %get-tuple-element.78), channel_id=1, source_target_pairs={{0,3},{1,2},{2,1},{3,0},{4,7},{5,6},{6,5},{7,4},{8,11},{9,10},{10,... | collective-permute-start | bytes 294920 | tf_op jit(solution)/shard_map/ppermute | solution.py:389
  78.1 7.5 %collective-permute-start.15 = (f32[3,64,128]{2,1,0:T(8,128)S(1)}, f32[3,64,128]{2,1,0:T(8,128)S(1)}, u32[]{:S(2)}, u32[]{:S(2)}) collective-permute-start(f32[3,64,128]{2,1,0:T(8,128)S(1)} %get-tuple-element.71), channel_id=1, source_target_pairs={{0,5},{1,4},{2,7},{3,6},{4,1},{5,0},{6,3},{7,2},{8,13},{9,12},{10,... | collective-permute-start | bytes 294920 | tf_op jit(solution)/shard_map/ppermute | solution.py:389
  79.9 5.7 %collective-permute-start.18 = (f32[3,64]{1,0:T(4,128)S(1)}, f32[3,64]{1,0:T(4,128)S(1)}, u32[]{:S(2)}, u32[]{:S(2)}) collective-permute-start(f32[3,64]{1,0:T(4,128)S(1)} %get-tuple-element.72.refs_2_), channel_id=1, source_target_pairs={{0,24},{8,16},{16,8},{24,0},{1,25},{9,17},{17,9},{25,1},{2,26},{10... | collective-permute-start | bytes 2312 | tf_op jit(solution)/shard_map/ppermute | solution.py:397
  82.4 3.6 %collective-permute-start.17 = (f32[3,64]{1,0:T(4,128)S(1)}, f32[3,64]{1,0:T(4,128)S(1)}, u32[]{:S(2)}, u32[]{:S(2)}) collective-permute-start(f32[3,64]{1,0:T(4,128)S(1)} %get-tuple-element.72.refs_2_), channel_id=1, source_target_pairs={{0,16},{8,24},{16,0},{24,8},{1,17},{9,25},{17,1},{25,9},{2,18},{10... | collective-permute-start | bytes 2312 | tf_op jit(solution)/shard_map/ppermute | solution.py:397
  82.9 3.6 %collective-permute-start.16 = (f32[3,64]{1,0:T(4,128)S(1)}, f32[3,64]{1,0:T(4,128)S(1)}, u32[]{:S(2)}, u32[]{:S(2)}) collective-permute-start(f32[3,64]{1,0:T(4,128)S(1)} %get-tuple-element.72.refs_2_), channel_id=1, source_target_pairs={{0,8},{8,0},{16,24},{24,16},{1,9},{9,1},{17,25},{25,17},{2,10},{10... | collective-permute-start | bytes 2312 | tf_op jit(solution)/shard_map/ppermute | solution.py:397

commit v9 on v8

--- a/solution.py
+++ b/solution.py
@@ -375,8 +375,8 @@
 
 
 def early_steps(devices, points):
-    half = devices // 2
-    return list(range(half + LANES // points, devices)) + list(range(half))
+    fill, half = LANES // points, devices // 2
+    return list(range(fill)) + list(range(half + fill, devices)) + list(range(fill, half))
 
 
 def steps_of(devices, points):
@@ -492,7 +492,7 @@
         [FAR, LOCAL],
         HEAVY,
         [pltpu.VMEM(state_now.shape, F32), pltpu.SemaphoreType.DMA],
-    )(info, kept_modes, velocity, *returned, extra[split])
+    )(info, kept_modes, velocity, *returned, extra[early.index(3)])
     terms = from_groups(emf)
 
     owned = call(

time: 88.1 us -> 87.8 us (level); the launches traced: 87.9 us -> 86.5 us
  starting transfers between devices: 41.5 us -> 37.8 us
  waiting for transfers between devices: 31.2 us -> 33.5 us
    ppermute x21, starting transfers between devices: 38 us -> 33.3 us  [exchange(): lax.ppermute(block, 'col', [(i, i ^ step) for i in range(devices)])]
    ppermute x21, waiting for transfers between devices: 30.3 us -> 33.4 us  [exchange(): lax.ppermute(block, 'col', [(i, i ^ step) for i in range(devices)])]
    ppermute x3, starting transfers between devices: 3.49 us -> 4.45 us  [from_groups(): lax.ppermute(value, 'grp', [(i, i ^ step) for i in range(groups)])]
  transfers between devices with their start and end apart: 24 -> 24, of which waited for: 11 -> 13; matrix products, arithmetic and copies ran while one was open for 0% -> 0% of each run, Pallas kernels for 8% -> 8%
where the time goes in v9:
time: 87.8 us; the launch traced here: 86.5 us
  starting transfers between devices  37.8 us (43%)
  waiting for transfers between devices  33.5 us (38%)
  Pallas kernels  14.4 us (16%)
    ppermute x21, waiting for transfers between devices, exchange(): lax.ppermute(block, 'col', [(i, i ^ step) for i in range(devices)])  33.4 us
    ppermute x21, starting transfers between devices, exchange(): lax.ppermute(block, 'col', [(i, i ^ step) for i in range(devices)])  33.3 us
    ppermute x3, starting transfers between devices, from_groups(): lax.ppermute(value, 'grp', [(i, i ^ step) for i in range(groups)])  4.45 us
    pallas_call x1, Pallas kernels, on_device(): call(functools.partial(first_kernel, devices), [shaped((8, columns), jnp....  3.76 us
    pallas_call x1, Pallas kernels, on_device(): call(functools.partial(state_kernel, steps), [shaped(state_now.shape), sh...  1.83 us
  transfers between devices with their start and end apart: 24, of which 13 were waited for; matrix products, arithmetic and copies ran while one was open for 0% of the time, Pallas kernels for 8%

profile of v9, /device:TPU:0, one launch (start us, length us, event | category | flops | bytes accessed | tf_op | source)
XLA Modules:
  0.0 86.5 jit_solution(3640409690844795478)
XLA Ops:
  0.7 3.8 %shard_map.121 = (s32[8,512]{1,0:T(8,128)S(1)}, f32[8,128]{1,0:T(8,128)S(1)}, f32[2,3,64,128]{3,2,1,0:T(8,128)S(1)}, f32[2,3,64,128]{3,2,1,0:T(8,128)S(1)}, f32[...) custom-call(s32[1]{0:T(128)} %bitcast.me_ref, ...), custom_call_target="tpu_custom_call" | custom-call | flops 1000000000 | bytes 1000000 | tf_op jit(solution)/shard_map/pallas_call | solution.py:430
  4.4 0.5 collective-permute-start
  5.0 4.7 %collective-permute-start.1 = (f32[2,3,64,128]{3,2,1,0:T(8,128)S(1)}, f32[2,3,64,128]{3,2,1,0:T(8,128)S(1)}, u32[]{:S(2)}, u32[]{:S(2)}) collective-permute-start(f32[2,3,64,128]{3,2,1,0:T(8,128)S(1)} %get-tuple-element.52), channel_id=1, source_target_pairs={{0,6},{1,7},{2,4},{3,5},{4,2},{5,3},{6,0},{7,1},{8,14},{9,15},{10,... | collective-permute-start | bytes 589832 | tf_op jit(solution)/shard_map/ppermute | solution.py:389
  9.6 0.1 collective-permute-start.2
  9.7 0.0 collective-permute-start.3
  9.7 1.5 %collective-permute-start.4 = (f32[2,3,64,128]{3,2,1,0:T(8,128)S(1)}, f32[2,3,64,128]{3,2,1,0:T(8,128)S(1)}, u32[]{:S(2)}, u32[]{:S(2)}) collective-permute-start(f32[2,3,64,128]{3,2,1,0:T(8,128)S(1)} %get-tuple-element.55), channel_id=1, source_target_pairs={{0,3},{1,2},{2,1},{3,0},{4,7},{5,6},{6,5},{7,4},{8,11},{9,10},{10,... | collective-permute-start | bytes 589832 | tf_op jit(solution)/shard_map/ppermute | solution.py:389
  11.2 1.4 %shard_map.122 = (bf16[512,512]{1,0:T(8,128)(2,1)S(1)}, bf16[512,512]{1,0:T(8,128)(2,1)S(1)}, bf16[512,512]{1,0:T(8,128)(2,1)S(1)}, bf16[512,512]{1,0:T(8,128)(2...) custom-call(f32[512,512]{1,0:T(8,128)S(1)} %copy-done, f32[512,512]{1,0:T(8,128)S(1)} %copy-done.1, ...), custom_call_target="tpu_custom_call" | custom-call | flops 10000000000 | bytes 10000000 | tf_op jit(solution)/shard_map/pallas_call | solution.py:444
  12.6 0.0 collective-permute-done.refs_5_
  12.6 2.7 %collective-permute-start.5 = (f32[2,3,64,128]{3,2,1,0:T(8,128)S(1)}, f32[2,3,64,128]{3,2,1,0:T(8,128)S(1)}, u32[]{:S(2)}, u32[]{:S(2)}) collective-permute-start(f32[2,3,64,128]{3,2,1,0:T(8,128)S(1)} %get-tuple-element.56), channel_id=1, source_target_pairs={{0,4},{1,5},{2,6},{3,7},{4,0},{5,1},{6,2},{7,3},{8,12},{9,13},{10,... | collective-permute-start | bytes 589832 | tf_op jit(solution)/shard_map/ppermute | solution.py:389
  15.3 0.3 collective-permute-done.1.refs_6_
  15.6 8.0 %collective-permute-start.6 = (f32[2,3,64,128]{3,2,1,0:T(8,128)S(1)}, f32[2,3,64,128]{3,2,1,0:T(8,128)S(1)}, u32[]{:S(2)}, u32[]{:S(2)}) collective-permute-start(f32[2,3,64,128]{3,2,1,0:T(8,128)S(1)} %get-tuple-element.57), channel_id=1, source_target_pairs={{0,5},{1,4},{2,7},{3,6},{4,1},{5,0},{6,3},{7,2},{8,13},{9,12},{10,... | collective-permute-start | bytes 589832 | tf_op jit(solution)/shard_map/ppermute | solution.py:389
  23.6 0.0 collective-permute-done.2.refs_7_
  23.6 0.2 collective-permute-done.3.refs_8_
  23.7 5.1 %collective-permute-done.4.refs_9_ = f32[2,3,64,128]{3,2,1,0:T(8,128)S(1)} collective-permute-done((f32[2,3,64,128]{3,2,1,0:T(8,128)S(1)}, f32[2,3,64,128]{3,2,1,0:T(8,128)S(1)}, u32[]{:S(2)}, u32[]{:S(2)}) %collective-permute-start.4) | collective-permute-done | bytes 196640 | tf_op jit(solution)/shard_map/ppermute | solution.py:389
  28.8 1.4 %shard_map.123.early_ref = f32[512,384]{1,0:T(8,128)S(1)} custom-call(s32[1]{0:T(128)} %bitcast.me_ref, bf16[512,512]{1,0:T(8,128)(2,1)S(1)} %get-tuple-element.46.refs_0_, bf16[512,512]{1,0:T(8,128)(2,1)S(1)} %get-tuple-element.47.refs_1_, bf16[512,512]{1,0:T(8,128)(2,1)S(1)} %get-tuple-element.48.refs_2_, bf16[512,512]{1,0:T(8,128)(2,1)S(1)} %get-tuple-element.49.refs_3_, ...), custom_call_target="tpu_custom_call" | custom-call | flops 10000000000 | bytes 10000000 | tf_op jit(solution)/shard_map/pallas_call | solution.py:453
  30.2 9.8 %collective-permute-done.5.refs_4_ = f32[2,3,64,128]{3,2,1,0:T(8,128)S(1)} collective-permute-done((f32[2,3,64,128]{3,2,1,0:T(8,128)S(1)}, f32[2,3,64,128]{3,2,1,0:T(8,128)S(1)}, u32[]{:S(2)}, u32[]{:S(2)}) %collective-permute-start.5) | collective-permute-done | bytes 196640 | tf_op jit(solution)/shard_map/ppermute | solution.py:389
  40.0 3.3 %collective-permute-done.6.refs_5_ = f32[2,3,64,128]{3,2,1,0:T(8,128)S(1)} collective-permute-done((f32[2,3,64,128]{3,2,1,0:T(8,128)S(1)}, f32[2,3,64,128]{3,2,1,0:T(8,128)S(1)}, u32[]{:S(2)}, u32[]{:S(2)}) %collective-permute-start.6) | collective-permute-done | bytes 196640 | tf_op jit(solution)/shard_map/ppermute | solution.py:389
  43.3 1.6 %shard_map.124 = (f32[3,64,128]{2,1,0:T(8,128)S(1)}, f32[3,64,128]{2,1,0:T(8,128)S(1)}, f32[3,64,128]{2,1,0:T(8,128)S(1)}, f32[3,64,128]{2,1,0:T(8,128)S(1)}, f3...) custom-call(s32[1]{0:T(128)} %bitcast.me_ref, ...), custom_call_target="tpu_custom_call" | custom-call | flops 1000000000 | bytes 1000000 | tf_op jit(solution)/shard_map/pallas_call | solution.py:461
  44.9 0.3 collective-permute-start.7
  45.2 2.5 %collective-permute-start.8 = (f32[3,64,128]{2,1,0:T(8,128)S(1)}, f32[3,64,128]{2,1,0:T(8,128)S(1)}, u32[]{:S(2)}, u32[]{:S(2)}) collective-permute-start(f32[3,64,128]{2,1,0:T(8,128)S(1)} %get-tuple-element.60), channel_id=1, source_target_pairs={{0,6},{1,7},{2,4},{3,5},{4,2},{5,3},{6,0},{7,1},{8,14},{9,15},{10,... | collective-permute-start | bytes 294920 | tf_op jit(solution)/shard_map/ppermute | solution.py:389
  47.8 0.9 collective-permute-start.9
  48.6 0.0 collective-permute-start.10
  48.6 1.9 %collective-permute-start.11 = (f32[3,64,128]{2,1,0:T(8,128)S(1)}, f32[3,64,128]{2,1,0:T(8,128)S(1)}, u32[]{:S(2)}, u32[]{:S(2)}) collective-permute-start(f32[3,64,128]{2,1,0:T(8,128)S(1)} %get-tuple-element.63), channel_id=1, source_target_pairs={{0,3},{1,2},{2,1},{3,0},{4,7},{5,6},{6,5},{7,4},{8,11},{9,10},{10,... | collective-permute-start | bytes 294920 | tf_op jit(solution)/shard_map/ppermute | solution.py:389
  50.5 0.0 collective-permute-done.7.refs_1_
  50.5 1.4 %collective-permute-start.12 = (f32[3,64,128]{2,1,0:T(8,128)S(1)}, f32[3,64,128]{2,1,0:T(8,128)S(1)}, u32[]{:S(2)}, u32[]{:S(2)}) collective-permute-start(f32[3,64,128]{2,1,0:T(8,128)S(1)} %get-tuple-element.64), channel_id=1, source_target_pairs={{0,4},{1,5},{2,6},{3,7},{4,0},{5,1},{6,2},{7,3},{8,12},{9,13},{10,... | collective-permute-start | bytes 294920 | tf_op jit(solution)/shard_map/ppermute | solution.py:389
  51.9 0.2 collective-permute-done.8.refs_2_
  52.1 0.9 %collective-permute-start.13 = (f32[3,64,128]{2,1,0:T(8,128)S(1)}, f32[3,64,128]{2,1,0:T(8,128)S(1)}, u32[]{:S(2)}, u32[]{:S(2)}) collective-permute-start(f32[3,64,128]{2,1,0:T(8,128)S(1)} %get-tuple-element.65), channel_id=1, source_target_pairs={{0,5},{1,4},{2,7},{3,6},{4,1},{5,0},{6,3},{7,2},{8,13},{9,12},{10,... | collective-permute-start | bytes 294920 | tf_op jit(solution)/shard_map/ppermute | solution.py:389
  53.0 1.7 %collective-permute-done.9.refs_3_ = f32[3,64,128]{2,1,0:T(8,128)S(1)} collective-permute-done((f32[3,64,128]{2,1,0:T(8,128)S(1)}, f32[3,64,128]{2,1,0:T(8,128)S(1)}, u32[]{:S(2)}, u32[]{:S(2)}) %collective-permute-start.9) | collective-permute-done | bytes 98336 | tf_op jit(solution)/shard_map/ppermute | solution.py:389
  54.7 4.6 %collective-permute-done.10.refs_4_ = f32[3,64,128]{2,1,0:T(8,128)S(1)} collective-permute-done((f32[3,64,128]{2,1,0:T(8,128)S(1)}, f32[3,64,128]{2,1,0:T(8,128)S(1)}, u32[]{:S(2)}, u32[]{:S(2)}) %collective-permute-start.10) | collective-permute-done | bytes 98336 | tf_op jit(solution)/shard_map/ppermute | solution.py:389
  59.3 1.9 %collective-permute-done.11.refs_5_ = f32[3,64,128]{2,1,0:T(8,128)S(1)} collective-permute-done((f32[3,64,128]{2,1,0:T(8,128)S(1)}, f32[3,64,128]{2,1,0:T(8,128)S(1)}, u32[]{:S(2)}, u32[]{:S(2)}) %collective-permute-start.11) | collective-permute-done | bytes 98336 | tf_op jit(solution)/shard_map/ppermute | solution.py:389
  61.2 1.2 %shard_map.125 = (f32[384,512]{1,0:T(8,128)S(1)}, bf16[128,512]{1,0:T(8,128)(2,1)S(1)}) custom-call(s32[8,512]{1,0:T(8,128)S(1)} %get-tuple-element.42.info_ref, f32[3,64,128]{2,1,0:T(8,128)S(1)} %get-tuple-element.58.refs_0_, f32[3,64,128]{2,1,0:T(8,128)S(1)} %collective-permute-done.7.refs_1_, f32[3,64,128]{2,1,0:T(8,128)S(1)} %collective-permute-done.8.refs_2_, ...), custom_call_target="tpu_custom_call" | custom-call | flops 10000000000 | bytes 10000000 | tf_op jit(solution)/shard_map/pallas_call | solution.py:472
  62.3 1.8 %collective-permute-done.13.refs_1_.refs_7_ = f32[3,64,128]{2,1,0:T(8,128)S(1)} collective-permute-done((f32[3,64,128]{2,1,0:T(8,128)S(1)}, f32[3,64,128]{2,1,0:T(8,128)S(1)}, u32[]{:S(2)}, u32[]{:S(2)}) %collective-permute-start.13) | collective-permute-done | bytes 98336 | tf_op jit(solution)/shard_map/ppermute | solution.py:389
  64.1 0.7 shard_map.126
  64.8 0.1 collective-permute-start.14
  64.9 1.8 %collective-permute-start.15 = (f32[3,64,128]{2,1,0:T(8,128)S(1)}, f32[3,64,128]{2,1,0:T(8,128)S(1)}, u32[]{:S(2)}, u32[]{:S(2)}) collective-permute-start(f32[3,64,128]{2,1,0:T(8,128)S(1)} %get-tuple-element.71), channel_id=1, source_target_pairs={{0,4},{1,5},{2,6},{3,7},{4,0},{5,1},{6,2},{7,3},{8,12},{9,13},{10,... | collective-permute-start | bytes 294920 | tf_op jit(solution)/shard_map/ppermute | solution.py:389
  66.7 0.1 collective-permute-start.20
  66.9 2.3 %collective-permute-start.21 = (f32[3,64,128]{2,1,0:T(8,128)S(1)}, f32[3,64,128]{2,1,0:T(8,128)S(1)}, u32[]{:S(2)}, u32[]{:S(2)}) collective-permute-start(f32[3,64,128]{2,1,0:T(8,128)S(1)} %get-tuple-element.76), channel_id=1, source_target_pairs={{0,6},{1,7},{2,4},{3,5},{4,2},{5,3},{6,0},{7,1},{8,14},{9,15},{10,... | collective-permute-start | bytes 294920 | tf_op jit(solution)/shard_map/ppermute | solution.py:389
  69.2 1.2 %collective-permute-start.22 = (f32[3,64,128]{2,1,0:T(8,128)S(1)}, f32[3,64,128]{2,1,0:T(8,128)S(1)}, u32[]{:S(2)}, u32[]{:S(2)}) collective-permute-start(f32[3,64,128]{2,1,0:T(8,128)S(1)} %get-tuple-element.77), channel_id=1, source_target_pairs={{0,7},{1,6},{2,5},{3,4},{4,3},{5,2},{6,1},{7,0},{8,15},{9,14},{10,... | collective-permute-start | bytes 294920 | tf_op jit(solution)/shard_map/ppermute | solution.py:389
  70.4 0.5 collective-permute-done.14.refs_8_.refs_5_
  70.9 1.8 %shard_map.127 = (f32[6,64,512]{2,1,0:T(8,128)}, f32[3,64]{1,0:T(4,128)S(1)}) custom-call(s32[8,512]{1,0:T(8,128)S(1)} %get-tuple-element.42.info_ref, s32[2,512]{1,0:T(2,128)S(1)} %copy-done.4, f32[6,64,512]{2,1,0:T(8,128)S(1)} %copy-done.3, f32[3,64,128]{2,1,0:T(8,128)S(1)} %get-tuple-element.58.refs_0_, f32[3,64,128]{2,1,0:T(8,128)S(1)} %collective-permute-done.7.refs_1_, ...), custom_call_target="tpu_custom_call" | custom-call | flops 10000000000 | bytes 10000000 | tf_op jit(solution)/shard_map/pallas_call | solution.py:488
  72.7 2.4 %collective-permute-start.16 = (f32[3,64,128]{2,1,0:T(8,128)S(1)}, f32[3,64,128]{2,1,0:T(8,128)S(1)}, u32[]{:S(2)}, u32[]{:S(2)}) collective-permute-start(f32[3,64,128]{2,1,0:T(8,128)S(1)} %get-tuple-element.72), channel_id=1, source_target_pairs={{0,5},{1,4},{2,7},{3,6},{4,1},{5,0},{6,3},{7,2},{8,13},{9,12},{10,... | collective-permute-start | bytes 294920 | tf_op jit(solution)/shard_map/ppermute | solution.py:389
  75.1 2.5 %collective-permute-start.19 = (f32[3,64]{1,0:T(4,128)S(1)}, f32[3,64]{1,0:T(4,128)S(1)}, u32[]{:S(2)}, u32[]{:S(2)}) collective-permute-start(f32[3,64]{1,0:T(4,128)S(1)} %get-tuple-element.73.refs_2_), channel_id=1, source_target_pairs={{0,24},{8,16},{16,8},{24,0},{1,25},{9,17},{17,9},{25,1},{2,26},{10... | collective-permute-start | bytes 2312 | tf_op jit(solution)/shard_map/ppermute | solution.py:397
  77.6 0.5 collective-permute-start.18
  78.1 1.2 %collective-permute-done.23.refs_4_ = f32[3,64,128]{2,1,0:T(8,128)S(1)} collective-permute-done((f32[3,64,128]{2,1,0:T(8,128)S(1)}, f32[3,64,128]{2,1,0:T(8,128)S(1)}, u32[]{:S(2)}, u32[]{:S(2)}) %collective-permute-start.23) | collective-permute-done | bytes 98336 | tf_op jit(solution)/shard_map/ppermute | solution.py:389
  79.3 1.5 %collective-permute-start.17 = (f32[3,64]{1,0:T(4,128)S(1)}, f32[3,64]{1,0:T(4,128)S(1)}, u32[]{:S(2)}, u32[]{:S(2)}) collective-permute-start(f32[3,64]{1,0:T(4,128)S(1)} %get-tuple-element.73.refs_2_), channel_id=1, source_target_pairs={{0,8},{8,0},{16,24},{24,16},{1,9},{9,1},{17,25},{25,17},{2,10},{10... | collective-permute-start | bytes 2312 | tf_op jit(solution)/shard_map/ppermute | solution.py:397
  80.8 1.2 %shard_map.128.refs_6_ = f32[6,512,128]{2,1,0:T(8,128)} custom-call(s32[1]{0:T(128)} %bitcast.me_ref, s32[8,512]{1,0:T(8,128)S(1)} %get-tuple-element.42.info_ref, f32[3,512,128]{2,1,0:T(8,128)S(1)} %get-tuple-element.70.solved_ref, f32[3,64,128]{2,1,0:T(8,128)S(1)} %get-tuple-element.74.refs_0_, f32[3,64,128]{2,1,0:T(8,128)S(1)} %collective-permute-done.20.refs_1_, ...), custom_call_target="tpu_custom_call" | custom-call | flops 10000000000 | bytes 10000000 | tf_op jit(solution)/shard_map/pallas_call | solution.py:498
  82.0 3.0 %collective-permute-done.16.refs_1_ = f32[3,64,128]{2,1,0:T(8,128)S(1)} collective-permute-done((f32[3,64,128]{2,1,0:T(8,128)S(1)}, f32[3,64,128]{2,1,0:T(8,128)S(1)}, u32[]{:S(2)}, u32[]{:S(2)}) %collective-permute-start.16) | collective-permute-done | bytes 98336 | tf_op jit(solution)/shard_map/ppermute | solution.py:389
  85.0 1.5 %shard_map.129 = (f32[6,512,128]{2,1,0:T(8,128)}, f32[3,64]{1,0:T(4,128)}) custom-call(s32[1]{0:T(128)} %bitcast.me_ref, s32[8,512]{1,0:T(8,128)S(1)} %get-tuple-element.42.info_ref, f32[3,512,128]{2,1,0:T(8,128)S(1)} %get-tuple-element.70.solved_ref, f32[3,64,128]{2,1,0:T(8,128)S(1)} %collective-permute-done.15.refs_0_, ...), custom_call_target="tpu_custom_call", output_to_operand_aliasing={{0}: (9, {})} | custom-call | flops 1000000000 | bytes 1000000 | tf_op jit(solution)/shard_map/pallas_call | solution.py:509
  (21 shorter events, 0.0 us)
Async XLA Ops:
  0.6 10.6 %copy-start = (f32[512,512]{1,0:T(8,128)S(1)}, f32[512,512]{1,0:T(8,128)}, u32[]{:S(2)}) copy-start(f32[512,512]{1,0:T(8,128)} %deriv_ref.1) | copy-start | bytes 3145732
  0.6 10.6 %copy-start.1 = (f32[512,512]{1,0:T(8,128)S(1)}, f32[512,512]{1,0:T(8,128)}, u32[]{:S(2)}) copy-start(f32[512,512]{1,0:T(8,128)} %inverse_ref.1) | copy-start | bytes 3145732
  0.7 10.6 %copy-start.2 = (f32[512,512]{1,0:T(8,128)S(1)}, f32[512,512]{1,0:T(8,128)}, u32[]{:S(2)}) copy-start(f32[512,512]{1,0:T(8,128)} %basis_ref.1) | copy-start | bytes 3145732
  0.7 10.5 %copy-start.5 = (f32[512]{0:T(512)S(1)}, f32[512]{0:T(512)}, u32[]{:S(2)}) copy-start(f32[512]{0:T(512)} %param.17) | copy-start | bytes 6148
  4.4 8.1 %collective-permute-start = (f32[2,3,64,128]{3,2,1,0:T(8,128)S(1)}, f32[2,3,64,128]{3,2,1,0:T(8,128)S(1)}, u32[]{:S(2)}, u32[]{:S(2)}) collective-permute-start(f32[2,3,64,128]{3,2,1,0:T(8,128)S(1)} %get-tuple-element.51), channel_id=1, source_target_pairs={{0,1},{1,0},{2,3},{3,2},{4,5},{5,4},{6,7},{7,6},{8,9},{9,8},{10,11... | collective-permute-start | bytes 589832 | tf_op jit(solution)/shard_map/ppermute | solution.py:389
  5.0 10.6 %collective-permute-start.1 = (f32[2,3,64,128]{3,2,1,0:T(8,128)S(1)}, f32[2,3,64,128]{3,2,1,0:T(8,128)S(1)}, u32[]{:S(2)}, u32[]{:S(2)}) collective-permute-start(f32[2,3,64,128]{3,2,1,0:T(8,128)S(1)} %get-tuple-element.52), channel_id=1, source_target_pairs={{0,6},{1,7},{2,4},{3,5},{4,2},{5,3},{6,0},{7,1},{8,14},{9,15},{10,... | collective-permute-start | bytes 589832 | tf_op jit(solution)/shard_map/ppermute | solution.py:389
  9.6 13.9 %collective-permute-start.2 = (f32[2,3,64,128]{3,2,1,0:T(8,128)S(1)}, f32[2,3,64,128]{3,2,1,0:T(8,128)S(1)}, u32[]{:S(2)}, u32[]{:S(2)}) collective-permute-start(f32[2,3,64,128]{3,2,1,0:T(8,128)S(1)} %get-tuple-element.53), channel_id=1, source_target_pairs={{0,7},{1,6},{2,5},{3,4},{4,3},{5,2},{6,1},{7,0},{8,15},{9,14},{10,... | collective-permute-start | bytes 589832 | tf_op jit(solution)/shard_map/ppermute | solution.py:389
  9.7 14.0 %collective-permute-start.3 = (f32[2,3,64,128]{3,2,1,0:T(8,128)S(1)}, f32[2,3,64,128]{3,2,1,0:T(8,128)S(1)}, u32[]{:S(2)}, u32[]{:S(2)}) collective-permute-start(f32[2,3,64,128]{3,2,1,0:T(8,128)S(1)} %get-tuple-element.54), channel_id=1, source_target_pairs={{0,2},{1,3},{2,0},{3,1},{4,6},{5,7},{6,4},{7,5},{8,10},{9,11},{10,... | collective-permute-start | bytes 589832 | tf_op jit(solution)/shard_map/ppermute | solution.py:389
  9.7 19.1 %collective-permute-start.4 = (f32[2,3,64,128]{3,2,1,0:T(8,128)S(1)}, f32[2,3,64,128]{3,2,1,0:T(8,128)S(1)}, u32[]{:S(2)}, u32[]{:S(2)}) collective-permute-start(f32[2,3,64,128]{3,2,1,0:T(8,128)S(1)} %get-tuple-element.55), channel_id=1, source_target_pairs={{0,3},{1,2},{2,1},{3,0},{4,7},{5,6},{6,5},{7,4},{8,11},{9,10},{10,... | collective-permute-start | bytes 589832 | tf_op jit(solution)/shard_map/ppermute | solution.py:389
  12.6 27.4 %collective-permute-start.5 = (f32[2,3,64,128]{3,2,1,0:T(8,128)S(1)}, f32[2,3,64,128]{3,2,1,0:T(8,128)S(1)}, u32[]{:S(2)}, u32[]{:S(2)}) collective-permute-start(f32[2,3,64,128]{3,2,1,0:T(8,128)S(1)} %get-tuple-element.56), channel_id=1, source_target_pairs={{0,4},{1,5},{2,6},{3,7},{4,0},{5,1},{6,2},{7,3},{8,12},{9,13},{10,... | collective-permute-start | bytes 589832 | tf_op jit(solution)/shard_map/ppermute | solution.py:389
  15.6 27.7 %collective-permute-start.6 = (f32[2,3,64,128]{3,2,1,0:T(8,128)S(1)}, f32[2,3,64,128]{3,2,1,0:T(8,128)S(1)}, u32[]{:S(2)}, u32[]{:S(2)}) collective-permute-start(f32[2,3,64,128]{3,2,1,0:T(8,128)S(1)} %get-tuple-element.57), channel_id=1, source_target_pairs={{0,5},{1,4},{2,7},{3,6},{4,1},{5,0},{6,3},{7,2},{8,13},{9,12},{10,... | collective-permute-start | bytes 589832 | tf_op jit(solution)/shard_map/ppermute | solution.py:389
  44.9 5.6 %collective-permute-start.7 = (f32[3,64,128]{2,1,0:T(8,128)S(1)}, f32[3,64,128]{2,1,0:T(8,128)S(1)}, u32[]{:S(2)}, u32[]{:S(2)}) collective-permute-start(f32[3,64,128]{2,1,0:T(8,128)S(1)} %get-tuple-element.59), channel_id=1, source_target_pairs={{0,1},{1,0},{2,3},{3,2},{4,5},{5,4},{6,7},{7,6},{8,9},{9,8},{10,11... | collective-permute-start | bytes 294920 | tf_op jit(solution)/shard_map/ppermute | solution.py:389
  45.2 6.9 %collective-permute-start.8 = (f32[3,64,128]{2,1,0:T(8,128)S(1)}, f32[3,64,128]{2,1,0:T(8,128)S(1)}, u32[]{:S(2)}, u32[]{:S(2)}) collective-permute-start(f32[3,64,128]{2,1,0:T(8,128)S(1)} %get-tuple-element.60), channel_id=1, source_target_pairs={{0,6},{1,7},{2,4},{3,5},{4,2},{5,3},{6,0},{7,1},{8,14},{9,15},{10,... | collective-permute-start | bytes 294920 | tf_op jit(solution)/shard_map/ppermute | solution.py:389
  47.8 6.9 %collective-permute-start.9 = (f32[3,64,128]{2,1,0:T(8,128)S(1)}, f32[3,64,128]{2,1,0:T(8,128)S(1)}, u32[]{:S(2)}, u32[]{:S(2)}) collective-permute-start(f32[3,64,128]{2,1,0:T(8,128)S(1)} %get-tuple-element.61), channel_id=1, source_target_pairs={{0,7},{1,6},{2,5},{3,4},{4,3},{5,2},{6,1},{7,0},{8,15},{9,14},{10,... | collective-permute-start | bytes 294920 | tf_op jit(solution)/shard_map/ppermute | solution.py:389
  48.6 10.7 %collective-permute-start.10 = (f32[3,64,128]{2,1,0:T(8,128)S(1)}, f32[3,64,128]{2,1,0:T(8,128)S(1)}, u32[]{:S(2)}, u32[]{:S(2)}) collective-permute-start(f32[3,64,128]{2,1,0:T(8,128)S(1)} %get-tuple-element.62), channel_id=1, source_target_pairs={{0,2},{1,3},{2,0},{3,1},{4,6},{5,7},{6,4},{7,5},{8,10},{9,11},{10,... | collective-permute-start | bytes 294920 | tf_op jit(solution)/shard_map/ppermute | solution.py:389
  48.6 12.5 %collective-permute-start.11 = (f32[3,64,128]{2,1,0:T(8,128)S(1)}, f32[3,64,128]{2,1,0:T(8,128)S(1)}, u32[]{:S(2)}, u32[]{:S(2)}) collective-permute-start(f32[3,64,128]{2,1,0:T(8,128)S(1)} %get-tuple-element.63), channel_id=1, source_target_pairs={{0,3},{1,2},{2,1},{3,0},{4,7},{5,6},{6,5},{7,4},{8,11},{9,10},{10,... | collective-permute-start | bytes 294920 | tf_op jit(solution)/shard_map/ppermute | solution.py:389
  50.5 11.8 %collective-permute-start.12 = (f32[3,64,128]{2,1,0:T(8,128)S(1)}, f32[3,64,128]{2,1,0:T(8,128)S(1)}, u32[]{:S(2)}, u32[]{:S(2)}) collective-permute-start(f32[3,64,128]{2,1,0:T(8,128)S(1)} %get-tuple-element.64), channel_id=1, source_target_pairs={{0,4},{1,5},{2,6},{3,7},{4,0},{5,1},{6,2},{7,3},{8,12},{9,13},{10,... | collective-permute-start | bytes 294920 | tf_op jit(solution)/shard_map/ppermute | solution.py:389
  52.1 12.0 %collective-permute-start.13 = (f32[3,64,128]{2,1,0:T(8,128)S(1)}, f32[3,64,128]{2,1,0:T(8,128)S(1)}, u32[]{:S(2)}, u32[]{:S(2)}) collective-permute-start(f32[3,64,128]{2,1,0:T(8,128)S(1)} %get-tuple-element.65), channel_id=1, source_target_pairs={{0,5},{1,4},{2,7},{3,6},{4,1},{5,0},{6,3},{7,2},{8,13},{9,12},{10,... | collective-permute-start | bytes 294920 | tf_op jit(solution)/shard_map/ppermute | solution.py:389
  64.1 6.8 %copy-start.3 = (f32[6,64,512]{2,1,0:T(8,128)S(1)}, f32[6,64,512]{2,1,0:T(8,128)}, u32[]{:S(2)}) copy-start(f32[6,64,512]{2,1,0:T(8,128)} %velocity_ref.1) | copy-start | bytes 2359300
  64.1 6.8 %copy-start.4 = (s32[2,512]{1,0:T(2,128)S(1)}, s32[2,512]{1,0:T(2,128)}, u32[]{:S(2)}) copy-start(s32[2,512]{1,0:T(2,128)} %modes_ref.1) | copy-start | bytes 12292
  64.8 6.1 %collective-permute-start.14 = (f32[3,64,128]{2,1,0:T(8,128)S(1)}, f32[3,64,128]{2,1,0:T(8,128)S(1)}, u32[]{:S(2)}, u32[]{:S(2)}) collective-permute-start(f32[3,64,128]{2,1,0:T(8,128)S(1)} %get-tuple-element.68), channel_id=1, source_target_pairs={{0,3},{1,2},{2,1},{3,0},{4,7},{5,6},{6,5},{7,4},{8,11},{9,10},{10,... | collective-permute-start | bytes 294920 | tf_op jit(solution)/shard_map/ppermute | solution.py:389
  64.9 17.1 %collective-permute-start.15 = (f32[3,64,128]{2,1,0:T(8,128)S(1)}, f32[3,64,128]{2,1,0:T(8,128)S(1)}, u32[]{:S(2)}, u32[]{:S(2)}) collective-permute-start(f32[3,64,128]{2,1,0:T(8,128)S(1)} %get-tuple-element.71), channel_id=1, source_target_pairs={{0,4},{1,5},{2,6},{3,7},{4,0},{5,1},{6,2},{7,3},{8,12},{9,13},{10,... | collective-permute-start | bytes 294920 | tf_op jit(solution)/shard_map/ppermute | solution.py:389
  66.7 6.0 %collective-permute-start.20 = (f32[3,64,128]{2,1,0:T(8,128)S(1)}, f32[3,64,128]{2,1,0:T(8,128)S(1)}, u32[]{:S(2)}, u32[]{:S(2)}) collective-permute-start(f32[3,64,128]{2,1,0:T(8,128)S(1)} %get-tuple-element.75), channel_id=1, source_target_pairs={{0,1},{1,0},{2,3},{3,2},{4,5},{5,4},{6,7},{7,6},{8,9},{9,8},{10,11... | collective-permute-start | bytes 294920 | tf_op jit(solution)/shard_map/ppermute | solution.py:389
  66.9 8.2 %collective-permute-start.21 = (f32[3,64,128]{2,1,0:T(8,128)S(1)}, f32[3,64,128]{2,1,0:T(8,128)S(1)}, u32[]{:S(2)}, u32[]{:S(2)}) collective-permute-start(f32[3,64,128]{2,1,0:T(8,128)S(1)} %get-tuple-element.76), channel_id=1, source_target_pairs={{0,6},{1,7},{2,4},{3,5},{4,2},{5,3},{6,0},{7,1},{8,14},{9,15},{10,... | collective-permute-start | bytes 294920 | tf_op jit(solution)/shard_map/ppermute | solution.py:389
  69.2 8.4 %collective-permute-start.22 = (f32[3,64,128]{2,1,0:T(8,128)S(1)}, f32[3,64,128]{2,1,0:T(8,128)S(1)}, u32[]{:S(2)}, u32[]{:S(2)}) collective-permute-start(f32[3,64,128]{2,1,0:T(8,128)S(1)} %get-tuple-element.77), channel_id=1, source_target_pairs={{0,7},{1,6},{2,5},{3,4},{4,3},{5,2},{6,1},{7,0},{8,15},{9,14},{10,... | collective-permute-start | bytes 294920 | tf_op jit(solution)/shard_map/ppermute | solution.py:389
  70.9 8.4 %collective-permute-start.23 = (f32[3,64,128]{2,1,0:T(8,128)S(1)}, f32[3,64,128]{2,1,0:T(8,128)S(1)}, u32[]{:S(2)}, u32[]{:S(2)}) collective-permute-start(f32[3,64,128]{2,1,0:T(8,128)S(1)} %get-tuple-element.78), channel_id=1, source_target_pairs={{0,2},{1,3},{2,0},{3,1},{4,6},{5,7},{6,4},{7,5},{8,10},{9,11},{10,... | collective-permute-start | bytes 294920 | tf_op jit(solution)/shard_map/ppermute | solution.py:389
  72.7 12.3 %collective-permute-start.16 = (f32[3,64,128]{2,1,0:T(8,128)S(1)}, f32[3,64,128]{2,1,0:T(8,128)S(1)}, u32[]{:S(2)}, u32[]{:S(2)}) collective-permute-start(f32[3,64,128]{2,1,0:T(8,128)S(1)} %get-tuple-element.72), channel_id=1, source_target_pairs={{0,5},{1,4},{2,7},{3,6},{4,1},{5,0},{6,3},{7,2},{8,13},{9,12},{10,... | collective-permute-start | bytes 294920 | tf_op jit(solution)/shard_map/ppermute | solution.py:389
  75.1 9.9 %collective-permute-start.19 = (f32[3,64]{1,0:T(4,128)S(1)}, f32[3,64]{1,0:T(4,128)S(1)}, u32[]{:S(2)}, u32[]{:S(2)}) collective-permute-start(f32[3,64]{1,0:T(4,128)S(1)} %get-tuple-element.73.refs_2_), channel_id=1, source_target_pairs={{0,24},{8,16},{16,8},{24,0},{1,25},{9,17},{17,9},{25,1},{2,26},{10... | collective-permute-start | bytes 2312 | tf_op jit(solution)/shard_map/ppermute | solution.py:397
  77.6 7.5 %collective-permute-start.18 = (f32[3,64]{1,0:T(4,128)S(1)}, f32[3,64]{1,0:T(4,128)S(1)}, u32[]{:S(2)}, u32[]{:S(2)}) collective-permute-start(f32[3,64]{1,0:T(4,128)S(1)} %get-tuple-element.73.refs_2_), channel_id=1, source_target_pairs={{0,16},{8,24},{16,0},{24,8},{1,17},{9,25},{17,1},{25,9},{2,18},{10... | collective-permute-start | bytes 2312 | tf_op jit(solution)/shard_map/ppermute | solution.py:397
  79.3 5.7 %collective-permute-start.17 = (f32[3,64]{1,0:T(4,128)S(1)}, f32[3,64]{1,0:T(4,128)S(1)}, u32[]{:S(2)}, u32[]{:S(2)}) collective-permute-start(f32[3,64]{1,0:T(4,128)S(1)} %get-tuple-element.73.refs_2_), channel_id=1, source_target_pairs={{0,8},{8,0},{16,24},{24,16},{1,9},{9,1},{17,25},{25,17},{2,10},{10... | collective-permute-start | bytes 2312 | tf_op jit(solution)/shard_map/ppermute | solution.py:397

commit v10 on v9

--- a/solution.py
+++ b/solution.py
@@ -359,13 +359,13 @@
     assemble(me_ref[0], steps, unused(info_ref, share), solved_ref, in_refs, out_hbm, rows_ref, sems)
 
 
-def assemble_late_kernel(steps, terms, me_ref, info_ref, solved_ref, *refs):
+def assemble_late_kernel(steps, me_ref, info_ref, solved_ref, *refs):
     in_refs, refs = refs[: len(steps)], refs[len(steps) :]
-    parts, (_, out_hbm, emf_ref, rows_ref, sems) = refs[:terms], refs[terms:]
-    parts = [ref[...] for ref in parts]
-    while len(parts) > 1:
-        parts = [parts[at] + parts[at + 1] for at in range(0, len(parts), 2)]
-    emf_ref[...] = parts[0]
+    terms_ref, _, out_hbm, emf_ref, rows_ref, sems = refs
+    emf = terms_ref[0]
+    for group in range(1, terms_ref.shape[0]):
+        emf = emf + terms_ref[group]
+    emf_ref[...] = emf
     share = in_refs[0].shape[2] // 2
     assemble(me_ref[0], steps, unused(info_ref, share), solved_ref, in_refs, out_hbm, rows_ref, sems)
 
@@ -388,13 +388,6 @@
     return [
         block if step == 0 else lax.ppermute(block, "col", [(i, i ^ step) for i in range(devices)])
         for step, block in zip(steps, blocks)
-    ]
-
-
-def from_groups(value):
-    groups = lax.axis_size("grp")
-    return [value] + [
-        lax.ppermute(value, "grp", [(i, i ^ step) for i in range(groups)]) for step in range(1, groups)
     ]
 
 
@@ -493,7 +486,7 @@
         HEAVY,
         [pltpu.VMEM(state_now.shape, F32), pltpu.SemaphoreType.DMA],
     )(info, kept_modes, velocity, *returned, extra[early.index(3)])
-    terms = from_groups(emf)
+    terms = lax.all_gather(emf, "grp")
 
     owned = call(
         functools.partial(assemble_early_kernel, early),
@@ -507,14 +500,14 @@
         ],
     )(me, info, solved, *extra[:split])
     owned, mean_emf = call(
-        functools.partial(assemble_late_kernel, late, len(terms)),
+        functools.partial(assemble_late_kernel, late),
         [shaped((comps, depth, lanes)), shaped((3, points))],
-        [SCALAR] + [LOCAL] * (2 + len(late) + len(terms)) + [FAR],
+        [SCALAR] + [LOCAL] * (3 + len(late)) + [FAR],
         [FAR, LOCAL],
         1,
         [pltpu.VMEM((comps, late_rows, lanes), F32), pltpu.SemaphoreType.DMA((comps,))],
-        aliases={3 + len(late) + len(terms): 0},
-    )(me, info, solved, *extra[split:], *terms, owned)
+        aliases={4 + len(late): 0},
+    )(me, info, solved, *extra[split:], terms, owned)
     return (state_next, owned, mean_emf)
 
 

time: 87.8 us -> 91.4 us (1.041)
  blocking collectives: 0 us -> 8.07 us
  starting transfers between devices: 37.8 us -> 33.3 us
    all_gather x0 -> x1, blocking collectives: none -> 8.07 us  [on_device(): terms = lax.all_gather(emf, 'grp')]
    ppermute x3 -> x0, starting transfers between devices: 4.45 us -> none  [from_groups(): lax.ppermute(value, 'grp', [(i, i ^ step) for i in range(groups)])]
  transfers between devices with their start and end apart: 24 -> 21, of which waited for: 13 -> 13; matrix products, arithmetic and copies ran while one was open for 0% -> 0% of each run, Pallas kernels for 8% -> 8%
where the time goes in v10:
time: 91.4 us; the launch traced here: 90.1 us
  waiting for transfers between devices  33.4 us (37%)
  starting transfers between devices  33.3 us (36%)
  Pallas kernels  14.4 us (16%)
  blocking collectives  8.07 us (9%)
    ppermute x21, waiting for transfers between devices, exchange(): lax.ppermute(block, 'col', [(i, i ^ step) for i in range(devices)])  33.4 us
    ppermute x21, starting transfers between devices, exchange(): lax.ppermute(block, 'col', [(i, i ^ step) for i in range(devices)])  33.3 us
    all_gather x1, blocking collectives, on_device(): terms = lax.all_gather(emf, 'grp')  8.07 us
    pallas_call x1, Pallas kernels, on_device(): call(functools.partial(first_kernel, devices), [shaped((8, columns), jnp....  3.76 us
    pallas_call x1, Pallas kernels, on_device(): call(functools.partial(state_kernel, steps), [shaped(state_now.shape), sh...  1.83 us
  transfers between devices with their start and end apart: 21, of which 13 were waited for; matrix products, arithmetic and copies ran while one was open for 0% of the time, Pallas kernels for 8%

profile of v10, /device:TPU:0, one launch (start us, length us, event | category | flops | bytes accessed | tf_op | source)
XLA Modules:
  0.0 90.1 jit_solution(15917090101315094347)
XLA Ops:
  0.7 3.8 %shard_map.121 = (s32[8,512]{1,0:T(8,128)S(1)}, f32[8,128]{1,0:T(8,128)S(1)}, f32[2,3,64,128]{3,2,1,0:T(8,128)S(1)}, f32[2,3,64,128]{3,2,1,0:T(8,128)S(1)}, f32[...) custom-call(s32[1]{0:T(128)} %bitcast.me_ref, ...), custom_call_target="tpu_custom_call" | custom-call | flops 1000000000 | bytes 1000000 | tf_op jit(solution)/shard_map/pallas_call | solution.py:423
  4.4 0.5 collective-permute-start
  5.0 4.7 %collective-permute-start.1 = (f32[2,3,64,128]{3,2,1,0:T(8,128)S(1)}, f32[2,3,64,128]{3,2,1,0:T(8,128)S(1)}, u32[]{:S(2)}, u32[]{:S(2)}) collective-permute-start(f32[2,3,64,128]{3,2,1,0:T(8,128)S(1)} %get-tuple-element.52), channel_id=1, source_target_pairs={{0,6},{1,7},{2,4},{3,5},{4,2},{5,3},{6,0},{7,1},{8,14},{9,15},{10,... | collective-permute-start | bytes 589832 | tf_op jit(solution)/shard_map/ppermute | solution.py:389
  9.6 0.1 collective-permute-start.2
  9.7 0.0 collective-permute-start.3
  9.7 1.5 %collective-permute-start.4 = (f32[2,3,64,128]{3,2,1,0:T(8,128)S(1)}, f32[2,3,64,128]{3,2,1,0:T(8,128)S(1)}, u32[]{:S(2)}, u32[]{:S(2)}) collective-permute-start(f32[2,3,64,128]{3,2,1,0:T(8,128)S(1)} %get-tuple-element.55), channel_id=1, source_target_pairs={{0,3},{1,2},{2,1},{3,0},{4,7},{5,6},{6,5},{7,4},{8,11},{9,10},{10,... | collective-permute-start | bytes 589832 | tf_op jit(solution)/shard_map/ppermute | solution.py:389
  11.2 1.4 %shard_map.122 = (bf16[512,512]{1,0:T(8,128)(2,1)S(1)}, bf16[512,512]{1,0:T(8,128)(2,1)S(1)}, bf16[512,512]{1,0:T(8,128)(2,1)S(1)}, bf16[512,512]{1,0:T(8,128)(2...) custom-call(f32[512,512]{1,0:T(8,128)S(1)} %copy-done, f32[512,512]{1,0:T(8,128)S(1)} %copy-done.1, ...), custom_call_target="tpu_custom_call" | custom-call | flops 10000000000 | bytes 10000000 | tf_op jit(solution)/shard_map/pallas_call | solution.py:437
  12.6 0.0 collective-permute-done.refs_5_
  12.6 2.7 %collective-permute-start.5 = (f32[2,3,64,128]{3,2,1,0:T(8,128)S(1)}, f32[2,3,64,128]{3,2,1,0:T(8,128)S(1)}, u32[]{:S(2)}, u32[]{:S(2)}) collective-permute-start(f32[2,3,64,128]{3,2,1,0:T(8,128)S(1)} %get-tuple-element.56), channel_id=1, source_target_pairs={{0,4},{1,5},{2,6},{3,7},{4,0},{5,1},{6,2},{7,3},{8,12},{9,13},{10,... | collective-permute-start | bytes 589832 | tf_op jit(solution)/shard_map/ppermute | solution.py:389
  15.3 0.3 collective-permute-done.1.refs_6_
  15.6 8.0 %collective-permute-start.6 = (f32[2,3,64,128]{3,2,1,0:T(8,128)S(1)}, f32[2,3,64,128]{3,2,1,0:T(8,128)S(1)}, u32[]{:S(2)}, u32[]{:S(2)}) collective-permute-start(f32[2,3,64,128]{3,2,1,0:T(8,128)S(1)} %get-tuple-element.57), channel_id=1, source_target_pairs={{0,5},{1,4},{2,7},{3,6},{4,1},{5,0},{6,3},{7,2},{8,13},{9,12},{10,... | collective-permute-start | bytes 589832 | tf_op jit(solution)/shard_map/ppermute | solution.py:389
  23.6 0.0 collective-permute-done.2.refs_7_
  23.6 0.2 collective-permute-done.3.refs_8_
  23.7 5.1 %collective-permute-done.4.refs_9_ = f32[2,3,64,128]{3,2,1,0:T(8,128)S(1)} collective-permute-done((f32[2,3,64,128]{3,2,1,0:T(8,128)S(1)}, f32[2,3,64,128]{3,2,1,0:T(8,128)S(1)}, u32[]{:S(2)}, u32[]{:S(2)}) %collective-permute-start.4) | collective-permute-done | bytes 196640 | tf_op jit(solution)/shard_map/ppermute | solution.py:389
  28.8 1.4 %shard_map.123.early_ref = f32[512,384]{1,0:T(8,128)S(1)} custom-call(s32[1]{0:T(128)} %bitcast.me_ref, bf16[512,512]{1,0:T(8,128)(2,1)S(1)} %get-tuple-element.46.refs_0_, bf16[512,512]{1,0:T(8,128)(2,1)S(1)} %get-tuple-element.47.refs_1_, bf16[512,512]{1,0:T(8,128)(2,1)S(1)} %get-tuple-element.48.refs_2_, bf16[512,512]{1,0:T(8,128)(2,1)S(1)} %get-tuple-element.49.refs_3_, ...), custom_call_target="tpu_custom_call" | custom-call | flops 10000000000 | bytes 10000000 | tf_op jit(solution)/shard_map/pallas_call | solution.py:446
  30.2 9.8 %collective-permute-done.5.refs_4_ = f32[2,3,64,128]{3,2,1,0:T(8,128)S(1)} collective-permute-done((f32[2,3,64,128]{3,2,1,0:T(8,128)S(1)}, f32[2,3,64,128]{3,2,1,0:T(8,128)S(1)}, u32[]{:S(2)}, u32[]{:S(2)}) %collective-permute-start.5) | collective-permute-done | bytes 196640 | tf_op jit(solution)/shard_map/ppermute | solution.py:389
  40.0 3.3 %collective-permute-done.6.refs_5_ = f32[2,3,64,128]{3,2,1,0:T(8,128)S(1)} collective-permute-done((f32[2,3,64,128]{3,2,1,0:T(8,128)S(1)}, f32[2,3,64,128]{3,2,1,0:T(8,128)S(1)}, u32[]{:S(2)}, u32[]{:S(2)}) %collective-permute-start.6) | collective-permute-done | bytes 196640 | tf_op jit(solution)/shard_map/ppermute | solution.py:389
  43.3 1.6 %shard_map.124 = (f32[3,64,128]{2,1,0:T(8,128)S(1)}, f32[3,64,128]{2,1,0:T(8,128)S(1)}, f32[3,64,128]{2,1,0:T(8,128)S(1)}, f32[3,64,128]{2,1,0:T(8,128)S(1)}, f3...) custom-call(s32[1]{0:T(128)} %bitcast.me_ref, ...), custom_call_target="tpu_custom_call" | custom-call | flops 1000000000 | bytes 1000000 | tf_op jit(solution)/shard_map/pallas_call | solution.py:454
  44.9 0.3 collective-permute-start.7
  45.2 2.5 %collective-permute-start.8 = (f32[3,64,128]{2,1,0:T(8,128)S(1)}, f32[3,64,128]{2,1,0:T(8,128)S(1)}, u32[]{:S(2)}, u32[]{:S(2)}) collective-permute-start(f32[3,64,128]{2,1,0:T(8,128)S(1)} %get-tuple-element.60), channel_id=1, source_target_pairs={{0,6},{1,7},{2,4},{3,5},{4,2},{5,3},{6,0},{7,1},{8,14},{9,15},{10,... | collective-permute-start | bytes 294920 | tf_op jit(solution)/shard_map/ppermute | solution.py:389
  47.8 0.9 collective-permute-start.9
  48.6 0.0 collective-permute-start.10
  48.6 1.9 %collective-permute-start.11 = (f32[3,64,128]{2,1,0:T(8,128)S(1)}, f32[3,64,128]{2,1,0:T(8,128)S(1)}, u32[]{:S(2)}, u32[]{:S(2)}) collective-permute-start(f32[3,64,128]{2,1,0:T(8,128)S(1)} %get-tuple-element.63), channel_id=1, source_target_pairs={{0,3},{1,2},{2,1},{3,0},{4,7},{5,6},{6,5},{7,4},{8,11},{9,10},{10,... | collective-permute-start | bytes 294920 | tf_op jit(solution)/shard_map/ppermute | solution.py:389
  50.5 0.0 collective-permute-done.7.refs_1_
  50.5 1.4 %collective-permute-start.12 = (f32[3,64,128]{2,1,0:T(8,128)S(1)}, f32[3,64,128]{2,1,0:T(8,128)S(1)}, u32[]{:S(2)}, u32[]{:S(2)}) collective-permute-start(f32[3,64,128]{2,1,0:T(8,128)S(1)} %get-tuple-element.64), channel_id=1, source_target_pairs={{0,4},{1,5},{2,6},{3,7},{4,0},{5,1},{6,2},{7,3},{8,12},{9,13},{10,... | collective-permute-start | bytes 294920 | tf_op jit(solution)/shard_map/ppermute | solution.py:389
  51.9 0.2 collective-permute-done.8.refs_2_
  52.1 0.9 %collective-permute-start.13 = (f32[3,64,128]{2,1,0:T(8,128)S(1)}, f32[3,64,128]{2,1,0:T(8,128)S(1)}, u32[]{:S(2)}, u32[]{:S(2)}) collective-permute-start(f32[3,64,128]{2,1,0:T(8,128)S(1)} %get-tuple-element.65), channel_id=1, source_target_pairs={{0,5},{1,4},{2,7},{3,6},{4,1},{5,0},{6,3},{7,2},{8,13},{9,12},{10,... | collective-permute-start | bytes 294920 | tf_op jit(solution)/shard_map/ppermute | solution.py:389
  53.0 1.7 %collective-permute-done.9.refs_3_ = f32[3,64,128]{2,1,0:T(8,128)S(1)} collective-permute-done((f32[3,64,128]{2,1,0:T(8,128)S(1)}, f32[3,64,128]{2,1,0:T(8,128)S(1)}, u32[]{:S(2)}, u32[]{:S(2)}) %collective-permute-start.9) | collective-permute-done | bytes 98336 | tf_op jit(solution)/shard_map/ppermute | solution.py:389
  54.7 4.6 %collective-permute-done.10.refs_4_ = f32[3,64,128]{2,1,0:T(8,128)S(1)} collective-permute-done((f32[3,64,128]{2,1,0:T(8,128)S(1)}, f32[3,64,128]{2,1,0:T(8,128)S(1)}, u32[]{:S(2)}, u32[]{:S(2)}) %collective-permute-start.10) | collective-permute-done | bytes 98336 | tf_op jit(solution)/shard_map/ppermute | solution.py:389
  59.3 1.9 %collective-permute-done.11.refs_5_ = f32[3,64,128]{2,1,0:T(8,128)S(1)} collective-permute-done((f32[3,64,128]{2,1,0:T(8,128)S(1)}, f32[3,64,128]{2,1,0:T(8,128)S(1)}, u32[]{:S(2)}, u32[]{:S(2)}) %collective-permute-start.11) | collective-permute-done | bytes 98336 | tf_op jit(solution)/shard_map/ppermute | solution.py:389
  61.2 1.2 %shard_map.125 = (f32[384,512]{1,0:T(8,128)S(1)}, bf16[128,512]{1,0:T(8,128)(2,1)S(1)}) custom-call(s32[8,512]{1,0:T(8,128)S(1)} %get-tuple-element.42.info_ref, f32[3,64,128]{2,1,0:T(8,128)S(1)} %get-tuple-element.58.refs_0_, f32[3,64,128]{2,1,0:T(8,128)S(1)} %collective-permute-done.7.refs_1_, f32[3,64,128]{2,1,0:T(8,128)S(1)} %collective-permute-done.8.refs_2_, ...), custom_call_target="tpu_custom_call" | custom-call | flops 10000000000 | bytes 10000000 | tf_op jit(solution)/shard_map/pallas_call | solution.py:465
  62.3 0.0 collective-permute-done.12.refs_0_.refs_6_
  62.3 1.8 %collective-permute-done.13.refs_1_.refs_7_ = f32[3,64,128]{2,1,0:T(8,128)S(1)} collective-permute-done((f32[3,64,128]{2,1,0:T(8,128)S(1)}, f32[3,64,128]{2,1,0:T(8,128)S(1)}, u32[]{:S(2)}, u32[]{:S(2)}) %collective-permute-start.13) | collective-permute-done | bytes 98336 | tf_op jit(solution)/shard_map/ppermute | solution.py:389
  64.1 0.7 shard_map.126
  64.8 0.1 collective-permute-start.14
  64.9 1.8 %collective-permute-start.15 = (f32[3,64,128]{2,1,0:T(8,128)S(1)}, f32[3,64,128]{2,1,0:T(8,128)S(1)}, u32[]{:S(2)}, u32[]{:S(2)}) collective-permute-start(f32[3,64,128]{2,1,0:T(8,128)S(1)} %get-tuple-element.71), channel_id=1, source_target_pairs={{0,4},{1,5},{2,6},{3,7},{4,0},{5,1},{6,2},{7,3},{8,12},{9,13},{10,... | collective-permute-start | bytes 294920 | tf_op jit(solution)/shard_map/ppermute | solution.py:389
  66.7 0.1 collective-permute-start.17
  66.9 2.3 %collective-permute-start.18 = (f32[3,64,128]{2,1,0:T(8,128)S(1)}, f32[3,64,128]{2,1,0:T(8,128)S(1)}, u32[]{:S(2)}, u32[]{:S(2)}) collective-permute-start(f32[3,64,128]{2,1,0:T(8,128)S(1)} %get-tuple-element.76), channel_id=1, source_target_pairs={{0,6},{1,7},{2,4},{3,5},{4,2},{5,3},{6,0},{7,1},{8,14},{9,15},{10,... | collective-permute-start | bytes 294920 | tf_op jit(solution)/shard_map/ppermute | solution.py:389
  69.2 1.2 %collective-permute-start.19 = (f32[3,64,128]{2,1,0:T(8,128)S(1)}, f32[3,64,128]{2,1,0:T(8,128)S(1)}, u32[]{:S(2)}, u32[]{:S(2)}) collective-permute-start(f32[3,64,128]{2,1,0:T(8,128)S(1)} %get-tuple-element.77), channel_id=1, source_target_pairs={{0,7},{1,6},{2,5},{3,4},{4,3},{5,2},{6,1},{7,0},{8,15},{9,14},{10,... | collective-permute-start | bytes 294920 | tf_op jit(solution)/shard_map/ppermute | solution.py:389
  70.4 0.5 collective-permute-done.14.refs_8_.refs_5_
  70.9 1.8 %shard_map.127 = (f32[6,64,512]{2,1,0:T(8,128)}, f32[3,64]{1,0:T(4,128)S(1)}) custom-call(s32[8,512]{1,0:T(8,128)S(1)} %get-tuple-element.42.info_ref, s32[2,512]{1,0:T(2,128)S(1)} %copy-done.4, f32[6,64,512]{2,1,0:T(8,128)S(1)} %copy-done.3, f32[3,64,128]{2,1,0:T(8,128)S(1)} %get-tuple-element.58.refs_0_, f32[3,64,128]{2,1,0:T(8,128)S(1)} %collective-permute-done.7.refs_1_, ...), custom_call_target="tpu_custom_call" | custom-call | flops 10000000000 | bytes 10000000 | tf_op jit(solution)/shard_map/pallas_call | solution.py:481
  72.7 2.4 %collective-permute-start.16 = (f32[3,64,128]{2,1,0:T(8,128)S(1)}, f32[3,64,128]{2,1,0:T(8,128)S(1)}, u32[]{:S(2)}, u32[]{:S(2)}) collective-permute-start(f32[3,64,128]{2,1,0:T(8,128)S(1)} %get-tuple-element.72), channel_id=1, source_target_pairs={{0,5},{1,4},{2,7},{3,6},{4,1},{5,0},{6,3},{7,2},{8,13},{9,12},{10,... | collective-permute-start | bytes 294920 | tf_op jit(solution)/shard_map/ppermute | solution.py:389
  75.1 1.2 %collective-permute-done.19.refs_3_ = f32[3,64,128]{2,1,0:T(8,128)S(1)} collective-permute-done((f32[3,64,128]{2,1,0:T(8,128)S(1)}, f32[3,64,128]{2,1,0:T(8,128)S(1)}, u32[]{:S(2)}, u32[]{:S(2)}) %collective-permute-start.19) | collective-permute-done | bytes 98336 | tf_op jit(solution)/shard_map/ppermute | solution.py:389
  76.3 3.0 %collective-permute-done.20.refs_4_ = f32[3,64,128]{2,1,0:T(8,128)S(1)} collective-permute-done((f32[3,64,128]{2,1,0:T(8,128)S(1)}, f32[3,64,128]{2,1,0:T(8,128)S(1)}, u32[]{:S(2)}, u32[]{:S(2)}) %collective-permute-start.20) | collective-permute-done | bytes 98336 | tf_op jit(solution)/shard_map/ppermute | solution.py:389
  79.3 1.2 %shard_map.128.refs_3_ = f32[6,512,128]{2,1,0:T(8,128)} custom-call(s32[1]{0:T(128)} %bitcast.me_ref, s32[8,512]{1,0:T(8,128)S(1)} %get-tuple-element.42.info_ref, f32[3,512,128]{2,1,0:T(8,128)S(1)} %get-tuple-element.70.solved_ref, f32[3,64,128]{2,1,0:T(8,128)S(1)} %get-tuple-element.74.refs_0_, f32[3,64,128]{2,1,0:T(8,128)S(1)} %collective-permute-done.17.refs_1_, ...), custom_call_target="tpu_custom_call" | custom-call | flops 10000000000 | bytes 10000000 | tf_op jit(solution)/shard_map/pallas_call | solution.py:491
  80.5 8.1 %all-gather.1.refs_2_ = f32[4,3,64]{2,1,0:T(4,128)S(1)} all-gather(f32[1,3,64]{2,1,0:T(4,128)S(1)} %bitcast.4), channel_id=2, replica_groups=mesh['grp'=4,'col'=8] {'grp'}, dimensions={0}, use_global_device_ids=true | all-gather | bytes 3840 | tf_op jit(solution)/shard_map/all_gather | solution.py:489
  88.6 0.0 collective-permute-done.15.refs_0_
  88.6 1.5 %shard_map.129 = (f32[6,512,128]{2,1,0:T(8,128)}, f32[3,64]{1,0:T(4,128)}) custom-call(s32[1]{0:T(128)} %bitcast.me_ref, s32[8,512]{1,0:T(8,128)S(1)} %get-tuple-element.42.info_ref, f32[3,512,128]{2,1,0:T(8,128)S(1)} %get-tuple-element.70.solved_ref, f32[3,64,128]{2,1,0:T(8,128)S(1)} %collective-permute-done.15.refs_0_, ...), custom_call_target="tpu_custom_call", output_to_operand_aliasing={{0}: (6, {})} | custom-call | flops 1000000000 | bytes 1000000 | tf_op jit(solution)/shard_map/pallas_call | solution.py:502
  (16 shorter events, 0.0 us)
Async XLA Ops:
  0.6 10.6 %copy-start = (f32[512,512]{1,0:T(8,128)S(1)}, f32[512,512]{1,0:T(8,128)}, u32[]{:S(2)}) copy-start(f32[512,512]{1,0:T(8,128)} %deriv_ref.1) | copy-start | bytes 3145732
  0.6 10.6 %copy-start.1 = (f32[512,512]{1,0:T(8,128)S(1)}, f32[512,512]{1,0:T(8,128)}, u32[]{:S(2)}) copy-start(f32[512,512]{1,0:T(8,128)} %inverse_ref.1) | copy-start | bytes 3145732
  0.7 10.6 %copy-start.2 = (f32[512,512]{1,0:T(8,128)S(1)}, f32[512,512]{1,0:T(8,128)}, u32[]{:S(2)}) copy-start(f32[512,512]{1,0:T(8,128)} %basis_ref.1) | copy-start | bytes 3145732
  0.7 10.5 %copy-start.5 = (f32[512]{0:T(512)S(1)}, f32[512]{0:T(512)}, u32[]{:S(2)}) copy-start(f32[512]{0:T(512)} %param.17) | copy-start | bytes 6148
  4.4 8.1 %collective-permute-start = (f32[2,3,64,128]{3,2,1,0:T(8,128)S(1)}, f32[2,3,64,128]{3,2,1,0:T(8,128)S(1)}, u32[]{:S(2)}, u32[]{:S(2)}) collective-permute-start(f32[2,3,64,128]{3,2,1,0:T(8,128)S(1)} %get-tuple-element.51), channel_id=1, source_target_pairs={{0,1},{1,0},{2,3},{3,2},{4,5},{5,4},{6,7},{7,6},{8,9},{9,8},{10,11... | collective-permute-start | bytes 589832 | tf_op jit(solution)/shard_map/ppermute | solution.py:389
  5.0 10.6 %collective-permute-start.1 = (f32[2,3,64,128]{3,2,1,0:T(8,128)S(1)}, f32[2,3,64,128]{3,2,1,0:T(8,128)S(1)}, u32[]{:S(2)}, u32[]{:S(2)}) collective-permute-start(f32[2,3,64,128]{3,2,1,0:T(8,128)S(1)} %get-tuple-element.52), channel_id=1, source_target_pairs={{0,6},{1,7},{2,4},{3,5},{4,2},{5,3},{6,0},{7,1},{8,14},{9,15},{10,... | collective-permute-start | bytes 589832 | tf_op jit(solution)/shard_map/ppermute | solution.py:389
  9.6 13.9 %collective-permute-start.2 = (f32[2,3,64,128]{3,2,1,0:T(8,128)S(1)}, f32[2,3,64,128]{3,2,1,0:T(8,128)S(1)}, u32[]{:S(2)}, u32[]{:S(2)}) collective-permute-start(f32[2,3,64,128]{3,2,1,0:T(8,128)S(1)} %get-tuple-element.53), channel_id=1, source_target_pairs={{0,7},{1,6},{2,5},{3,4},{4,3},{5,2},{6,1},{7,0},{8,15},{9,14},{10,... | collective-permute-start | bytes 589832 | tf_op jit(solution)/shard_map/ppermute | solution.py:389
  9.7 14.0 %collective-permute-start.3 = (f32[2,3,64,128]{3,2,1,0:T(8,128)S(1)}, f32[2,3,64,128]{3,2,1,0:T(8,128)S(1)}, u32[]{:S(2)}, u32[]{:S(2)}) collective-permute-start(f32[2,3,64,128]{3,2,1,0:T(8,128)S(1)} %get-tuple-element.54), channel_id=1, source_target_pairs={{0,2},{1,3},{2,0},{3,1},{4,6},{5,7},{6,4},{7,5},{8,10},{9,11},{10,... | collective-permute-start | bytes 589832 | tf_op jit(solution)/shard_map/ppermute | solution.py:389
  9.7 19.1 %collective-permute-start.4 = (f32[2,3,64,128]{3,2,1,0:T(8,128)S(1)}, f32[2,3,64,128]{3,2,1,0:T(8,128)S(1)}, u32[]{:S(2)}, u32[]{:S(2)}) collective-permute-start(f32[2,3,64,128]{3,2,1,0:T(8,128)S(1)} %get-tuple-element.55), channel_id=1, source_target_pairs={{0,3},{1,2},{2,1},{3,0},{4,7},{5,6},{6,5},{7,4},{8,11},{9,10},{10,... | collective-permute-start | bytes 589832 | tf_op jit(solution)/shard_map/ppermute | solution.py:389
  12.6 27.4 %collective-permute-start.5 = (f32[2,3,64,128]{3,2,1,0:T(8,128)S(1)}, f32[2,3,64,128]{3,2,1,0:T(8,128)S(1)}, u32[]{:S(2)}, u32[]{:S(2)}) collective-permute-start(f32[2,3,64,128]{3,2,1,0:T(8,128)S(1)} %get-tuple-element.56), channel_id=1, source_target_pairs={{0,4},{1,5},{2,6},{3,7},{4,0},{5,1},{6,2},{7,3},{8,12},{9,13},{10,... | collective-permute-start | bytes 589832 | tf_op jit(solution)/shard_map/ppermute | solution.py:389
  15.6 27.7 %collective-permute-start.6 = (f32[2,3,64,128]{3,2,1,0:T(8,128)S(1)}, f32[2,3,64,128]{3,2,1,0:T(8,128)S(1)}, u32[]{:S(2)}, u32[]{:S(2)}) collective-permute-start(f32[2,3,64,128]{3,2,1,0:T(8,128)S(1)} %get-tuple-element.57), channel_id=1, source_target_pairs={{0,5},{1,4},{2,7},{3,6},{4,1},{5,0},{6,3},{7,2},{8,13},{9,12},{10,... | collective-permute-start | bytes 589832 | tf_op jit(solution)/shard_map/ppermute | solution.py:389
  44.9 5.6 %collective-permute-start.7 = (f32[3,64,128]{2,1,0:T(8,128)S(1)}, f32[3,64,128]{2,1,0:T(8,128)S(1)}, u32[]{:S(2)}, u32[]{:S(2)}) collective-permute-start(f32[3,64,128]{2,1,0:T(8,128)S(1)} %get-tuple-element.59), channel_id=1, source_target_pairs={{0,1},{1,0},{2,3},{3,2},{4,5},{5,4},{6,7},{7,6},{8,9},{9,8},{10,11... | collective-permute-start | bytes 294920 | tf_op jit(solution)/shard_map/ppermute | solution.py:389
  45.2 6.9 %collective-permute-start.8 = (f32[3,64,128]{2,1,0:T(8,128)S(1)}, f32[3,64,128]{2,1,0:T(8,128)S(1)}, u32[]{:S(2)}, u32[]{:S(2)}) collective-permute-start(f32[3,64,128]{2,1,0:T(8,128)S(1)} %get-tuple-element.60), channel_id=1, source_target_pairs={{0,6},{1,7},{2,4},{3,5},{4,2},{5,3},{6,0},{7,1},{8,14},{9,15},{10,... | collective-permute-start | bytes 294920 | tf_op jit(solution)/shard_map/ppermute | solution.py:389
  47.8 6.9 %collective-permute-start.9 = (f32[3,64,128]{2,1,0:T(8,128)S(1)}, f32[3,64,128]{2,1,0:T(8,128)S(1)}, u32[]{:S(2)}, u32[]{:S(2)}) collective-permute-start(f32[3,64,128]{2,1,0:T(8,128)S(1)} %get-tuple-element.61), channel_id=1, source_target_pairs={{0,7},{1,6},{2,5},{3,4},{4,3},{5,2},{6,1},{7,0},{8,15},{9,14},{10,... | collective-permute-start | bytes 294920 | tf_op jit(solution)/shard_map/ppermute | solution.py:389
  48.6 10.7 %collective-permute-start.10 = (f32[3,64,128]{2,1,0:T(8,128)S(1)}, f32[3,64,128]{2,1,0:T(8,128)S(1)}, u32[]{:S(2)}, u32[]{:S(2)}) collective-permute-start(f32[3,64,128]{2,1,0:T(8,128)S(1)} %get-tuple-element.62), channel_id=1, source_target_pairs={{0,2},{1,3},{2,0},{3,1},{4,6},{5,7},{6,4},{7,5},{8,10},{9,11},{10,... | collective-permute-start | bytes 294920 | tf_op jit(solution)/shard_map/ppermute | solution.py:389
  48.6 12.5 %collective-permute-start.11 = (f32[3,64,128]{2,1,0:T(8,128)S(1)}, f32[3,64,128]{2,1,0:T(8,128)S(1)}, u32[]{:S(2)}, u32[]{:S(2)}) collective-permute-start(f32[3,64,128]{2,1,0:T(8,128)S(1)} %get-tuple-element.63), channel_id=1, source_target_pairs={{0,3},{1,2},{2,1},{3,0},{4,7},{5,6},{6,5},{7,4},{8,11},{9,10},{10,... | collective-permute-start | bytes 294920 | tf_op jit(solution)/shard_map/ppermute | solution.py:389
  50.5 11.8 %collective-permute-start.12 = (f32[3,64,128]{2,1,0:T(8,128)S(1)}, f32[3,64,128]{2,1,0:T(8,128)S(1)}, u32[]{:S(2)}, u32[]{:S(2)}) collective-permute-start(f32[3,64,128]{2,1,0:T(8,128)S(1)} %get-tuple-element.64), channel_id=1, source_target_pairs={{0,4},{1,5},{2,6},{3,7},{4,0},{5,1},{6,2},{7,3},{8,12},{9,13},{10,... | collective-permute-start | bytes 294920 | tf_op jit(solution)/shard_map/ppermute | solution.py:389
  52.1 12.0 %collective-permute-start.13 = (f32[3,64,128]{2,1,0:T(8,128)S(1)}, f32[3,64,128]{2,1,0:T(8,128)S(1)}, u32[]{:S(2)}, u32[]{:S(2)}) collective-permute-start(f32[3,64,128]{2,1,0:T(8,128)S(1)} %get-tuple-element.65), channel_id=1, source_target_pairs={{0,5},{1,4},{2,7},{3,6},{4,1},{5,0},{6,3},{7,2},{8,13},{9,12},{10,... | collective-permute-start | bytes 294920 | tf_op jit(solution)/shard_map/ppermute | solution.py:389
  64.1 6.8 %copy-start.3 = (f32[6,64,512]{2,1,0:T(8,128)S(1)}, f32[6,64,512]{2,1,0:T(8,128)}, u32[]{:S(2)}) copy-start(f32[6,64,512]{2,1,0:T(8,128)} %velocity_ref.1) | copy-start | bytes 2359300
  64.1 6.8 %copy-start.4 = (s32[2,512]{1,0:T(2,128)S(1)}, s32[2,512]{1,0:T(2,128)}, u32[]{:S(2)}) copy-start(s32[2,512]{1,0:T(2,128)} %modes_ref.1) | copy-start | bytes 12292
  64.8 6.1 %collective-permute-start.14 = (f32[3,64,128]{2,1,0:T(8,128)S(1)}, f32[3,64,128]{2,1,0:T(8,128)S(1)}, u32[]{:S(2)}, u32[]{:S(2)}) collective-permute-start(f32[3,64,128]{2,1,0:T(8,128)S(1)} %get-tuple-element.68), channel_id=1, source_target_pairs={{0,3},{1,2},{2,1},{3,0},{4,7},{5,6},{6,5},{7,4},{8,11},{9,10},{10,... | collective-permute-start | bytes 294920 | tf_op jit(solution)/shard_map/ppermute | solution.py:389
  64.9 23.7 %collective-permute-start.15 = (f32[3,64,128]{2,1,0:T(8,128)S(1)}, f32[3,64,128]{2,1,0:T(8,128)S(1)}, u32[]{:S(2)}, u32[]{:S(2)}) collective-permute-start(f32[3,64,128]{2,1,0:T(8,128)S(1)} %get-tuple-element.71), channel_id=1, source_target_pairs={{0,4},{1,5},{2,6},{3,7},{4,0},{5,1},{6,2},{7,3},{8,12},{9,13},{10,... | collective-permute-start | bytes 294920 | tf_op jit(solution)/shard_map/ppermute | solution.py:389
  66.7 6.0 %collective-permute-start.17 = (f32[3,64,128]{2,1,0:T(8,128)S(1)}, f32[3,64,128]{2,1,0:T(8,128)S(1)}, u32[]{:S(2)}, u32[]{:S(2)}) collective-permute-start(f32[3,64,128]{2,1,0:T(8,128)S(1)} %get-tuple-element.75), channel_id=1, source_target_pairs={{0,1},{1,0},{2,3},{3,2},{4,5},{5,4},{6,7},{7,6},{8,9},{9,8},{10,11... | collective-permute-start | bytes 294920 | tf_op jit(solution)/shard_map/ppermute | solution.py:389
  66.9 8.2 %collective-permute-start.18 = (f32[3,64,128]{2,1,0:T(8,128)S(1)}, f32[3,64,128]{2,1,0:T(8,128)S(1)}, u32[]{:S(2)}, u32[]{:S(2)}) collective-permute-start(f32[3,64,128]{2,1,0:T(8,128)S(1)} %get-tuple-element.76), channel_id=1, source_target_pairs={{0,6},{1,7},{2,4},{3,5},{4,2},{5,3},{6,0},{7,1},{8,14},{9,15},{10,... | collective-permute-start | bytes 294920 | tf_op jit(solution)/shard_map/ppermute | solution.py:389
  69.2 7.1 %collective-permute-start.19 = (f32[3,64,128]{2,1,0:T(8,128)S(1)}, f32[3,64,128]{2,1,0:T(8,128)S(1)}, u32[]{:S(2)}, u32[]{:S(2)}) collective-permute-start(f32[3,64,128]{2,1,0:T(8,128)S(1)} %get-tuple-element.77), channel_id=1, source_target_pairs={{0,7},{1,6},{2,5},{3,4},{4,3},{5,2},{6,1},{7,0},{8,15},{9,14},{10,... | collective-permute-start | bytes 294920 | tf_op jit(solution)/shard_map/ppermute | solution.py:389
  70.9 8.4 %collective-permute-start.20 = (f32[3,64,128]{2,1,0:T(8,128)S(1)}, f32[3,64,128]{2,1,0:T(8,128)S(1)}, u32[]{:S(2)}, u32[]{:S(2)}) collective-permute-start(f32[3,64,128]{2,1,0:T(8,128)S(1)} %get-tuple-element.78), channel_id=1, source_target_pairs={{0,2},{1,3},{2,0},{3,1},{4,6},{5,7},{6,4},{7,5},{8,10},{9,11},{10,... | collective-permute-start | bytes 294920 | tf_op jit(solution)/shard_map/ppermute | solution.py:389
  72.7 15.9 %collective-permute-start.16 = (f32[3,64,128]{2,1,0:T(8,128)S(1)}, f32[3,64,128]{2,1,0:T(8,128)S(1)}, u32[]{:S(2)}, u32[]{:S(2)}) collective-permute-start(f32[3,64,128]{2,1,0:T(8,128)S(1)} %get-tuple-element.72), channel_id=1, source_target_pairs={{0,5},{1,4},{2,7},{3,6},{4,1},{5,0},{6,3},{7,2},{8,13},{9,12},{10,... | collective-permute-start | bytes 294920 | tf_op jit(solution)/shard_map/ppermute | solution.py:389

commit v11 on v9

--- a/solution.py
+++ b/solution.py
@@ -370,6 +370,10 @@
     assemble(me_ref[0], steps, unused(info_ref, share), solved_ref, in_refs, out_hbm, rows_ref, sems)
 
 
+def near_first(steps, devices):
+    return [step for step in steps if step < devices // 2] + [step for step in steps if step >= devices // 2]
+
+
 def late_steps(devices, points):
     return list(range(devices // 2, devices // 2 + LANES // points))
 
@@ -391,11 +395,12 @@
     ]
 
 
-def from_groups(value):
+def pair_sums(value, step):
     groups = lax.axis_size("grp")
-    return [value] + [
-        lax.ppermute(value, "grp", [(i, i ^ step) for i in range(groups)]) for step in range(1, groups)
-    ]
+    while 2 * step < groups:
+        value = value + lax.ppermute(value, "grp", [(i, i ^ step) for i in range(groups)])
+        step = 2 * step
+    return [value, lax.ppermute(value, "grp", [(i, i ^ step) for i in range(groups)])]
 
 
 def on_device(
@@ -469,6 +474,7 @@
     solved = outs[devices]
     returned = exchange(outs[:devices], steps)
 
+    early_back, steps_back = near_first(early, devices), near_first(early, devices) + late
     begun, chosen = call(
         functools.partial(surplus_early_kernel, early),
         [shaped((comps * points, columns)), shaped((len(late) * share, columns), BF16)],
@@ -477,13 +483,13 @@
         HEAVY,
     )(info, *returned[:split])
     outs = call(
-        functools.partial(surplus_late_kernel, late, steps),
+        functools.partial(surplus_late_kernel, late, steps_back),
         back,
         [LOCAL] * (2 + len(late)),
         [LOCAL] * devices,
         1,
     )(begun, chosen, *returned[split:])
-    extra = exchange(outs, steps)
+    extra = exchange(outs, steps_back)
 
     state_next, emf = call(
         functools.partial(state_kernel, steps),
@@ -492,11 +498,11 @@
         [FAR, LOCAL],
         HEAVY,
         [pltpu.VMEM(state_now.shape, F32), pltpu.SemaphoreType.DMA],
-    )(info, kept_modes, velocity, *returned, extra[early.index(3)])
-    terms = from_groups(emf)
+    )(info, kept_modes, velocity, *returned, extra[early_back.index(3)])
+    terms = pair_sums(emf, 1)
 
     owned = call(
-        functools.partial(assemble_early_kernel, early),
+        functools.partial(assemble_early_kernel, early_back),
         shaped((comps, depth, lanes)),
         [SCALAR] + [LOCAL] * (2 + split),
         FAR,

time: 87.8 us -> 87.8 us (level); the launches traced: 86.5 us -> 87.6 us
  waiting for transfers between devices: 33.5 us -> 36.4 us
  starting transfers between devices: 37.8 us -> 36 us
    ppermute x3 -> x2, waiting for transfers between devices: 0.01 us -> 2.1 us  [pair_sums(): lax.ppermute(value, 'grp', [(i, i ^ step) for i in range(groups)])]
    ppermute x3 -> x2, starting transfers between devices: 4.45 us -> 3.08 us  [pair_sums(): lax.ppermute(value, 'grp', [(i, i ^ step) for i in range(groups)])]
  transfers between devices with their start and end apart: 24 -> 23, of which waited for: 13 -> 13; matrix products, arithmetic and copies ran while one was open for 0% -> 0% of each run, Pallas kernels for 8% -> 8%
where the time goes in v11:
time: 87.8 us; the launch traced here: 87.6 us
  waiting for transfers between devices  36.4 us (41%)
  starting transfers between devices  36 us (41%)
  Pallas kernels  14.4 us (16%)
    ppermute x21, waiting for transfers between devices, exchange(): lax.ppermute(block, 'col', [(i, i ^ step) for i in range(devices)])  34.3 us
    ppermute x21, starting transfers between devices, exchange(): lax.ppermute(block, 'col', [(i, i ^ step) for i in range(devices)])  32.9 us
    pallas_call x1, Pallas kernels, on_device(): call(functools.partial(first_kernel, devices), [shaped((8, columns), jnp....  3.76 us
    ppermute x2, starting transfers between devices, pair_sums(): lax.ppermute(value, 'grp', [(i, i ^ step) for i in range(groups)])  3.08 us
    ppermute x2, waiting for transfers between devices, pair_sums(): lax.ppermute(value, 'grp', [(i, i ^ step) for i in range(groups)])  2.1 us
    pallas_call x1, Pallas kernels, on_device(): call(functools.partial(state_kernel, steps), [shaped(state_now.shape), sh...  1.83 us
  transfers between devices with their start and end apart: 23, of which 13 were waited for; matrix products, arithmetic and copies ran while one was open for 0% of the time, Pallas kernels for 8%

profile of v11, /device:TPU:0, one launch (start us, length us, event | category | flops | bytes accessed | tf_op | source)
XLA Modules:
  0.0 87.6 jit_solution(12993999637057269876)
XLA Ops:
  0.7 3.8 %shard_map.121 = (s32[8,512]{1,0:T(8,128)S(1)}, f32[8,128]{1,0:T(8,128)S(1)}, f32[2,3,64,128]{3,2,1,0:T(8,128)S(1)}, f32[2,3,64,128]{3,2,1,0:T(8,128)S(1)}, f32[...) custom-call(s32[1]{0:T(128)} %bitcast.me_ref, ...), custom_call_target="tpu_custom_call" | custom-call | flops 1000000000 | bytes 1000000 | tf_op jit(solution)/shard_map/pallas_call | solution.py:435
  4.4 0.5 collective-permute-start
  5.0 4.7 %collective-permute-start.1 = (f32[2,3,64,128]{3,2,1,0:T(8,128)S(1)}, f32[2,3,64,128]{3,2,1,0:T(8,128)S(1)}, u32[]{:S(2)}, u32[]{:S(2)}) collective-permute-start(f32[2,3,64,128]{3,2,1,0:T(8,128)S(1)} %get-tuple-element.52), channel_id=1, source_target_pairs={{0,6},{1,7},{2,4},{3,5},{4,2},{5,3},{6,0},{7,1},{8,14},{9,15},{10,... | collective-permute-start | bytes 589832 | tf_op jit(solution)/shard_map/ppermute | solution.py:393
  9.6 0.1 collective-permute-start.2
  9.7 0.0 collective-permute-start.3
  9.7 1.5 %collective-permute-start.4 = (f32[2,3,64,128]{3,2,1,0:T(8,128)S(1)}, f32[2,3,64,128]{3,2,1,0:T(8,128)S(1)}, u32[]{:S(2)}, u32[]{:S(2)}) collective-permute-start(f32[2,3,64,128]{3,2,1,0:T(8,128)S(1)} %get-tuple-element.55), channel_id=1, source_target_pairs={{0,3},{1,2},{2,1},{3,0},{4,7},{5,6},{6,5},{7,4},{8,11},{9,10},{10,... | collective-permute-start | bytes 589832 | tf_op jit(solution)/shard_map/ppermute | solution.py:393
  11.2 1.4 %shard_map.122 = (bf16[512,512]{1,0:T(8,128)(2,1)S(1)}, bf16[512,512]{1,0:T(8,128)(2,1)S(1)}, bf16[512,512]{1,0:T(8,128)(2,1)S(1)}, bf16[512,512]{1,0:T(8,128)(2...) custom-call(f32[512,512]{1,0:T(8,128)S(1)} %copy-done, f32[512,512]{1,0:T(8,128)S(1)} %copy-done.1, ...), custom_call_target="tpu_custom_call" | custom-call | flops 10000000000 | bytes 10000000 | tf_op jit(solution)/shard_map/pallas_call | solution.py:449
  12.6 2.7 %collective-permute-start.5 = (f32[2,3,64,128]{3,2,1,0:T(8,128)S(1)}, f32[2,3,64,128]{3,2,1,0:T(8,128)S(1)}, u32[]{:S(2)}, u32[]{:S(2)}) collective-permute-start(f32[2,3,64,128]{3,2,1,0:T(8,128)S(1)} %get-tuple-element.56), channel_id=1, source_target_pairs={{0,4},{1,5},{2,6},{3,7},{4,0},{5,1},{6,2},{7,3},{8,12},{9,13},{10,... | collective-permute-start | bytes 589832 | tf_op jit(solution)/shard_map/ppermute | solution.py:393
  15.3 0.3 collective-permute-done.1.refs_6_
  15.6 8.0 %collective-permute-start.6 = (f32[2,3,64,128]{3,2,1,0:T(8,128)S(1)}, f32[2,3,64,128]{3,2,1,0:T(8,128)S(1)}, u32[]{:S(2)}, u32[]{:S(2)}) collective-permute-start(f32[2,3,64,128]{3,2,1,0:T(8,128)S(1)} %get-tuple-element.57), channel_id=1, source_target_pairs={{0,5},{1,4},{2,7},{3,6},{4,1},{5,0},{6,3},{7,2},{8,13},{9,12},{10,... | collective-permute-start | bytes 589832 | tf_op jit(solution)/shard_map/ppermute | solution.py:393
  23.6 0.2 collective-permute-done.3.refs_8_
  23.7 5.1 %collective-permute-done.4.refs_9_ = f32[2,3,64,128]{3,2,1,0:T(8,128)S(1)} collective-permute-done((f32[2,3,64,128]{3,2,1,0:T(8,128)S(1)}, f32[2,3,64,128]{3,2,1,0:T(8,128)S(1)}, u32[]{:S(2)}, u32[]{:S(2)}) %collective-permute-start.4) | collective-permute-done | bytes 196640 | tf_op jit(solution)/shard_map/ppermute | solution.py:393
  28.8 1.4 %shard_map.123.early_ref = f32[512,384]{1,0:T(8,128)S(1)} custom-call(s32[1]{0:T(128)} %bitcast.me_ref, bf16[512,512]{1,0:T(8,128)(2,1)S(1)} %get-tuple-element.46.refs_0_, bf16[512,512]{1,0:T(8,128)(2,1)S(1)} %get-tuple-element.47.refs_1_, bf16[512,512]{1,0:T(8,128)(2,1)S(1)} %get-tuple-element.48.refs_2_, bf16[512,512]{1,0:T(8,128)(2,1)S(1)} %get-tuple-element.49.refs_3_, ...), custom_call_target="tpu_custom_call" | custom-call | flops 10000000000 | bytes 10000000 | tf_op jit(solution)/shard_map/pallas_call | solution.py:458
  30.2 9.8 %collective-permute-done.5.refs_4_ = f32[2,3,64,128]{3,2,1,0:T(8,128)S(1)} collective-permute-done((f32[2,3,64,128]{3,2,1,0:T(8,128)S(1)}, f32[2,3,64,128]{3,2,1,0:T(8,128)S(1)}, u32[]{:S(2)}, u32[]{:S(2)}) %collective-permute-start.5) | collective-permute-done | bytes 196640 | tf_op jit(solution)/shard_map/ppermute | solution.py:393
  40.0 3.3 %collective-permute-done.6.refs_5_ = f32[2,3,64,128]{3,2,1,0:T(8,128)S(1)} collective-permute-done((f32[2,3,64,128]{3,2,1,0:T(8,128)S(1)}, f32[2,3,64,128]{3,2,1,0:T(8,128)S(1)}, u32[]{:S(2)}, u32[]{:S(2)}) %collective-permute-start.6) | collective-permute-done | bytes 196640 | tf_op jit(solution)/shard_map/ppermute | solution.py:393
  43.3 1.6 %shard_map.124 = (f32[3,64,128]{2,1,0:T(8,128)S(1)}, f32[3,64,128]{2,1,0:T(8,128)S(1)}, f32[3,64,128]{2,1,0:T(8,128)S(1)}, f32[3,64,128]{2,1,0:T(8,128)S(1)}, f3...) custom-call(s32[1]{0:T(128)} %bitcast.me_ref, ...), custom_call_target="tpu_custom_call" | custom-call | flops 1000000000 | bytes 1000000 | tf_op jit(solution)/shard_map/pallas_call | solution.py:466
  44.9 0.3 collective-permute-start.7
  45.2 2.5 %collective-permute-start.8 = (f32[3,64,128]{2,1,0:T(8,128)S(1)}, f32[3,64,128]{2,1,0:T(8,128)S(1)}, u32[]{:S(2)}, u32[]{:S(2)}) collective-permute-start(f32[3,64,128]{2,1,0:T(8,128)S(1)} %get-tuple-element.60), channel_id=1, source_target_pairs={{0,6},{1,7},{2,4},{3,5},{4,2},{5,3},{6,0},{7,1},{8,14},{9,15},{10,... | collective-permute-start | bytes 294920 | tf_op jit(solution)/shard_map/ppermute | solution.py:393
  47.8 0.9 collective-permute-start.9
  48.6 0.0 collective-permute-start.10
  48.6 1.9 %collective-permute-start.11 = (f32[3,64,128]{2,1,0:T(8,128)S(1)}, f32[3,64,128]{2,1,0:T(8,128)S(1)}, u32[]{:S(2)}, u32[]{:S(2)}) collective-permute-start(f32[3,64,128]{2,1,0:T(8,128)S(1)} %get-tuple-element.63), channel_id=1, source_target_pairs={{0,3},{1,2},{2,1},{3,0},{4,7},{5,6},{6,5},{7,4},{8,11},{9,10},{10,... | collective-permute-start | bytes 294920 | tf_op jit(solution)/shard_map/ppermute | solution.py:393
  50.5 0.0 collective-permute-done.7.refs_1_
  50.5 1.4 %collective-permute-start.12 = (f32[3,64,128]{2,1,0:T(8,128)S(1)}, f32[3,64,128]{2,1,0:T(8,128)S(1)}, u32[]{:S(2)}, u32[]{:S(2)}) collective-permute-start(f32[3,64,128]{2,1,0:T(8,128)S(1)} %get-tuple-element.64), channel_id=1, source_target_pairs={{0,4},{1,5},{2,6},{3,7},{4,0},{5,1},{6,2},{7,3},{8,12},{9,13},{10,... | collective-permute-start | bytes 294920 | tf_op jit(solution)/shard_map/ppermute | solution.py:393
  51.9 0.2 collective-permute-done.8.refs_2_
  52.1 0.9 %collective-permute-start.13 = (f32[3,64,128]{2,1,0:T(8,128)S(1)}, f32[3,64,128]{2,1,0:T(8,128)S(1)}, u32[]{:S(2)}, u32[]{:S(2)}) collective-permute-start(f32[3,64,128]{2,1,0:T(8,128)S(1)} %get-tuple-element.65), channel_id=1, source_target_pairs={{0,5},{1,4},{2,7},{3,6},{4,1},{5,0},{6,3},{7,2},{8,13},{9,12},{10,... | collective-permute-start | bytes 294920 | tf_op jit(solution)/shard_map/ppermute | solution.py:393
  53.0 1.7 %collective-permute-done.9.refs_3_ = f32[3,64,128]{2,1,0:T(8,128)S(1)} collective-permute-done((f32[3,64,128]{2,1,0:T(8,128)S(1)}, f32[3,64,128]{2,1,0:T(8,128)S(1)}, u32[]{:S(2)}, u32[]{:S(2)}) %collective-permute-start.9) | collective-permute-done | bytes 98336 | tf_op jit(solution)/shard_map/ppermute | solution.py:393
  54.7 4.6 %collective-permute-done.10.refs_4_ = f32[3,64,128]{2,1,0:T(8,128)S(1)} collective-permute-done((f32[3,64,128]{2,1,0:T(8,128)S(1)}, f32[3,64,128]{2,1,0:T(8,128)S(1)}, u32[]{:S(2)}, u32[]{:S(2)}) %collective-permute-start.10) | collective-permute-done | bytes 98336 | tf_op jit(solution)/shard_map/ppermute | solution.py:393
  59.3 1.9 %collective-permute-done.11.refs_5_ = f32[3,64,128]{2,1,0:T(8,128)S(1)} collective-permute-done((f32[3,64,128]{2,1,0:T(8,128)S(1)}, f32[3,64,128]{2,1,0:T(8,128)S(1)}, u32[]{:S(2)}, u32[]{:S(2)}) %collective-permute-start.11) | collective-permute-done | bytes 98336 | tf_op jit(solution)/shard_map/ppermute | solution.py:393
  61.2 1.2 %shard_map.125 = (f32[384,512]{1,0:T(8,128)S(1)}, bf16[128,512]{1,0:T(8,128)(2,1)S(1)}) custom-call(s32[8,512]{1,0:T(8,128)S(1)} %get-tuple-element.42.info_ref, f32[3,64,128]{2,1,0:T(8,128)S(1)} %get-tuple-element.58.refs_0_, f32[3,64,128]{2,1,0:T(8,128)S(1)} %collective-permute-done.7.refs_1_, f32[3,64,128]{2,1,0:T(8,128)S(1)} %collective-permute-done.8.refs_2_, ...), custom_call_target="tpu_custom_call" | custom-call | flops 10000000000 | bytes 10000000 | tf_op jit(solution)/shard_map/pallas_call | solution.py:478
  62.3 1.8 %collective-permute-done.13.refs_1_.refs_7_ = f32[3,64,128]{2,1,0:T(8,128)S(1)} collective-permute-done((f32[3,64,128]{2,1,0:T(8,128)S(1)}, f32[3,64,128]{2,1,0:T(8,128)S(1)}, u32[]{:S(2)}, u32[]{:S(2)}) %collective-permute-start.13) | collective-permute-done | bytes 98336 | tf_op jit(solution)/shard_map/ppermute | solution.py:393
  64.1 0.7 shard_map.126
  64.8 0.1 collective-permute-start.14
  64.9 0.3 collective-permute-start.19
  65.2 1.8 %collective-permute-start.20 = (f32[3,64,128]{2,1,0:T(8,128)S(1)}, f32[3,64,128]{2,1,0:T(8,128)S(1)}, u32[]{:S(2)}, u32[]{:S(2)}) collective-permute-start(f32[3,64,128]{2,1,0:T(8,128)S(1)} %get-tuple-element.76), channel_id=1, source_target_pairs={{0,2},{1,3},{2,0},{3,1},{4,6},{5,7},{6,4},{7,5},{8,10},{9,11},{10,... | collective-permute-start | bytes 294920 | tf_op jit(solution)/shard_map/ppermute | solution.py:393
  67.0 1.6 %collective-permute-start.21 = (f32[3,64,128]{2,1,0:T(8,128)S(1)}, f32[3,64,128]{2,1,0:T(8,128)S(1)}, u32[]{:S(2)}, u32[]{:S(2)}) collective-permute-start(f32[3,64,128]{2,1,0:T(8,128)S(1)} %get-tuple-element.77), channel_id=1, source_target_pairs={{0,6},{1,7},{2,4},{3,5},{4,2},{5,3},{6,0},{7,1},{8,14},{9,15},{10,... | collective-permute-start | bytes 294920 | tf_op jit(solution)/shard_map/ppermute | solution.py:393
  68.6 1.6 %collective-permute-start.22 = (f32[3,64,128]{2,1,0:T(8,128)S(1)}, f32[3,64,128]{2,1,0:T(8,128)S(1)}, u32[]{:S(2)}, u32[]{:S(2)}) collective-permute-start(f32[3,64,128]{2,1,0:T(8,128)S(1)} %get-tuple-element.78), channel_id=1, source_target_pairs={{0,7},{1,6},{2,5},{3,4},{4,3},{5,2},{6,1},{7,0},{8,15},{9,14},{10,... | collective-permute-start | bytes 294920 | tf_op jit(solution)/shard_map/ppermute | solution.py:393
  70.2 0.0 collective-permute-done.14.refs_8_.refs_3_
  70.2 1.8 %shard_map.127 = (f32[6,64,512]{2,1,0:T(8,128)}, f32[3,64]{1,0:T(4,128)S(1)}) custom-call(s32[8,512]{1,0:T(8,128)S(1)} %get-tuple-element.42.info_ref, s32[2,512]{1,0:T(2,128)S(1)} %copy-done.4, f32[6,64,512]{2,1,0:T(8,128)S(1)} %copy-done.3, f32[3,64,128]{2,1,0:T(8,128)S(1)} %get-tuple-element.58.refs_0_, f32[3,64,128]{2,1,0:T(8,128)S(1)} %collective-permute-done.7.refs_1_, ...), custom_call_target="tpu_custom_call" | custom-call | flops 10000000000 | bytes 10000000 | tf_op jit(solution)/shard_map/pallas_call | solution.py:494
  72.0 1.6 %collective-permute-start.17 = (f32[3,64]{1,0:T(4,128)S(1)}, f32[3,64]{1,0:T(4,128)S(1)}, u32[]{:S(2)}, u32[]{:S(2)}) collective-permute-start(f32[3,64]{1,0:T(4,128)S(1)} %get-tuple-element.73), channel_id=1, source_target_pairs={{0,8},{8,0},{16,24},{24,16},{1,9},{9,1},{17,25},{25,17},{2,10},{10... | collective-permute-start | bytes 2312 | tf_op jit(solution)/shard_map/ppermute | solution.py:401
  73.6 2.1 %collective-permute-done.17 = f32[3,64]{1,0:T(4,128)S(1)} collective-permute-done((f32[3,64]{1,0:T(4,128)S(1)}, f32[3,64]{1,0:T(4,128)S(1)}, u32[]{:S(2)}, u32[]{:S(2)}) %collective-permute-start.17) | collective-permute-done | bytes 800 | tf_op jit(solution)/shard_map/ppermute | solution.py:401
  75.7 2.2 %collective-permute-start.16 = (f32[3,64,128]{2,1,0:T(8,128)S(1)}, f32[3,64,128]{2,1,0:T(8,128)S(1)}, u32[]{:S(2)}, u32[]{:S(2)}) collective-permute-start(f32[3,64,128]{2,1,0:T(8,128)S(1)} %get-tuple-element.72), channel_id=1, source_target_pairs={{0,5},{1,4},{2,7},{3,6},{4,1},{5,0},{6,3},{7,2},{8,13},{9,12},{10,... | collective-permute-start | bytes 294920 | tf_op jit(solution)/shard_map/ppermute | solution.py:393
  77.9 0.0 collective-permute-done.20.refs_2_
  77.9 1.5 %collective-permute-start.18 = (f32[3,64]{1,0:T(4,128)S(1)}, f32[3,64]{1,0:T(4,128)S(1)}, u32[]{:S(2)}, u32[]{:S(2)}) collective-permute-start(f32[3,64]{1,0:T(4,128)S(1)} %add.3.refs_2_), channel_id=1, source_target_pairs={{0,16},{8,24},{16,0},{24,8},{1,17},{9,25},{17,1},{25,9},{2,18},{10... | collective-permute-start | bytes 2312 | tf_op jit(solution)/shard_map/ppermute | solution.py:403
  79.4 0.0 collective-permute-done.21.refs_4_
  79.4 1.2 %shard_map.128.refs_4_ = f32[6,512,128]{2,1,0:T(8,128)} custom-call(s32[1]{0:T(128)} %bitcast.me_ref, s32[8,512]{1,0:T(8,128)S(1)} %get-tuple-element.42.info_ref, f32[3,512,128]{2,1,0:T(8,128)S(1)} %get-tuple-element.70.solved_ref, f32[3,64,128]{2,1,0:T(8,128)S(1)} %get-tuple-element.74.refs_0_, f32[3,64,128]{2,1,0:T(8,128)S(1)} %collective-permute-done.19.refs_1_, ...), custom_call_target="tpu_custom_call" | custom-call | flops 10000000000 | bytes 10000000 | tf_op jit(solution)/shard_map/pallas_call | solution.py:504
  80.6 4.0 %collective-permute-done.15.refs_0_ = f32[3,64,128]{2,1,0:T(8,128)S(1)} collective-permute-done((f32[3,64,128]{2,1,0:T(8,128)S(1)}, f32[3,64,128]{2,1,0:T(8,128)S(1)}, u32[]{:S(2)}, u32[]{:S(2)}) %collective-permute-start.15) | collective-permute-done | bytes 98336 | tf_op jit(solution)/shard_map/ppermute | solution.py:393
  84.7 1.5 %collective-permute-done.16.refs_1_ = f32[3,64,128]{2,1,0:T(8,128)S(1)} collective-permute-done((f32[3,64,128]{2,1,0:T(8,128)S(1)}, f32[3,64,128]{2,1,0:T(8,128)S(1)}, u32[]{:S(2)}, u32[]{:S(2)}) %collective-permute-start.16) | collective-permute-done | bytes 98336 | tf_op jit(solution)/shard_map/ppermute | solution.py:393
  86.2 1.4 %shard_map.129 = (f32[6,512,128]{2,1,0:T(8,128)}, f32[3,64]{1,0:T(4,128)}) custom-call(s32[1]{0:T(128)} %bitcast.me_ref, s32[8,512]{1,0:T(8,128)S(1)} %get-tuple-element.42.info_ref, f32[3,512,128]{2,1,0:T(8,128)S(1)} %get-tuple-element.70.solved_ref, f32[3,64,128]{2,1,0:T(8,128)S(1)} %collective-permute-done.15.refs_0_, ...), custom_call_target="tpu_custom_call", output_to_operand_aliasing={{0}: (7, {})} | custom-call | flops 1000000000 | bytes 1000000 | tf_op jit(solution)/shard_map/pallas_call | solution.py:515
  (20 shorter events, 0.0 us)
Async XLA Ops:
  0.6 10.6 %copy-start = (f32[512,512]{1,0:T(8,128)S(1)}, f32[512,512]{1,0:T(8,128)}, u32[]{:S(2)}) copy-start(f32[512,512]{1,0:T(8,128)} %deriv_ref.1) | copy-start | bytes 3145732
  0.6 10.6 %copy-start.1 = (f32[512,512]{1,0:T(8,128)S(1)}, f32[512,512]{1,0:T(8,128)}, u32[]{:S(2)}) copy-start(f32[512,512]{1,0:T(8,128)} %inverse_ref.1) | copy-start | bytes 3145732
  0.7 10.6 %copy-start.2 = (f32[512,512]{1,0:T(8,128)S(1)}, f32[512,512]{1,0:T(8,128)}, u32[]{:S(2)}) copy-start(f32[512,512]{1,0:T(8,128)} %basis_ref.1) | copy-start | bytes 3145732
  0.7 10.5 %copy-start.5 = (f32[512]{0:T(512)S(1)}, f32[512]{0:T(512)}, u32[]{:S(2)}) copy-start(f32[512]{0:T(512)} %param.17) | copy-start | bytes 6148
  4.4 8.1 %collective-permute-start = (f32[2,3,64,128]{3,2,1,0:T(8,128)S(1)}, f32[2,3,64,128]{3,2,1,0:T(8,128)S(1)}, u32[]{:S(2)}, u32[]{:S(2)}) collective-permute-start(f32[2,3,64,128]{3,2,1,0:T(8,128)S(1)} %get-tuple-element.51), channel_id=1, source_target_pairs={{0,1},{1,0},{2,3},{3,2},{4,5},{5,4},{6,7},{7,6},{8,9},{9,8},{10,11... | collective-permute-start | bytes 589832 | tf_op jit(solution)/shard_map/ppermute | solution.py:393
  5.0 10.6 %collective-permute-start.1 = (f32[2,3,64,128]{3,2,1,0:T(8,128)S(1)}, f32[2,3,64,128]{3,2,1,0:T(8,128)S(1)}, u32[]{:S(2)}, u32[]{:S(2)}) collective-permute-start(f32[2,3,64,128]{3,2,1,0:T(8,128)S(1)} %get-tuple-element.52), channel_id=1, source_target_pairs={{0,6},{1,7},{2,4},{3,5},{4,2},{5,3},{6,0},{7,1},{8,14},{9,15},{10,... | collective-permute-start | bytes 589832 | tf_op jit(solution)/shard_map/ppermute | solution.py:393
  9.6 13.9 %collective-permute-start.2 = (f32[2,3,64,128]{3,2,1,0:T(8,128)S(1)}, f32[2,3,64,128]{3,2,1,0:T(8,128)S(1)}, u32[]{:S(2)}, u32[]{:S(2)}) collective-permute-start(f32[2,3,64,128]{3,2,1,0:T(8,128)S(1)} %get-tuple-element.53), channel_id=1, source_target_pairs={{0,7},{1,6},{2,5},{3,4},{4,3},{5,2},{6,1},{7,0},{8,15},{9,14},{10,... | collective-permute-start | bytes 589832 | tf_op jit(solution)/shard_map/ppermute | solution.py:393
  9.7 14.0 %collective-permute-start.3 = (f32[2,3,64,128]{3,2,1,0:T(8,128)S(1)}, f32[2,3,64,128]{3,2,1,0:T(8,128)S(1)}, u32[]{:S(2)}, u32[]{:S(2)}) collective-permute-start(f32[2,3,64,128]{3,2,1,0:T(8,128)S(1)} %get-tuple-element.54), channel_id=1, source_target_pairs={{0,2},{1,3},{2,0},{3,1},{4,6},{5,7},{6,4},{7,5},{8,10},{9,11},{10,... | collective-permute-start | bytes 589832 | tf_op jit(solution)/shard_map/ppermute | solution.py:393
  9.7 19.1 %collective-permute-start.4 = (f32[2,3,64,128]{3,2,1,0:T(8,128)S(1)}, f32[2,3,64,128]{3,2,1,0:T(8,128)S(1)}, u32[]{:S(2)}, u32[]{:S(2)}) collective-permute-start(f32[2,3,64,128]{3,2,1,0:T(8,128)S(1)} %get-tuple-element.55), channel_id=1, source_target_pairs={{0,3},{1,2},{2,1},{3,0},{4,7},{5,6},{6,5},{7,4},{8,11},{9,10},{10,... | collective-permute-start | bytes 589832 | tf_op jit(solution)/shard_map/ppermute | solution.py:393
  12.6 27.4 %collective-permute-start.5 = (f32[2,3,64,128]{3,2,1,0:T(8,128)S(1)}, f32[2,3,64,128]{3,2,1,0:T(8,128)S(1)}, u32[]{:S(2)}, u32[]{:S(2)}) collective-permute-start(f32[2,3,64,128]{3,2,1,0:T(8,128)S(1)} %get-tuple-element.56), channel_id=1, source_target_pairs={{0,4},{1,5},{2,6},{3,7},{4,0},{5,1},{6,2},{7,3},{8,12},{9,13},{10,... | collective-permute-start | bytes 589832 | tf_op jit(solution)/shard_map/ppermute | solution.py:393
  15.6 27.7 %collective-permute-start.6 = (f32[2,3,64,128]{3,2,1,0:T(8,128)S(1)}, f32[2,3,64,128]{3,2,1,0:T(8,128)S(1)}, u32[]{:S(2)}, u32[]{:S(2)}) collective-permute-start(f32[2,3,64,128]{3,2,1,0:T(8,128)S(1)} %get-tuple-element.57), channel_id=1, source_target_pairs={{0,5},{1,4},{2,7},{3,6},{4,1},{5,0},{6,3},{7,2},{8,13},{9,12},{10,... | collective-permute-start | bytes 589832 | tf_op jit(solution)/shard_map/ppermute | solution.py:393
  44.9 5.6 %collective-permute-start.7 = (f32[3,64,128]{2,1,0:T(8,128)S(1)}, f32[3,64,128]{2,1,0:T(8,128)S(1)}, u32[]{:S(2)}, u32[]{:S(2)}) collective-permute-start(f32[3,64,128]{2,1,0:T(8,128)S(1)} %get-tuple-element.59), channel_id=1, source_target_pairs={{0,1},{1,0},{2,3},{3,2},{4,5},{5,4},{6,7},{7,6},{8,9},{9,8},{10,11... | collective-permute-start | bytes 294920 | tf_op jit(solution)/shard_map/ppermute | solution.py:393
  45.2 6.9 %collective-permute-start.8 = (f32[3,64,128]{2,1,0:T(8,128)S(1)}, f32[3,64,128]{2,1,0:T(8,128)S(1)}, u32[]{:S(2)}, u32[]{:S(2)}) collective-permute-start(f32[3,64,128]{2,1,0:T(8,128)S(1)} %get-tuple-element.60), channel_id=1, source_target_pairs={{0,6},{1,7},{2,4},{3,5},{4,2},{5,3},{6,0},{7,1},{8,14},{9,15},{10,... | collective-permute-start | bytes 294920 | tf_op jit(solution)/shard_map/ppermute | solution.py:393
  47.8 6.9 %collective-permute-start.9 = (f32[3,64,128]{2,1,0:T(8,128)S(1)}, f32[3,64,128]{2,1,0:T(8,128)S(1)}, u32[]{:S(2)}, u32[]{:S(2)}) collective-permute-start(f32[3,64,128]{2,1,0:T(8,128)S(1)} %get-tuple-element.61), channel_id=1, source_target_pairs={{0,7},{1,6},{2,5},{3,4},{4,3},{5,2},{6,1},{7,0},{8,15},{9,14},{10,... | collective-permute-start | bytes 294920 | tf_op jit(solution)/shard_map/ppermute | solution.py:393
  48.6 10.7 %collective-permute-start.10 = (f32[3,64,128]{2,1,0:T(8,128)S(1)}, f32[3,64,128]{2,1,0:T(8,128)S(1)}, u32[]{:S(2)}, u32[]{:S(2)}) collective-permute-start(f32[3,64,128]{2,1,0:T(8,128)S(1)} %get-tuple-element.62), channel_id=1, source_target_pairs={{0,2},{1,3},{2,0},{3,1},{4,6},{5,7},{6,4},{7,5},{8,10},{9,11},{10,... | collective-permute-start | bytes 294920 | tf_op jit(solution)/shard_map/ppermute | solution.py:393
  48.6 12.5 %collective-permute-start.11 = (f32[3,64,128]{2,1,0:T(8,128)S(1)}, f32[3,64,128]{2,1,0:T(8,128)S(1)}, u32[]{:S(2)}, u32[]{:S(2)}) collective-permute-start(f32[3,64,128]{2,1,0:T(8,128)S(1)} %get-tuple-element.63), channel_id=1, source_target_pairs={{0,3},{1,2},{2,1},{3,0},{4,7},{5,6},{6,5},{7,4},{8,11},{9,10},{10,... | collective-permute-start | bytes 294920 | tf_op jit(solution)/shard_map/ppermute | solution.py:393
  50.5 11.8 %collective-permute-start.12 = (f32[3,64,128]{2,1,0:T(8,128)S(1)}, f32[3,64,128]{2,1,0:T(8,128)S(1)}, u32[]{:S(2)}, u32[]{:S(2)}) collective-permute-start(f32[3,64,128]{2,1,0:T(8,128)S(1)} %get-tuple-element.64), channel_id=1, source_target_pairs={{0,4},{1,5},{2,6},{3,7},{4,0},{5,1},{6,2},{7,3},{8,12},{9,13},{10,... | collective-permute-start | bytes 294920 | tf_op jit(solution)/shard_map/ppermute | solution.py:393
  52.1 12.0 %collective-permute-start.13 = (f32[3,64,128]{2,1,0:T(8,128)S(1)}, f32[3,64,128]{2,1,0:T(8,128)S(1)}, u32[]{:S(2)}, u32[]{:S(2)}) collective-permute-start(f32[3,64,128]{2,1,0:T(8,128)S(1)} %get-tuple-element.65), channel_id=1, source_target_pairs={{0,5},{1,4},{2,7},{3,6},{4,1},{5,0},{6,3},{7,2},{8,13},{9,12},{10,... | collective-permute-start | bytes 294920 | tf_op jit(solution)/shard_map/ppermute | solution.py:393
  64.1 6.0 %copy-start.3 = (f32[6,64,512]{2,1,0:T(8,128)S(1)}, f32[6,64,512]{2,1,0:T(8,128)}, u32[]{:S(2)}) copy-start(f32[6,64,512]{2,1,0:T(8,128)} %velocity_ref.1) | copy-start | bytes 2359300
  64.1 6.0 %copy-start.4 = (s32[2,512]{1,0:T(2,128)S(1)}, s32[2,512]{1,0:T(2,128)}, u32[]{:S(2)}) copy-start(s32[2,512]{1,0:T(2,128)} %modes_ref.1) | copy-start | bytes 12292
  64.8 5.4 %collective-permute-start.14 = (f32[3,64,128]{2,1,0:T(8,128)S(1)}, f32[3,64,128]{2,1,0:T(8,128)S(1)}, u32[]{:S(2)}, u32[]{:S(2)}) collective-permute-start(f32[3,64,128]{2,1,0:T(8,128)S(1)} %get-tuple-element.68), channel_id=1, source_target_pairs={{0,3},{1,2},{2,1},{3,0},{4,7},{5,6},{6,5},{7,4},{8,11},{9,10},{10,... | collective-permute-start | bytes 294920 | tf_op jit(solution)/shard_map/ppermute | solution.py:393
  64.9 10.8 %collective-permute-start.19 = (f32[3,64,128]{2,1,0:T(8,128)S(1)}, f32[3,64,128]{2,1,0:T(8,128)S(1)}, u32[]{:S(2)}, u32[]{:S(2)}) collective-permute-start(f32[3,64,128]{2,1,0:T(8,128)S(1)} %get-tuple-element.75), channel_id=1, source_target_pairs={{0,1},{1,0},{2,3},{3,2},{4,5},{5,4},{6,7},{7,6},{8,9},{9,8},{10,11... | collective-permute-start | bytes 294920 | tf_op jit(solution)/shard_map/ppermute | solution.py:393
  65.2 12.6 %collective-permute-start.20 = (f32[3,64,128]{2,1,0:T(8,128)S(1)}, f32[3,64,128]{2,1,0:T(8,128)S(1)}, u32[]{:S(2)}, u32[]{:S(2)}) collective-permute-start(f32[3,64,128]{2,1,0:T(8,128)S(1)} %get-tuple-element.76), channel_id=1, source_target_pairs={{0,2},{1,3},{2,0},{3,1},{4,6},{5,7},{6,4},{7,5},{8,10},{9,11},{10,... | collective-permute-start | bytes 294920 | tf_op jit(solution)/shard_map/ppermute | solution.py:393
  67.0 12.4 %collective-permute-start.21 = (f32[3,64,128]{2,1,0:T(8,128)S(1)}, f32[3,64,128]{2,1,0:T(8,128)S(1)}, u32[]{:S(2)}, u32[]{:S(2)}) collective-permute-start(f32[3,64,128]{2,1,0:T(8,128)S(1)} %get-tuple-element.77), channel_id=1, source_target_pairs={{0,6},{1,7},{2,4},{3,5},{4,2},{5,3},{6,0},{7,1},{8,14},{9,15},{10,... | collective-permute-start | bytes 294920 | tf_op jit(solution)/shard_map/ppermute | solution.py:393
  68.6 10.8 %collective-permute-start.22 = (f32[3,64,128]{2,1,0:T(8,128)S(1)}, f32[3,64,128]{2,1,0:T(8,128)S(1)}, u32[]{:S(2)}, u32[]{:S(2)}) collective-permute-start(f32[3,64,128]{2,1,0:T(8,128)S(1)} %get-tuple-element.78), channel_id=1, source_target_pairs={{0,7},{1,6},{2,5},{3,4},{4,3},{5,2},{6,1},{7,0},{8,15},{9,14},{10,... | collective-permute-start | bytes 294920 | tf_op jit(solution)/shard_map/ppermute | solution.py:393
  72.0 3.7 %collective-permute-start.17 = (f32[3,64]{1,0:T(4,128)S(1)}, f32[3,64]{1,0:T(4,128)S(1)}, u32[]{:S(2)}, u32[]{:S(2)}) collective-permute-start(f32[3,64]{1,0:T(4,128)S(1)} %get-tuple-element.73), channel_id=1, source_target_pairs={{0,8},{8,0},{16,24},{24,16},{1,9},{9,1},{17,25},{25,17},{2,10},{10... | collective-permute-start | bytes 2312 | tf_op jit(solution)/shard_map/ppermute | solution.py:401
  75.7 9.0 %collective-permute-start.15 = (f32[3,64,128]{2,1,0:T(8,128)S(1)}, f32[3,64,128]{2,1,0:T(8,128)S(1)}, u32[]{:S(2)}, u32[]{:S(2)}) collective-permute-start(f32[3,64,128]{2,1,0:T(8,128)S(1)} %get-tuple-element.71), channel_id=1, source_target_pairs={{0,4},{1,5},{2,6},{3,7},{4,0},{5,1},{6,2},{7,3},{8,12},{9,13},{10,... | collective-permute-start | bytes 294920 | tf_op jit(solution)/shard_map/ppermute | solution.py:393
  75.7 10.5 %collective-permute-start.16 = (f32[3,64,128]{2,1,0:T(8,128)S(1)}, f32[3,64,128]{2,1,0:T(8,128)S(1)}, u32[]{:S(2)}, u32[]{:S(2)}) collective-permute-start(f32[3,64,128]{2,1,0:T(8,128)S(1)} %get-tuple-element.72), channel_id=1, source_target_pairs={{0,5},{1,4},{2,7},{3,6},{4,1},{5,0},{6,3},{7,2},{8,13},{9,12},{10,... | collective-permute-start | bytes 294920 | tf_op jit(solution)/shard_map/ppermute | solution.py:393
  77.9 8.3 %collective-permute-start.18 = (f32[3,64]{1,0:T(4,128)S(1)}, f32[3,64]{1,0:T(4,128)S(1)}, u32[]{:S(2)}, u32[]{:S(2)}) collective-permute-start(f32[3,64]{1,0:T(4,128)S(1)} %add.3.refs_2_), channel_id=1, source_target_pairs={{0,16},{8,24},{16,0},{24,8},{1,17},{9,25},{17,1},{25,9},{2,18},{10... | collective-permute-start | bytes 2312 | tf_op jit(solution)/shard_map/ppermute | solution.py:403

commit v12 on v9

--- a/solution.py
+++ b/solution.py
@@ -63,6 +63,14 @@
     high = x.astype(BF16)
     low = (x - high.astype(F32)).astype(BF16)
     return high, low
+
+
+def arrived(refs):
+    return [ref.at[at % 2] for at, ref in enumerate(refs)]
+
+
+def halves(refs):
+    return [ref.at[half] for ref in refs for half in range(2)]
 
 
 def selector(places, rows):
@@ -131,7 +139,7 @@
     rows = comps * points
     both = jnp.concatenate([state.reshape(rows, columns), local.reshape(rows, columns)], axis=0)
     placed = sum_parts(lax.dot_general(three_parts(both), chosen, NT, preferred_element_type=F32))
-    for step, out in zip(steps_of(devices, points), out_refs):
+    for step, out in zip(steps_of(devices, points), halves(out_refs)):
         taken = placed[:, step * share : (step + 1) * share]
         for kind in range(2):
             real = 2 * kind * points
@@ -142,7 +150,7 @@
 def first_kernel(
     devices, me_ref, owner_hbm, modes_hbm, state_hbm, now_hbm, old_hbm, info_ref, wave_ref, *refs
 ):
-    out_refs, (owner_ref, modes_ref, state_ref, now_ref, old_ref, sems) = refs[:devices], refs[devices:]
+    out_refs, (owner_ref, modes_ref, state_ref, now_ref, old_ref, sems) = refs[:-6], refs[-6:]
     columns = owner_ref.shape[1]
     copies = [
         pltpu.make_async_copy(owner_hbm, owner_ref, sems.at[0]),
@@ -215,14 +223,14 @@
 
 
 def solve_early_kernel(steps, me_ref, *refs):
-    operators, in_refs, (out_ref, state, local) = refs[:4], refs[4:-3], refs[-3:]
+    operators, in_refs, (out_ref, state, local) = refs[:4], arrived(refs[4:-3]), refs[-3:]
     out_ref[...] = projected(me_ref[0], operators, steps, in_refs, state, local)
 
 
 def solve_late_kernel(steps, order, me_ref, wave_ref, values_ref, basis_ref, early_ref, *refs):
     operators, refs = refs[:4], refs[4:]
-    in_refs, refs = refs[: len(steps)], refs[len(steps) :]
-    out_refs, (solved_ref, state, local, after) = refs[:-4], refs[-4:]
+    in_refs, refs = arrived(refs[: len(steps)]), refs[len(steps) :]
+    out_refs, (solved_ref, state, local, after) = halves(refs[:-4]), refs[-4:]
     me = me_ref[0]
     pairs, points, lanes = out_refs[0].shape
     project = early_ref[...] + projected(me, operators, steps, in_refs, state, local)
@@ -253,7 +261,7 @@
 
 
 def surplus_early_kernel(steps, info_ref, *refs):
-    in_refs, (out_ref, late_ref) = refs[:-2], refs[-2:]
+    in_refs, (out_ref, late_ref) = arrived(refs[:-2]), refs[-2:]
     columns = info_ref.shape[1]
     share = in_refs[0].shape[2] // 2
     chosen = lax.dot_general(
@@ -270,7 +278,7 @@
 
 
 def surplus_late_kernel(steps, order, early_ref, chosen_ref, *refs):
-    in_refs, out_refs = refs[: len(steps)], refs[len(steps) :]
+    in_refs, out_refs = arrived(refs[: len(steps)]), halves(refs[len(steps) :])
     pairs, points, lanes = in_refs[0].shape
     share = lanes // 2
     extra = early_ref[...] + sum_parts(
@@ -285,7 +293,7 @@
 
 
 def state_kernel(order, info_ref, modes_ref, velocity_ref, *refs):
-    in_refs, (_, state_hbm, emf_ref, state_ref, sem) = refs[: len(order)], refs[len(order) :]
+    in_refs, (_, state_hbm, emf_ref, state_ref, sem) = arrived(refs[: len(order)]), refs[len(order) :]
     comps, points, columns = state_ref.shape
     state = sum_parts(
         jnp.dot(
@@ -354,13 +362,13 @@
 
 
 def assemble_early_kernel(steps, me_ref, info_ref, solved_ref, *refs):
-    in_refs, (out_hbm, rows_ref, sems) = refs[: len(steps)], refs[len(steps) :]
+    in_refs, (out_hbm, rows_ref, sems) = arrived(refs[: len(steps)]), refs[len(steps) :]
     share = in_refs[0].shape[2] // 2
     assemble(me_ref[0], steps, unused(info_ref, share), solved_ref, in_refs, out_hbm, rows_ref, sems)
 
 
 def assemble_late_kernel(steps, terms, me_ref, info_ref, solved_ref, *refs):
-    in_refs, refs = refs[: len(steps)], refs[len(steps) :]
+    in_refs, refs = arrived(refs[: len(steps)]), refs[len(steps) :]
     parts, (_, out_hbm, emf_ref, rows_ref, sems) = refs[:terms], refs[terms:]
     parts = [ref[...] for ref in parts]
     while len(parts) > 1:
@@ -383,12 +391,21 @@
     return early_steps(devices, points) + late_steps(devices, points)
 
 
+def send(blocks, steps):
+    devices = len(steps)
+    return [
+        lax.ppermute(block, "col", [(i, i ^ step) for i in range(devices)]) if step else block
+        for step, block in zip(steps[::2], blocks)
+    ]
+
+
+def hand_over(block):
+    devices = lax.axis_size("col")
+    return lax.ppermute(block, "col", [(i, i ^ 1) for i in range(devices)])
+
+
 def exchange(blocks, steps):
-    devices = len(blocks)
-    return [
-        block if step == 0 else lax.ppermute(block, "col", [(i, i ^ step) for i in range(devices)])
-        for step, block in zip(steps, blocks)
-    ]
+    return [array for block in send(blocks, steps) for array in (block, hand_over(block))]
 
 
 def from_groups(value):
@@ -420,7 +437,7 @@
     early, late = early_steps(devices, points), late_steps(devices, points)
     split = len(early)
     early_rows, late_rows = split * points, len(late) * points
-    back = [shaped((PAIRS, points, lanes))] * devices
+    back = [shaped((2, PAIRS, points, lanes))] * (devices // 2)
     me = lax.axis_index("col").astype(jnp.int32).reshape(1)
     far = [
         pltpu.with_memory_space_constraint(array, pltpu.HBM)
@@ -429,9 +446,9 @@
 
     outs = call(
         functools.partial(first_kernel, devices),
-        [shaped((8, columns), jnp.int32), shaped((8, lanes))] + [shaped((2, PAIRS, points, lanes))] * devices,
+        [shaped((8, columns), jnp.int32), shaped((8, lanes))] + [shaped((2, 2, PAIRS, points, lanes))] * (devices // 2),
         [SCALAR] + [FAR] * 5,
-        [LOCAL] * (2 + devices),
+        [LOCAL] * (2 + devices // 2),
         1,
         [pltpu.VMEM((1, columns), jnp.int32), pltpu.VMEM((2, columns), jnp.int32)]
         + [pltpu.VMEM((comps, points, columns), F32)] * 3
@@ -462,12 +479,12 @@
         functools.partial(solve_late_kernel, late, steps),
         back + [shaped((PAIRS, depth, lanes))],
         [SCALAR] + [LOCAL] * (8 + len(late)),
-        [LOCAL] * (devices + 1),
+        [LOCAL] * (devices // 2 + 1),
         1,
         [pltpu.VMEM((late_rows, width), F32)] * 2 + [pltpu.VMEM((depth, width), F32)],
     )(me, wave, values, basis, begun, *operators[:4], *forward[split:])
-    solved = outs[devices]
-    returned = exchange(outs[:devices], steps)
+    solved = outs[-1]
+    returned = exchange(outs[:-1], steps)
 
     begun, chosen = call(
         functools.partial(surplus_early_kernel, early),
@@ -480,10 +497,12 @@
         functools.partial(surplus_late_kernel, late, steps),
         back,
         [LOCAL] * (2 + len(late)),
-        [LOCAL] * devices,
+        [LOCAL] * (devices // 2),
         1,
     )(begun, chosen, *returned[split:])
-    extra = exchange(outs, steps)
+    sent = send(outs, steps)
+    own = steps[::2].index(0)
+    handed = hand_over(sent[own])
 
     state_next, emf = call(
         functools.partial(state_kernel, steps),
@@ -492,8 +511,15 @@
         [FAR, LOCAL],
         HEAVY,
         [pltpu.VMEM(state_now.shape, F32), pltpu.SemaphoreType.DMA],
-    )(info, kept_modes, velocity, *returned, extra[early.index(3)])
+    )(info, kept_modes, velocity, *returned, handed)
     terms = from_groups(emf)
+    near = steps[::2].index(2)
+    sent[near], _ = lax.optimization_barrier((sent[near], terms[-1]))
+    extra = [
+        array
+        for at, block in enumerate(sent)
+        for array in (block, handed if at == own else hand_over(block))
+    ]
 
     owned = call(
         functools.partial(assemble_early_kernel, early),

time: 87.8 us -> 90 us (1.025); the launches traced: 86.5 us -> 89.9 us
  waiting for transfers between devices: 33.5 us -> 54 us
  starting transfers between devices: 37.8 us -> 20.5 us
    ppermute x21, waiting for transfers between devices: 33.4 us -> 53.2 us  [the longest x9 52.7 us: send(): lax.ppermute(block, 'col', [(i, i ^ step) for i in range(devices)])]
    ppermute x21, starting transfers between devices: 33.3 us -> 15 us  [the longest x9 14.6 us: send(): lax.ppermute(block, 'col', [(i, i ^ step) for i in range(devices)])]
    ppermute x3, starting transfers between devices: 4.45 us -> 5.53 us  [from_groups(): lax.ppermute(value, 'grp', [(i, i ^ step) for i in range(groups)])]
  transfers between devices with their start and end apart: 24 -> 24, of which waited for: 13 -> 11; matrix products, arithmetic and copies ran while one was open for 0% -> 0% of each run, Pallas kernels for 8% -> 8%
where the time goes in v12:
time: 90 us; the launch traced here: 89.9 us
  waiting for transfers between devices  54 us (60%)
  starting transfers between devices  20.5 us (23%)
  Pallas kernels  14.5 us (16%)
    ppermute x9, waiting for transfers between devices, send(): lax.ppermute(block, 'col', [(i, i ^ step) for i in range(devices)])  52.7 us
    ppermute x9, starting transfers between devices, send(): lax.ppermute(block, 'col', [(i, i ^ step) for i in range(devices)])  14.6 us
    ppermute x3, starting transfers between devices, from_groups(): lax.ppermute(value, 'grp', [(i, i ^ step) for i in range(groups)])  5.53 us
    pallas_call x1, Pallas kernels, on_device(): call(functools.partial(first_kernel, devices), [shaped((8, columns), jnp....  3.76 us
    pallas_call x1, Pallas kernels, on_device(): call(functools.partial(state_kernel, steps), [shaped(state_now.shape), sh...  1.85 us
  transfers between devices with their start and end apart: 24, of which 11 were waited for; matrix products, arithmetic and copies ran while one was open for 0% of the time, Pallas kernels for 8%

profile of v12, /device:TPU:0, one launch (start us, length us, event | category | flops | bytes accessed | tf_op | source)
XLA Modules:
  0.0 89.9 jit_solution(7341739934479989343)
XLA Ops:
  0.7 3.8 %shard_map.121 = (s32[8,512]{1,0:T(8,128)S(1)}, f32[8,128]{1,0:T(8,128)S(1)}, f32[2,2,3,64,128]{4,3,2,1,0:T(8,128)S(1)}, f32[2,2,3,64,128]{4,3,2,1,0:T(8,128)S(1...) custom-call(s32[1]{0:T(128)} %bitcast.me_ref, s32[1,512]{1,0:T(1,128)} %bitcast.4, ...), custom_call_target="tpu_custom_call" | custom-call | flops 1000000000 | bytes 1000000 | tf_op jit(solution)/shard_map/pallas_call | solution.py:447
  4.4 5.1 %collective-permute-start.1 = (f32[2,2,3,64,128]{4,3,2,1,0:T(8,128)S(1)}, f32[2,2,3,64,128]{4,3,2,1,0:T(8,128)S(1)}, u32[]{:S(2)}, u32[]{:S(2)}) collective-permute-start(f32[2,2,3,64,128]{4,3,2,1,0:T(8,128)S(1)} %get-tuple-element.40), channel_id=1, source_target_pairs={{0,6},{1,7},{2,4},{3,5},{4,2},{5,3},{6,0},{7,1},{8,14},{9,15},{10,... | collective-permute-start | bytes 1179656 | tf_op jit(solution)/shard_map/ppermute | solution.py:397
  9.6 0.0 collective-permute-start.3
  9.6 0.0 collective-permute-start
  9.6 0.6 collective-permute-start.5
  10.2 9.4 %collective-permute-done.1.refs_6_ = f32[2,2,3,64,128]{4,3,2,1,0:T(8,128)S(1)} collective-permute-done((f32[2,2,3,64,128]{4,3,2,1,0:T(8,128)S(1)}, f32[2,2,3,64,128]{4,3,2,1,0:T(8,128)S(1)}, u32[]{:S(2)}, u32[]{:S(2)}) %collective-permute-start.1) | collective-permute-done | bytes 393248 | tf_op jit(solution)/shard_map/ppermute | solution.py:397
  19.6 0.0 collective-permute-start.2
  19.6 8.6 %collective-permute-done.3.refs_8_ = f32[2,2,3,64,128]{4,3,2,1,0:T(8,128)S(1)} collective-permute-done((f32[2,2,3,64,128]{4,3,2,1,0:T(8,128)S(1)}, f32[2,2,3,64,128]{4,3,2,1,0:T(8,128)S(1)}, u32[]{:S(2)}, u32[]{:S(2)}) %collective-permute-start.3) | collective-permute-done | bytes 393248 | tf_op jit(solution)/shard_map/ppermute | solution.py:397
  28.3 1.4 %shard_map.122 = (bf16[512,512]{1,0:T(8,128)(2,1)S(1)}, bf16[512,512]{1,0:T(8,128)(2,1)S(1)}, bf16[512,512]{1,0:T(8,128)(2,1)S(1)}, bf16[512,512]{1,0:T(8,128)(2...) custom-call(f32[512,512]{1,0:T(8,128)S(1)} %copy-done, f32[512,512]{1,0:T(8,128)S(1)} %copy-done.1, ...), custom_call_target="tpu_custom_call" | custom-call | flops 10000000000 | bytes 10000000 | tf_op jit(solution)/shard_map/pallas_call | solution.py:461
  29.6 13.5 %collective-permute-done.5.refs_4_ = f32[2,2,3,64,128]{4,3,2,1,0:T(8,128)S(1)} collective-permute-done((f32[2,2,3,64,128]{4,3,2,1,0:T(8,128)S(1)}, f32[2,2,3,64,128]{4,3,2,1,0:T(8,128)S(1)}, u32[]{:S(2)}, u32[]{:S(2)}) %collective-permute-start.5) | collective-permute-done | bytes 393248 | tf_op jit(solution)/shard_map/ppermute | solution.py:397
  43.1 0.0 collective-permute-done.refs_5_
  43.1 0.0 collective-permute-done.2.refs_7_
  43.1 0.0 collective-permute-done.4.refs_9_
  43.1 1.4 %shard_map.123.early_ref = f32[512,384]{1,0:T(8,128)S(1)} custom-call(s32[1]{0:T(128)} %bitcast.me_ref, bf16[512,512]{1,0:T(8,128)(2,1)S(1)} %get-tuple-element.35.refs_0_, bf16[512,512]{1,0:T(8,128)(2,1)S(1)} %get-tuple-element.36.refs_1_, bf16[512,512]{1,0:T(8,128)(2,1)S(1)} %get-tuple-element.37.refs_2_, bf16[512,512]{1,0:T(8,128)(2,1)S(1)} %get-tuple-element.38.refs_3_, ...), custom_call_target="tpu_custom_call" | custom-call | flops 10000000000 | bytes 10000000 | tf_op jit(solution)/shard_map/pallas_call | solution.py:470
  44.6 0.3 collective-permute-done.6.refs_5_
  44.8 1.5 %shard_map.124 = (f32[2,3,64,128]{3,2,1,0:T(8,128)S(1)}, f32[2,3,64,128]{3,2,1,0:T(8,128)S(1)}, f32[2,3,64,128]{3,2,1,0:T(8,128)S(1)}, f32[2,3,64,128]{3,2,1,0:T(8,128)S(1)}, f32[3,512,128]{2,1,0:T(8,128)S(1)}) custom-call(s32[1]{0:T(128)} %bitcast.me_ref, f32[8,128]{1,0:T(8,128)S(1)} %get-tuple-element.32.wave_ref, ...), custom_call_target="tpu_custom_call" | custom-call | flops 1000000000 | bytes 1000000 | tf_op jit(solution)/shard_map/pallas_call | solution.py:478
  46.4 2.5 %collective-permute-start.8 = (f32[2,3,64,128]{3,2,1,0:T(8,128)S(1)}, f32[2,3,64,128]{3,2,1,0:T(8,128)S(1)}, u32[]{:S(2)}, u32[]{:S(2)}) collective-permute-start(f32[2,3,64,128]{3,2,1,0:T(8,128)S(1)} %get-tuple-element.44), channel_id=1, source_target_pairs={{0,6},{1,7},{2,4},{3,5},{4,2},{5,3},{6,0},{7,1},{8,14},{9,15},{10,... | collective-permute-start | bytes 589832 | tf_op jit(solution)/shard_map/ppermute | solution.py:397
  48.9 0.0 collective-permute-start.10
  48.9 0.0 collective-permute-start.7
  48.9 1.9 %collective-permute-start.12 = (f32[2,3,64,128]{3,2,1,0:T(8,128)S(1)}, f32[2,3,64,128]{3,2,1,0:T(8,128)S(1)}, u32[]{:S(2)}, u32[]{:S(2)}) collective-permute-start(f32[2,3,64,128]{3,2,1,0:T(8,128)S(1)} %get-tuple-element.46), channel_id=1, source_target_pairs={{0,4},{1,5},{2,6},{3,7},{4,0},{5,1},{6,2},{7,3},{8,12},{9,13},{10,... | collective-permute-start | bytes 589832 | tf_op jit(solution)/shard_map/ppermute | solution.py:397
  50.8 5.2 %collective-permute-done.8.refs_2_ = f32[2,3,64,128]{3,2,1,0:T(8,128)S(1)} collective-permute-done((f32[2,3,64,128]{3,2,1,0:T(8,128)S(1)}, f32[2,3,64,128]{3,2,1,0:T(8,128)S(1)}, u32[]{:S(2)}, u32[]{:S(2)}) %collective-permute-start.8) | collective-permute-done | bytes 196640 | tf_op jit(solution)/shard_map/ppermute | solution.py:397
  56.1 0.0 collective-permute-start.9
  56.1 6.4 %collective-permute-done.10.refs_4_ = f32[2,3,64,128]{3,2,1,0:T(8,128)S(1)} collective-permute-done((f32[2,3,64,128]{3,2,1,0:T(8,128)S(1)}, f32[2,3,64,128]{3,2,1,0:T(8,128)S(1)}, u32[]{:S(2)}, u32[]{:S(2)}) %collective-permute-start.10) | collective-permute-done | bytes 196640 | tf_op jit(solution)/shard_map/ppermute | solution.py:397
  62.5 0.0 collective-permute-start.11
  62.5 2.7 %collective-permute-done.12.refs_0_.refs_6_ = f32[2,3,64,128]{3,2,1,0:T(8,128)S(1)} collective-permute-done((f32[2,3,64,128]{3,2,1,0:T(8,128)S(1)}, f32[2,3,64,128]{3,2,1,0:T(8,128)S(1)}, u32[]{:S(2)}, u32[]{:S(2)}) %collective-permute-start.12) | collective-permute-done | bytes 196640 | tf_op jit(solution)/shard_map/ppermute | solution.py:397
  65.3 0.0 collective-permute-done.11.refs_5_
  65.3 1.2 %shard_map.125 = (f32[384,512]{1,0:T(8,128)S(1)}, bf16[128,512]{1,0:T(8,128)(2,1)S(1)}) custom-call(s32[8,512]{1,0:T(8,128)S(1)} %get-tuple-element.31.info_ref, f32[2,3,64,128]{3,2,1,0:T(8,128)S(1)} %get-tuple-element.43.refs_0_, f32[2,3,64,128]{3,2,1,0:T(8,128)S(1)} %collective-permute-done.7.refs_1_, ...), custom_call_target="tpu_custom_call" | custom-call | flops 10000000000 | bytes 10000000 | tf_op jit(solution)/shard_map/pallas_call | solution.py:489
  66.4 0.3 collective-permute-done.13.refs_1_.refs_7_
  66.7 0.7 shard_map.126
  67.4 0.3 collective-permute-start.14
  67.7 1.3 %collective-permute-start.20 = (f32[2,3,64,128]{3,2,1,0:T(8,128)S(1)}, f32[2,3,64,128]{3,2,1,0:T(8,128)S(1)}, u32[]{:S(2)}, u32[]{:S(2)}) collective-permute-start(f32[2,3,64,128]{3,2,1,0:T(8,128)S(1)} %get-tuple-element.54), channel_id=1, source_target_pairs={{0,6},{1,7},{2,4},{3,5},{4,2},{5,3},{6,0},{7,1},{8,14},{9,15},{10,... | collective-permute-start | bytes 589832 | tf_op jit(solution)/shard_map/ppermute | solution.py:397
  69.1 0.0 collective-permute-start.22
  69.1 1.9 %shard_map.127 = (f32[6,64,512]{2,1,0:T(8,128)}, f32[3,64]{1,0:T(4,128)S(1)}) custom-call(s32[8,512]{1,0:T(8,128)S(1)} %get-tuple-element.31.info_ref, s32[2,512]{1,0:T(2,128)S(1)} %copy-done.4, f32[6,64,512]{2,1,0:T(8,128)S(1)} %copy-done.3, f32[2,3,64,128]{3,2,1,0:T(8,128)S(1)} %get-tuple-element.43.refs_0_, ...), custom_call_target="tpu_custom_call" | custom-call | flops 10000000000 | bytes 10000000 | tf_op jit(solution)/shard_map/pallas_call | solution.py:507
  71.0 2.5 %collective-permute-start.19 = (f32[3,64]{1,0:T(4,128)S(1)}, f32[3,64]{1,0:T(4,128)S(1)}, u32[]{:S(2)}, u32[]{:S(2)}) collective-permute-start(f32[3,64]{1,0:T(4,128)S(1)} %get-tuple-element.53.refs_2_), channel_id=1, source_target_pairs={{0,24},{8,16},{16,8},{24,0},{1,25},{9,17},{17,9},{25,1},{2,26},{10... | collective-permute-start | bytes 2312 | tf_op jit(solution)/shard_map/ppermute | solution.py:414
  73.5 3.0 %collective-permute-start.15 = (f32[2,3,64,128]{3,2,1,0:T(8,128)S(1)}, f32[2,3,64,128]{3,2,1,0:T(8,128)S(1)}, u32[]{:S(2)}, u32[]{:S(2)}) collective-permute-start(f32[2,3,64,128]{3,2,1,0:T(8,128)S(1)} %get-tuple-element.52), channel_id=1, source_target_pairs={{0,4},{1,5},{2,6},{3,7},{4,0},{5,1},{6,2},{7,3},{8,12},{9,13},{10,... | collective-permute-start | bytes 589832 | tf_op jit(solution)/shard_map/ppermute | solution.py:397
  76.5 0.8 collective-permute-done.20.refs_2_
  77.3 0.0 collective-permute-start.21
  77.3 6.0 %collective-permute-done.22.refs_4_ = f32[2,3,64,128]{3,2,1,0:T(8,128)S(1)} collective-permute-done((f32[2,3,64,128]{3,2,1,0:T(8,128)S(1)}, f32[2,3,64,128]{3,2,1,0:T(8,128)S(1)}, u32[]{:S(2)}, u32[]{:S(2)}) %collective-permute-start.22) | collective-permute-done | bytes 196640 | tf_op jit(solution)/shard_map/ppermute | solution.py:397
  83.3 0.0 collective-permute-done.19.refs_5_
  83.3 0.0 collective-permute-start.23
  83.3 1.5 %collective-permute-start.17 = (f32[3,64]{1,0:T(4,128)S(1)}, f32[3,64]{1,0:T(4,128)S(1)}, u32[]{:S(2)}, u32[]{:S(2)}) collective-permute-start(f32[3,64]{1,0:T(4,128)S(1)} %get-tuple-element.53.refs_2_), channel_id=1, source_target_pairs={{0,8},{8,0},{16,24},{24,16},{1,9},{9,1},{17,25},{25,17},{2,10},{10... | collective-permute-start | bytes 2312 | tf_op jit(solution)/shard_map/ppermute | solution.py:414
  84.8 1.5 %collective-permute-start.18 = (f32[3,64]{1,0:T(4,128)S(1)}, f32[3,64]{1,0:T(4,128)S(1)}, u32[]{:S(2)}, u32[]{:S(2)}) collective-permute-start(f32[3,64]{1,0:T(4,128)S(1)} %get-tuple-element.53.refs_2_), channel_id=1, source_target_pairs={{0,16},{8,24},{16,0},{24,8},{1,17},{9,25},{17,1},{25,9},{2,18},{10... | collective-permute-start | bytes 2312 | tf_op jit(solution)/shard_map/ppermute | solution.py:414
  86.3 0.0 collective-permute-done.21.refs_3_
  86.4 0.0 collective-permute-done.23.refs_5_
  86.4 1.2 %shard_map.128.refs_6_ = f32[6,512,128]{2,1,0:T(8,128)} custom-call(s32[1]{0:T(128)} %bitcast.me_ref, s32[8,512]{1,0:T(8,128)S(1)} %get-tuple-element.31.info_ref, f32[3,512,128]{2,1,0:T(8,128)S(1)} %get-tuple-element.51.solved_ref, f32[2,3,64,128]{3,2,1,0:T(8,128)S(1)} %get-tuple-element.49.refs_0_, ...), custom_call_target="tpu_custom_call" | custom-call | flops 10000000000 | bytes 10000000 | tf_op jit(solution)/shard_map/pallas_call | solution.py:524
  87.6 0.0 collective-permute-done.17.refs_3_
  87.6 0.8 collective-permute-done.18.refs_4_
  88.4 1.4 %shard_map.129 = (f32[6,512,128]{2,1,0:T(8,128)}, f32[3,64]{1,0:T(4,128)}) custom-call(s32[1]{0:T(128)} %bitcast.me_ref, s32[8,512]{1,0:T(8,128)S(1)} %get-tuple-element.31.info_ref, f32[3,512,128]{2,1,0:T(8,128)S(1)} %get-tuple-element.51.solved_ref, f32[2,3,64,128]{3,2,1,0:T(8,128)S(1)} %collective-permute-done.15.refs_0_, ...), custom_call_target="tpu_custom_call", output_to_operand_aliasing={{0}: (9, {})} | custom-call | flops 1000000000 | bytes 1000000 | tf_op jit(solution)/shard_map/pallas_call | solution.py:535
  (21 shorter events, 0.0 us)
Async XLA Ops:
  0.6 27.6 %copy-start = (f32[512,512]{1,0:T(8,128)S(1)}, f32[512,512]{1,0:T(8,128)}, u32[]{:S(2)}) copy-start(f32[512,512]{1,0:T(8,128)} %deriv_ref.1) | copy-start | bytes 3145732
  0.6 27.6 %copy-start.1 = (f32[512,512]{1,0:T(8,128)S(1)}, f32[512,512]{1,0:T(8,128)}, u32[]{:S(2)}) copy-start(f32[512,512]{1,0:T(8,128)} %inverse_ref.1) | copy-start | bytes 3145732
  0.7 27.6 %copy-start.2 = (f32[512,512]{1,0:T(8,128)S(1)}, f32[512,512]{1,0:T(8,128)}, u32[]{:S(2)}) copy-start(f32[512,512]{1,0:T(8,128)} %basis_ref.1) | copy-start | bytes 3145732
  0.7 27.6 %copy-start.5 = (f32[512]{0:T(512)S(1)}, f32[512]{0:T(512)}, u32[]{:S(2)}) copy-start(f32[512]{0:T(512)} %param.17) | copy-start | bytes 6148
  4.4 15.2 %collective-permute-start.1 = (f32[2,2,3,64,128]{4,3,2,1,0:T(8,128)S(1)}, f32[2,2,3,64,128]{4,3,2,1,0:T(8,128)S(1)}, u32[]{:S(2)}, u32[]{:S(2)}) collective-permute-start(f32[2,2,3,64,128]{4,3,2,1,0:T(8,128)S(1)} %get-tuple-element.40), channel_id=1, source_target_pairs={{0,6},{1,7},{2,4},{3,5},{4,2},{5,3},{6,0},{7,1},{8,14},{9,15},{10,... | collective-permute-start | bytes 1179656 | tf_op jit(solution)/shard_map/ppermute | solution.py:397
  9.6 18.7 %collective-permute-start.3 = (f32[2,2,3,64,128]{4,3,2,1,0:T(8,128)S(1)}, f32[2,2,3,64,128]{4,3,2,1,0:T(8,128)S(1)}, u32[]{:S(2)}, u32[]{:S(2)}) collective-permute-start(f32[2,2,3,64,128]{4,3,2,1,0:T(8,128)S(1)} %get-tuple-element.41), channel_id=1, source_target_pairs={{0,2},{1,3},{2,0},{3,1},{4,6},{5,7},{6,4},{7,5},{8,10},{9,11},{10,... | collective-permute-start | bytes 1179656 | tf_op jit(solution)/shard_map/ppermute | solution.py:397
  9.6 33.5 %collective-permute-start = (f32[2,2,3,64,128]{4,3,2,1,0:T(8,128)S(1)}, f32[2,2,3,64,128]{4,3,2,1,0:T(8,128)S(1)}, u32[]{:S(2)}, u32[]{:S(2)}) collective-permute-start(f32[2,2,3,64,128]{4,3,2,1,0:T(8,128)S(1)} %get-tuple-element.39.refs_4_), channel_id=1, source_target_pairs={{0,1},{1,0},{2,3},{3,2},{4,5},{5,4},{6,7},{7,6},{8,9},{9,8},{10,11... | collective-permute-start | bytes 1179656 | tf_op jit(solution)/shard_map/ppermute | solution.py:404
  9.6 33.5 %collective-permute-start.5 = (f32[2,2,3,64,128]{4,3,2,1,0:T(8,128)S(1)}, f32[2,2,3,64,128]{4,3,2,1,0:T(8,128)S(1)}, u32[]{:S(2)}, u32[]{:S(2)}) collective-permute-start(f32[2,2,3,64,128]{4,3,2,1,0:T(8,128)S(1)} %get-tuple-element.42), channel_id=1, source_target_pairs={{0,4},{1,5},{2,6},{3,7},{4,0},{5,1},{6,2},{7,3},{8,12},{9,13},{10,... | collective-permute-start | bytes 1179656 | tf_op jit(solution)/shard_map/ppermute | solution.py:397
  19.6 23.5 %collective-permute-start.2 = (f32[2,2,3,64,128]{4,3,2,1,0:T(8,128)S(1)}, f32[2,2,3,64,128]{4,3,2,1,0:T(8,128)S(1)}, u32[]{:S(2)}, u32[]{:S(2)}) collective-permute-start(f32[2,2,3,64,128]{4,3,2,1,0:T(8,128)S(1)} %collective-permute-done.1.refs_6_), channel_id=1, source_target_pairs={{0,1},{1,0},{2,3},{3,2},{4,5},{5,4},{6,7},{7,6},{8,9},{9,8},{10,11... | collective-permute-start | bytes 1179656 | tf_op jit(solution)/shard_map/ppermute | solution.py:404
  28.2 14.9 %collective-permute-start.4 = (f32[2,2,3,64,128]{4,3,2,1,0:T(8,128)S(1)}, f32[2,2,3,64,128]{4,3,2,1,0:T(8,128)S(1)}, u32[]{:S(2)}, u32[]{:S(2)}) collective-permute-start(f32[2,2,3,64,128]{4,3,2,1,0:T(8,128)S(1)} %collective-permute-done.3.refs_8_), channel_id=1, source_target_pairs={{0,1},{1,0},{2,3},{3,2},{4,5},{5,4},{6,7},{7,6},{8,9},{9,8},{10,11... | collective-permute-start | bytes 1179656 | tf_op jit(solution)/shard_map/ppermute | solution.py:404
  43.1 1.7 %collective-permute-start.6 = (f32[2,2,3,64,128]{4,3,2,1,0:T(8,128)S(1)}, f32[2,2,3,64,128]{4,3,2,1,0:T(8,128)S(1)}, u32[]{:S(2)}, u32[]{:S(2)}) collective-permute-start(f32[2,2,3,64,128]{4,3,2,1,0:T(8,128)S(1)} %collective-permute-done.5.refs_4_), channel_id=1, source_target_pairs={{0,1},{1,0},{2,3},{3,2},{4,5},{5,4},{6,7},{7,6},{8,9},{9,8},{10,11... | collective-permute-start | bytes 1179656 | tf_op jit(solution)/shard_map/ppermute | solution.py:404
  46.4 9.7 %collective-permute-start.8 = (f32[2,3,64,128]{3,2,1,0:T(8,128)S(1)}, f32[2,3,64,128]{3,2,1,0:T(8,128)S(1)}, u32[]{:S(2)}, u32[]{:S(2)}) collective-permute-start(f32[2,3,64,128]{3,2,1,0:T(8,128)S(1)} %get-tuple-element.44), channel_id=1, source_target_pairs={{0,6},{1,7},{2,4},{3,5},{4,2},{5,3},{6,0},{7,1},{8,14},{9,15},{10,... | collective-permute-start | bytes 589832 | tf_op jit(solution)/shard_map/ppermute | solution.py:397
  48.9 13.6 %collective-permute-start.10 = (f32[2,3,64,128]{3,2,1,0:T(8,128)S(1)}, f32[2,3,64,128]{3,2,1,0:T(8,128)S(1)}, u32[]{:S(2)}, u32[]{:S(2)}) collective-permute-start(f32[2,3,64,128]{3,2,1,0:T(8,128)S(1)} %get-tuple-element.45), channel_id=1, source_target_pairs={{0,2},{1,3},{2,0},{3,1},{4,6},{5,7},{6,4},{7,5},{8,10},{9,11},{10,... | collective-permute-start | bytes 589832 | tf_op jit(solution)/shard_map/ppermute | solution.py:397
  48.9 16.3 %collective-permute-start.7 = (f32[2,3,64,128]{3,2,1,0:T(8,128)S(1)}, f32[2,3,64,128]{3,2,1,0:T(8,128)S(1)}, u32[]{:S(2)}, u32[]{:S(2)}) collective-permute-start(f32[2,3,64,128]{3,2,1,0:T(8,128)S(1)} %get-tuple-element.43.refs_0_), channel_id=1, source_target_pairs={{0,1},{1,0},{2,3},{3,2},{4,5},{5,4},{6,7},{7,6},{8,9},{9,8},{10,11... | collective-permute-start | bytes 589832 | tf_op jit(solution)/shard_map/ppermute | solution.py:404
  48.9 16.3 %collective-permute-start.12 = (f32[2,3,64,128]{3,2,1,0:T(8,128)S(1)}, f32[2,3,64,128]{3,2,1,0:T(8,128)S(1)}, u32[]{:S(2)}, u32[]{:S(2)}) collective-permute-start(f32[2,3,64,128]{3,2,1,0:T(8,128)S(1)} %get-tuple-element.46), channel_id=1, source_target_pairs={{0,4},{1,5},{2,6},{3,7},{4,0},{5,1},{6,2},{7,3},{8,12},{9,13},{10,... | collective-permute-start | bytes 589832 | tf_op jit(solution)/shard_map/ppermute | solution.py:397
  56.1 9.2 %collective-permute-start.9 = (f32[2,3,64,128]{3,2,1,0:T(8,128)S(1)}, f32[2,3,64,128]{3,2,1,0:T(8,128)S(1)}, u32[]{:S(2)}, u32[]{:S(2)}) collective-permute-start(f32[2,3,64,128]{3,2,1,0:T(8,128)S(1)} %collective-permute-done.8.refs_2_), channel_id=1, source_target_pairs={{0,1},{1,0},{2,3},{3,2},{4,5},{5,4},{6,7},{7,6},{8,9},{9,8},{10,11... | collective-permute-start | bytes 589832 | tf_op jit(solution)/shard_map/ppermute | solution.py:404
  62.5 2.8 %collective-permute-start.11 = (f32[2,3,64,128]{3,2,1,0:T(8,128)S(1)}, f32[2,3,64,128]{3,2,1,0:T(8,128)S(1)}, u32[]{:S(2)}, u32[]{:S(2)}) collective-permute-start(f32[2,3,64,128]{3,2,1,0:T(8,128)S(1)} %collective-permute-done.10.refs_4_), channel_id=1, source_target_pairs={{0,1},{1,0},{2,3},{3,2},{4,5},{5,4},{6,7},{7,6},{8,9},{9,8},{10,11... | collective-permute-start | bytes 589832 | tf_op jit(solution)/shard_map/ppermute | solution.py:404
  65.2 1.4 %collective-permute-start.13 = (f32[2,3,64,128]{3,2,1,0:T(8,128)S(1)}, f32[2,3,64,128]{3,2,1,0:T(8,128)S(1)}, u32[]{:S(2)}, u32[]{:S(2)}) collective-permute-start(f32[2,3,64,128]{3,2,1,0:T(8,128)S(1)} %collective-permute-done.12.refs_0_.refs_6_), channel_id=1, source_target_pairs={{0,1},{1,0},{2,3},{3,2},{4,5},{5,4},{6,7},{7,6},{8,9},{9,8},{10,11... | collective-permute-start | bytes 589832 | tf_op jit(solution)/shard_map/ppermute | solution.py:404
  66.7 2.4 %copy-start.3 = (f32[6,64,512]{2,1,0:T(8,128)S(1)}, f32[6,64,512]{2,1,0:T(8,128)}, u32[]{:S(2)}) copy-start(f32[6,64,512]{2,1,0:T(8,128)} %velocity_ref.1) | copy-start | bytes 2359300
  66.7 2.4 %copy-start.4 = (s32[2,512]{1,0:T(2,128)S(1)}, s32[2,512]{1,0:T(2,128)}, u32[]{:S(2)}) copy-start(s32[2,512]{1,0:T(2,128)} %modes_ref.1) | copy-start | bytes 12292
  67.4 1.7 %collective-permute-start.14 = (f32[2,3,64,128]{3,2,1,0:T(8,128)S(1)}, f32[2,3,64,128]{3,2,1,0:T(8,128)S(1)}, u32[]{:S(2)}, u32[]{:S(2)}) collective-permute-start(f32[2,3,64,128]{3,2,1,0:T(8,128)S(1)} %get-tuple-element.49.refs_0_), channel_id=1, source_target_pairs={{0,1},{1,0},{2,3},{3,2},{4,5},{5,4},{6,7},{7,6},{8,9},{9,8},{10,11... | collective-permute-start | bytes 589832 | tf_op jit(solution)/shard_map/ppermute | solution.py:404
  67.7 9.6 %collective-permute-start.20 = (f32[2,3,64,128]{3,2,1,0:T(8,128)S(1)}, f32[2,3,64,128]{3,2,1,0:T(8,128)S(1)}, u32[]{:S(2)}, u32[]{:S(2)}) collective-permute-start(f32[2,3,64,128]{3,2,1,0:T(8,128)S(1)} %get-tuple-element.54), channel_id=1, source_target_pairs={{0,6},{1,7},{2,4},{3,5},{4,2},{5,3},{6,0},{7,1},{8,14},{9,15},{10,... | collective-permute-start | bytes 589832 | tf_op jit(solution)/shard_map/ppermute | solution.py:397
  69.1 14.2 %collective-permute-start.22 = (f32[2,3,64,128]{3,2,1,0:T(8,128)S(1)}, f32[2,3,64,128]{3,2,1,0:T(8,128)S(1)}, u32[]{:S(2)}, u32[]{:S(2)}) collective-permute-start(f32[2,3,64,128]{3,2,1,0:T(8,128)S(1)} %get-tuple-element.55), channel_id=1, source_target_pairs={{0,2},{1,3},{2,0},{3,1},{4,6},{5,7},{6,4},{7,5},{8,10},{9,11},{10,... | collective-permute-start | bytes 589832 | tf_op jit(solution)/shard_map/ppermute | solution.py:397
  71.0 12.4 %collective-permute-start.19 = (f32[3,64]{1,0:T(4,128)S(1)}, f32[3,64]{1,0:T(4,128)S(1)}, u32[]{:S(2)}, u32[]{:S(2)}) collective-permute-start(f32[3,64]{1,0:T(4,128)S(1)} %get-tuple-element.53.refs_2_), channel_id=1, source_target_pairs={{0,24},{8,16},{16,8},{24,0},{1,25},{9,17},{17,9},{25,1},{2,26},{10... | collective-permute-start | bytes 2312 | tf_op jit(solution)/shard_map/ppermute | solution.py:414
  73.5 12.9 %collective-permute-start.15 = (f32[2,3,64,128]{3,2,1,0:T(8,128)S(1)}, f32[2,3,64,128]{3,2,1,0:T(8,128)S(1)}, u32[]{:S(2)}, u32[]{:S(2)}) collective-permute-start(f32[2,3,64,128]{3,2,1,0:T(8,128)S(1)} %get-tuple-element.52), channel_id=1, source_target_pairs={{0,4},{1,5},{2,6},{3,7},{4,0},{5,1},{6,2},{7,3},{8,12},{9,13},{10,... | collective-permute-start | bytes 589832 | tf_op jit(solution)/shard_map/ppermute | solution.py:397
  77.3 9.0 %collective-permute-start.21 = (f32[2,3,64,128]{3,2,1,0:T(8,128)S(1)}, f32[2,3,64,128]{3,2,1,0:T(8,128)S(1)}, u32[]{:S(2)}, u32[]{:S(2)}) collective-permute-start(f32[2,3,64,128]{3,2,1,0:T(8,128)S(1)} %collective-permute-done.20.refs_2_), channel_id=1, source_target_pairs={{0,1},{1,0},{2,3},{3,2},{4,5},{5,4},{6,7},{7,6},{8,9},{9,8},{10,11... | collective-permute-start | bytes 589832 | tf_op jit(solution)/shard_map/ppermute | solution.py:404
  83.3 3.0 %collective-permute-start.23 = (f32[2,3,64,128]{3,2,1,0:T(8,128)S(1)}, f32[2,3,64,128]{3,2,1,0:T(8,128)S(1)}, u32[]{:S(2)}, u32[]{:S(2)}) collective-permute-start(f32[2,3,64,128]{3,2,1,0:T(8,128)S(1)} %collective-permute-done.22.refs_4_), channel_id=1, source_target_pairs={{0,1},{1,0},{2,3},{3,2},{4,5},{5,4},{6,7},{7,6},{8,9},{9,8},{10,11... | collective-permute-start | bytes 589832 | tf_op jit(solution)/shard_map/ppermute | solution.py:404
  83.3 4.3 %collective-permute-start.17 = (f32[3,64]{1,0:T(4,128)S(1)}, f32[3,64]{1,0:T(4,128)S(1)}, u32[]{:S(2)}, u32[]{:S(2)}) collective-permute-start(f32[3,64]{1,0:T(4,128)S(1)} %get-tuple-element.53.refs_2_), channel_id=1, source_target_pairs={{0,8},{8,0},{16,24},{24,16},{1,9},{9,1},{17,25},{25,17},{2,10},{10... | collective-permute-start | bytes 2312 | tf_op jit(solution)/shard_map/ppermute | solution.py:414
  84.8 3.6 %collective-permute-start.18 = (f32[3,64]{1,0:T(4,128)S(1)}, f32[3,64]{1,0:T(4,128)S(1)}, u32[]{:S(2)}, u32[]{:S(2)}) collective-permute-start(f32[3,64]{1,0:T(4,128)S(1)} %get-tuple-element.53.refs_2_), channel_id=1, source_target_pairs={{0,16},{8,24},{16,0},{24,8},{1,17},{9,25},{17,1},{25,9},{2,18},{10... | collective-permute-start | bytes 2312 | tf_op jit(solution)/shard_map/ppermute | solution.py:414
  86.3 2.1 %collective-permute-start.16 = (f32[2,3,64,128]{3,2,1,0:T(8,128)S(1)}, f32[2,3,64,128]{3,2,1,0:T(8,128)S(1)}, u32[]{:S(2)}, u32[]{:S(2)}) collective-permute-start(f32[2,3,64,128]{3,2,1,0:T(8,128)S(1)} %collective-permute-done.15.refs_0_), channel_id=1, source_target_pairs={{0,1},{1,0},{2,3},{3,2},{4,5},{5,4},{6,7},{7,6},{8,9},{9,8},{10,11... | collective-permute-start | bytes 589832 | tf_op jit(solution)/shard_map/ppermute | solution.py:404

commit v13 on v11

--- a/solution.py
+++ b/solution.py
@@ -387,12 +387,16 @@
     return early_steps(devices, points) + late_steps(devices, points)
 
 
-def exchange(blocks, steps):
+def exchange(blocks, steps, held=None, until=None):
     devices = len(blocks)
-    return [
-        block if step == 0 else lax.ppermute(block, "col", [(i, i ^ step) for i in range(devices)])
-        for step, block in zip(steps, blocks)
-    ]
+    arrived = {}
+    for step, block in sorted(zip(steps, blocks), key=lambda pair: pair[0] == held):
+        if step == held:
+            block, _ = lax.optimization_barrier((block, arrived[until]))
+        arrived[step] = (
+            block if step == 0 else lax.ppermute(block, "col", [(i, i ^ step) for i in range(devices)])
+        )
+    return [arrived[step] for step in steps]
 
 
 def pair_sums(value, step):
@@ -474,7 +478,6 @@
     solved = outs[devices]
     returned = exchange(outs[:devices], steps)
 
-    early_back, steps_back = near_first(early, devices), near_first(early, devices) + late
     begun, chosen = call(
         functools.partial(surplus_early_kernel, early),
         [shaped((comps * points, columns)), shaped((len(late) * share, columns), BF16)],
@@ -483,13 +486,13 @@
         HEAVY,
     )(info, *returned[:split])
     outs = call(
-        functools.partial(surplus_late_kernel, late, steps_back),
+        functools.partial(surplus_late_kernel, late, steps),
         back,
         [LOCAL] * (2 + len(late)),
         [LOCAL] * devices,
         1,
     )(begun, chosen, *returned[split:])
-    extra = exchange(outs, steps_back)
+    extra = exchange(outs, steps, 2, 1)
 
     state_next, emf = call(
         functools.partial(state_kernel, steps),
@@ -498,11 +501,11 @@
         [FAR, LOCAL],
         HEAVY,
         [pltpu.VMEM(state_now.shape, F32), pltpu.SemaphoreType.DMA],
-    )(info, kept_modes, velocity, *returned, extra[early_back.index(3)])
+    )(info, kept_modes, velocity, *returned, extra[early.index(1)])
     terms = pair_sums(emf, 1)
 
     owned = call(
-        functools.partial(assemble_early_kernel, early_back),
+        functools.partial(assemble_early_kernel, early),
         shaped((comps, depth, lanes)),
         [SCALAR] + [LOCAL] * (2 + split),
         FAR,

time: 87.8 us -> 87.8 us (level)
  no operation moved by 1% of the time
where the time goes in v13:
time: 87.8 us; the launch traced here: 87.5 us
  waiting for transfers between devices  36.9 us (42%)
  starting transfers between devices  35.4 us (40%)
  Pallas kernels  14.4 us (16%)
    ppermute x21, waiting for transfers between devices, exchange(): lax.ppermute(block, 'col', [(i, i ^ step) for i in range(devices)])  34.8 us
    ppermute x21, starting transfers between devices, exchange(): lax.ppermute(block, 'col', [(i, i ^ step) for i in range(devices)])  32.3 us
    pallas_call x1, Pallas kernels, on_device(): call(functools.partial(first_kernel, devices), [shaped((8, columns), jnp....  3.76 us
    ppermute x2, starting transfers between devices, pair_sums(): lax.ppermute(value, 'grp', [(i, i ^ step) for i in range(groups)])  3.07 us
    ppermute x2, waiting for transfers between devices, pair_sums(): lax.ppermute(value, 'grp', [(i, i ^ step) for i in range(groups)])  2.1 us
    pallas_call x1, Pallas kernels, on_device(): call(functools.partial(state_kernel, steps), [shaped(state_now.shape), sh...  1.83 us
  transfers between devices with their start and end apart: 23, of which 13 were waited for; matrix products, arithmetic and copies ran while one was open for 0% of the time, Pallas kernels for 8%

profile of v13, /device:TPU:0, one launch (start us, length us, event | category | flops | bytes accessed | tf_op | source)
XLA Modules:
  0.0 87.5 jit_solution(16560237468061505978)
XLA Ops:
  0.7 3.8 %shard_map.121 = (s32[8,512]{1,0:T(8,128)S(1)}, f32[8,128]{1,0:T(8,128)S(1)}, f32[2,3,64,128]{3,2,1,0:T(8,128)S(1)}, f32[2,3,64,128]{3,2,1,0:T(8,128)S(1)}, f32[...) custom-call(s32[1]{0:T(128)} %bitcast.me_ref, ...), custom_call_target="tpu_custom_call" | custom-call | flops 1000000000 | bytes 1000000 | tf_op jit(solution)/shard_map/pallas_call | solution.py:439
  4.4 0.5 collective-permute-start
  5.0 4.7 %collective-permute-start.1 = (f32[2,3,64,128]{3,2,1,0:T(8,128)S(1)}, f32[2,3,64,128]{3,2,1,0:T(8,128)S(1)}, u32[]{:S(2)}, u32[]{:S(2)}) collective-permute-start(f32[2,3,64,128]{3,2,1,0:T(8,128)S(1)} %get-tuple-element.53), channel_id=1, source_target_pairs={{0,6},{1,7},{2,4},{3,5},{4,2},{5,3},{6,0},{7,1},{8,14},{9,15},{10,... | collective-permute-start | bytes 589832 | tf_op jit(solution)/shard_map/ppermute | solution.py:397
  9.6 0.1 collective-permute-start.2
  9.7 0.0 collective-permute-start.3
  9.7 1.5 %collective-permute-start.4 = (f32[2,3,64,128]{3,2,1,0:T(8,128)S(1)}, f32[2,3,64,128]{3,2,1,0:T(8,128)S(1)}, u32[]{:S(2)}, u32[]{:S(2)}) collective-permute-start(f32[2,3,64,128]{3,2,1,0:T(8,128)S(1)} %get-tuple-element.56), channel_id=1, source_target_pairs={{0,3},{1,2},{2,1},{3,0},{4,7},{5,6},{6,5},{7,4},{8,11},{9,10},{10,... | collective-permute-start | bytes 589832 | tf_op jit(solution)/shard_map/ppermute | solution.py:397
  11.2 1.4 %shard_map.122 = (bf16[512,512]{1,0:T(8,128)(2,1)S(1)}, bf16[512,512]{1,0:T(8,128)(2,1)S(1)}, bf16[512,512]{1,0:T(8,128)(2,1)S(1)}, bf16[512,512]{1,0:T(8,128)(2...) custom-call(f32[512,512]{1,0:T(8,128)S(1)} %copy-done, f32[512,512]{1,0:T(8,128)S(1)} %copy-done.1, ...), custom_call_target="tpu_custom_call" | custom-call | flops 10000000000 | bytes 10000000 | tf_op jit(solution)/shard_map/pallas_call | solution.py:453
  12.6 0.0 collective-permute-done.refs_5_
  12.6 2.7 %collective-permute-start.5 = (f32[2,3,64,128]{3,2,1,0:T(8,128)S(1)}, f32[2,3,64,128]{3,2,1,0:T(8,128)S(1)}, u32[]{:S(2)}, u32[]{:S(2)}) collective-permute-start(f32[2,3,64,128]{3,2,1,0:T(8,128)S(1)} %get-tuple-element.57), channel_id=1, source_target_pairs={{0,4},{1,5},{2,6},{3,7},{4,0},{5,1},{6,2},{7,3},{8,12},{9,13},{10,... | collective-permute-start | bytes 589832 | tf_op jit(solution)/shard_map/ppermute | solution.py:397
  15.3 0.3 collective-permute-done.1.refs_6_
  15.6 8.0 %collective-permute-start.6 = (f32[2,3,64,128]{3,2,1,0:T(8,128)S(1)}, f32[2,3,64,128]{3,2,1,0:T(8,128)S(1)}, u32[]{:S(2)}, u32[]{:S(2)}) collective-permute-start(f32[2,3,64,128]{3,2,1,0:T(8,128)S(1)} %get-tuple-element.58), channel_id=1, source_target_pairs={{0,5},{1,4},{2,7},{3,6},{4,1},{5,0},{6,3},{7,2},{8,13},{9,12},{10,... | collective-permute-start | bytes 589832 | tf_op jit(solution)/shard_map/ppermute | solution.py:397
  23.6 0.2 collective-permute-done.3.refs_8_
  23.7 5.1 %collective-permute-done.4.refs_9_ = f32[2,3,64,128]{3,2,1,0:T(8,128)S(1)} collective-permute-done((f32[2,3,64,128]{3,2,1,0:T(8,128)S(1)}, f32[2,3,64,128]{3,2,1,0:T(8,128)S(1)}, u32[]{:S(2)}, u32[]{:S(2)}) %collective-permute-start.4) | collective-permute-done | bytes 196640 | tf_op jit(solution)/shard_map/ppermute | solution.py:397
  28.8 1.4 %shard_map.123.early_ref = f32[512,384]{1,0:T(8,128)S(1)} custom-call(s32[1]{0:T(128)} %bitcast.me_ref, bf16[512,512]{1,0:T(8,128)(2,1)S(1)} %get-tuple-element.47.refs_0_, bf16[512,512]{1,0:T(8,128)(2,1)S(1)} %get-tuple-element.48.refs_1_, bf16[512,512]{1,0:T(8,128)(2,1)S(1)} %get-tuple-element.49.refs_2_, bf16[512,512]{1,0:T(8,128)(2,1)S(1)} %get-tuple-element.50.refs_3_, ...), custom_call_target="tpu_custom_call" | custom-call | flops 10000000000 | bytes 10000000 | tf_op jit(solution)/shard_map/pallas_call | solution.py:462
  30.2 9.8 %collective-permute-done.5.refs_4_ = f32[2,3,64,128]{3,2,1,0:T(8,128)S(1)} collective-permute-done((f32[2,3,64,128]{3,2,1,0:T(8,128)S(1)}, f32[2,3,64,128]{3,2,1,0:T(8,128)S(1)}, u32[]{:S(2)}, u32[]{:S(2)}) %collective-permute-start.5) | collective-permute-done | bytes 196640 | tf_op jit(solution)/shard_map/ppermute | solution.py:397
  40.0 3.3 %collective-permute-done.6.refs_5_ = f32[2,3,64,128]{3,2,1,0:T(8,128)S(1)} collective-permute-done((f32[2,3,64,128]{3,2,1,0:T(8,128)S(1)}, f32[2,3,64,128]{3,2,1,0:T(8,128)S(1)}, u32[]{:S(2)}, u32[]{:S(2)}) %collective-permute-start.6) | collective-permute-done | bytes 196640 | tf_op jit(solution)/shard_map/ppermute | solution.py:397
  43.3 1.6 %shard_map.124 = (f32[3,64,128]{2,1,0:T(8,128)S(1)}, f32[3,64,128]{2,1,0:T(8,128)S(1)}, f32[3,64,128]{2,1,0:T(8,128)S(1)}, f32[3,64,128]{2,1,0:T(8,128)S(1)}, f3...) custom-call(s32[1]{0:T(128)} %bitcast.me_ref, ...), custom_call_target="tpu_custom_call" | custom-call | flops 1000000000 | bytes 1000000 | tf_op jit(solution)/shard_map/pallas_call | solution.py:470
  44.9 0.3 collective-permute-start.7
  45.2 2.5 %collective-permute-start.8 = (f32[3,64,128]{2,1,0:T(8,128)S(1)}, f32[3,64,128]{2,1,0:T(8,128)S(1)}, u32[]{:S(2)}, u32[]{:S(2)}) collective-permute-start(f32[3,64,128]{2,1,0:T(8,128)S(1)} %get-tuple-element.61), channel_id=1, source_target_pairs={{0,6},{1,7},{2,4},{3,5},{4,2},{5,3},{6,0},{7,1},{8,14},{9,15},{10,... | collective-permute-start | bytes 294920 | tf_op jit(solution)/shard_map/ppermute | solution.py:397
  47.8 0.9 collective-permute-start.9
  48.6 0.0 collective-permute-start.10
  48.6 1.9 %collective-permute-start.11 = (f32[3,64,128]{2,1,0:T(8,128)S(1)}, f32[3,64,128]{2,1,0:T(8,128)S(1)}, u32[]{:S(2)}, u32[]{:S(2)}) collective-permute-start(f32[3,64,128]{2,1,0:T(8,128)S(1)} %get-tuple-element.64), channel_id=1, source_target_pairs={{0,3},{1,2},{2,1},{3,0},{4,7},{5,6},{6,5},{7,4},{8,11},{9,10},{10,... | collective-permute-start | bytes 294920 | tf_op jit(solution)/shard_map/ppermute | solution.py:397
  50.5 1.4 %collective-permute-start.12 = (f32[3,64,128]{2,1,0:T(8,128)S(1)}, f32[3,64,128]{2,1,0:T(8,128)S(1)}, u32[]{:S(2)}, u32[]{:S(2)}) collective-permute-start(f32[3,64,128]{2,1,0:T(8,128)S(1)} %get-tuple-element.65), channel_id=1, source_target_pairs={{0,4},{1,5},{2,6},{3,7},{4,0},{5,1},{6,2},{7,3},{8,12},{9,13},{10,... | collective-permute-start | bytes 294920 | tf_op jit(solution)/shard_map/ppermute | solution.py:397
  51.9 0.2 collective-permute-done.8.refs_2_
  52.1 0.9 %collective-permute-start.13 = (f32[3,64,128]{2,1,0:T(8,128)S(1)}, f32[3,64,128]{2,1,0:T(8,128)S(1)}, u32[]{:S(2)}, u32[]{:S(2)}) collective-permute-start(f32[3,64,128]{2,1,0:T(8,128)S(1)} %get-tuple-element.66), channel_id=1, source_target_pairs={{0,5},{1,4},{2,7},{3,6},{4,1},{5,0},{6,3},{7,2},{8,13},{9,12},{10,... | collective-permute-start | bytes 294920 | tf_op jit(solution)/shard_map/ppermute | solution.py:397
  53.0 1.7 %collective-permute-done.9.refs_3_ = f32[3,64,128]{2,1,0:T(8,128)S(1)} collective-permute-done((f32[3,64,128]{2,1,0:T(8,128)S(1)}, f32[3,64,128]{2,1,0:T(8,128)S(1)}, u32[]{:S(2)}, u32[]{:S(2)}) %collective-permute-start.9) | collective-permute-done | bytes 98336 | tf_op jit(solution)/shard_map/ppermute | solution.py:397
  54.7 4.6 %collective-permute-done.10.refs_4_ = f32[3,64,128]{2,1,0:T(8,128)S(1)} collective-permute-done((f32[3,64,128]{2,1,0:T(8,128)S(1)}, f32[3,64,128]{2,1,0:T(8,128)S(1)}, u32[]{:S(2)}, u32[]{:S(2)}) %collective-permute-start.10) | collective-permute-done | bytes 98336 | tf_op jit(solution)/shard_map/ppermute | solution.py:397
  59.3 1.9 %collective-permute-done.11.refs_5_ = f32[3,64,128]{2,1,0:T(8,128)S(1)} collective-permute-done((f32[3,64,128]{2,1,0:T(8,128)S(1)}, f32[3,64,128]{2,1,0:T(8,128)S(1)}, u32[]{:S(2)}, u32[]{:S(2)}) %collective-permute-start.11) | collective-permute-done | bytes 98336 | tf_op jit(solution)/shard_map/ppermute | solution.py:397
  61.2 1.2 %shard_map.125 = (f32[384,512]{1,0:T(8,128)S(1)}, bf16[128,512]{1,0:T(8,128)(2,1)S(1)}) custom-call(s32[8,512]{1,0:T(8,128)S(1)} %get-tuple-element.43.info_ref, f32[3,64,128]{2,1,0:T(8,128)S(1)} %get-tuple-element.59.refs_0_, f32[3,64,128]{2,1,0:T(8,128)S(1)} %collective-permute-done.7.refs_1_, f32[3,64,128]{2,1,0:T(8,128)S(1)} %collective-permute-done.8.refs_2_, ...), custom_call_target="tpu_custom_call" | custom-call | flops 10000000000 | bytes 10000000 | tf_op jit(solution)/shard_map/pallas_call | solution.py:481
  62.3 1.8 %collective-permute-done.13.refs_1_.refs_7_ = f32[3,64,128]{2,1,0:T(8,128)S(1)} collective-permute-done((f32[3,64,128]{2,1,0:T(8,128)S(1)}, f32[3,64,128]{2,1,0:T(8,128)S(1)}, u32[]{:S(2)}, u32[]{:S(2)}) %collective-permute-start.13) | collective-permute-done | bytes 98336 | tf_op jit(solution)/shard_map/ppermute | solution.py:397
  64.1 0.7 shard_map.126
  64.8 0.3 collective-permute-start.14
  65.2 1.4 %collective-permute-start.19 = (f32[3,64,128]{2,1,0:T(8,128)S(1)}, f32[3,64,128]{2,1,0:T(8,128)S(1)}, u32[]{:S(2)}, u32[]{:S(2)}) collective-permute-start(f32[3,64,128]{2,1,0:T(8,128)S(1)} %get-tuple-element.76), channel_id=1, source_target_pairs={{0,6},{1,7},{2,4},{3,5},{4,2},{5,3},{6,0},{7,1},{8,14},{9,15},{10,... | collective-permute-start | bytes 294920 | tf_op jit(solution)/shard_map/ppermute | solution.py:397
  66.6 2.0 %collective-permute-start.20 = (f32[3,64,128]{2,1,0:T(8,128)S(1)}, f32[3,64,128]{2,1,0:T(8,128)S(1)}, u32[]{:S(2)}, u32[]{:S(2)}) collective-permute-start(f32[3,64,128]{2,1,0:T(8,128)S(1)} %get-tuple-element.77), channel_id=1, source_target_pairs={{0,7},{1,6},{2,5},{3,4},{4,3},{5,2},{6,1},{7,0},{8,15},{9,14},{10,... | collective-permute-start | bytes 294920 | tf_op jit(solution)/shard_map/ppermute | solution.py:397
  68.5 0.0 collective-permute-done.14.refs_8_.refs_1_
  68.5 2.2 %collective-permute-start.21 = (f32[3,64,128]{2,1,0:T(8,128)S(1)}, f32[3,64,128]{2,1,0:T(8,128)S(1)}, u32[]{:S(2)}, u32[]{:S(2)}) collective-permute-start(f32[3,64,128]{2,1,0:T(8,128)S(1)} %get-tuple-element.79), channel_id=1, source_target_pairs={{0,2},{1,3},{2,0},{3,1},{4,6},{5,7},{6,4},{7,5},{8,10},{9,11},{10,... | collective-permute-start | bytes 294920 | tf_op jit(solution)/shard_map/ppermute | solution.py:397
  70.7 1.8 %shard_map.127 = (f32[6,64,512]{2,1,0:T(8,128)}, f32[3,64]{1,0:T(4,128)S(1)}) custom-call(s32[8,512]{1,0:T(8,128)S(1)} %get-tuple-element.43.info_ref, s32[2,512]{1,0:T(2,128)S(1)} %copy-done.4, f32[6,64,512]{2,1,0:T(8,128)S(1)} %copy-done.3, f32[3,64,128]{2,1,0:T(8,128)S(1)} %get-tuple-element.59.refs_0_, f32[3,64,128]{2,1,0:T(8,128)S(1)} %collective-permute-done.7.refs_1_, ...), custom_call_target="tpu_custom_call" | custom-call | flops 10000000000 | bytes 10000000 | tf_op jit(solution)/shard_map/pallas_call | solution.py:497
  72.6 1.6 %collective-permute-start.17 = (f32[3,64]{1,0:T(4,128)S(1)}, f32[3,64]{1,0:T(4,128)S(1)}, u32[]{:S(2)}, u32[]{:S(2)}) collective-permute-start(f32[3,64]{1,0:T(4,128)S(1)} %get-tuple-element.74), channel_id=1, source_target_pairs={{0,8},{8,0},{16,24},{24,16},{1,9},{9,1},{17,25},{25,17},{2,10},{10... | collective-permute-start | bytes 2312 | tf_op jit(solution)/shard_map/ppermute | solution.py:405
  74.1 2.1 %collective-permute-done.17 = f32[3,64]{1,0:T(4,128)S(1)} collective-permute-done((f32[3,64]{1,0:T(4,128)S(1)}, f32[3,64]{1,0:T(4,128)S(1)}, u32[]{:S(2)}, u32[]{:S(2)}) %collective-permute-start.17) | collective-permute-done | bytes 800 | tf_op jit(solution)/shard_map/ppermute | solution.py:405
  76.2 0.0 collective-permute-start.15
  76.3 1.0 %collective-permute-start.16 = (f32[3,64,128]{2,1,0:T(8,128)S(1)}, f32[3,64,128]{2,1,0:T(8,128)S(1)}, u32[]{:S(2)}, u32[]{:S(2)}) collective-permute-start(f32[3,64,128]{2,1,0:T(8,128)S(1)} %get-tuple-element.73), channel_id=1, source_target_pairs={{0,5},{1,4},{2,7},{3,6},{4,1},{5,0},{6,3},{7,2},{8,13},{9,12},{10,... | collective-permute-start | bytes 294920 | tf_op jit(solution)/shard_map/ppermute | solution.py:397
  77.3 1.5 %collective-permute-start.18 = (f32[3,64]{1,0:T(4,128)S(1)}, f32[3,64]{1,0:T(4,128)S(1)}, u32[]{:S(2)}, u32[]{:S(2)}) collective-permute-start(f32[3,64]{1,0:T(4,128)S(1)} %add.3.refs_2_), channel_id=1, source_target_pairs={{0,16},{8,24},{16,0},{24,8},{1,17},{9,25},{17,1},{25,9},{2,18},{10... | collective-permute-start | bytes 2312 | tf_op jit(solution)/shard_map/ppermute | solution.py:407
  78.8 0.0 collective-permute-done.22.refs_5_
  78.8 1.2 %shard_map.128.refs_4_ = f32[6,512,128]{2,1,0:T(8,128)} custom-call(s32[1]{0:T(128)} %bitcast.me_ref, s32[8,512]{1,0:T(8,128)S(1)} %get-tuple-element.43.info_ref, f32[3,512,128]{2,1,0:T(8,128)S(1)} %get-tuple-element.71.solved_ref, f32[3,64,128]{2,1,0:T(8,128)S(1)} %get-tuple-element.75.refs_0_, f32[3,64,128]{2,1,0:T(8,128)S(1)} %collective-permute-done.14.refs_8_.refs_1_, ...), custom_call_target="tpu_custom_call" | custom-call | flops 10000000000 | bytes 10000000 | tf_op jit(solution)/shard_map/pallas_call | solution.py:507
  80.1 5.5 %collective-permute-done.15.refs_0_ = f32[3,64,128]{2,1,0:T(8,128)S(1)} collective-permute-done((f32[3,64,128]{2,1,0:T(8,128)S(1)}, f32[3,64,128]{2,1,0:T(8,128)S(1)}, u32[]{:S(2)}, u32[]{:S(2)}) %collective-permute-start.15) | collective-permute-done | bytes 98336 | tf_op jit(solution)/shard_map/ppermute | solution.py:397
  85.6 0.5 collective-permute-done.16.refs_1_
  86.1 0.0 collective-permute-done.18.refs_3_
  86.1 1.5 %shard_map.129 = (f32[6,512,128]{2,1,0:T(8,128)}, f32[3,64]{1,0:T(4,128)}) custom-call(s32[1]{0:T(128)} %bitcast.me_ref, s32[8,512]{1,0:T(8,128)S(1)} %get-tuple-element.43.info_ref, f32[3,512,128]{2,1,0:T(8,128)S(1)} %get-tuple-element.71.solved_ref, f32[3,64,128]{2,1,0:T(8,128)S(1)} %collective-permute-done.15.refs_0_, ...), custom_call_target="tpu_custom_call", output_to_operand_aliasing={{0}: (7, {})} | custom-call | flops 1000000000 | bytes 1000000 | tf_op jit(solution)/shard_map/pallas_call | solution.py:518
  (20 shorter events, 0.0 us)
Async XLA Ops:
  0.6 10.6 %copy-start = (f32[512,512]{1,0:T(8,128)S(1)}, f32[512,512]{1,0:T(8,128)}, u32[]{:S(2)}) copy-start(f32[512,512]{1,0:T(8,128)} %deriv_ref.1) | copy-start | bytes 3145732
  0.6 10.6 %copy-start.1 = (f32[512,512]{1,0:T(8,128)S(1)}, f32[512,512]{1,0:T(8,128)}, u32[]{:S(2)}) copy-start(f32[512,512]{1,0:T(8,128)} %inverse_ref.1) | copy-start | bytes 3145732
  0.7 10.6 %copy-start.2 = (f32[512,512]{1,0:T(8,128)S(1)}, f32[512,512]{1,0:T(8,128)}, u32[]{:S(2)}) copy-start(f32[512,512]{1,0:T(8,128)} %basis_ref.1) | copy-start | bytes 3145732
  0.7 10.5 %copy-start.5 = (f32[512]{0:T(512)S(1)}, f32[512]{0:T(512)}, u32[]{:S(2)}) copy-start(f32[512]{0:T(512)} %param.17) | copy-start | bytes 6148
  4.4 8.1 %collective-permute-start = (f32[2,3,64,128]{3,2,1,0:T(8,128)S(1)}, f32[2,3,64,128]{3,2,1,0:T(8,128)S(1)}, u32[]{:S(2)}, u32[]{:S(2)}) collective-permute-start(f32[2,3,64,128]{3,2,1,0:T(8,128)S(1)} %get-tuple-element.52), channel_id=1, source_target_pairs={{0,1},{1,0},{2,3},{3,2},{4,5},{5,4},{6,7},{7,6},{8,9},{9,8},{10,11... | collective-permute-start | bytes 589832 | tf_op jit(solution)/shard_map/ppermute | solution.py:397
  5.0 10.6 %collective-permute-start.1 = (f32[2,3,64,128]{3,2,1,0:T(8,128)S(1)}, f32[2,3,64,128]{3,2,1,0:T(8,128)S(1)}, u32[]{:S(2)}, u32[]{:S(2)}) collective-permute-start(f32[2,3,64,128]{3,2,1,0:T(8,128)S(1)} %get-tuple-element.53), channel_id=1, source_target_pairs={{0,6},{1,7},{2,4},{3,5},{4,2},{5,3},{6,0},{7,1},{8,14},{9,15},{10,... | collective-permute-start | bytes 589832 | tf_op jit(solution)/shard_map/ppermute | solution.py:397
  9.6 13.9 %collective-permute-start.2 = (f32[2,3,64,128]{3,2,1,0:T(8,128)S(1)}, f32[2,3,64,128]{3,2,1,0:T(8,128)S(1)}, u32[]{:S(2)}, u32[]{:S(2)}) collective-permute-start(f32[2,3,64,128]{3,2,1,0:T(8,128)S(1)} %get-tuple-element.54), channel_id=1, source_target_pairs={{0,7},{1,6},{2,5},{3,4},{4,3},{5,2},{6,1},{7,0},{8,15},{9,14},{10,... | collective-permute-start | bytes 589832 | tf_op jit(solution)/shard_map/ppermute | solution.py:397
  9.7 14.0 %collective-permute-start.3 = (f32[2,3,64,128]{3,2,1,0:T(8,128)S(1)}, f32[2,3,64,128]{3,2,1,0:T(8,128)S(1)}, u32[]{:S(2)}, u32[]{:S(2)}) collective-permute-start(f32[2,3,64,128]{3,2,1,0:T(8,128)S(1)} %get-tuple-element.55), channel_id=1, source_target_pairs={{0,2},{1,3},{2,0},{3,1},{4,6},{5,7},{6,4},{7,5},{8,10},{9,11},{10,... | collective-permute-start | bytes 589832 | tf_op jit(solution)/shard_map/ppermute | solution.py:397
  9.7 19.1 %collective-permute-start.4 = (f32[2,3,64,128]{3,2,1,0:T(8,128)S(1)}, f32[2,3,64,128]{3,2,1,0:T(8,128)S(1)}, u32[]{:S(2)}, u32[]{:S(2)}) collective-permute-start(f32[2,3,64,128]{3,2,1,0:T(8,128)S(1)} %get-tuple-element.56), channel_id=1, source_target_pairs={{0,3},{1,2},{2,1},{3,0},{4,7},{5,6},{6,5},{7,4},{8,11},{9,10},{10,... | collective-permute-start | bytes 589832 | tf_op jit(solution)/shard_map/ppermute | solution.py:397
  12.6 27.4 %collective-permute-start.5 = (f32[2,3,64,128]{3,2,1,0:T(8,128)S(1)}, f32[2,3,64,128]{3,2,1,0:T(8,128)S(1)}, u32[]{:S(2)}, u32[]{:S(2)}) collective-permute-start(f32[2,3,64,128]{3,2,1,0:T(8,128)S(1)} %get-tuple-element.57), channel_id=1, source_target_pairs={{0,4},{1,5},{2,6},{3,7},{4,0},{5,1},{6,2},{7,3},{8,12},{9,13},{10,... | collective-permute-start | bytes 589832 | tf_op jit(solution)/shard_map/ppermute | solution.py:397
  15.6 27.7 %collective-permute-start.6 = (f32[2,3,64,128]{3,2,1,0:T(8,128)S(1)}, f32[2,3,64,128]{3,2,1,0:T(8,128)S(1)}, u32[]{:S(2)}, u32[]{:S(2)}) collective-permute-start(f32[2,3,64,128]{3,2,1,0:T(8,128)S(1)} %get-tuple-element.58), channel_id=1, source_target_pairs={{0,5},{1,4},{2,7},{3,6},{4,1},{5,0},{6,3},{7,2},{8,13},{9,12},{10,... | collective-permute-start | bytes 589832 | tf_op jit(solution)/shard_map/ppermute | solution.py:397
  44.9 5.6 %collective-permute-start.7 = (f32[3,64,128]{2,1,0:T(8,128)S(1)}, f32[3,64,128]{2,1,0:T(8,128)S(1)}, u32[]{:S(2)}, u32[]{:S(2)}) collective-permute-start(f32[3,64,128]{2,1,0:T(8,128)S(1)} %get-tuple-element.60), channel_id=1, source_target_pairs={{0,1},{1,0},{2,3},{3,2},{4,5},{5,4},{6,7},{7,6},{8,9},{9,8},{10,11... | collective-permute-start | bytes 294920 | tf_op jit(solution)/shard_map/ppermute | solution.py:397
  45.2 6.9 %collective-permute-start.8 = (f32[3,64,128]{2,1,0:T(8,128)S(1)}, f32[3,64,128]{2,1,0:T(8,128)S(1)}, u32[]{:S(2)}, u32[]{:S(2)}) collective-permute-start(f32[3,64,128]{2,1,0:T(8,128)S(1)} %get-tuple-element.61), channel_id=1, source_target_pairs={{0,6},{1,7},{2,4},{3,5},{4,2},{5,3},{6,0},{7,1},{8,14},{9,15},{10,... | collective-permute-start | bytes 294920 | tf_op jit(solution)/shard_map/ppermute | solution.py:397
  47.8 6.9 %collective-permute-start.9 = (f32[3,64,128]{2,1,0:T(8,128)S(1)}, f32[3,64,128]{2,1,0:T(8,128)S(1)}, u32[]{:S(2)}, u32[]{:S(2)}) collective-permute-start(f32[3,64,128]{2,1,0:T(8,128)S(1)} %get-tuple-element.62), channel_id=1, source_target_pairs={{0,7},{1,6},{2,5},{3,4},{4,3},{5,2},{6,1},{7,0},{8,15},{9,14},{10,... | collective-permute-start | bytes 294920 | tf_op jit(solution)/shard_map/ppermute | solution.py:397
  48.6 10.7 %collective-permute-start.10 = (f32[3,64,128]{2,1,0:T(8,128)S(1)}, f32[3,64,128]{2,1,0:T(8,128)S(1)}, u32[]{:S(2)}, u32[]{:S(2)}) collective-permute-start(f32[3,64,128]{2,1,0:T(8,128)S(1)} %get-tuple-element.63), channel_id=1, source_target_pairs={{0,2},{1,3},{2,0},{3,1},{4,6},{5,7},{6,4},{7,5},{8,10},{9,11},{10,... | collective-permute-start | bytes 294920 | tf_op jit(solution)/shard_map/ppermute | solution.py:397
  48.6 12.5 %collective-permute-start.11 = (f32[3,64,128]{2,1,0:T(8,128)S(1)}, f32[3,64,128]{2,1,0:T(8,128)S(1)}, u32[]{:S(2)}, u32[]{:S(2)}) collective-permute-start(f32[3,64,128]{2,1,0:T(8,128)S(1)} %get-tuple-element.64), channel_id=1, source_target_pairs={{0,3},{1,2},{2,1},{3,0},{4,7},{5,6},{6,5},{7,4},{8,11},{9,10},{10,... | collective-permute-start | bytes 294920 | tf_op jit(solution)/shard_map/ppermute | solution.py:397
  50.5 11.8 %collective-permute-start.12 = (f32[3,64,128]{2,1,0:T(8,128)S(1)}, f32[3,64,128]{2,1,0:T(8,128)S(1)}, u32[]{:S(2)}, u32[]{:S(2)}) collective-permute-start(f32[3,64,128]{2,1,0:T(8,128)S(1)} %get-tuple-element.65), channel_id=1, source_target_pairs={{0,4},{1,5},{2,6},{3,7},{4,0},{5,1},{6,2},{7,3},{8,12},{9,13},{10,... | collective-permute-start | bytes 294920 | tf_op jit(solution)/shard_map/ppermute | solution.py:397
  52.1 12.0 %collective-permute-start.13 = (f32[3,64,128]{2,1,0:T(8,128)S(1)}, f32[3,64,128]{2,1,0:T(8,128)S(1)}, u32[]{:S(2)}, u32[]{:S(2)}) collective-permute-start(f32[3,64,128]{2,1,0:T(8,128)S(1)} %get-tuple-element.66), channel_id=1, source_target_pairs={{0,5},{1,4},{2,7},{3,6},{4,1},{5,0},{6,3},{7,2},{8,13},{9,12},{10,... | collective-permute-start | bytes 294920 | tf_op jit(solution)/shard_map/ppermute | solution.py:397
  64.1 6.6 %copy-start.3 = (f32[6,64,512]{2,1,0:T(8,128)S(1)}, f32[6,64,512]{2,1,0:T(8,128)}, u32[]{:S(2)}) copy-start(f32[6,64,512]{2,1,0:T(8,128)} %velocity_ref.1) | copy-start | bytes 2359300
  64.1 6.6 %copy-start.4 = (s32[2,512]{1,0:T(2,128)S(1)}, s32[2,512]{1,0:T(2,128)}, u32[]{:S(2)}) copy-start(s32[2,512]{1,0:T(2,128)} %modes_ref.1) | copy-start | bytes 12292
  64.8 3.7 %collective-permute-start.14 = (f32[3,64,128]{2,1,0:T(8,128)S(1)}, f32[3,64,128]{2,1,0:T(8,128)S(1)}, u32[]{:S(2)}, u32[]{:S(2)}) collective-permute-start(f32[3,64,128]{2,1,0:T(8,128)S(1)} %get-tuple-element.69), channel_id=1, source_target_pairs={{0,1},{1,0},{2,3},{3,2},{4,5},{5,4},{6,7},{7,6},{8,9},{9,8},{10,11... | collective-permute-start | bytes 294920 | tf_op jit(solution)/shard_map/ppermute | solution.py:397
  65.2 11.1 %collective-permute-start.19 = (f32[3,64,128]{2,1,0:T(8,128)S(1)}, f32[3,64,128]{2,1,0:T(8,128)S(1)}, u32[]{:S(2)}, u32[]{:S(2)}) collective-permute-start(f32[3,64,128]{2,1,0:T(8,128)S(1)} %get-tuple-element.76), channel_id=1, source_target_pairs={{0,6},{1,7},{2,4},{3,5},{4,2},{5,3},{6,0},{7,1},{8,14},{9,15},{10,... | collective-permute-start | bytes 294920 | tf_op jit(solution)/shard_map/ppermute | solution.py:397
  66.6 10.7 %collective-permute-start.20 = (f32[3,64,128]{2,1,0:T(8,128)S(1)}, f32[3,64,128]{2,1,0:T(8,128)S(1)}, u32[]{:S(2)}, u32[]{:S(2)}) collective-permute-start(f32[3,64,128]{2,1,0:T(8,128)S(1)} %get-tuple-element.77), channel_id=1, source_target_pairs={{0,7},{1,6},{2,5},{3,4},{4,3},{5,2},{6,1},{7,0},{8,15},{9,14},{10,... | collective-permute-start | bytes 294920 | tf_op jit(solution)/shard_map/ppermute | solution.py:397
  68.5 10.3 %collective-permute-start.22 = (f32[3,64,128]{2,1,0:T(8,128)S(1)}, f32[3,64,128]{2,1,0:T(8,128)S(1)}, u32[]{:S(2)}, u32[]{:S(2)}) collective-permute-start(f32[3,64,128]{2,1,0:T(8,128)S(1)} %get-tuple-element.80), channel_id=1, source_target_pairs={{0,3},{1,2},{2,1},{3,0},{4,7},{5,6},{6,5},{7,4},{8,11},{9,10},{10,... | collective-permute-start | bytes 294920 | tf_op jit(solution)/shard_map/ppermute | solution.py:397
  68.5 10.3 %collective-permute-start.21 = (f32[3,64,128]{2,1,0:T(8,128)S(1)}, f32[3,64,128]{2,1,0:T(8,128)S(1)}, u32[]{:S(2)}, u32[]{:S(2)}) collective-permute-start(f32[3,64,128]{2,1,0:T(8,128)S(1)} %get-tuple-element.79), channel_id=1, source_target_pairs={{0,2},{1,3},{2,0},{3,1},{4,6},{5,7},{6,4},{7,5},{8,10},{9,11},{10,... | collective-permute-start | bytes 294920 | tf_op jit(solution)/shard_map/ppermute | solution.py:397
  72.6 3.7 %collective-permute-start.17 = (f32[3,64]{1,0:T(4,128)S(1)}, f32[3,64]{1,0:T(4,128)S(1)}, u32[]{:S(2)}, u32[]{:S(2)}) collective-permute-start(f32[3,64]{1,0:T(4,128)S(1)} %get-tuple-element.74), channel_id=1, source_target_pairs={{0,8},{8,0},{16,24},{24,16},{1,9},{9,1},{17,25},{25,17},{2,10},{10... | collective-permute-start | bytes 2312 | tf_op jit(solution)/shard_map/ppermute | solution.py:405
  76.2 9.3 %collective-permute-start.15 = (f32[3,64,128]{2,1,0:T(8,128)S(1)}, f32[3,64,128]{2,1,0:T(8,128)S(1)}, u32[]{:S(2)}, u32[]{:S(2)}) collective-permute-start(f32[3,64,128]{2,1,0:T(8,128)S(1)} %get-tuple-element.72), channel_id=1, source_target_pairs={{0,4},{1,5},{2,6},{3,7},{4,0},{5,1},{6,2},{7,3},{8,12},{9,13},{10,... | collective-permute-start | bytes 294920 | tf_op jit(solution)/shard_map/ppermute | solution.py:397
  76.3 9.8 %collective-permute-start.16 = (f32[3,64,128]{2,1,0:T(8,128)S(1)}, f32[3,64,128]{2,1,0:T(8,128)S(1)}, u32[]{:S(2)}, u32[]{:S(2)}) collective-permute-start(f32[3,64,128]{2,1,0:T(8,128)S(1)} %get-tuple-element.73), channel_id=1, source_target_pairs={{0,5},{1,4},{2,7},{3,6},{4,1},{5,0},{6,3},{7,2},{8,13},{9,12},{10,... | collective-permute-start | bytes 294920 | tf_op jit(solution)/shard_map/ppermute | solution.py:397
  77.3 8.8 %collective-permute-start.18 = (f32[3,64]{1,0:T(4,128)S(1)}, f32[3,64]{1,0:T(4,128)S(1)}, u32[]{:S(2)}, u32[]{:S(2)}) collective-permute-start(f32[3,64]{1,0:T(4,128)S(1)} %add.3.refs_2_), channel_id=1, source_target_pairs={{0,16},{8,24},{16,0},{24,8},{1,17},{9,25},{17,1},{25,9},{2,18},{10... | collective-permute-start | bytes 2312 | tf_op jit(solution)/shard_map/ppermute | solution.py:407

commit v14 on v13

--- a/solution.py
+++ b/solution.py
@@ -399,12 +399,11 @@
     return [arrived[step] for step in steps]
 
 
-def pair_sums(value, step):
+def from_groups(value):
     groups = lax.axis_size("grp")
-    while 2 * step < groups:
-        value = value + lax.ppermute(value, "grp", [(i, i ^ step) for i in range(groups)])
-        step = 2 * step
-    return [value, lax.ppermute(value, "grp", [(i, i ^ step) for i in range(groups)])]
+    return [value] + [
+        lax.ppermute(value, "grp", [(i, i ^ step) for i in range(groups)]) for step in range(1, groups)
+    ]
 
 
 def on_device(
@@ -502,7 +501,7 @@
         HEAVY,
         [pltpu.VMEM(state_now.shape, F32), pltpu.SemaphoreType.DMA],
     )(info, kept_modes, velocity, *returned, extra[early.index(1)])
-    terms = pair_sums(emf, 1)
+    terms = from_groups(emf)
 
     owned = call(
         functools.partial(assemble_early_kernel, early),

time: 87.8 us -> 87.6 us (level)
  waiting for transfers between devices: 36.9 us -> 30.7 us
  starting transfers between devices: 35.4 us -> 41.4 us
    ppermute x21, waiting for transfers between devices: 34.8 us -> 29 us  [exchange(): lax.ppermute(block, 'col', [(i, i ^ step) for i in range(devices)])]
    ppermute x21, starting transfers between devices: 32.3 us -> 37.9 us  [exchange(): lax.ppermute(block, 'col', [(i, i ^ step) for i in range(devices)])]
    ppermute x2 -> x3, starting transfers between devices: 3.07 us -> 3.49 us  [from_groups(): lax.ppermute(value, 'grp', [(i, i ^ step) for i in range(groups)])]
    ppermute x2 -> x3, waiting for transfers between devices: 2.1 us -> 1.77 us  [from_groups(): lax.ppermute(value, 'grp', [(i, i ^ step) for i in range(groups)])]
  transfers between devices with their start and end apart: 23 -> 24, of which waited for: 13 -> 13; matrix products, arithmetic and copies ran while one was open for 0% -> 0% of each run, Pallas kernels for 8% -> 8%
where the time goes in v14:
time: 87.6 us; the launch traced here: 87.4 us
  starting transfers between devices  41.4 us (47%)
  waiting for transfers between devices  30.7 us (35%)
  Pallas kernels  14.4 us (16%)
    ppermute x21, starting transfers between devices, exchange(): lax.ppermute(block, 'col', [(i, i ^ step) for i in range(devices)])  37.9 us
    ppermute x21, waiting for transfers between devices, exchange(): lax.ppermute(block, 'col', [(i, i ^ step) for i in range(devices)])  29 us
    pallas_call x1, Pallas kernels, on_device(): call(functools.partial(first_kernel, devices), [shaped((8, columns), jnp....  3.76 us
    ppermute x3, starting transfers between devices, from_groups(): lax.ppermute(value, 'grp', [(i, i ^ step) for i in range(groups)])  3.49 us
    pallas_call x1, Pallas kernels, on_device(): call(functools.partial(state_kernel, steps), [shaped(state_now.shape), sh...  1.83 us
    ppermute x3, waiting for transfers between devices, from_groups(): lax.ppermute(value, 'grp', [(i, i ^ step) for i in range(groups)])  1.77 us
  transfers between devices with their start and end apart: 24, of which 13 were waited for; matrix products, arithmetic and copies ran while one was open for 0% of the time, Pallas kernels for 8%

profile of v14, /device:TPU:0, one launch (start us, length us, event | category | flops | bytes accessed | tf_op | source)
XLA Modules:
  0.0 87.4 jit_solution(17949463925994439619)
XLA Ops:
  0.7 3.8 %shard_map.121 = (s32[8,512]{1,0:T(8,128)S(1)}, f32[8,128]{1,0:T(8,128)S(1)}, f32[2,3,64,128]{3,2,1,0:T(8,128)S(1)}, f32[2,3,64,128]{3,2,1,0:T(8,128)S(1)}, f32[...) custom-call(s32[1]{0:T(128)} %bitcast.me_ref, ...), custom_call_target="tpu_custom_call" | custom-call | flops 1000000000 | bytes 1000000 | tf_op jit(solution)/shard_map/pallas_call | solution.py:438
  4.4 0.5 collective-permute-start
  5.0 4.7 %collective-permute-start.1 = (f32[2,3,64,128]{3,2,1,0:T(8,128)S(1)}, f32[2,3,64,128]{3,2,1,0:T(8,128)S(1)}, u32[]{:S(2)}, u32[]{:S(2)}) collective-permute-start(f32[2,3,64,128]{3,2,1,0:T(8,128)S(1)} %get-tuple-element.53), channel_id=1, source_target_pairs={{0,6},{1,7},{2,4},{3,5},{4,2},{5,3},{6,0},{7,1},{8,14},{9,15},{10,... | collective-permute-start | bytes 589832 | tf_op jit(solution)/shard_map/ppermute | solution.py:397
  9.6 0.1 collective-permute-start.2
  9.7 0.0 collective-permute-start.3
  9.7 1.5 %collective-permute-start.4 = (f32[2,3,64,128]{3,2,1,0:T(8,128)S(1)}, f32[2,3,64,128]{3,2,1,0:T(8,128)S(1)}, u32[]{:S(2)}, u32[]{:S(2)}) collective-permute-start(f32[2,3,64,128]{3,2,1,0:T(8,128)S(1)} %get-tuple-element.56), channel_id=1, source_target_pairs={{0,3},{1,2},{2,1},{3,0},{4,7},{5,6},{6,5},{7,4},{8,11},{9,10},{10,... | collective-permute-start | bytes 589832 | tf_op jit(solution)/shard_map/ppermute | solution.py:397
  11.2 1.4 %shard_map.122 = (bf16[512,512]{1,0:T(8,128)(2,1)S(1)}, bf16[512,512]{1,0:T(8,128)(2,1)S(1)}, bf16[512,512]{1,0:T(8,128)(2,1)S(1)}, bf16[512,512]{1,0:T(8,128)(2...) custom-call(f32[512,512]{1,0:T(8,128)S(1)} %copy-done, f32[512,512]{1,0:T(8,128)S(1)} %copy-done.1, ...), custom_call_target="tpu_custom_call" | custom-call | flops 10000000000 | bytes 10000000 | tf_op jit(solution)/shard_map/pallas_call | solution.py:452
  12.6 0.0 collective-permute-done.refs_5_
  12.6 2.7 %collective-permute-start.5 = (f32[2,3,64,128]{3,2,1,0:T(8,128)S(1)}, f32[2,3,64,128]{3,2,1,0:T(8,128)S(1)}, u32[]{:S(2)}, u32[]{:S(2)}) collective-permute-start(f32[2,3,64,128]{3,2,1,0:T(8,128)S(1)} %get-tuple-element.57), channel_id=1, source_target_pairs={{0,4},{1,5},{2,6},{3,7},{4,0},{5,1},{6,2},{7,3},{8,12},{9,13},{10,... | collective-permute-start | bytes 589832 | tf_op jit(solution)/shard_map/ppermute | solution.py:397
  15.3 0.3 collective-permute-done.1.refs_6_
  15.6 8.0 %collective-permute-start.6 = (f32[2,3,64,128]{3,2,1,0:T(8,128)S(1)}, f32[2,3,64,128]{3,2,1,0:T(8,128)S(1)}, u32[]{:S(2)}, u32[]{:S(2)}) collective-permute-start(f32[2,3,64,128]{3,2,1,0:T(8,128)S(1)} %get-tuple-element.58), channel_id=1, source_target_pairs={{0,5},{1,4},{2,7},{3,6},{4,1},{5,0},{6,3},{7,2},{8,13},{9,12},{10,... | collective-permute-start | bytes 589832 | tf_op jit(solution)/shard_map/ppermute | solution.py:397
  23.6 0.2 collective-permute-done.3.refs_8_
  23.7 5.1 %collective-permute-done.4.refs_9_ = f32[2,3,64,128]{3,2,1,0:T(8,128)S(1)} collective-permute-done((f32[2,3,64,128]{3,2,1,0:T(8,128)S(1)}, f32[2,3,64,128]{3,2,1,0:T(8,128)S(1)}, u32[]{:S(2)}, u32[]{:S(2)}) %collective-permute-start.4) | collective-permute-done | bytes 196640 | tf_op jit(solution)/shard_map/ppermute | solution.py:397
  28.8 1.4 %shard_map.123.early_ref = f32[512,384]{1,0:T(8,128)S(1)} custom-call(s32[1]{0:T(128)} %bitcast.me_ref, bf16[512,512]{1,0:T(8,128)(2,1)S(1)} %get-tuple-element.47.refs_0_, bf16[512,512]{1,0:T(8,128)(2,1)S(1)} %get-tuple-element.48.refs_1_, bf16[512,512]{1,0:T(8,128)(2,1)S(1)} %get-tuple-element.49.refs_2_, bf16[512,512]{1,0:T(8,128)(2,1)S(1)} %get-tuple-element.50.refs_3_, ...), custom_call_target="tpu_custom_call" | custom-call | flops 10000000000 | bytes 10000000 | tf_op jit(solution)/shard_map/pallas_call | solution.py:461
  30.2 9.8 %collective-permute-done.5.refs_4_ = f32[2,3,64,128]{3,2,1,0:T(8,128)S(1)} collective-permute-done((f32[2,3,64,128]{3,2,1,0:T(8,128)S(1)}, f32[2,3,64,128]{3,2,1,0:T(8,128)S(1)}, u32[]{:S(2)}, u32[]{:S(2)}) %collective-permute-start.5) | collective-permute-done | bytes 196640 | tf_op jit(solution)/shard_map/ppermute | solution.py:397
  40.0 3.3 %collective-permute-done.6.refs_5_ = f32[2,3,64,128]{3,2,1,0:T(8,128)S(1)} collective-permute-done((f32[2,3,64,128]{3,2,1,0:T(8,128)S(1)}, f32[2,3,64,128]{3,2,1,0:T(8,128)S(1)}, u32[]{:S(2)}, u32[]{:S(2)}) %collective-permute-start.6) | collective-permute-done | bytes 196640 | tf_op jit(solution)/shard_map/ppermute | solution.py:397
  43.3 1.6 %shard_map.124 = (f32[3,64,128]{2,1,0:T(8,128)S(1)}, f32[3,64,128]{2,1,0:T(8,128)S(1)}, f32[3,64,128]{2,1,0:T(8,128)S(1)}, f32[3,64,128]{2,1,0:T(8,128)S(1)}, f3...) custom-call(s32[1]{0:T(128)} %bitcast.me_ref, ...), custom_call_target="tpu_custom_call" | custom-call | flops 1000000000 | bytes 1000000 | tf_op jit(solution)/shard_map/pallas_call | solution.py:469
  44.9 0.3 collective-permute-start.7
  45.2 2.5 %collective-permute-start.8 = (f32[3,64,128]{2,1,0:T(8,128)S(1)}, f32[3,64,128]{2,1,0:T(8,128)S(1)}, u32[]{:S(2)}, u32[]{:S(2)}) collective-permute-start(f32[3,64,128]{2,1,0:T(8,128)S(1)} %get-tuple-element.61), channel_id=1, source_target_pairs={{0,6},{1,7},{2,4},{3,5},{4,2},{5,3},{6,0},{7,1},{8,14},{9,15},{10,... | collective-permute-start | bytes 294920 | tf_op jit(solution)/shard_map/ppermute | solution.py:397
  47.8 0.9 collective-permute-start.9
  48.6 0.0 collective-permute-start.10
  48.6 1.9 %collective-permute-start.11 = (f32[3,64,128]{2,1,0:T(8,128)S(1)}, f32[3,64,128]{2,1,0:T(8,128)S(1)}, u32[]{:S(2)}, u32[]{:S(2)}) collective-permute-start(f32[3,64,128]{2,1,0:T(8,128)S(1)} %get-tuple-element.64), channel_id=1, source_target_pairs={{0,3},{1,2},{2,1},{3,0},{4,7},{5,6},{6,5},{7,4},{8,11},{9,10},{10,... | collective-permute-start | bytes 294920 | tf_op jit(solution)/shard_map/ppermute | solution.py:397
  50.5 0.0 collective-permute-done.7.refs_1_
  50.5 1.4 %collective-permute-start.12 = (f32[3,64,128]{2,1,0:T(8,128)S(1)}, f32[3,64,128]{2,1,0:T(8,128)S(1)}, u32[]{:S(2)}, u32[]{:S(2)}) collective-permute-start(f32[3,64,128]{2,1,0:T(8,128)S(1)} %get-tuple-element.65), channel_id=1, source_target_pairs={{0,4},{1,5},{2,6},{3,7},{4,0},{5,1},{6,2},{7,3},{8,12},{9,13},{10,... | collective-permute-start | bytes 294920 | tf_op jit(solution)/shard_map/ppermute | solution.py:397
  51.9 0.2 collective-permute-done.8.refs_2_
  52.1 0.9 %collective-permute-start.13 = (f32[3,64,128]{2,1,0:T(8,128)S(1)}, f32[3,64,128]{2,1,0:T(8,128)S(1)}, u32[]{:S(2)}, u32[]{:S(2)}) collective-permute-start(f32[3,64,128]{2,1,0:T(8,128)S(1)} %get-tuple-element.66), channel_id=1, source_target_pairs={{0,5},{1,4},{2,7},{3,6},{4,1},{5,0},{6,3},{7,2},{8,13},{9,12},{10,... | collective-permute-start | bytes 294920 | tf_op jit(solution)/shard_map/ppermute | solution.py:397
  53.0 1.7 %collective-permute-done.9.refs_3_ = f32[3,64,128]{2,1,0:T(8,128)S(1)} collective-permute-done((f32[3,64,128]{2,1,0:T(8,128)S(1)}, f32[3,64,128]{2,1,0:T(8,128)S(1)}, u32[]{:S(2)}, u32[]{:S(2)}) %collective-permute-start.9) | collective-permute-done | bytes 98336 | tf_op jit(solution)/shard_map/ppermute | solution.py:397
  54.7 4.6 %collective-permute-done.10.refs_4_ = f32[3,64,128]{2,1,0:T(8,128)S(1)} collective-permute-done((f32[3,64,128]{2,1,0:T(8,128)S(1)}, f32[3,64,128]{2,1,0:T(8,128)S(1)}, u32[]{:S(2)}, u32[]{:S(2)}) %collective-permute-start.10) | collective-permute-done | bytes 98336 | tf_op jit(solution)/shard_map/ppermute | solution.py:397
  59.3 1.9 %collective-permute-done.11.refs_5_ = f32[3,64,128]{2,1,0:T(8,128)S(1)} collective-permute-done((f32[3,64,128]{2,1,0:T(8,128)S(1)}, f32[3,64,128]{2,1,0:T(8,128)S(1)}, u32[]{:S(2)}, u32[]{:S(2)}) %collective-permute-start.11) | collective-permute-done | bytes 98336 | tf_op jit(solution)/shard_map/ppermute | solution.py:397
  61.2 1.2 %shard_map.125 = (f32[384,512]{1,0:T(8,128)S(1)}, bf16[128,512]{1,0:T(8,128)(2,1)S(1)}) custom-call(s32[8,512]{1,0:T(8,128)S(1)} %get-tuple-element.43.info_ref, f32[3,64,128]{2,1,0:T(8,128)S(1)} %get-tuple-element.59.refs_0_, f32[3,64,128]{2,1,0:T(8,128)S(1)} %collective-permute-done.7.refs_1_, f32[3,64,128]{2,1,0:T(8,128)S(1)} %collective-permute-done.8.refs_2_, ...), custom_call_target="tpu_custom_call" | custom-call | flops 10000000000 | bytes 10000000 | tf_op jit(solution)/shard_map/pallas_call | solution.py:480
  62.3 1.8 %collective-permute-done.13.refs_1_.refs_7_ = f32[3,64,128]{2,1,0:T(8,128)S(1)} collective-permute-done((f32[3,64,128]{2,1,0:T(8,128)S(1)}, f32[3,64,128]{2,1,0:T(8,128)S(1)}, u32[]{:S(2)}, u32[]{:S(2)}) %collective-permute-start.13) | collective-permute-done | bytes 98336 | tf_op jit(solution)/shard_map/ppermute | solution.py:397
  64.1 0.7 shard_map.126
  64.8 0.3 collective-permute-start.14
  65.2 0.0 collective-permute-start.15
  65.2 1.7 %collective-permute-start.20 = (f32[3,64,128]{2,1,0:T(8,128)S(1)}, f32[3,64,128]{2,1,0:T(8,128)S(1)}, u32[]{:S(2)}, u32[]{:S(2)}) collective-permute-start(f32[3,64,128]{2,1,0:T(8,128)S(1)} %get-tuple-element.76), channel_id=1, source_target_pairs={{0,6},{1,7},{2,4},{3,5},{4,2},{5,3},{6,0},{7,1},{8,14},{9,15},{10,... | collective-permute-start | bytes 294920 | tf_op jit(solution)/shard_map/ppermute | solution.py:397
  66.9 1.7 %collective-permute-start.21 = (f32[3,64,128]{2,1,0:T(8,128)S(1)}, f32[3,64,128]{2,1,0:T(8,128)S(1)}, u32[]{:S(2)}, u32[]{:S(2)}) collective-permute-start(f32[3,64,128]{2,1,0:T(8,128)S(1)} %get-tuple-element.77), channel_id=1, source_target_pairs={{0,7},{1,6},{2,5},{3,4},{4,3},{5,2},{6,1},{7,0},{8,15},{9,14},{10,... | collective-permute-start | bytes 294920 | tf_op jit(solution)/shard_map/ppermute | solution.py:397
  68.5 0.3 collective-permute-start.23
  68.9 1.8 %collective-permute-start.22 = (f32[3,64,128]{2,1,0:T(8,128)S(1)}, f32[3,64,128]{2,1,0:T(8,128)S(1)}, u32[]{:S(2)}, u32[]{:S(2)}) collective-permute-start(f32[3,64,128]{2,1,0:T(8,128)S(1)} %get-tuple-element.79), channel_id=1, source_target_pairs={{0,2},{1,3},{2,0},{3,1},{4,6},{5,7},{6,4},{7,5},{8,10},{9,11},{10,... | collective-permute-start | bytes 294920 | tf_op jit(solution)/shard_map/ppermute | solution.py:397
  70.7 1.8 %shard_map.127 = (f32[6,64,512]{2,1,0:T(8,128)}, f32[3,64]{1,0:T(4,128)S(1)}) custom-call(s32[8,512]{1,0:T(8,128)S(1)} %get-tuple-element.43.info_ref, s32[2,512]{1,0:T(2,128)S(1)} %copy-done.4, f32[6,64,512]{2,1,0:T(8,128)S(1)} %copy-done.3, f32[3,64,128]{2,1,0:T(8,128)S(1)} %get-tuple-element.59.refs_0_, f32[3,64,128]{2,1,0:T(8,128)S(1)} %collective-permute-done.7.refs_1_, ...), custom_call_target="tpu_custom_call" | custom-call | flops 10000000000 | bytes 10000000 | tf_op jit(solution)/shard_map/pallas_call | solution.py:496
  72.6 0.2 collective-permute-done.20.refs_2_
  72.8 6.6 %collective-permute-start.16 = (f32[3,64,128]{2,1,0:T(8,128)S(1)}, f32[3,64,128]{2,1,0:T(8,128)S(1)}, u32[]{:S(2)}, u32[]{:S(2)}) collective-permute-start(f32[3,64,128]{2,1,0:T(8,128)S(1)} %get-tuple-element.73), channel_id=1, source_target_pairs={{0,5},{1,4},{2,7},{3,6},{4,1},{5,0},{6,3},{7,2},{8,13},{9,12},{10,... | collective-permute-start | bytes 294920 | tf_op jit(solution)/shard_map/ppermute | solution.py:397
  79.4 2.4 %collective-permute-start.19 = (f32[3,64]{1,0:T(4,128)S(1)}, f32[3,64]{1,0:T(4,128)S(1)}, u32[]{:S(2)}, u32[]{:S(2)}) collective-permute-start(f32[3,64]{1,0:T(4,128)S(1)} %get-tuple-element.74.refs_2_), channel_id=1, source_target_pairs={{0,24},{8,16},{16,8},{24,0},{1,25},{9,17},{17,9},{25,1},{2,26},{10... | collective-permute-start | bytes 2312 | tf_op jit(solution)/shard_map/ppermute | solution.py:405
  81.9 0.5 collective-permute-start.18
  82.4 0.5 collective-permute-start.17
  82.9 1.2 %shard_map.128.refs_6_ = f32[6,512,128]{2,1,0:T(8,128)} custom-call(s32[1]{0:T(128)} %bitcast.me_ref, s32[8,512]{1,0:T(8,128)S(1)} %get-tuple-element.43.info_ref, f32[3,512,128]{2,1,0:T(8,128)S(1)} %get-tuple-element.71.solved_ref, f32[3,64,128]{2,1,0:T(8,128)S(1)} %get-tuple-element.75.refs_0_, f32[3,64,128]{2,1,0:T(8,128)S(1)} %collective-permute-done.14.refs_8_.refs_1_, ...), custom_call_target="tpu_custom_call" | custom-call | flops 10000000000 | bytes 10000000 | tf_op jit(solution)/shard_map/pallas_call | solution.py:506
  84.2 1.3 %collective-permute-done.18.refs_4_ = f32[3,64]{1,0:T(4,128)S(1)} collective-permute-done((f32[3,64]{1,0:T(4,128)S(1)}, f32[3,64]{1,0:T(4,128)S(1)}, u32[]{:S(2)}, u32[]{:S(2)}) %collective-permute-start.18) | collective-permute-done | bytes 800 | tf_op jit(solution)/shard_map/ppermute | solution.py:405
  85.5 0.5 collective-permute-done.17.refs_3_
  86.0 1.4 %shard_map.129 = (f32[6,512,128]{2,1,0:T(8,128)}, f32[3,64]{1,0:T(4,128)}) custom-call(s32[1]{0:T(128)} %bitcast.me_ref, s32[8,512]{1,0:T(8,128)S(1)} %get-tuple-element.43.info_ref, f32[3,512,128]{2,1,0:T(8,128)S(1)} %get-tuple-element.71.solved_ref, f32[3,64,128]{2,1,0:T(8,128)S(1)} %collective-permute-done.15.refs_0_, ...), custom_call_target="tpu_custom_call", output_to_operand_aliasing={{0}: (9, {})} | custom-call | flops 1000000000 | bytes 1000000 | tf_op jit(solution)/shard_map/pallas_call | solution.py:517
  (21 shorter events, 0.0 us)
Async XLA Ops:
  0.6 10.6 %copy-start = (f32[512,512]{1,0:T(8,128)S(1)}, f32[512,512]{1,0:T(8,128)}, u32[]{:S(2)}) copy-start(f32[512,512]{1,0:T(8,128)} %deriv_ref.1) | copy-start | bytes 3145732
  0.6 10.6 %copy-start.1 = (f32[512,512]{1,0:T(8,128)S(1)}, f32[512,512]{1,0:T(8,128)}, u32[]{:S(2)}) copy-start(f32[512,512]{1,0:T(8,128)} %inverse_ref.1) | copy-start | bytes 3145732
  0.7 10.6 %copy-start.2 = (f32[512,512]{1,0:T(8,128)S(1)}, f32[512,512]{1,0:T(8,128)}, u32[]{:S(2)}) copy-start(f32[512,512]{1,0:T(8,128)} %basis_ref.1) | copy-start | bytes 3145732
  0.7 10.5 %copy-start.5 = (f32[512]{0:T(512)S(1)}, f32[512]{0:T(512)}, u32[]{:S(2)}) copy-start(f32[512]{0:T(512)} %param.17) | copy-start | bytes 6148
  4.4 8.1 %collective-permute-start = (f32[2,3,64,128]{3,2,1,0:T(8,128)S(1)}, f32[2,3,64,128]{3,2,1,0:T(8,128)S(1)}, u32[]{:S(2)}, u32[]{:S(2)}) collective-permute-start(f32[2,3,64,128]{3,2,1,0:T(8,128)S(1)} %get-tuple-element.52), channel_id=1, source_target_pairs={{0,1},{1,0},{2,3},{3,2},{4,5},{5,4},{6,7},{7,6},{8,9},{9,8},{10,11... | collective-permute-start | bytes 589832 | tf_op jit(solution)/shard_map/ppermute | solution.py:397
  5.0 10.6 %collective-permute-start.1 = (f32[2,3,64,128]{3,2,1,0:T(8,128)S(1)}, f32[2,3,64,128]{3,2,1,0:T(8,128)S(1)}, u32[]{:S(2)}, u32[]{:S(2)}) collective-permute-start(f32[2,3,64,128]{3,2,1,0:T(8,128)S(1)} %get-tuple-element.53), channel_id=1, source_target_pairs={{0,6},{1,7},{2,4},{3,5},{4,2},{5,3},{6,0},{7,1},{8,14},{9,15},{10,... | collective-permute-start | bytes 589832 | tf_op jit(solution)/shard_map/ppermute | solution.py:397
  9.6 13.9 %collective-permute-start.2 = (f32[2,3,64,128]{3,2,1,0:T(8,128)S(1)}, f32[2,3,64,128]{3,2,1,0:T(8,128)S(1)}, u32[]{:S(2)}, u32[]{:S(2)}) collective-permute-start(f32[2,3,64,128]{3,2,1,0:T(8,128)S(1)} %get-tuple-element.54), channel_id=1, source_target_pairs={{0,7},{1,6},{2,5},{3,4},{4,3},{5,2},{6,1},{7,0},{8,15},{9,14},{10,... | collective-permute-start | bytes 589832 | tf_op jit(solution)/shard_map/ppermute | solution.py:397
  9.7 14.0 %collective-permute-start.3 = (f32[2,3,64,128]{3,2,1,0:T(8,128)S(1)}, f32[2,3,64,128]{3,2,1,0:T(8,128)S(1)}, u32[]{:S(2)}, u32[]{:S(2)}) collective-permute-start(f32[2,3,64,128]{3,2,1,0:T(8,128)S(1)} %get-tuple-element.55), channel_id=1, source_target_pairs={{0,2},{1,3},{2,0},{3,1},{4,6},{5,7},{6,4},{7,5},{8,10},{9,11},{10,... | collective-permute-start | bytes 589832 | tf_op jit(solution)/shard_map/ppermute | solution.py:397
  9.7 19.1 %collective-permute-start.4 = (f32[2,3,64,128]{3,2,1,0:T(8,128)S(1)}, f32[2,3,64,128]{3,2,1,0:T(8,128)S(1)}, u32[]{:S(2)}, u32[]{:S(2)}) collective-permute-start(f32[2,3,64,128]{3,2,1,0:T(8,128)S(1)} %get-tuple-element.56), channel_id=1, source_target_pairs={{0,3},{1,2},{2,1},{3,0},{4,7},{5,6},{6,5},{7,4},{8,11},{9,10},{10,... | collective-permute-start | bytes 589832 | tf_op jit(solution)/shard_map/ppermute | solution.py:397
  12.6 27.4 %collective-permute-start.5 = (f32[2,3,64,128]{3,2,1,0:T(8,128)S(1)}, f32[2,3,64,128]{3,2,1,0:T(8,128)S(1)}, u32[]{:S(2)}, u32[]{:S(2)}) collective-permute-start(f32[2,3,64,128]{3,2,1,0:T(8,128)S(1)} %get-tuple-element.57), channel_id=1, source_target_pairs={{0,4},{1,5},{2,6},{3,7},{4,0},{5,1},{6,2},{7,3},{8,12},{9,13},{10,... | collective-permute-start | bytes 589832 | tf_op jit(solution)/shard_map/ppermute | solution.py:397
  15.6 27.7 %collective-permute-start.6 = (f32[2,3,64,128]{3,2,1,0:T(8,128)S(1)}, f32[2,3,64,128]{3,2,1,0:T(8,128)S(1)}, u32[]{:S(2)}, u32[]{:S(2)}) collective-permute-start(f32[2,3,64,128]{3,2,1,0:T(8,128)S(1)} %get-tuple-element.58), channel_id=1, source_target_pairs={{0,5},{1,4},{2,7},{3,6},{4,1},{5,0},{6,3},{7,2},{8,13},{9,12},{10,... | collective-permute-start | bytes 589832 | tf_op jit(solution)/shard_map/ppermute | solution.py:397
  44.9 5.6 %collective-permute-start.7 = (f32[3,64,128]{2,1,0:T(8,128)S(1)}, f32[3,64,128]{2,1,0:T(8,128)S(1)}, u32[]{:S(2)}, u32[]{:S(2)}) collective-permute-start(f32[3,64,128]{2,1,0:T(8,128)S(1)} %get-tuple-element.60), channel_id=1, source_target_pairs={{0,1},{1,0},{2,3},{3,2},{4,5},{5,4},{6,7},{7,6},{8,9},{9,8},{10,11... | collective-permute-start | bytes 294920 | tf_op jit(solution)/shard_map/ppermute | solution.py:397
  45.2 6.9 %collective-permute-start.8 = (f32[3,64,128]{2,1,0:T(8,128)S(1)}, f32[3,64,128]{2,1,0:T(8,128)S(1)}, u32[]{:S(2)}, u32[]{:S(2)}) collective-permute-start(f32[3,64,128]{2,1,0:T(8,128)S(1)} %get-tuple-element.61), channel_id=1, source_target_pairs={{0,6},{1,7},{2,4},{3,5},{4,2},{5,3},{6,0},{7,1},{8,14},{9,15},{10,... | collective-permute-start | bytes 294920 | tf_op jit(solution)/shard_map/ppermute | solution.py:397
  47.8 6.9 %collective-permute-start.9 = (f32[3,64,128]{2,1,0:T(8,128)S(1)}, f32[3,64,128]{2,1,0:T(8,128)S(1)}, u32[]{:S(2)}, u32[]{:S(2)}) collective-permute-start(f32[3,64,128]{2,1,0:T(8,128)S(1)} %get-tuple-element.62), channel_id=1, source_target_pairs={{0,7},{1,6},{2,5},{3,4},{4,3},{5,2},{6,1},{7,0},{8,15},{9,14},{10,... | collective-permute-start | bytes 294920 | tf_op jit(solution)/shard_map/ppermute | solution.py:397
  48.6 10.7 %collective-permute-start.10 = (f32[3,64,128]{2,1,0:T(8,128)S(1)}, f32[3,64,128]{2,1,0:T(8,128)S(1)}, u32[]{:S(2)}, u32[]{:S(2)}) collective-permute-start(f32[3,64,128]{2,1,0:T(8,128)S(1)} %get-tuple-element.63), channel_id=1, source_target_pairs={{0,2},{1,3},{2,0},{3,1},{4,6},{5,7},{6,4},{7,5},{8,10},{9,11},{10,... | collective-permute-start | bytes 294920 | tf_op jit(solution)/shard_map/ppermute | solution.py:397
  48.6 12.5 %collective-permute-start.11 = (f32[3,64,128]{2,1,0:T(8,128)S(1)}, f32[3,64,128]{2,1,0:T(8,128)S(1)}, u32[]{:S(2)}, u32[]{:S(2)}) collective-permute-start(f32[3,64,128]{2,1,0:T(8,128)S(1)} %get-tuple-element.64), channel_id=1, source_target_pairs={{0,3},{1,2},{2,1},{3,0},{4,7},{5,6},{6,5},{7,4},{8,11},{9,10},{10,... | collective-permute-start | bytes 294920 | tf_op jit(solution)/shard_map/ppermute | solution.py:397
  50.5 11.8 %collective-permute-start.12 = (f32[3,64,128]{2,1,0:T(8,128)S(1)}, f32[3,64,128]{2,1,0:T(8,128)S(1)}, u32[]{:S(2)}, u32[]{:S(2)}) collective-permute-start(f32[3,64,128]{2,1,0:T(8,128)S(1)} %get-tuple-element.65), channel_id=1, source_target_pairs={{0,4},{1,5},{2,6},{3,7},{4,0},{5,1},{6,2},{7,3},{8,12},{9,13},{10,... | collective-permute-start | bytes 294920 | tf_op jit(solution)/shard_map/ppermute | solution.py:397
  52.1 12.0 %collective-permute-start.13 = (f32[3,64,128]{2,1,0:T(8,128)S(1)}, f32[3,64,128]{2,1,0:T(8,128)S(1)}, u32[]{:S(2)}, u32[]{:S(2)}) collective-permute-start(f32[3,64,128]{2,1,0:T(8,128)S(1)} %get-tuple-element.66), channel_id=1, source_target_pairs={{0,5},{1,4},{2,7},{3,6},{4,1},{5,0},{6,3},{7,2},{8,13},{9,12},{10,... | collective-permute-start | bytes 294920 | tf_op jit(solution)/shard_map/ppermute | solution.py:397
  64.1 6.6 %copy-start.3 = (f32[6,64,512]{2,1,0:T(8,128)S(1)}, f32[6,64,512]{2,1,0:T(8,128)}, u32[]{:S(2)}) copy-start(f32[6,64,512]{2,1,0:T(8,128)} %velocity_ref.1) | copy-start | bytes 2359300
  64.1 6.6 %copy-start.4 = (s32[2,512]{1,0:T(2,128)S(1)}, s32[2,512]{1,0:T(2,128)}, u32[]{:S(2)}) copy-start(s32[2,512]{1,0:T(2,128)} %modes_ref.1) | copy-start | bytes 12292
  64.8 4.1 %collective-permute-start.14 = (f32[3,64,128]{2,1,0:T(8,128)S(1)}, f32[3,64,128]{2,1,0:T(8,128)S(1)}, u32[]{:S(2)}, u32[]{:S(2)}) collective-permute-start(f32[3,64,128]{2,1,0:T(8,128)S(1)} %get-tuple-element.69), channel_id=1, source_target_pairs={{0,1},{1,0},{2,3},{3,2},{4,5},{5,4},{6,7},{7,6},{8,9},{9,8},{10,11... | collective-permute-start | bytes 294920 | tf_op jit(solution)/shard_map/ppermute | solution.py:397
  65.2 19.0 %collective-permute-start.15 = (f32[3,64,128]{2,1,0:T(8,128)S(1)}, f32[3,64,128]{2,1,0:T(8,128)S(1)}, u32[]{:S(2)}, u32[]{:S(2)}) collective-permute-start(f32[3,64,128]{2,1,0:T(8,128)S(1)} %get-tuple-element.72), channel_id=1, source_target_pairs={{0,4},{1,5},{2,6},{3,7},{4,0},{5,1},{6,2},{7,3},{8,12},{9,13},{10,... | collective-permute-start | bytes 294920 | tf_op jit(solution)/shard_map/ppermute | solution.py:397
  65.2 7.6 %collective-permute-start.20 = (f32[3,64,128]{2,1,0:T(8,128)S(1)}, f32[3,64,128]{2,1,0:T(8,128)S(1)}, u32[]{:S(2)}, u32[]{:S(2)}) collective-permute-start(f32[3,64,128]{2,1,0:T(8,128)S(1)} %get-tuple-element.76), channel_id=1, source_target_pairs={{0,6},{1,7},{2,4},{3,5},{4,2},{5,3},{6,0},{7,1},{8,14},{9,15},{10,... | collective-permute-start | bytes 294920 | tf_op jit(solution)/shard_map/ppermute | solution.py:397
  66.9 12.5 %collective-permute-start.21 = (f32[3,64,128]{2,1,0:T(8,128)S(1)}, f32[3,64,128]{2,1,0:T(8,128)S(1)}, u32[]{:S(2)}, u32[]{:S(2)}) collective-permute-start(f32[3,64,128]{2,1,0:T(8,128)S(1)} %get-tuple-element.77), channel_id=1, source_target_pairs={{0,7},{1,6},{2,5},{3,4},{4,3},{5,2},{6,1},{7,0},{8,15},{9,14},{10,... | collective-permute-start | bytes 294920 | tf_op jit(solution)/shard_map/ppermute | solution.py:397
  68.5 13.3 %collective-permute-start.23 = (f32[3,64,128]{2,1,0:T(8,128)S(1)}, f32[3,64,128]{2,1,0:T(8,128)S(1)}, u32[]{:S(2)}, u32[]{:S(2)}) collective-permute-start(f32[3,64,128]{2,1,0:T(8,128)S(1)} %get-tuple-element.80), channel_id=1, source_target_pairs={{0,3},{1,2},{2,1},{3,0},{4,7},{5,6},{6,5},{7,4},{8,11},{9,10},{10,... | collective-permute-start | bytes 294920 | tf_op jit(solution)/shard_map/ppermute | solution.py:397
  68.9 13.5 %collective-permute-start.22 = (f32[3,64,128]{2,1,0:T(8,128)S(1)}, f32[3,64,128]{2,1,0:T(8,128)S(1)}, u32[]{:S(2)}, u32[]{:S(2)}) collective-permute-start(f32[3,64,128]{2,1,0:T(8,128)S(1)} %get-tuple-element.79), channel_id=1, source_target_pairs={{0,2},{1,3},{2,0},{3,1},{4,6},{5,7},{6,4},{7,5},{8,10},{9,11},{10,... | collective-permute-start | bytes 294920 | tf_op jit(solution)/shard_map/ppermute | solution.py:397
  72.8 11.4 %collective-permute-start.16 = (f32[3,64,128]{2,1,0:T(8,128)S(1)}, f32[3,64,128]{2,1,0:T(8,128)S(1)}, u32[]{:S(2)}, u32[]{:S(2)}) collective-permute-start(f32[3,64,128]{2,1,0:T(8,128)S(1)} %get-tuple-element.73), channel_id=1, source_target_pairs={{0,5},{1,4},{2,7},{3,6},{4,1},{5,0},{6,3},{7,2},{8,13},{9,12},{10,... | collective-permute-start | bytes 294920 | tf_op jit(solution)/shard_map/ppermute | solution.py:397
  79.4 4.8 %collective-permute-start.19 = (f32[3,64]{1,0:T(4,128)S(1)}, f32[3,64]{1,0:T(4,128)S(1)}, u32[]{:S(2)}, u32[]{:S(2)}) collective-permute-start(f32[3,64]{1,0:T(4,128)S(1)} %get-tuple-element.74.refs_2_), channel_id=1, source_target_pairs={{0,24},{8,16},{16,8},{24,0},{1,25},{9,17},{17,9},{25,1},{2,26},{10... | collective-permute-start | bytes 2312 | tf_op jit(solution)/shard_map/ppermute | solution.py:405
  81.9 3.6 %collective-permute-start.18 = (f32[3,64]{1,0:T(4,128)S(1)}, f32[3,64]{1,0:T(4,128)S(1)}, u32[]{:S(2)}, u32[]{:S(2)}) collective-permute-start(f32[3,64]{1,0:T(4,128)S(1)} %get-tuple-element.74.refs_2_), channel_id=1, source_target_pairs={{0,16},{8,24},{16,0},{24,8},{1,17},{9,25},{17,1},{25,9},{2,18},{10... | collective-permute-start | bytes 2312 | tf_op jit(solution)/shard_map/ppermute | solution.py:405
  82.4 3.6 %collective-permute-start.17 = (f32[3,64]{1,0:T(4,128)S(1)}, f32[3,64]{1,0:T(4,128)S(1)}, u32[]{:S(2)}, u32[]{:S(2)}) collective-permute-start(f32[3,64]{1,0:T(4,128)S(1)} %get-tuple-element.74.refs_2_), channel_id=1, source_target_pairs={{0,8},{8,0},{16,24},{24,16},{1,9},{9,1},{17,25},{25,17},{2,10},{10... | collective-permute-start | bytes 2312 | tf_op jit(solution)/shard_map/ppermute | solution.py:405

commit v15 on v14

--- a/solution.py
+++ b/solution.py
@@ -130,7 +130,9 @@
     local = state + TIME_STEP * (forcing - RK_ALPHA * (wave * state))
     rows = comps * points
     both = jnp.concatenate([state.reshape(rows, columns), local.reshape(rows, columns)], axis=0)
-    placed = sum_parts(lax.dot_general(three_parts(both), chosen, NT, preferred_element_type=F32))
+    high, low = two_parts(both)
+    placed = lax.dot_general(jnp.concatenate([high, low], axis=0), chosen, NT, preferred_element_type=F32)
+    placed = placed[: 2 * rows] + placed[2 * rows :]
     for step, out in zip(steps_of(devices, points), out_refs):
         taken = placed[:, step * share : (step + 1) * share]
         for kind in range(2):
@@ -359,13 +361,8 @@
     assemble(me_ref[0], steps, unused(info_ref, share), solved_ref, in_refs, out_hbm, rows_ref, sems)
 
 
-def assemble_late_kernel(steps, terms, me_ref, info_ref, solved_ref, *refs):
-    in_refs, refs = refs[: len(steps)], refs[len(steps) :]
-    parts, (_, out_hbm, emf_ref, rows_ref, sems) = refs[:terms], refs[terms:]
-    parts = [ref[...] for ref in parts]
-    while len(parts) > 1:
-        parts = [parts[at] + parts[at + 1] for at in range(0, len(parts), 2)]
-    emf_ref[...] = parts[0]
+def assemble_late_kernel(steps, me_ref, info_ref, solved_ref, *refs):
+    in_refs, (_, out_hbm, rows_ref, sems) = refs[: len(steps)], refs[len(steps) :]
     share = in_refs[0].shape[2] // 2
     assemble(me_ref[0], steps, unused(info_ref, share), solved_ref, in_refs, out_hbm, rows_ref, sems)
 
@@ -514,15 +511,18 @@
             pltpu.SemaphoreType.DMA((comps * early_rows // LANES,)),
         ],
     )(me, info, solved, *extra[:split])
-    owned, mean_emf = call(
-        functools.partial(assemble_late_kernel, late, len(terms)),
-        [shaped((comps, depth, lanes)), shaped((3, points))],
-        [SCALAR] + [LOCAL] * (2 + len(late) + len(terms)) + [FAR],
-        [FAR, LOCAL],
+    owned = call(
+        functools.partial(assemble_late_kernel, late),
+        shaped((comps, depth, lanes)),
+        [SCALAR] + [LOCAL] * (2 + len(late)) + [FAR],
+        FAR,
         1,
         [pltpu.VMEM((comps, late_rows, lanes), F32), pltpu.SemaphoreType.DMA((comps,))],
-        aliases={3 + len(late) + len(terms): 0},
-    )(me, info, solved, *extra[split:], *terms, owned)
+        aliases={3 + len(late): 0},
+    )(me, info, solved, *extra[split:], owned)
+    while len(terms) > 1:
+        terms = [terms[at] + terms[at + 1] for at in range(0, len(terms), 2)]
+    mean_emf = terms[0]
     return (state_next, owned, mean_emf)
 
 

time: 87.6 us -> 90.4 us (1.032); the launches traced: 87.4 us -> 88.6 us
  waiting for transfers between devices: 30.7 us -> 32.4 us
    ppermute x21, waiting for transfers between devices: 29 us -> 32.4 us  [exchange(): lax.ppermute(block, 'col', [(i, i ^ step) for i in range(devices)])]
    ppermute x3, waiting for transfers between devices: 1.77 us -> 0.01 us  [from_groups(): lax.ppermute(value, 'grp', [(i, i ^ step) for i in range(groups)])]
  transfers between devices with their start and end apart: 24 -> 24, of which waited for: 13 -> 14; matrix products, arithmetic and copies ran while one was open for 0% -> 1% of each run, Pallas kernels for 8% -> 6%
where the time goes in v15:
time: 90.4 us; the launch traced here: 88.6 us
  starting transfers between devices  41.3 us (46%)
  waiting for transfers between devices  32.4 us (36%)
  Pallas kernels  13.5 us (15%)
    ppermute x21, starting transfers between devices, exchange(): lax.ppermute(block, 'col', [(i, i ^ step) for i in range(devices)])  37.8 us
    ppermute x21, waiting for transfers between devices, exchange(): lax.ppermute(block, 'col', [(i, i ^ step) for i in range(devices)])  32.4 us
    ppermute x3, starting transfers between devices, from_groups(): lax.ppermute(value, 'grp', [(i, i ^ step) for i in range(groups)])  3.55 us
    pallas_call x1, Pallas kernels, on_device(): call(functools.partial(first_kernel, devices), [shaped((8, columns), jnp....  3.37 us
    pallas_call x1, Pallas kernels, on_device(): call(functools.partial(state_kernel, steps), [shaped(state_now.shape), sh...  1.83 us
  transfers between devices with their start and end apart: 24, of which 14 were waited for; matrix products, arithmetic and copies ran while one was open for 1% of the time, Pallas kernels for 6%

profile of v15, /device:TPU:0, one launch (start us, length us, event | category | flops | bytes accessed | tf_op | source)
XLA Modules:
  0.0 88.6 jit_solution(7681851221512799836)
XLA Ops:
  0.7 3.4 %shard_map.121 = (s32[8,512]{1,0:T(8,128)S(1)}, f32[8,128]{1,0:T(8,128)S(1)}, f32[2,3,64,128]{3,2,1,0:T(8,128)S(1)}, f32[2,3,64,128]{3,2,1,0:T(8,128)S(1)}, f32[...) custom-call(s32[1]{0:T(128)} %bitcast.me_ref, ...), custom_call_target="tpu_custom_call" | custom-call | flops 1000000000 | bytes 1000000 | tf_op jit(solution)/shard_map/pallas_call | solution.py:435
  4.1 0.5 collective-permute-start
  4.6 4.7 %collective-permute-start.1 = (f32[2,3,64,128]{3,2,1,0:T(8,128)S(1)}, f32[2,3,64,128]{3,2,1,0:T(8,128)S(1)}, u32[]{:S(2)}, u32[]{:S(2)}) collective-permute-start(f32[2,3,64,128]{3,2,1,0:T(8,128)S(1)} %get-tuple-element.51), channel_id=1, source_target_pairs={{0,6},{1,7},{2,4},{3,5},{4,2},{5,3},{6,0},{7,1},{8,14},{9,15},{10,... | collective-permute-start | bytes 589832 | tf_op jit(solution)/shard_map/ppermute | solution.py:394
  9.3 0.1 collective-permute-start.2
  9.3 0.0 collective-permute-start.3
  9.3 1.5 %collective-permute-start.4 = (f32[2,3,64,128]{3,2,1,0:T(8,128)S(1)}, f32[2,3,64,128]{3,2,1,0:T(8,128)S(1)}, u32[]{:S(2)}, u32[]{:S(2)}) collective-permute-start(f32[2,3,64,128]{3,2,1,0:T(8,128)S(1)} %get-tuple-element.54), channel_id=1, source_target_pairs={{0,3},{1,2},{2,1},{3,0},{4,7},{5,6},{6,5},{7,4},{8,11},{9,10},{10,... | collective-permute-start | bytes 589832 | tf_op jit(solution)/shard_map/ppermute | solution.py:394
  10.8 1.4 %shard_map.122 = (bf16[512,512]{1,0:T(8,128)(2,1)S(1)}, bf16[512,512]{1,0:T(8,128)(2,1)S(1)}, bf16[512,512]{1,0:T(8,128)(2,1)S(1)}, bf16[512,512]{1,0:T(8,128)(2...) custom-call(f32[512,512]{1,0:T(8,128)S(1)} %copy-done, f32[512,512]{1,0:T(8,128)S(1)} %copy-done.1, ...), custom_call_target="tpu_custom_call" | custom-call | flops 10000000000 | bytes 10000000 | tf_op jit(solution)/shard_map/pallas_call | solution.py:449
  12.2 2.7 %collective-permute-start.5 = (f32[2,3,64,128]{3,2,1,0:T(8,128)S(1)}, f32[2,3,64,128]{3,2,1,0:T(8,128)S(1)}, u32[]{:S(2)}, u32[]{:S(2)}) collective-permute-start(f32[2,3,64,128]{3,2,1,0:T(8,128)S(1)} %get-tuple-element.55), channel_id=1, source_target_pairs={{0,4},{1,5},{2,6},{3,7},{4,0},{5,1},{6,2},{7,3},{8,12},{9,13},{10,... | collective-permute-start | bytes 589832 | tf_op jit(solution)/shard_map/ppermute | solution.py:394
  14.9 0.3 collective-permute-done.1.refs_6_
  15.2 8.0 %collective-permute-start.6 = (f32[2,3,64,128]{3,2,1,0:T(8,128)S(1)}, f32[2,3,64,128]{3,2,1,0:T(8,128)S(1)}, u32[]{:S(2)}, u32[]{:S(2)}) collective-permute-start(f32[2,3,64,128]{3,2,1,0:T(8,128)S(1)} %get-tuple-element.56), channel_id=1, source_target_pairs={{0,5},{1,4},{2,7},{3,6},{4,1},{5,0},{6,3},{7,2},{8,13},{9,12},{10,... | collective-permute-start | bytes 589832 | tf_op jit(solution)/shard_map/ppermute | solution.py:394
  23.2 0.0 collective-permute-done.2.refs_7_
  23.2 0.2 collective-permute-done.3.refs_8_
  23.4 5.1 %collective-permute-done.4.refs_9_ = f32[2,3,64,128]{3,2,1,0:T(8,128)S(1)} collective-permute-done((f32[2,3,64,128]{3,2,1,0:T(8,128)S(1)}, f32[2,3,64,128]{3,2,1,0:T(8,128)S(1)}, u32[]{:S(2)}, u32[]{:S(2)}) %collective-permute-start.4) | collective-permute-done | bytes 196640 | tf_op jit(solution)/shard_map/ppermute | solution.py:394
  28.4 1.4 %shard_map.123.early_ref = f32[512,384]{1,0:T(8,128)S(1)} custom-call(s32[1]{0:T(128)} %bitcast.me_ref, bf16[512,512]{1,0:T(8,128)(2,1)S(1)} %get-tuple-element.45.refs_0_, bf16[512,512]{1,0:T(8,128)(2,1)S(1)} %get-tuple-element.46.refs_1_, bf16[512,512]{1,0:T(8,128)(2,1)S(1)} %get-tuple-element.47.refs_2_, bf16[512,512]{1,0:T(8,128)(2,1)S(1)} %get-tuple-element.48.refs_3_, ...), custom_call_target="tpu_custom_call" | custom-call | flops 10000000000 | bytes 10000000 | tf_op jit(solution)/shard_map/pallas_call | solution.py:458
  29.9 9.8 %collective-permute-done.5.refs_4_ = f32[2,3,64,128]{3,2,1,0:T(8,128)S(1)} collective-permute-done((f32[2,3,64,128]{3,2,1,0:T(8,128)S(1)}, f32[2,3,64,128]{3,2,1,0:T(8,128)S(1)}, u32[]{:S(2)}, u32[]{:S(2)}) %collective-permute-start.5) | collective-permute-done | bytes 196640 | tf_op jit(solution)/shard_map/ppermute | solution.py:394
  39.6 3.3 %collective-permute-done.6.refs_5_ = f32[2,3,64,128]{3,2,1,0:T(8,128)S(1)} collective-permute-done((f32[2,3,64,128]{3,2,1,0:T(8,128)S(1)}, f32[2,3,64,128]{3,2,1,0:T(8,128)S(1)}, u32[]{:S(2)}, u32[]{:S(2)}) %collective-permute-start.6) | collective-permute-done | bytes 196640 | tf_op jit(solution)/shard_map/ppermute | solution.py:394
  42.9 1.6 %shard_map.124 = (f32[3,64,128]{2,1,0:T(8,128)S(1)}, f32[3,64,128]{2,1,0:T(8,128)S(1)}, f32[3,64,128]{2,1,0:T(8,128)S(1)}, f32[3,64,128]{2,1,0:T(8,128)S(1)}, f3...) custom-call(s32[1]{0:T(128)} %bitcast.me_ref, ...), custom_call_target="tpu_custom_call" | custom-call | flops 1000000000 | bytes 1000000 | tf_op jit(solution)/shard_map/pallas_call | solution.py:466
  44.5 0.3 collective-permute-start.7
  44.8 2.5 %collective-permute-start.8 = (f32[3,64,128]{2,1,0:T(8,128)S(1)}, f32[3,64,128]{2,1,0:T(8,128)S(1)}, u32[]{:S(2)}, u32[]{:S(2)}) collective-permute-start(f32[3,64,128]{2,1,0:T(8,128)S(1)} %get-tuple-element.59), channel_id=1, source_target_pairs={{0,6},{1,7},{2,4},{3,5},{4,2},{5,3},{6,0},{7,1},{8,14},{9,15},{10,... | collective-permute-start | bytes 294920 | tf_op jit(solution)/shard_map/ppermute | solution.py:394
  47.4 0.9 collective-permute-start.9
  48.2 0.0 collective-permute-start.10
  48.2 1.9 %collective-permute-start.11 = (f32[3,64,128]{2,1,0:T(8,128)S(1)}, f32[3,64,128]{2,1,0:T(8,128)S(1)}, u32[]{:S(2)}, u32[]{:S(2)}) collective-permute-start(f32[3,64,128]{2,1,0:T(8,128)S(1)} %get-tuple-element.62), channel_id=1, source_target_pairs={{0,3},{1,2},{2,1},{3,0},{4,7},{5,6},{6,5},{7,4},{8,11},{9,10},{10,... | collective-permute-start | bytes 294920 | tf_op jit(solution)/shard_map/ppermute | solution.py:394
  50.1 1.4 %collective-permute-start.12 = (f32[3,64,128]{2,1,0:T(8,128)S(1)}, f32[3,64,128]{2,1,0:T(8,128)S(1)}, u32[]{:S(2)}, u32[]{:S(2)}) collective-permute-start(f32[3,64,128]{2,1,0:T(8,128)S(1)} %get-tuple-element.63), channel_id=1, source_target_pairs={{0,4},{1,5},{2,6},{3,7},{4,0},{5,1},{6,2},{7,3},{8,12},{9,13},{10,... | collective-permute-start | bytes 294920 | tf_op jit(solution)/shard_map/ppermute | solution.py:394
  51.5 0.2 collective-permute-done.8.refs_2_
  51.7 0.9 %collective-permute-start.13 = (f32[3,64,128]{2,1,0:T(8,128)S(1)}, f32[3,64,128]{2,1,0:T(8,128)S(1)}, u32[]{:S(2)}, u32[]{:S(2)}) collective-permute-start(f32[3,64,128]{2,1,0:T(8,128)S(1)} %get-tuple-element.64), channel_id=1, source_target_pairs={{0,5},{1,4},{2,7},{3,6},{4,1},{5,0},{6,3},{7,2},{8,13},{9,12},{10,... | collective-permute-start | bytes 294920 | tf_op jit(solution)/shard_map/ppermute | solution.py:394
  52.6 1.7 %collective-permute-done.9.refs_3_ = f32[3,64,128]{2,1,0:T(8,128)S(1)} collective-permute-done((f32[3,64,128]{2,1,0:T(8,128)S(1)}, f32[3,64,128]{2,1,0:T(8,128)S(1)}, u32[]{:S(2)}, u32[]{:S(2)}) %collective-permute-start.9) | collective-permute-done | bytes 98336 | tf_op jit(solution)/shard_map/ppermute | solution.py:394
  54.3 4.6 %collective-permute-done.10.refs_4_ = f32[3,64,128]{2,1,0:T(8,128)S(1)} collective-permute-done((f32[3,64,128]{2,1,0:T(8,128)S(1)}, f32[3,64,128]{2,1,0:T(8,128)S(1)}, u32[]{:S(2)}, u32[]{:S(2)}) %collective-permute-start.10) | collective-permute-done | bytes 98336 | tf_op jit(solution)/shard_map/ppermute | solution.py:394
  58.9 1.9 %collective-permute-done.11.refs_5_ = f32[3,64,128]{2,1,0:T(8,128)S(1)} collective-permute-done((f32[3,64,128]{2,1,0:T(8,128)S(1)}, f32[3,64,128]{2,1,0:T(8,128)S(1)}, u32[]{:S(2)}, u32[]{:S(2)}) %collective-permute-start.11) | collective-permute-done | bytes 98336 | tf_op jit(solution)/shard_map/ppermute | solution.py:394
  60.8 1.2 %shard_map.125 = (f32[384,512]{1,0:T(8,128)S(1)}, bf16[128,512]{1,0:T(8,128)(2,1)S(1)}) custom-call(s32[8,512]{1,0:T(8,128)S(1)} %get-tuple-element.41.info_ref, f32[3,64,128]{2,1,0:T(8,128)S(1)} %get-tuple-element.57.refs_0_, f32[3,64,128]{2,1,0:T(8,128)S(1)} %collective-permute-done.7.refs_1_, f32[3,64,128]{2,1,0:T(8,128)S(1)} %collective-permute-done.8.refs_2_, ...), custom_call_target="tpu_custom_call" | custom-call | flops 10000000000 | bytes 10000000 | tf_op jit(solution)/shard_map/pallas_call | solution.py:477
  61.9 1.8 %collective-permute-done.13.refs_1_.refs_7_ = f32[3,64,128]{2,1,0:T(8,128)S(1)} collective-permute-done((f32[3,64,128]{2,1,0:T(8,128)S(1)}, f32[3,64,128]{2,1,0:T(8,128)S(1)}, u32[]{:S(2)}, u32[]{:S(2)}) %collective-permute-start.13) | collective-permute-done | bytes 98336 | tf_op jit(solution)/shard_map/ppermute | solution.py:394
  63.7 0.7 shard_map.126
  64.4 0.3 collective-permute-start.14
  64.8 1.0 %collective-permute-done.14.refs_8_.refs_1_ = f32[3,64,128]{2,1,0:T(8,128)S(1)} collective-permute-done((f32[3,64,128]{2,1,0:T(8,128)S(1)}, f32[3,64,128]{2,1,0:T(8,128)S(1)}, u32[]{:S(2)}, u32[]{:S(2)}) %collective-permute-start.14) | collective-permute-done | bytes 98336 | tf_op jit(solution)/shard_map/ppermute | solution.py:394
  65.8 1.8 %shard_map.127 = (f32[6,64,512]{2,1,0:T(8,128)}, f32[3,64]{1,0:T(4,128)S(1)}) custom-call(s32[8,512]{1,0:T(8,128)S(1)} %get-tuple-element.41.info_ref, s32[2,512]{1,0:T(2,128)S(1)} %copy-done.4, f32[6,64,512]{2,1,0:T(8,128)S(1)} %copy-done.3, f32[3,64,128]{2,1,0:T(8,128)S(1)} %get-tuple-element.57.refs_0_, f32[3,64,128]{2,1,0:T(8,128)S(1)} %collective-permute-done.7.refs_1_, ...), custom_call_target="tpu_custom_call" | custom-call | flops 10000000000 | bytes 10000000 | tf_op jit(solution)/shard_map/pallas_call | solution.py:493
  67.6 2.5 %collective-permute-start.23 = (f32[3,64]{1,0:T(4,128)S(1)}, f32[3,64]{1,0:T(4,128)S(1)}, u32[]{:S(2)}, u32[]{:S(2)}) collective-permute-start(f32[3,64]{1,0:T(4,128)S(1)} %get-tuple-element.78), channel_id=1, source_target_pairs={{0,24},{8,16},{16,8},{24,0},{1,25},{9,17},{17,9},{25,1},{2,26},{10... | collective-permute-start | bytes 2312 | tf_op jit(solution)/shard_map/ppermute | solution.py:402
  70.1 0.5 collective-permute-start.22
  70.6 0.6 collective-permute-start.21
  71.2 1.9 %collective-permute-start.17 = (f32[3,64,128]{2,1,0:T(8,128)S(1)}, f32[3,64,128]{2,1,0:T(8,128)S(1)}, u32[]{:S(2)}, u32[]{:S(2)}) collective-permute-start(f32[3,64,128]{2,1,0:T(8,128)S(1)} %get-tuple-element.73), channel_id=1, source_target_pairs={{0,6},{1,7},{2,4},{3,5},{4,2},{5,3},{6,0},{7,1},{8,14},{9,15},{10,... | collective-permute-start | bytes 294920 | tf_op jit(solution)/shard_map/ppermute | solution.py:394
  73.1 0.7 collective-permute-start.18
  73.8 1.3 %collective-permute-start.20 = (f32[3,64,128]{2,1,0:T(8,128)S(1)}, f32[3,64,128]{2,1,0:T(8,128)S(1)}, u32[]{:S(2)}, u32[]{:S(2)}) collective-permute-start(f32[3,64,128]{2,1,0:T(8,128)S(1)} %get-tuple-element.77), channel_id=1, source_target_pairs={{0,3},{1,2},{2,1},{3,0},{4,7},{5,6},{6,5},{7,4},{8,11},{9,10},{10,... | collective-permute-start | bytes 294920 | tf_op jit(solution)/shard_map/ppermute | solution.py:394
  75.1 1.7 %collective-permute-start.19 = (f32[3,64,128]{2,1,0:T(8,128)S(1)}, f32[3,64,128]{2,1,0:T(8,128)S(1)}, u32[]{:S(2)}, u32[]{:S(2)}) collective-permute-start(f32[3,64,128]{2,1,0:T(8,128)S(1)} %get-tuple-element.76), channel_id=1, source_target_pairs={{0,2},{1,3},{2,0},{3,1},{4,6},{5,7},{6,4},{7,5},{8,10},{9,11},{10,... | collective-permute-start | bytes 294920 | tf_op jit(solution)/shard_map/ppermute | solution.py:394
  76.8 0.6 add_add_fusion
  77.3 0.6 collective-permute-done.17.refs_2_
  78.0 6.5 %collective-permute-start.16 = (f32[3,64,128]{2,1,0:T(8,128)S(1)}, f32[3,64,128]{2,1,0:T(8,128)S(1)}, u32[]{:S(2)}, u32[]{:S(2)}) collective-permute-start(f32[3,64,128]{2,1,0:T(8,128)S(1)} %get-tuple-element.71), channel_id=1, source_target_pairs={{0,5},{1,4},{2,7},{3,6},{4,1},{5,0},{6,3},{7,2},{8,13},{9,12},{10,... | collective-permute-start | bytes 294920 | tf_op jit(solution)/shard_map/ppermute | solution.py:394
  84.5 1.2 %collective-permute-done.19.refs_4_ = f32[3,64,128]{2,1,0:T(8,128)S(1)} collective-permute-done((f32[3,64,128]{2,1,0:T(8,128)S(1)}, f32[3,64,128]{2,1,0:T(8,128)S(1)}, u32[]{:S(2)}, u32[]{:S(2)}) %collective-permute-start.19) | collective-permute-done | bytes 98336 | tf_op jit(solution)/shard_map/ppermute | solution.py:394
  85.7 1.2 %shard_map.128.refs_2_ = f32[6,512,128]{2,1,0:T(8,128)} custom-call(s32[1]{0:T(128)} %bitcast.me_ref, s32[8,512]{1,0:T(8,128)S(1)} %get-tuple-element.41.info_ref, f32[3,512,128]{2,1,0:T(8,128)S(1)} %get-tuple-element.69.solved_ref, f32[3,64,128]{2,1,0:T(8,128)S(1)} %get-tuple-element.72.refs_0_, f32[3,64,128]{2,1,0:T(8,128)S(1)} %collective-permute-done.14.refs_8_.refs_1_, ...), custom_call_target="tpu_custom_call" | custom-call | flops 10000000000 | bytes 10000000 | tf_op jit(solution)/shard_map/pallas_call | solution.py:503
  86.9 0.8 collective-permute-done.16.refs_1_
  87.7 0.9 shard_map.129
  (22 shorter events, 0.1 us)
Async XLA Ops:
  0.6 10.2 %copy-start = (f32[512,512]{1,0:T(8,128)S(1)}, f32[512,512]{1,0:T(8,128)}, u32[]{:S(2)}) copy-start(f32[512,512]{1,0:T(8,128)} %deriv_ref.1) | copy-start | bytes 3145732
  0.6 10.2 %copy-start.1 = (f32[512,512]{1,0:T(8,128)S(1)}, f32[512,512]{1,0:T(8,128)}, u32[]{:S(2)}) copy-start(f32[512,512]{1,0:T(8,128)} %inverse_ref.1) | copy-start | bytes 3145732
  0.7 10.2 %copy-start.2 = (f32[512,512]{1,0:T(8,128)S(1)}, f32[512,512]{1,0:T(8,128)}, u32[]{:S(2)}) copy-start(f32[512,512]{1,0:T(8,128)} %basis_ref.1) | copy-start | bytes 3145732
  0.7 10.2 %copy-start.5 = (f32[512]{0:T(512)S(1)}, f32[512]{0:T(512)}, u32[]{:S(2)}) copy-start(f32[512]{0:T(512)} %param.17) | copy-start | bytes 6148
  4.1 8.1 %collective-permute-start = (f32[2,3,64,128]{3,2,1,0:T(8,128)S(1)}, f32[2,3,64,128]{3,2,1,0:T(8,128)S(1)}, u32[]{:S(2)}, u32[]{:S(2)}) collective-permute-start(f32[2,3,64,128]{3,2,1,0:T(8,128)S(1)} %get-tuple-element.50), channel_id=1, source_target_pairs={{0,1},{1,0},{2,3},{3,2},{4,5},{5,4},{6,7},{7,6},{8,9},{9,8},{10,11... | collective-permute-start | bytes 589832 | tf_op jit(solution)/shard_map/ppermute | solution.py:394
  4.6 10.6 %collective-permute-start.1 = (f32[2,3,64,128]{3,2,1,0:T(8,128)S(1)}, f32[2,3,64,128]{3,2,1,0:T(8,128)S(1)}, u32[]{:S(2)}, u32[]{:S(2)}) collective-permute-start(f32[2,3,64,128]{3,2,1,0:T(8,128)S(1)} %get-tuple-element.51), channel_id=1, source_target_pairs={{0,6},{1,7},{2,4},{3,5},{4,2},{5,3},{6,0},{7,1},{8,14},{9,15},{10,... | collective-permute-start | bytes 589832 | tf_op jit(solution)/shard_map/ppermute | solution.py:394
  9.3 13.9 %collective-permute-start.2 = (f32[2,3,64,128]{3,2,1,0:T(8,128)S(1)}, f32[2,3,64,128]{3,2,1,0:T(8,128)S(1)}, u32[]{:S(2)}, u32[]{:S(2)}) collective-permute-start(f32[2,3,64,128]{3,2,1,0:T(8,128)S(1)} %get-tuple-element.52), channel_id=1, source_target_pairs={{0,7},{1,6},{2,5},{3,4},{4,3},{5,2},{6,1},{7,0},{8,15},{9,14},{10,... | collective-permute-start | bytes 589832 | tf_op jit(solution)/shard_map/ppermute | solution.py:394
  9.3 14.0 %collective-permute-start.3 = (f32[2,3,64,128]{3,2,1,0:T(8,128)S(1)}, f32[2,3,64,128]{3,2,1,0:T(8,128)S(1)}, u32[]{:S(2)}, u32[]{:S(2)}) collective-permute-start(f32[2,3,64,128]{3,2,1,0:T(8,128)S(1)} %get-tuple-element.53), channel_id=1, source_target_pairs={{0,2},{1,3},{2,0},{3,1},{4,6},{5,7},{6,4},{7,5},{8,10},{9,11},{10,... | collective-permute-start | bytes 589832 | tf_op jit(solution)/shard_map/ppermute | solution.py:394
  9.3 19.1 %collective-permute-start.4 = (f32[2,3,64,128]{3,2,1,0:T(8,128)S(1)}, f32[2,3,64,128]{3,2,1,0:T(8,128)S(1)}, u32[]{:S(2)}, u32[]{:S(2)}) collective-permute-start(f32[2,3,64,128]{3,2,1,0:T(8,128)S(1)} %get-tuple-element.54), channel_id=1, source_target_pairs={{0,3},{1,2},{2,1},{3,0},{4,7},{5,6},{6,5},{7,4},{8,11},{9,10},{10,... | collective-permute-start | bytes 589832 | tf_op jit(solution)/shard_map/ppermute | solution.py:394
  12.2 27.4 %collective-permute-start.5 = (f32[2,3,64,128]{3,2,1,0:T(8,128)S(1)}, f32[2,3,64,128]{3,2,1,0:T(8,128)S(1)}, u32[]{:S(2)}, u32[]{:S(2)}) collective-permute-start(f32[2,3,64,128]{3,2,1,0:T(8,128)S(1)} %get-tuple-element.55), channel_id=1, source_target_pairs={{0,4},{1,5},{2,6},{3,7},{4,0},{5,1},{6,2},{7,3},{8,12},{9,13},{10,... | collective-permute-start | bytes 589832 | tf_op jit(solution)/shard_map/ppermute | solution.py:394
  15.2 27.7 %collective-permute-start.6 = (f32[2,3,64,128]{3,2,1,0:T(8,128)S(1)}, f32[2,3,64,128]{3,2,1,0:T(8,128)S(1)}, u32[]{:S(2)}, u32[]{:S(2)}) collective-permute-start(f32[2,3,64,128]{3,2,1,0:T(8,128)S(1)} %get-tuple-element.56), channel_id=1, source_target_pairs={{0,5},{1,4},{2,7},{3,6},{4,1},{5,0},{6,3},{7,2},{8,13},{9,12},{10,... | collective-permute-start | bytes 589832 | tf_op jit(solution)/shard_map/ppermute | solution.py:394
  44.5 5.6 %collective-permute-start.7 = (f32[3,64,128]{2,1,0:T(8,128)S(1)}, f32[3,64,128]{2,1,0:T(8,128)S(1)}, u32[]{:S(2)}, u32[]{:S(2)}) collective-permute-start(f32[3,64,128]{2,1,0:T(8,128)S(1)} %get-tuple-element.58), channel_id=1, source_target_pairs={{0,1},{1,0},{2,3},{3,2},{4,5},{5,4},{6,7},{7,6},{8,9},{9,8},{10,11... | collective-permute-start | bytes 294920 | tf_op jit(solution)/shard_map/ppermute | solution.py:394
  44.8 6.9 %collective-permute-start.8 = (f32[3,64,128]{2,1,0:T(8,128)S(1)}, f32[3,64,128]{2,1,0:T(8,128)S(1)}, u32[]{:S(2)}, u32[]{:S(2)}) collective-permute-start(f32[3,64,128]{2,1,0:T(8,128)S(1)} %get-tuple-element.59), channel_id=1, source_target_pairs={{0,6},{1,7},{2,4},{3,5},{4,2},{5,3},{6,0},{7,1},{8,14},{9,15},{10,... | collective-permute-start | bytes 294920 | tf_op jit(solution)/shard_map/ppermute | solution.py:394
  47.4 6.9 %collective-permute-start.9 = (f32[3,64,128]{2,1,0:T(8,128)S(1)}, f32[3,64,128]{2,1,0:T(8,128)S(1)}, u32[]{:S(2)}, u32[]{:S(2)}) collective-permute-start(f32[3,64,128]{2,1,0:T(8,128)S(1)} %get-tuple-element.60), channel_id=1, source_target_pairs={{0,7},{1,6},{2,5},{3,4},{4,3},{5,2},{6,1},{7,0},{8,15},{9,14},{10,... | collective-permute-start | bytes 294920 | tf_op jit(solution)/shard_map/ppermute | solution.py:394
  48.2 10.6 %collective-permute-start.10 = (f32[3,64,128]{2,1,0:T(8,128)S(1)}, f32[3,64,128]{2,1,0:T(8,128)S(1)}, u32[]{:S(2)}, u32[]{:S(2)}) collective-permute-start(f32[3,64,128]{2,1,0:T(8,128)S(1)} %get-tuple-element.61), channel_id=1, source_target_pairs={{0,2},{1,3},{2,0},{3,1},{4,6},{5,7},{6,4},{7,5},{8,10},{9,11},{10,... | collective-permute-start | bytes 294920 | tf_op jit(solution)/shard_map/ppermute | solution.py:394
  48.2 12.5 %collective-permute-start.11 = (f32[3,64,128]{2,1,0:T(8,128)S(1)}, f32[3,64,128]{2,1,0:T(8,128)S(1)}, u32[]{:S(2)}, u32[]{:S(2)}) collective-permute-start(f32[3,64,128]{2,1,0:T(8,128)S(1)} %get-tuple-element.62), channel_id=1, source_target_pairs={{0,3},{1,2},{2,1},{3,0},{4,7},{5,6},{6,5},{7,4},{8,11},{9,10},{10,... | collective-permute-start | bytes 294920 | tf_op jit(solution)/shard_map/ppermute | solution.py:394
  50.1 11.8 %collective-permute-start.12 = (f32[3,64,128]{2,1,0:T(8,128)S(1)}, f32[3,64,128]{2,1,0:T(8,128)S(1)}, u32[]{:S(2)}, u32[]{:S(2)}) collective-permute-start(f32[3,64,128]{2,1,0:T(8,128)S(1)} %get-tuple-element.63), channel_id=1, source_target_pairs={{0,4},{1,5},{2,6},{3,7},{4,0},{5,1},{6,2},{7,3},{8,12},{9,13},{10,... | collective-permute-start | bytes 294920 | tf_op jit(solution)/shard_map/ppermute | solution.py:394
  51.7 12.0 %collective-permute-start.13 = (f32[3,64,128]{2,1,0:T(8,128)S(1)}, f32[3,64,128]{2,1,0:T(8,128)S(1)}, u32[]{:S(2)}, u32[]{:S(2)}) collective-permute-start(f32[3,64,128]{2,1,0:T(8,128)S(1)} %get-tuple-element.64), channel_id=1, source_target_pairs={{0,5},{1,4},{2,7},{3,6},{4,1},{5,0},{6,3},{7,2},{8,13},{9,12},{10,... | collective-permute-start | bytes 294920 | tf_op jit(solution)/shard_map/ppermute | solution.py:394
  63.7 2.1 %copy-start.3 = (f32[6,64,512]{2,1,0:T(8,128)S(1)}, f32[6,64,512]{2,1,0:T(8,128)}, u32[]{:S(2)}) copy-start(f32[6,64,512]{2,1,0:T(8,128)} %velocity_ref.1) | copy-start | bytes 2359300
  63.7 2.1 %copy-start.4 = (s32[2,512]{1,0:T(2,128)S(1)}, s32[2,512]{1,0:T(2,128)}, u32[]{:S(2)}) copy-start(s32[2,512]{1,0:T(2,128)} %modes_ref.1) | copy-start | bytes 12292
  64.4 1.4 %collective-permute-start.14 = (f32[3,64,128]{2,1,0:T(8,128)S(1)}, f32[3,64,128]{2,1,0:T(8,128)S(1)}, u32[]{:S(2)}, u32[]{:S(2)}) collective-permute-start(f32[3,64,128]{2,1,0:T(8,128)S(1)} %get-tuple-element.67), channel_id=1, source_target_pairs={{0,1},{1,0},{2,3},{3,2},{4,5},{5,4},{6,7},{7,6},{8,9},{9,8},{10,11... | collective-permute-start | bytes 294920 | tf_op jit(solution)/shard_map/ppermute | solution.py:394
  67.6 5.5 %collective-permute-start.23 = (f32[3,64]{1,0:T(4,128)S(1)}, f32[3,64]{1,0:T(4,128)S(1)}, u32[]{:S(2)}, u32[]{:S(2)}) collective-permute-start(f32[3,64]{1,0:T(4,128)S(1)} %get-tuple-element.78), channel_id=1, source_target_pairs={{0,24},{8,16},{16,8},{24,0},{1,25},{9,17},{17,9},{25,1},{2,26},{10... | collective-permute-start | bytes 2312 | tf_op jit(solution)/shard_map/ppermute | solution.py:402
  70.1 3.6 %collective-permute-start.22 = (f32[3,64]{1,0:T(4,128)S(1)}, f32[3,64]{1,0:T(4,128)S(1)}, u32[]{:S(2)}, u32[]{:S(2)}) collective-permute-start(f32[3,64]{1,0:T(4,128)S(1)} %get-tuple-element.78), channel_id=1, source_target_pairs={{0,16},{8,24},{16,0},{24,8},{1,17},{9,25},{17,1},{25,9},{2,18},{10... | collective-permute-start | bytes 2312 | tf_op jit(solution)/shard_map/ppermute | solution.py:402
  70.6 4.4 %collective-permute-start.21 = (f32[3,64]{1,0:T(4,128)S(1)}, f32[3,64]{1,0:T(4,128)S(1)}, u32[]{:S(2)}, u32[]{:S(2)}) collective-permute-start(f32[3,64]{1,0:T(4,128)S(1)} %get-tuple-element.78), channel_id=1, source_target_pairs={{0,8},{8,0},{16,24},{24,16},{1,9},{9,1},{17,25},{25,17},{2,10},{10... | collective-permute-start | bytes 2312 | tf_op jit(solution)/shard_map/ppermute | solution.py:402
  71.2 15.8 %collective-permute-start.15 = (f32[3,64,128]{2,1,0:T(8,128)S(1)}, f32[3,64,128]{2,1,0:T(8,128)S(1)}, u32[]{:S(2)}, u32[]{:S(2)}) collective-permute-start(f32[3,64,128]{2,1,0:T(8,128)S(1)} %get-tuple-element.70), channel_id=1, source_target_pairs={{0,4},{1,5},{2,6},{3,7},{4,0},{5,1},{6,2},{7,3},{8,12},{9,13},{10,... | collective-permute-start | bytes 294920 | tf_op jit(solution)/shard_map/ppermute | solution.py:394
  71.2 6.8 %collective-permute-start.17 = (f32[3,64,128]{2,1,0:T(8,128)S(1)}, f32[3,64,128]{2,1,0:T(8,128)S(1)}, u32[]{:S(2)}, u32[]{:S(2)}) collective-permute-start(f32[3,64,128]{2,1,0:T(8,128)S(1)} %get-tuple-element.73), channel_id=1, source_target_pairs={{0,6},{1,7},{2,4},{3,5},{4,2},{5,3},{6,0},{7,1},{8,14},{9,15},{10,... | collective-permute-start | bytes 294920 | tf_op jit(solution)/shard_map/ppermute | solution.py:394
  73.1 11.4 %collective-permute-start.18 = (f32[3,64,128]{2,1,0:T(8,128)S(1)}, f32[3,64,128]{2,1,0:T(8,128)S(1)}, u32[]{:S(2)}, u32[]{:S(2)}) collective-permute-start(f32[3,64,128]{2,1,0:T(8,128)S(1)} %get-tuple-element.74), channel_id=1, source_target_pairs={{0,7},{1,6},{2,5},{3,4},{4,3},{5,2},{6,1},{7,0},{8,15},{9,14},{10,... | collective-permute-start | bytes 294920 | tf_op jit(solution)/shard_map/ppermute | solution.py:394
  73.8 10.7 %collective-permute-start.20 = (f32[3,64,128]{2,1,0:T(8,128)S(1)}, f32[3,64,128]{2,1,0:T(8,128)S(1)}, u32[]{:S(2)}, u32[]{:S(2)}) collective-permute-start(f32[3,64,128]{2,1,0:T(8,128)S(1)} %get-tuple-element.77), channel_id=1, source_target_pairs={{0,3},{1,2},{2,1},{3,0},{4,7},{5,6},{6,5},{7,4},{8,11},{9,10},{10,... | collective-permute-start | bytes 294920 | tf_op jit(solution)/shard_map/ppermute | solution.py:394
  75.1 10.6 %collective-permute-start.19 = (f32[3,64,128]{2,1,0:T(8,128)S(1)}, f32[3,64,128]{2,1,0:T(8,128)S(1)}, u32[]{:S(2)}, u32[]{:S(2)}) collective-permute-start(f32[3,64,128]{2,1,0:T(8,128)S(1)} %get-tuple-element.76), channel_id=1, source_target_pairs={{0,2},{1,3},{2,0},{3,1},{4,6},{5,7},{6,4},{7,5},{8,10},{9,11},{10,... | collective-permute-start | bytes 294920 | tf_op jit(solution)/shard_map/ppermute | solution.py:394
  78.0 9.7 %collective-permute-start.16 = (f32[3,64,128]{2,1,0:T(8,128)S(1)}, f32[3,64,128]{2,1,0:T(8,128)S(1)}, u32[]{:S(2)}, u32[]{:S(2)}) collective-permute-start(f32[3,64,128]{2,1,0:T(8,128)S(1)} %get-tuple-element.71), channel_id=1, source_target_pairs={{0,5},{1,4},{2,7},{3,6},{4,1},{5,0},{6,3},{7,2},{8,13},{9,12},{10,... | collective-permute-start | bytes 294920 | tf_op jit(solution)/shard_map/ppermute | solution.py:394

commit v16 on v14

--- a/solution.py
+++ b/solution.py
@@ -130,7 +130,9 @@
     local = state + TIME_STEP * (forcing - RK_ALPHA * (wave * state))
     rows = comps * points
     both = jnp.concatenate([state.reshape(rows, columns), local.reshape(rows, columns)], axis=0)
-    placed = sum_parts(lax.dot_general(three_parts(both), chosen, NT, preferred_element_type=F32))
+    high, low = two_parts(both)
+    placed = lax.dot_general(jnp.concatenate([high, low], axis=0), chosen, NT, preferred_element_type=F32)
+    placed = placed[: 2 * rows] + placed[2 * rows :]
     for step, out in zip(steps_of(devices, points), out_refs):
         taken = placed[:, step * share : (step + 1) * share]
         for kind in range(2):

time: 87.6 us -> 87.2 us (level)
  no operation moved by 1% of the time
where the time goes in v16:
time: 87.2 us; the launch traced here: 87 us
  starting transfers between devices  41.4 us (47%)
  waiting for transfers between devices  30.7 us (35%)
  Pallas kernels  14.1 us (16%)
    ppermute x21, starting transfers between devices, exchange(): lax.ppermute(block, 'col', [(i, i ^ step) for i in range(devices)])  37.9 us
    ppermute x21, waiting for transfers between devices, exchange(): lax.ppermute(block, 'col', [(i, i ^ step) for i in range(devices)])  29 us
    ppermute x3, starting transfers between devices, from_groups(): lax.ppermute(value, 'grp', [(i, i ^ step) for i in range(groups)])  3.49 us
    pallas_call x1, Pallas kernels, on_device(): call(functools.partial(first_kernel, devices), [shaped((8, columns), jnp....  3.37 us
    pallas_call x1, Pallas kernels, on_device(): call(functools.partial(state_kernel, steps), [shaped(state_now.shape), sh...  1.83 us
    ppermute x3, waiting for transfers between devices, from_groups(): lax.ppermute(value, 'grp', [(i, i ^ step) for i in range(groups)])  1.78 us
  transfers between devices with their start and end apart: 24, of which 13 were waited for; matrix products, arithmetic and copies ran while one was open for 0% of the time, Pallas kernels for 8%

profile of v16, /device:TPU:0, one launch (start us, length us, event | category | flops | bytes accessed | tf_op | source)
XLA Modules:
  0.0 87.0 jit_solution(4242568258509957749)
XLA Ops:
  0.7 3.4 %shard_map.121 = (s32[8,512]{1,0:T(8,128)S(1)}, f32[8,128]{1,0:T(8,128)S(1)}, f32[2,3,64,128]{3,2,1,0:T(8,128)S(1)}, f32[2,3,64,128]{3,2,1,0:T(8,128)S(1)}, f32[...) custom-call(s32[1]{0:T(128)} %bitcast.me_ref, ...), custom_call_target="tpu_custom_call" | custom-call | flops 1000000000 | bytes 1000000 | tf_op jit(solution)/shard_map/pallas_call | solution.py:440
  4.1 0.5 collective-permute-start
  4.6 4.7 %collective-permute-start.1 = (f32[2,3,64,128]{3,2,1,0:T(8,128)S(1)}, f32[2,3,64,128]{3,2,1,0:T(8,128)S(1)}, u32[]{:S(2)}, u32[]{:S(2)}) collective-permute-start(f32[2,3,64,128]{3,2,1,0:T(8,128)S(1)} %get-tuple-element.53), channel_id=1, source_target_pairs={{0,6},{1,7},{2,4},{3,5},{4,2},{5,3},{6,0},{7,1},{8,14},{9,15},{10,... | collective-permute-start | bytes 589832 | tf_op jit(solution)/shard_map/ppermute | solution.py:399
  9.3 0.1 collective-permute-start.2
  9.3 0.0 collective-permute-start.3
  9.3 1.5 %collective-permute-start.4 = (f32[2,3,64,128]{3,2,1,0:T(8,128)S(1)}, f32[2,3,64,128]{3,2,1,0:T(8,128)S(1)}, u32[]{:S(2)}, u32[]{:S(2)}) collective-permute-start(f32[2,3,64,128]{3,2,1,0:T(8,128)S(1)} %get-tuple-element.56), channel_id=1, source_target_pairs={{0,3},{1,2},{2,1},{3,0},{4,7},{5,6},{6,5},{7,4},{8,11},{9,10},{10,... | collective-permute-start | bytes 589832 | tf_op jit(solution)/shard_map/ppermute | solution.py:399
  10.8 1.4 %shard_map.122 = (bf16[512,512]{1,0:T(8,128)(2,1)S(1)}, bf16[512,512]{1,0:T(8,128)(2,1)S(1)}, bf16[512,512]{1,0:T(8,128)(2,1)S(1)}, bf16[512,512]{1,0:T(8,128)(2...) custom-call(f32[512,512]{1,0:T(8,128)S(1)} %copy-done, f32[512,512]{1,0:T(8,128)S(1)} %copy-done.1, ...), custom_call_target="tpu_custom_call" | custom-call | flops 10000000000 | bytes 10000000 | tf_op jit(solution)/shard_map/pallas_call | solution.py:454
  12.2 2.7 %collective-permute-start.5 = (f32[2,3,64,128]{3,2,1,0:T(8,128)S(1)}, f32[2,3,64,128]{3,2,1,0:T(8,128)S(1)}, u32[]{:S(2)}, u32[]{:S(2)}) collective-permute-start(f32[2,3,64,128]{3,2,1,0:T(8,128)S(1)} %get-tuple-element.57), channel_id=1, source_target_pairs={{0,4},{1,5},{2,6},{3,7},{4,0},{5,1},{6,2},{7,3},{8,12},{9,13},{10,... | collective-permute-start | bytes 589832 | tf_op jit(solution)/shard_map/ppermute | solution.py:399
  14.9 0.3 collective-permute-done.1.refs_6_
  15.2 8.0 %collective-permute-start.6 = (f32[2,3,64,128]{3,2,1,0:T(8,128)S(1)}, f32[2,3,64,128]{3,2,1,0:T(8,128)S(1)}, u32[]{:S(2)}, u32[]{:S(2)}) collective-permute-start(f32[2,3,64,128]{3,2,1,0:T(8,128)S(1)} %get-tuple-element.58), channel_id=1, source_target_pairs={{0,5},{1,4},{2,7},{3,6},{4,1},{5,0},{6,3},{7,2},{8,13},{9,12},{10,... | collective-permute-start | bytes 589832 | tf_op jit(solution)/shard_map/ppermute | solution.py:399
  23.2 0.0 collective-permute-done.2.refs_7_
  23.2 0.2 collective-permute-done.3.refs_8_
  23.4 5.1 %collective-permute-done.4.refs_9_ = f32[2,3,64,128]{3,2,1,0:T(8,128)S(1)} collective-permute-done((f32[2,3,64,128]{3,2,1,0:T(8,128)S(1)}, f32[2,3,64,128]{3,2,1,0:T(8,128)S(1)}, u32[]{:S(2)}, u32[]{:S(2)}) %collective-permute-start.4) | collective-permute-done | bytes 196640 | tf_op jit(solution)/shard_map/ppermute | solution.py:399
  28.4 1.4 %shard_map.123.early_ref = f32[512,384]{1,0:T(8,128)S(1)} custom-call(s32[1]{0:T(128)} %bitcast.me_ref, bf16[512,512]{1,0:T(8,128)(2,1)S(1)} %get-tuple-element.47.refs_0_, bf16[512,512]{1,0:T(8,128)(2,1)S(1)} %get-tuple-element.48.refs_1_, bf16[512,512]{1,0:T(8,128)(2,1)S(1)} %get-tuple-element.49.refs_2_, bf16[512,512]{1,0:T(8,128)(2,1)S(1)} %get-tuple-element.50.refs_3_, ...), custom_call_target="tpu_custom_call" | custom-call | flops 10000000000 | bytes 10000000 | tf_op jit(solution)/shard_map/pallas_call | solution.py:463
  29.9 9.8 %collective-permute-done.5.refs_4_ = f32[2,3,64,128]{3,2,1,0:T(8,128)S(1)} collective-permute-done((f32[2,3,64,128]{3,2,1,0:T(8,128)S(1)}, f32[2,3,64,128]{3,2,1,0:T(8,128)S(1)}, u32[]{:S(2)}, u32[]{:S(2)}) %collective-permute-start.5) | collective-permute-done | bytes 196640 | tf_op jit(solution)/shard_map/ppermute | solution.py:399
  39.6 3.3 %collective-permute-done.6.refs_5_ = f32[2,3,64,128]{3,2,1,0:T(8,128)S(1)} collective-permute-done((f32[2,3,64,128]{3,2,1,0:T(8,128)S(1)}, f32[2,3,64,128]{3,2,1,0:T(8,128)S(1)}, u32[]{:S(2)}, u32[]{:S(2)}) %collective-permute-start.6) | collective-permute-done | bytes 196640 | tf_op jit(solution)/shard_map/ppermute | solution.py:399
  42.9 1.6 %shard_map.124 = (f32[3,64,128]{2,1,0:T(8,128)S(1)}, f32[3,64,128]{2,1,0:T(8,128)S(1)}, f32[3,64,128]{2,1,0:T(8,128)S(1)}, f32[3,64,128]{2,1,0:T(8,128)S(1)}, f3...) custom-call(s32[1]{0:T(128)} %bitcast.me_ref, ...), custom_call_target="tpu_custom_call" | custom-call | flops 1000000000 | bytes 1000000 | tf_op jit(solution)/shard_map/pallas_call | solution.py:471
  44.5 0.3 collective-permute-start.7
  44.8 2.5 %collective-permute-start.8 = (f32[3,64,128]{2,1,0:T(8,128)S(1)}, f32[3,64,128]{2,1,0:T(8,128)S(1)}, u32[]{:S(2)}, u32[]{:S(2)}) collective-permute-start(f32[3,64,128]{2,1,0:T(8,128)S(1)} %get-tuple-element.61), channel_id=1, source_target_pairs={{0,6},{1,7},{2,4},{3,5},{4,2},{5,3},{6,0},{7,1},{8,14},{9,15},{10,... | collective-permute-start | bytes 294920 | tf_op jit(solution)/shard_map/ppermute | solution.py:399
  47.4 0.9 collective-permute-start.9
  48.2 0.0 collective-permute-start.10
  48.2 1.9 %collective-permute-start.11 = (f32[3,64,128]{2,1,0:T(8,128)S(1)}, f32[3,64,128]{2,1,0:T(8,128)S(1)}, u32[]{:S(2)}, u32[]{:S(2)}) collective-permute-start(f32[3,64,128]{2,1,0:T(8,128)S(1)} %get-tuple-element.64), channel_id=1, source_target_pairs={{0,3},{1,2},{2,1},{3,0},{4,7},{5,6},{6,5},{7,4},{8,11},{9,10},{10,... | collective-permute-start | bytes 294920 | tf_op jit(solution)/shard_map/ppermute | solution.py:399
  50.1 1.4 %collective-permute-start.12 = (f32[3,64,128]{2,1,0:T(8,128)S(1)}, f32[3,64,128]{2,1,0:T(8,128)S(1)}, u32[]{:S(2)}, u32[]{:S(2)}) collective-permute-start(f32[3,64,128]{2,1,0:T(8,128)S(1)} %get-tuple-element.65), channel_id=1, source_target_pairs={{0,4},{1,5},{2,6},{3,7},{4,0},{5,1},{6,2},{7,3},{8,12},{9,13},{10,... | collective-permute-start | bytes 294920 | tf_op jit(solution)/shard_map/ppermute | solution.py:399
  51.5 0.2 collective-permute-done.8.refs_2_
  51.7 0.9 %collective-permute-start.13 = (f32[3,64,128]{2,1,0:T(8,128)S(1)}, f32[3,64,128]{2,1,0:T(8,128)S(1)}, u32[]{:S(2)}, u32[]{:S(2)}) collective-permute-start(f32[3,64,128]{2,1,0:T(8,128)S(1)} %get-tuple-element.66), channel_id=1, source_target_pairs={{0,5},{1,4},{2,7},{3,6},{4,1},{5,0},{6,3},{7,2},{8,13},{9,12},{10,... | collective-permute-start | bytes 294920 | tf_op jit(solution)/shard_map/ppermute | solution.py:399
  52.6 1.7 %collective-permute-done.9.refs_3_ = f32[3,64,128]{2,1,0:T(8,128)S(1)} collective-permute-done((f32[3,64,128]{2,1,0:T(8,128)S(1)}, f32[3,64,128]{2,1,0:T(8,128)S(1)}, u32[]{:S(2)}, u32[]{:S(2)}) %collective-permute-start.9) | collective-permute-done | bytes 98336 | tf_op jit(solution)/shard_map/ppermute | solution.py:399
  54.3 4.6 %collective-permute-done.10.refs_4_ = f32[3,64,128]{2,1,0:T(8,128)S(1)} collective-permute-done((f32[3,64,128]{2,1,0:T(8,128)S(1)}, f32[3,64,128]{2,1,0:T(8,128)S(1)}, u32[]{:S(2)}, u32[]{:S(2)}) %collective-permute-start.10) | collective-permute-done | bytes 98336 | tf_op jit(solution)/shard_map/ppermute | solution.py:399
  58.9 1.9 %collective-permute-done.11.refs_5_ = f32[3,64,128]{2,1,0:T(8,128)S(1)} collective-permute-done((f32[3,64,128]{2,1,0:T(8,128)S(1)}, f32[3,64,128]{2,1,0:T(8,128)S(1)}, u32[]{:S(2)}, u32[]{:S(2)}) %collective-permute-start.11) | collective-permute-done | bytes 98336 | tf_op jit(solution)/shard_map/ppermute | solution.py:399
  60.8 1.2 %shard_map.125 = (f32[384,512]{1,0:T(8,128)S(1)}, bf16[128,512]{1,0:T(8,128)(2,1)S(1)}) custom-call(s32[8,512]{1,0:T(8,128)S(1)} %get-tuple-element.43.info_ref, f32[3,64,128]{2,1,0:T(8,128)S(1)} %get-tuple-element.59.refs_0_, f32[3,64,128]{2,1,0:T(8,128)S(1)} %collective-permute-done.7.refs_1_, f32[3,64,128]{2,1,0:T(8,128)S(1)} %collective-permute-done.8.refs_2_, ...), custom_call_target="tpu_custom_call" | custom-call | flops 10000000000 | bytes 10000000 | tf_op jit(solution)/shard_map/pallas_call | solution.py:482
  61.9 0.0 collective-permute-done.12.refs_0_.refs_6_
  61.9 1.8 %collective-permute-done.13.refs_1_.refs_7_ = f32[3,64,128]{2,1,0:T(8,128)S(1)} collective-permute-done((f32[3,64,128]{2,1,0:T(8,128)S(1)}, f32[3,64,128]{2,1,0:T(8,128)S(1)}, u32[]{:S(2)}, u32[]{:S(2)}) %collective-permute-start.13) | collective-permute-done | bytes 98336 | tf_op jit(solution)/shard_map/ppermute | solution.py:399
  63.7 0.7 shard_map.126
  64.4 0.3 collective-permute-start.14
  64.8 0.0 collective-permute-start.15
  64.8 1.7 %collective-permute-start.20 = (f32[3,64,128]{2,1,0:T(8,128)S(1)}, f32[3,64,128]{2,1,0:T(8,128)S(1)}, u32[]{:S(2)}, u32[]{:S(2)}) collective-permute-start(f32[3,64,128]{2,1,0:T(8,128)S(1)} %get-tuple-element.76), channel_id=1, source_target_pairs={{0,6},{1,7},{2,4},{3,5},{4,2},{5,3},{6,0},{7,1},{8,14},{9,15},{10,... | collective-permute-start | bytes 294920 | tf_op jit(solution)/shard_map/ppermute | solution.py:399
  66.5 1.7 %collective-permute-start.21 = (f32[3,64,128]{2,1,0:T(8,128)S(1)}, f32[3,64,128]{2,1,0:T(8,128)S(1)}, u32[]{:S(2)}, u32[]{:S(2)}) collective-permute-start(f32[3,64,128]{2,1,0:T(8,128)S(1)} %get-tuple-element.77), channel_id=1, source_target_pairs={{0,7},{1,6},{2,5},{3,4},{4,3},{5,2},{6,1},{7,0},{8,15},{9,14},{10,... | collective-permute-start | bytes 294920 | tf_op jit(solution)/shard_map/ppermute | solution.py:399
  68.1 0.3 collective-permute-start.23
  68.5 1.9 %collective-permute-start.22 = (f32[3,64,128]{2,1,0:T(8,128)S(1)}, f32[3,64,128]{2,1,0:T(8,128)S(1)}, u32[]{:S(2)}, u32[]{:S(2)}) collective-permute-start(f32[3,64,128]{2,1,0:T(8,128)S(1)} %get-tuple-element.79), channel_id=1, source_target_pairs={{0,2},{1,3},{2,0},{3,1},{4,6},{5,7},{6,4},{7,5},{8,10},{9,11},{10,... | collective-permute-start | bytes 294920 | tf_op jit(solution)/shard_map/ppermute | solution.py:399
  70.3 1.8 %shard_map.127 = (f32[6,64,512]{2,1,0:T(8,128)}, f32[3,64]{1,0:T(4,128)S(1)}) custom-call(s32[8,512]{1,0:T(8,128)S(1)} %get-tuple-element.43.info_ref, s32[2,512]{1,0:T(2,128)S(1)} %copy-done.4, f32[6,64,512]{2,1,0:T(8,128)S(1)} %copy-done.3, f32[3,64,128]{2,1,0:T(8,128)S(1)} %get-tuple-element.59.refs_0_, f32[3,64,128]{2,1,0:T(8,128)S(1)} %collective-permute-done.7.refs_1_, ...), custom_call_target="tpu_custom_call" | custom-call | flops 10000000000 | bytes 10000000 | tf_op jit(solution)/shard_map/pallas_call | solution.py:498
  72.2 0.2 collective-permute-done.20.refs_2_
  72.3 6.7 %collective-permute-start.16 = (f32[3,64,128]{2,1,0:T(8,128)S(1)}, f32[3,64,128]{2,1,0:T(8,128)S(1)}, u32[]{:S(2)}, u32[]{:S(2)}) collective-permute-start(f32[3,64,128]{2,1,0:T(8,128)S(1)} %get-tuple-element.73), channel_id=1, source_target_pairs={{0,5},{1,4},{2,7},{3,6},{4,1},{5,0},{6,3},{7,2},{8,13},{9,12},{10,... | collective-permute-start | bytes 294920 | tf_op jit(solution)/shard_map/ppermute | solution.py:399
  79.0 2.4 %collective-permute-start.19 = (f32[3,64]{1,0:T(4,128)S(1)}, f32[3,64]{1,0:T(4,128)S(1)}, u32[]{:S(2)}, u32[]{:S(2)}) collective-permute-start(f32[3,64]{1,0:T(4,128)S(1)} %get-tuple-element.74.refs_2_), channel_id=1, source_target_pairs={{0,24},{8,16},{16,8},{24,0},{1,25},{9,17},{17,9},{25,1},{2,26},{10... | collective-permute-start | bytes 2312 | tf_op jit(solution)/shard_map/ppermute | solution.py:407
  81.5 0.5 collective-permute-start.18
  82.0 0.5 collective-permute-start.17
  82.5 1.2 %shard_map.128.refs_6_ = f32[6,512,128]{2,1,0:T(8,128)} custom-call(s32[1]{0:T(128)} %bitcast.me_ref, s32[8,512]{1,0:T(8,128)S(1)} %get-tuple-element.43.info_ref, f32[3,512,128]{2,1,0:T(8,128)S(1)} %get-tuple-element.71.solved_ref, f32[3,64,128]{2,1,0:T(8,128)S(1)} %get-tuple-element.75.refs_0_, f32[3,64,128]{2,1,0:T(8,128)S(1)} %collective-permute-done.14.refs_8_.refs_1_, ...), custom_call_target="tpu_custom_call" | custom-call | flops 10000000000 | bytes 10000000 | tf_op jit(solution)/shard_map/pallas_call | solution.py:508
  83.8 1.3 %collective-permute-done.18.refs_4_ = f32[3,64]{1,0:T(4,128)S(1)} collective-permute-done((f32[3,64]{1,0:T(4,128)S(1)}, f32[3,64]{1,0:T(4,128)S(1)}, u32[]{:S(2)}, u32[]{:S(2)}) %collective-permute-start.18) | collective-permute-done | bytes 800 | tf_op jit(solution)/shard_map/ppermute | solution.py:407
  85.1 0.5 collective-permute-done.17.refs_3_
  85.6 1.4 %shard_map.129 = (f32[6,512,128]{2,1,0:T(8,128)}, f32[3,64]{1,0:T(4,128)}) custom-call(s32[1]{0:T(128)} %bitcast.me_ref, s32[8,512]{1,0:T(8,128)S(1)} %get-tuple-element.43.info_ref, f32[3,512,128]{2,1,0:T(8,128)S(1)} %get-tuple-element.71.solved_ref, f32[3,64,128]{2,1,0:T(8,128)S(1)} %collective-permute-done.15.refs_0_, ...), custom_call_target="tpu_custom_call", output_to_operand_aliasing={{0}: (9, {})} | custom-call | flops 1000000000 | bytes 1000000 | tf_op jit(solution)/shard_map/pallas_call | solution.py:519
  (21 shorter events, 0.0 us)
Async XLA Ops:
  0.6 10.2 %copy-start = (f32[512,512]{1,0:T(8,128)S(1)}, f32[512,512]{1,0:T(8,128)}, u32[]{:S(2)}) copy-start(f32[512,512]{1,0:T(8,128)} %deriv_ref.1) | copy-start | bytes 3145732
  0.6 10.2 %copy-start.1 = (f32[512,512]{1,0:T(8,128)S(1)}, f32[512,512]{1,0:T(8,128)}, u32[]{:S(2)}) copy-start(f32[512,512]{1,0:T(8,128)} %inverse_ref.1) | copy-start | bytes 3145732
  0.7 10.2 %copy-start.2 = (f32[512,512]{1,0:T(8,128)S(1)}, f32[512,512]{1,0:T(8,128)}, u32[]{:S(2)}) copy-start(f32[512,512]{1,0:T(8,128)} %basis_ref.1) | copy-start | bytes 3145732
  0.7 10.2 %copy-start.5 = (f32[512]{0:T(512)S(1)}, f32[512]{0:T(512)}, u32[]{:S(2)}) copy-start(f32[512]{0:T(512)} %param.17) | copy-start | bytes 6148
  4.1 8.1 %collective-permute-start = (f32[2,3,64,128]{3,2,1,0:T(8,128)S(1)}, f32[2,3,64,128]{3,2,1,0:T(8,128)S(1)}, u32[]{:S(2)}, u32[]{:S(2)}) collective-permute-start(f32[2,3,64,128]{3,2,1,0:T(8,128)S(1)} %get-tuple-element.52), channel_id=1, source_target_pairs={{0,1},{1,0},{2,3},{3,2},{4,5},{5,4},{6,7},{7,6},{8,9},{9,8},{10,11... | collective-permute-start | bytes 589832 | tf_op jit(solution)/shard_map/ppermute | solution.py:399
  4.6 10.6 %collective-permute-start.1 = (f32[2,3,64,128]{3,2,1,0:T(8,128)S(1)}, f32[2,3,64,128]{3,2,1,0:T(8,128)S(1)}, u32[]{:S(2)}, u32[]{:S(2)}) collective-permute-start(f32[2,3,64,128]{3,2,1,0:T(8,128)S(1)} %get-tuple-element.53), channel_id=1, source_target_pairs={{0,6},{1,7},{2,4},{3,5},{4,2},{5,3},{6,0},{7,1},{8,14},{9,15},{10,... | collective-permute-start | bytes 589832 | tf_op jit(solution)/shard_map/ppermute | solution.py:399
  9.3 13.9 %collective-permute-start.2 = (f32[2,3,64,128]{3,2,1,0:T(8,128)S(1)}, f32[2,3,64,128]{3,2,1,0:T(8,128)S(1)}, u32[]{:S(2)}, u32[]{:S(2)}) collective-permute-start(f32[2,3,64,128]{3,2,1,0:T(8,128)S(1)} %get-tuple-element.54), channel_id=1, source_target_pairs={{0,7},{1,6},{2,5},{3,4},{4,3},{5,2},{6,1},{7,0},{8,15},{9,14},{10,... | collective-permute-start | bytes 589832 | tf_op jit(solution)/shard_map/ppermute | solution.py:399
  9.3 14.0 %collective-permute-start.3 = (f32[2,3,64,128]{3,2,1,0:T(8,128)S(1)}, f32[2,3,64,128]{3,2,1,0:T(8,128)S(1)}, u32[]{:S(2)}, u32[]{:S(2)}) collective-permute-start(f32[2,3,64,128]{3,2,1,0:T(8,128)S(1)} %get-tuple-element.55), channel_id=1, source_target_pairs={{0,2},{1,3},{2,0},{3,1},{4,6},{5,7},{6,4},{7,5},{8,10},{9,11},{10,... | collective-permute-start | bytes 589832 | tf_op jit(solution)/shard_map/ppermute | solution.py:399
  9.3 19.1 %collective-permute-start.4 = (f32[2,3,64,128]{3,2,1,0:T(8,128)S(1)}, f32[2,3,64,128]{3,2,1,0:T(8,128)S(1)}, u32[]{:S(2)}, u32[]{:S(2)}) collective-permute-start(f32[2,3,64,128]{3,2,1,0:T(8,128)S(1)} %get-tuple-element.56), channel_id=1, source_target_pairs={{0,3},{1,2},{2,1},{3,0},{4,7},{5,6},{6,5},{7,4},{8,11},{9,10},{10,... | collective-permute-start | bytes 589832 | tf_op jit(solution)/shard_map/ppermute | solution.py:399
  12.2 27.4 %collective-permute-start.5 = (f32[2,3,64,128]{3,2,1,0:T(8,128)S(1)}, f32[2,3,64,128]{3,2,1,0:T(8,128)S(1)}, u32[]{:S(2)}, u32[]{:S(2)}) collective-permute-start(f32[2,3,64,128]{3,2,1,0:T(8,128)S(1)} %get-tuple-element.57), channel_id=1, source_target_pairs={{0,4},{1,5},{2,6},{3,7},{4,0},{5,1},{6,2},{7,3},{8,12},{9,13},{10,... | collective-permute-start | bytes 589832 | tf_op jit(solution)/shard_map/ppermute | solution.py:399
  15.2 27.7 %collective-permute-start.6 = (f32[2,3,64,128]{3,2,1,0:T(8,128)S(1)}, f32[2,3,64,128]{3,2,1,0:T(8,128)S(1)}, u32[]{:S(2)}, u32[]{:S(2)}) collective-permute-start(f32[2,3,64,128]{3,2,1,0:T(8,128)S(1)} %get-tuple-element.58), channel_id=1, source_target_pairs={{0,5},{1,4},{2,7},{3,6},{4,1},{5,0},{6,3},{7,2},{8,13},{9,12},{10,... | collective-permute-start | bytes 589832 | tf_op jit(solution)/shard_map/ppermute | solution.py:399
  44.5 5.6 %collective-permute-start.7 = (f32[3,64,128]{2,1,0:T(8,128)S(1)}, f32[3,64,128]{2,1,0:T(8,128)S(1)}, u32[]{:S(2)}, u32[]{:S(2)}) collective-permute-start(f32[3,64,128]{2,1,0:T(8,128)S(1)} %get-tuple-element.60), channel_id=1, source_target_pairs={{0,1},{1,0},{2,3},{3,2},{4,5},{5,4},{6,7},{7,6},{8,9},{9,8},{10,11... | collective-permute-start | bytes 294920 | tf_op jit(solution)/shard_map/ppermute | solution.py:399
  44.8 6.9 %collective-permute-start.8 = (f32[3,64,128]{2,1,0:T(8,128)S(1)}, f32[3,64,128]{2,1,0:T(8,128)S(1)}, u32[]{:S(2)}, u32[]{:S(2)}) collective-permute-start(f32[3,64,128]{2,1,0:T(8,128)S(1)} %get-tuple-element.61), channel_id=1, source_target_pairs={{0,6},{1,7},{2,4},{3,5},{4,2},{5,3},{6,0},{7,1},{8,14},{9,15},{10,... | collective-permute-start | bytes 294920 | tf_op jit(solution)/shard_map/ppermute | solution.py:399
  47.4 6.9 %collective-permute-start.9 = (f32[3,64,128]{2,1,0:T(8,128)S(1)}, f32[3,64,128]{2,1,0:T(8,128)S(1)}, u32[]{:S(2)}, u32[]{:S(2)}) collective-permute-start(f32[3,64,128]{2,1,0:T(8,128)S(1)} %get-tuple-element.62), channel_id=1, source_target_pairs={{0,7},{1,6},{2,5},{3,4},{4,3},{5,2},{6,1},{7,0},{8,15},{9,14},{10,... | collective-permute-start | bytes 294920 | tf_op jit(solution)/shard_map/ppermute | solution.py:399
  48.2 10.6 %collective-permute-start.10 = (f32[3,64,128]{2,1,0:T(8,128)S(1)}, f32[3,64,128]{2,1,0:T(8,128)S(1)}, u32[]{:S(2)}, u32[]{:S(2)}) collective-permute-start(f32[3,64,128]{2,1,0:T(8,128)S(1)} %get-tuple-element.63), channel_id=1, source_target_pairs={{0,2},{1,3},{2,0},{3,1},{4,6},{5,7},{6,4},{7,5},{8,10},{9,11},{10,... | collective-permute-start | bytes 294920 | tf_op jit(solution)/shard_map/ppermute | solution.py:399
  48.2 12.5 %collective-permute-start.11 = (f32[3,64,128]{2,1,0:T(8,128)S(1)}, f32[3,64,128]{2,1,0:T(8,128)S(1)}, u32[]{:S(2)}, u32[]{:S(2)}) collective-permute-start(f32[3,64,128]{2,1,0:T(8,128)S(1)} %get-tuple-element.64), channel_id=1, source_target_pairs={{0,3},{1,2},{2,1},{3,0},{4,7},{5,6},{6,5},{7,4},{8,11},{9,10},{10,... | collective-permute-start | bytes 294920 | tf_op jit(solution)/shard_map/ppermute | solution.py:399
  50.1 11.8 %collective-permute-start.12 = (f32[3,64,128]{2,1,0:T(8,128)S(1)}, f32[3,64,128]{2,1,0:T(8,128)S(1)}, u32[]{:S(2)}, u32[]{:S(2)}) collective-permute-start(f32[3,64,128]{2,1,0:T(8,128)S(1)} %get-tuple-element.65), channel_id=1, source_target_pairs={{0,4},{1,5},{2,6},{3,7},{4,0},{5,1},{6,2},{7,3},{8,12},{9,13},{10,... | collective-permute-start | bytes 294920 | tf_op jit(solution)/shard_map/ppermute | solution.py:399
  51.7 12.0 %collective-permute-start.13 = (f32[3,64,128]{2,1,0:T(8,128)S(1)}, f32[3,64,128]{2,1,0:T(8,128)S(1)}, u32[]{:S(2)}, u32[]{:S(2)}) collective-permute-start(f32[3,64,128]{2,1,0:T(8,128)S(1)} %get-tuple-element.66), channel_id=1, source_target_pairs={{0,5},{1,4},{2,7},{3,6},{4,1},{5,0},{6,3},{7,2},{8,13},{9,12},{10,... | collective-permute-start | bytes 294920 | tf_op jit(solution)/shard_map/ppermute | solution.py:399
  63.7 6.6 %copy-start.3 = (f32[6,64,512]{2,1,0:T(8,128)S(1)}, f32[6,64,512]{2,1,0:T(8,128)}, u32[]{:S(2)}) copy-start(f32[6,64,512]{2,1,0:T(8,128)} %velocity_ref.1) | copy-start | bytes 2359300
  63.7 6.6 %copy-start.4 = (s32[2,512]{1,0:T(2,128)S(1)}, s32[2,512]{1,0:T(2,128)}, u32[]{:S(2)}) copy-start(s32[2,512]{1,0:T(2,128)} %modes_ref.1) | copy-start | bytes 12292
  64.4 4.1 %collective-permute-start.14 = (f32[3,64,128]{2,1,0:T(8,128)S(1)}, f32[3,64,128]{2,1,0:T(8,128)S(1)}, u32[]{:S(2)}, u32[]{:S(2)}) collective-permute-start(f32[3,64,128]{2,1,0:T(8,128)S(1)} %get-tuple-element.69), channel_id=1, source_target_pairs={{0,1},{1,0},{2,3},{3,2},{4,5},{5,4},{6,7},{7,6},{8,9},{9,8},{10,11... | collective-permute-start | bytes 294920 | tf_op jit(solution)/shard_map/ppermute | solution.py:399
  64.8 19.0 %collective-permute-start.15 = (f32[3,64,128]{2,1,0:T(8,128)S(1)}, f32[3,64,128]{2,1,0:T(8,128)S(1)}, u32[]{:S(2)}, u32[]{:S(2)}) collective-permute-start(f32[3,64,128]{2,1,0:T(8,128)S(1)} %get-tuple-element.72), channel_id=1, source_target_pairs={{0,4},{1,5},{2,6},{3,7},{4,0},{5,1},{6,2},{7,3},{8,12},{9,13},{10,... | collective-permute-start | bytes 294920 | tf_op jit(solution)/shard_map/ppermute | solution.py:399
  64.8 7.6 %collective-permute-start.20 = (f32[3,64,128]{2,1,0:T(8,128)S(1)}, f32[3,64,128]{2,1,0:T(8,128)S(1)}, u32[]{:S(2)}, u32[]{:S(2)}) collective-permute-start(f32[3,64,128]{2,1,0:T(8,128)S(1)} %get-tuple-element.76), channel_id=1, source_target_pairs={{0,6},{1,7},{2,4},{3,5},{4,2},{5,3},{6,0},{7,1},{8,14},{9,15},{10,... | collective-permute-start | bytes 294920 | tf_op jit(solution)/shard_map/ppermute | solution.py:399
  66.5 12.6 %collective-permute-start.21 = (f32[3,64,128]{2,1,0:T(8,128)S(1)}, f32[3,64,128]{2,1,0:T(8,128)S(1)}, u32[]{:S(2)}, u32[]{:S(2)}) collective-permute-start(f32[3,64,128]{2,1,0:T(8,128)S(1)} %get-tuple-element.77), channel_id=1, source_target_pairs={{0,7},{1,6},{2,5},{3,4},{4,3},{5,2},{6,1},{7,0},{8,15},{9,14},{10,... | collective-permute-start | bytes 294920 | tf_op jit(solution)/shard_map/ppermute | solution.py:399
  68.1 13.3 %collective-permute-start.23 = (f32[3,64,128]{2,1,0:T(8,128)S(1)}, f32[3,64,128]{2,1,0:T(8,128)S(1)}, u32[]{:S(2)}, u32[]{:S(2)}) collective-permute-start(f32[3,64,128]{2,1,0:T(8,128)S(1)} %get-tuple-element.80), channel_id=1, source_target_pairs={{0,3},{1,2},{2,1},{3,0},{4,7},{5,6},{6,5},{7,4},{8,11},{9,10},{10,... | collective-permute-start | bytes 294920 | tf_op jit(solution)/shard_map/ppermute | solution.py:399
  68.5 13.5 %collective-permute-start.22 = (f32[3,64,128]{2,1,0:T(8,128)S(1)}, f32[3,64,128]{2,1,0:T(8,128)S(1)}, u32[]{:S(2)}, u32[]{:S(2)}) collective-permute-start(f32[3,64,128]{2,1,0:T(8,128)S(1)} %get-tuple-element.79), channel_id=1, source_target_pairs={{0,2},{1,3},{2,0},{3,1},{4,6},{5,7},{6,4},{7,5},{8,10},{9,11},{10,... | collective-permute-start | bytes 294920 | tf_op jit(solution)/shard_map/ppermute | solution.py:399
  72.3 11.4 %collective-permute-start.16 = (f32[3,64,128]{2,1,0:T(8,128)S(1)}, f32[3,64,128]{2,1,0:T(8,128)S(1)}, u32[]{:S(2)}, u32[]{:S(2)}) collective-permute-start(f32[3,64,128]{2,1,0:T(8,128)S(1)} %get-tuple-element.73), channel_id=1, source_target_pairs={{0,5},{1,4},{2,7},{3,6},{4,1},{5,0},{6,3},{7,2},{8,13},{9,12},{10,... | collective-permute-start | bytes 294920 | tf_op jit(solution)/shard_map/ppermute | solution.py:399
  79.0 4.8 %collective-permute-start.19 = (f32[3,64]{1,0:T(4,128)S(1)}, f32[3,64]{1,0:T(4,128)S(1)}, u32[]{:S(2)}, u32[]{:S(2)}) collective-permute-start(f32[3,64]{1,0:T(4,128)S(1)} %get-tuple-element.74.refs_2_), channel_id=1, source_target_pairs={{0,24},{8,16},{16,8},{24,0},{1,25},{9,17},{17,9},{25,1},{2,26},{10... | collective-permute-start | bytes 2312 | tf_op jit(solution)/shard_map/ppermute | solution.py:407
  81.5 3.6 %collective-permute-start.18 = (f32[3,64]{1,0:T(4,128)S(1)}, f32[3,64]{1,0:T(4,128)S(1)}, u32[]{:S(2)}, u32[]{:S(2)}) collective-permute-start(f32[3,64]{1,0:T(4,128)S(1)} %get-tuple-element.74.refs_2_), channel_id=1, source_target_pairs={{0,16},{8,24},{16,0},{24,8},{1,17},{9,25},{17,1},{25,9},{2,18},{10... | collective-permute-start | bytes 2312 | tf_op jit(solution)/shard_map/ppermute | solution.py:407
  82.0 3.6 %collective-permute-start.17 = (f32[3,64]{1,0:T(4,128)S(1)}, f32[3,64]{1,0:T(4,128)S(1)}, u32[]{:S(2)}, u32[]{:S(2)}) collective-permute-start(f32[3,64]{1,0:T(4,128)S(1)} %get-tuple-element.74.refs_2_), channel_id=1, source_target_pairs={{0,8},{8,0},{16,24},{24,16},{1,9},{9,1},{17,25},{25,17},{2,10},{10... | collective-permute-start | bytes 2312 | tf_op jit(solution)/shard_map/ppermute | solution.py:407

commit v17 on v16

--- a/solution.py
+++ b/solution.py
@@ -254,6 +254,11 @@
     return jnp.concatenate(rows, axis=0)
 
 
+def sum_halves(x):
+    rows = x.shape[0] // 2
+    return x[:rows] + x[rows:]
+
+
 def surplus_early_kernel(steps, info_ref, *refs):
     in_refs, (out_ref, late_ref) = refs[:-2], refs[-2:]
     columns = info_ref.shape[1]
@@ -266,8 +271,8 @@
     first, last = late[0] * share, (late[-1] + 1) * share
     late_ref[...] = chosen[first:last]
     kept = jnp.concatenate([chosen[:first], chosen[last:]], axis=0)
-    out_ref[...] = sum_parts(
-        jnp.dot(three_parts(side_by_side(steps, in_refs)), kept, preferred_element_type=F32)
+    out_ref[...] = sum_halves(
+        jnp.dot(jnp.concatenate(two_parts(side_by_side(steps, in_refs)), axis=0), kept, preferred_element_type=F32)
     )
 
 
@@ -275,8 +280,8 @@
     in_refs, out_refs = refs[: len(steps)], refs[len(steps) :]
     pairs, points, lanes = in_refs[0].shape
     share = lanes // 2
-    extra = early_ref[...] + sum_parts(
-        jnp.dot(three_parts(side_by_side(steps, in_refs)), chosen_ref[...], preferred_element_type=F32)
+    extra = early_ref[...] + sum_halves(
+        jnp.dot(jnp.concatenate(two_parts(side_by_side(steps, in_refs)), axis=0), chosen_ref[...], preferred_element_type=F32)
     )
     for step, out in zip(order, out_refs):
         taken = extra[:, step * share : (step + 1) * share]

time: 87.2 us -> 87 us (level)
  no operation moved by 1% of the time
where the time goes in v17:
time: 87 us; the launch traced here: 86.9 us
  starting transfers between devices  41.4 us (48%)
  waiting for transfers between devices  30.9 us (36%)
  Pallas kernels  13.8 us (16%)
    ppermute x21, starting transfers between devices, exchange(): lax.ppermute(block, 'col', [(i, i ^ step) for i in range(devices)])  37.9 us
    ppermute x21, waiting for transfers between devices, exchange(): lax.ppermute(block, 'col', [(i, i ^ step) for i in range(devices)])  29.2 us
    ppermute x3, starting transfers between devices, from_groups(): lax.ppermute(value, 'grp', [(i, i ^ step) for i in range(groups)])  3.49 us
    pallas_call x1, Pallas kernels, on_device(): call(functools.partial(first_kernel, devices), [shaped((8, columns), jnp....  3.37 us
    pallas_call x1, Pallas kernels, on_device(): call(functools.partial(state_kernel, steps), [shaped(state_now.shape), sh...  1.83 us
    ppermute x3, waiting for transfers between devices, from_groups(): lax.ppermute(value, 'grp', [(i, i ^ step) for i in range(groups)])  1.76 us
  transfers between devices with their start and end apart: 24, of which 13 were waited for; matrix products, arithmetic and copies ran while one was open for 0% of the time, Pallas kernels for 8%

profile of v17, /device:TPU:0, one launch (start us, length us, event | category | flops | bytes accessed | tf_op | source)
XLA Modules:
  0.0 86.9 jit_solution(9287462617646975386)
XLA Ops:
  0.7 3.4 %shard_map.121 = (s32[8,512]{1,0:T(8,128)S(1)}, f32[8,128]{1,0:T(8,128)S(1)}, f32[2,3,64,128]{3,2,1,0:T(8,128)S(1)}, f32[2,3,64,128]{3,2,1,0:T(8,128)S(1)}, f32[...) custom-call(s32[1]{0:T(128)} %bitcast.me_ref, ...), custom_call_target="tpu_custom_call" | custom-call | flops 1000000000 | bytes 1000000 | tf_op jit(solution)/shard_map/pallas_call | solution.py:445
  4.1 0.5 collective-permute-start
  4.6 4.7 %collective-permute-start.1 = (f32[2,3,64,128]{3,2,1,0:T(8,128)S(1)}, f32[2,3,64,128]{3,2,1,0:T(8,128)S(1)}, u32[]{:S(2)}, u32[]{:S(2)}) collective-permute-start(f32[2,3,64,128]{3,2,1,0:T(8,128)S(1)} %get-tuple-element.53), channel_id=1, source_target_pairs={{0,6},{1,7},{2,4},{3,5},{4,2},{5,3},{6,0},{7,1},{8,14},{9,15},{10,... | collective-permute-start | bytes 589832 | tf_op jit(solution)/shard_map/ppermute | solution.py:404
  9.3 0.1 collective-permute-start.2
  9.3 0.0 collective-permute-start.3
  9.3 1.5 %collective-permute-start.4 = (f32[2,3,64,128]{3,2,1,0:T(8,128)S(1)}, f32[2,3,64,128]{3,2,1,0:T(8,128)S(1)}, u32[]{:S(2)}, u32[]{:S(2)}) collective-permute-start(f32[2,3,64,128]{3,2,1,0:T(8,128)S(1)} %get-tuple-element.56), channel_id=1, source_target_pairs={{0,3},{1,2},{2,1},{3,0},{4,7},{5,6},{6,5},{7,4},{8,11},{9,10},{10,... | collective-permute-start | bytes 589832 | tf_op jit(solution)/shard_map/ppermute | solution.py:404
  10.8 1.4 %shard_map.122 = (bf16[512,512]{1,0:T(8,128)(2,1)S(1)}, bf16[512,512]{1,0:T(8,128)(2,1)S(1)}, bf16[512,512]{1,0:T(8,128)(2,1)S(1)}, bf16[512,512]{1,0:T(8,128)(2...) custom-call(f32[512,512]{1,0:T(8,128)S(1)} %copy-done, f32[512,512]{1,0:T(8,128)S(1)} %copy-done.1, ...), custom_call_target="tpu_custom_call" | custom-call | flops 10000000000 | bytes 10000000 | tf_op jit(solution)/shard_map/pallas_call | solution.py:459
  12.2 0.0 collective-permute-done.refs_5_
  12.2 2.7 %collective-permute-start.5 = (f32[2,3,64,128]{3,2,1,0:T(8,128)S(1)}, f32[2,3,64,128]{3,2,1,0:T(8,128)S(1)}, u32[]{:S(2)}, u32[]{:S(2)}) collective-permute-start(f32[2,3,64,128]{3,2,1,0:T(8,128)S(1)} %get-tuple-element.57), channel_id=1, source_target_pairs={{0,4},{1,5},{2,6},{3,7},{4,0},{5,1},{6,2},{7,3},{8,12},{9,13},{10,... | collective-permute-start | bytes 589832 | tf_op jit(solution)/shard_map/ppermute | solution.py:404
  14.9 0.3 collective-permute-done.1.refs_6_
  15.2 8.0 %collective-permute-start.6 = (f32[2,3,64,128]{3,2,1,0:T(8,128)S(1)}, f32[2,3,64,128]{3,2,1,0:T(8,128)S(1)}, u32[]{:S(2)}, u32[]{:S(2)}) collective-permute-start(f32[2,3,64,128]{3,2,1,0:T(8,128)S(1)} %get-tuple-element.58), channel_id=1, source_target_pairs={{0,5},{1,4},{2,7},{3,6},{4,1},{5,0},{6,3},{7,2},{8,13},{9,12},{10,... | collective-permute-start | bytes 589832 | tf_op jit(solution)/shard_map/ppermute | solution.py:404
  23.2 0.0 collective-permute-done.2.refs_7_
  23.2 0.2 collective-permute-done.3.refs_8_
  23.4 5.1 %collective-permute-done.4.refs_9_ = f32[2,3,64,128]{3,2,1,0:T(8,128)S(1)} collective-permute-done((f32[2,3,64,128]{3,2,1,0:T(8,128)S(1)}, f32[2,3,64,128]{3,2,1,0:T(8,128)S(1)}, u32[]{:S(2)}, u32[]{:S(2)}) %collective-permute-start.4) | collective-permute-done | bytes 196640 | tf_op jit(solution)/shard_map/ppermute | solution.py:404
  28.4 1.4 %shard_map.123.early_ref = f32[512,384]{1,0:T(8,128)S(1)} custom-call(s32[1]{0:T(128)} %bitcast.me_ref, bf16[512,512]{1,0:T(8,128)(2,1)S(1)} %get-tuple-element.47.refs_0_, bf16[512,512]{1,0:T(8,128)(2,1)S(1)} %get-tuple-element.48.refs_1_, bf16[512,512]{1,0:T(8,128)(2,1)S(1)} %get-tuple-element.49.refs_2_, bf16[512,512]{1,0:T(8,128)(2,1)S(1)} %get-tuple-element.50.refs_3_, ...), custom_call_target="tpu_custom_call" | custom-call | flops 10000000000 | bytes 10000000 | tf_op jit(solution)/shard_map/pallas_call | solution.py:468
  29.9 9.8 %collective-permute-done.5.refs_4_ = f32[2,3,64,128]{3,2,1,0:T(8,128)S(1)} collective-permute-done((f32[2,3,64,128]{3,2,1,0:T(8,128)S(1)}, f32[2,3,64,128]{3,2,1,0:T(8,128)S(1)}, u32[]{:S(2)}, u32[]{:S(2)}) %collective-permute-start.5) | collective-permute-done | bytes 196640 | tf_op jit(solution)/shard_map/ppermute | solution.py:404
  39.6 3.3 %collective-permute-done.6.refs_5_ = f32[2,3,64,128]{3,2,1,0:T(8,128)S(1)} collective-permute-done((f32[2,3,64,128]{3,2,1,0:T(8,128)S(1)}, f32[2,3,64,128]{3,2,1,0:T(8,128)S(1)}, u32[]{:S(2)}, u32[]{:S(2)}) %collective-permute-start.6) | collective-permute-done | bytes 196640 | tf_op jit(solution)/shard_map/ppermute | solution.py:404
  42.9 1.6 %shard_map.124 = (f32[3,64,128]{2,1,0:T(8,128)S(1)}, f32[3,64,128]{2,1,0:T(8,128)S(1)}, f32[3,64,128]{2,1,0:T(8,128)S(1)}, f32[3,64,128]{2,1,0:T(8,128)S(1)}, f3...) custom-call(s32[1]{0:T(128)} %bitcast.me_ref, ...), custom_call_target="tpu_custom_call" | custom-call | flops 1000000000 | bytes 1000000 | tf_op jit(solution)/shard_map/pallas_call | solution.py:476
  44.5 0.3 collective-permute-start.7
  44.8 2.5 %collective-permute-start.8 = (f32[3,64,128]{2,1,0:T(8,128)S(1)}, f32[3,64,128]{2,1,0:T(8,128)S(1)}, u32[]{:S(2)}, u32[]{:S(2)}) collective-permute-start(f32[3,64,128]{2,1,0:T(8,128)S(1)} %get-tuple-element.61), channel_id=1, source_target_pairs={{0,6},{1,7},{2,4},{3,5},{4,2},{5,3},{6,0},{7,1},{8,14},{9,15},{10,... | collective-permute-start | bytes 294920 | tf_op jit(solution)/shard_map/ppermute | solution.py:404
  47.4 0.9 collective-permute-start.9
  48.2 1.9 %collective-permute-start.11 = (f32[3,64,128]{2,1,0:T(8,128)S(1)}, f32[3,64,128]{2,1,0:T(8,128)S(1)}, u32[]{:S(2)}, u32[]{:S(2)}) collective-permute-start(f32[3,64,128]{2,1,0:T(8,128)S(1)} %get-tuple-element.64), channel_id=1, source_target_pairs={{0,3},{1,2},{2,1},{3,0},{4,7},{5,6},{6,5},{7,4},{8,11},{9,10},{10,... | collective-permute-start | bytes 294920 | tf_op jit(solution)/shard_map/ppermute | solution.py:404
  50.1 0.0 collective-permute-done.7.refs_1_
  50.1 1.4 %collective-permute-start.12 = (f32[3,64,128]{2,1,0:T(8,128)S(1)}, f32[3,64,128]{2,1,0:T(8,128)S(1)}, u32[]{:S(2)}, u32[]{:S(2)}) collective-permute-start(f32[3,64,128]{2,1,0:T(8,128)S(1)} %get-tuple-element.65), channel_id=1, source_target_pairs={{0,4},{1,5},{2,6},{3,7},{4,0},{5,1},{6,2},{7,3},{8,12},{9,13},{10,... | collective-permute-start | bytes 294920 | tf_op jit(solution)/shard_map/ppermute | solution.py:404
  51.5 0.2 collective-permute-done.8.refs_2_
  51.7 0.9 %collective-permute-start.13 = (f32[3,64,128]{2,1,0:T(8,128)S(1)}, f32[3,64,128]{2,1,0:T(8,128)S(1)}, u32[]{:S(2)}, u32[]{:S(2)}) collective-permute-start(f32[3,64,128]{2,1,0:T(8,128)S(1)} %get-tuple-element.66), channel_id=1, source_target_pairs={{0,5},{1,4},{2,7},{3,6},{4,1},{5,0},{6,3},{7,2},{8,13},{9,12},{10,... | collective-permute-start | bytes 294920 | tf_op jit(solution)/shard_map/ppermute | solution.py:404
  52.6 1.7 %collective-permute-done.9.refs_3_ = f32[3,64,128]{2,1,0:T(8,128)S(1)} collective-permute-done((f32[3,64,128]{2,1,0:T(8,128)S(1)}, f32[3,64,128]{2,1,0:T(8,128)S(1)}, u32[]{:S(2)}, u32[]{:S(2)}) %collective-permute-start.9) | collective-permute-done | bytes 98336 | tf_op jit(solution)/shard_map/ppermute | solution.py:404
  54.3 4.6 %collective-permute-done.10.refs_4_ = f32[3,64,128]{2,1,0:T(8,128)S(1)} collective-permute-done((f32[3,64,128]{2,1,0:T(8,128)S(1)}, f32[3,64,128]{2,1,0:T(8,128)S(1)}, u32[]{:S(2)}, u32[]{:S(2)}) %collective-permute-start.10) | collective-permute-done | bytes 98336 | tf_op jit(solution)/shard_map/ppermute | solution.py:404
  58.9 1.9 %collective-permute-done.11.refs_5_ = f32[3,64,128]{2,1,0:T(8,128)S(1)} collective-permute-done((f32[3,64,128]{2,1,0:T(8,128)S(1)}, f32[3,64,128]{2,1,0:T(8,128)S(1)}, u32[]{:S(2)}, u32[]{:S(2)}) %collective-permute-start.11) | collective-permute-done | bytes 98336 | tf_op jit(solution)/shard_map/ppermute | solution.py:404
  60.8 1.0 %shard_map.125 = (f32[384,512]{1,0:T(8,128)S(1)}, bf16[128,512]{1,0:T(8,128)(2,1)S(1)}) custom-call(s32[8,512]{1,0:T(8,128)S(1)} %get-tuple-element.43.info_ref, f32[3,64,128]{2,1,0:T(8,128)S(1)} %get-tuple-element.59.refs_0_, f32[3,64,128]{2,1,0:T(8,128)S(1)} %collective-permute-done.7.refs_1_, f32[3,64,128]{2,1,0:T(8,128)S(1)} %collective-permute-done.8.refs_2_, ...), custom_call_target="tpu_custom_call" | custom-call | flops 10000000000 | bytes 10000000 | tf_op jit(solution)/shard_map/pallas_call | solution.py:487
  61.7 0.0 collective-permute-done.12.refs_0_.refs_6_
  61.7 2.0 %collective-permute-done.13.refs_1_.refs_7_ = f32[3,64,128]{2,1,0:T(8,128)S(1)} collective-permute-done((f32[3,64,128]{2,1,0:T(8,128)S(1)}, f32[3,64,128]{2,1,0:T(8,128)S(1)}, u32[]{:S(2)}, u32[]{:S(2)}) %collective-permute-start.13) | collective-permute-done | bytes 98336 | tf_op jit(solution)/shard_map/ppermute | solution.py:404
  63.7 0.6 shard_map.126
  64.3 0.3 collective-permute-start.14
  64.7 1.7 %collective-permute-start.20 = (f32[3,64,128]{2,1,0:T(8,128)S(1)}, f32[3,64,128]{2,1,0:T(8,128)S(1)}, u32[]{:S(2)}, u32[]{:S(2)}) collective-permute-start(f32[3,64,128]{2,1,0:T(8,128)S(1)} %get-tuple-element.76), channel_id=1, source_target_pairs={{0,6},{1,7},{2,4},{3,5},{4,2},{5,3},{6,0},{7,1},{8,14},{9,15},{10,... | collective-permute-start | bytes 294920 | tf_op jit(solution)/shard_map/ppermute | solution.py:404
  66.4 1.7 %collective-permute-start.21 = (f32[3,64,128]{2,1,0:T(8,128)S(1)}, f32[3,64,128]{2,1,0:T(8,128)S(1)}, u32[]{:S(2)}, u32[]{:S(2)}) collective-permute-start(f32[3,64,128]{2,1,0:T(8,128)S(1)} %get-tuple-element.77), channel_id=1, source_target_pairs={{0,7},{1,6},{2,5},{3,4},{4,3},{5,2},{6,1},{7,0},{8,15},{9,14},{10,... | collective-permute-start | bytes 294920 | tf_op jit(solution)/shard_map/ppermute | solution.py:404
  68.0 0.3 collective-permute-start.23
  68.4 1.9 %collective-permute-start.22 = (f32[3,64,128]{2,1,0:T(8,128)S(1)}, f32[3,64,128]{2,1,0:T(8,128)S(1)}, u32[]{:S(2)}, u32[]{:S(2)}) collective-permute-start(f32[3,64,128]{2,1,0:T(8,128)S(1)} %get-tuple-element.79), channel_id=1, source_target_pairs={{0,2},{1,3},{2,0},{3,1},{4,6},{5,7},{6,4},{7,5},{8,10},{9,11},{10,... | collective-permute-start | bytes 294920 | tf_op jit(solution)/shard_map/ppermute | solution.py:404
  70.2 1.8 %shard_map.127 = (f32[6,64,512]{2,1,0:T(8,128)}, f32[3,64]{1,0:T(4,128)S(1)}) custom-call(s32[8,512]{1,0:T(8,128)S(1)} %get-tuple-element.43.info_ref, s32[2,512]{1,0:T(2,128)S(1)} %copy-done.4, f32[6,64,512]{2,1,0:T(8,128)S(1)} %copy-done.3, f32[3,64,128]{2,1,0:T(8,128)S(1)} %get-tuple-element.59.refs_0_, f32[3,64,128]{2,1,0:T(8,128)S(1)} %collective-permute-done.7.refs_1_, ...), custom_call_target="tpu_custom_call" | custom-call | flops 10000000000 | bytes 10000000 | tf_op jit(solution)/shard_map/pallas_call | solution.py:503
  72.1 0.2 collective-permute-done.20.refs_2_
  72.2 6.7 %collective-permute-start.16 = (f32[3,64,128]{2,1,0:T(8,128)S(1)}, f32[3,64,128]{2,1,0:T(8,128)S(1)}, u32[]{:S(2)}, u32[]{:S(2)}) collective-permute-start(f32[3,64,128]{2,1,0:T(8,128)S(1)} %get-tuple-element.73), channel_id=1, source_target_pairs={{0,5},{1,4},{2,7},{3,6},{4,1},{5,0},{6,3},{7,2},{8,13},{9,12},{10,... | collective-permute-start | bytes 294920 | tf_op jit(solution)/shard_map/ppermute | solution.py:404
  78.9 2.4 %collective-permute-start.19 = (f32[3,64]{1,0:T(4,128)S(1)}, f32[3,64]{1,0:T(4,128)S(1)}, u32[]{:S(2)}, u32[]{:S(2)}) collective-permute-start(f32[3,64]{1,0:T(4,128)S(1)} %get-tuple-element.74.refs_2_), channel_id=1, source_target_pairs={{0,24},{8,16},{16,8},{24,0},{1,25},{9,17},{17,9},{25,1},{2,26},{10... | collective-permute-start | bytes 2312 | tf_op jit(solution)/shard_map/ppermute | solution.py:412
  81.4 0.5 collective-permute-start.18
  81.9 0.6 collective-permute-start.17
  82.4 1.2 %shard_map.128.refs_6_ = f32[6,512,128]{2,1,0:T(8,128)} custom-call(s32[1]{0:T(128)} %bitcast.me_ref, s32[8,512]{1,0:T(8,128)S(1)} %get-tuple-element.43.info_ref, f32[3,512,128]{2,1,0:T(8,128)S(1)} %get-tuple-element.71.solved_ref, f32[3,64,128]{2,1,0:T(8,128)S(1)} %get-tuple-element.75.refs_0_, f32[3,64,128]{2,1,0:T(8,128)S(1)} %collective-permute-done.14.refs_8_.refs_1_, ...), custom_call_target="tpu_custom_call" | custom-call | flops 10000000000 | bytes 10000000 | tf_op jit(solution)/shard_map/pallas_call | solution.py:513
  83.7 1.3 %collective-permute-done.18.refs_4_ = f32[3,64]{1,0:T(4,128)S(1)} collective-permute-done((f32[3,64]{1,0:T(4,128)S(1)}, f32[3,64]{1,0:T(4,128)S(1)}, u32[]{:S(2)}, u32[]{:S(2)}) %collective-permute-start.18) | collective-permute-done | bytes 800 | tf_op jit(solution)/shard_map/ppermute | solution.py:412
  85.0 0.5 collective-permute-done.17.refs_3_
  85.4 1.4 %shard_map.129 = (f32[6,512,128]{2,1,0:T(8,128)}, f32[3,64]{1,0:T(4,128)}) custom-call(s32[1]{0:T(128)} %bitcast.me_ref, s32[8,512]{1,0:T(8,128)S(1)} %get-tuple-element.43.info_ref, f32[3,512,128]{2,1,0:T(8,128)S(1)} %get-tuple-element.71.solved_ref, f32[3,64,128]{2,1,0:T(8,128)S(1)} %collective-permute-done.15.refs_0_, ...), custom_call_target="tpu_custom_call", output_to_operand_aliasing={{0}: (9, {})} | custom-call | flops 1000000000 | bytes 1000000 | tf_op jit(solution)/shard_map/pallas_call | solution.py:524
  (21 shorter events, 0.0 us)
Async XLA Ops:
  0.6 10.2 %copy-start = (f32[512,512]{1,0:T(8,128)S(1)}, f32[512,512]{1,0:T(8,128)}, u32[]{:S(2)}) copy-start(f32[512,512]{1,0:T(8,128)} %deriv_ref.1) | copy-start | bytes 3145732
  0.6 10.2 %copy-start.1 = (f32[512,512]{1,0:T(8,128)S(1)}, f32[512,512]{1,0:T(8,128)}, u32[]{:S(2)}) copy-start(f32[512,512]{1,0:T(8,128)} %inverse_ref.1) | copy-start | bytes 3145732
  0.7 10.2 %copy-start.2 = (f32[512,512]{1,0:T(8,128)S(1)}, f32[512,512]{1,0:T(8,128)}, u32[]{:S(2)}) copy-start(f32[512,512]{1,0:T(8,128)} %basis_ref.1) | copy-start | bytes 3145732
  0.7 10.2 %copy-start.5 = (f32[512]{0:T(512)S(1)}, f32[512]{0:T(512)}, u32[]{:S(2)}) copy-start(f32[512]{0:T(512)} %param.17) | copy-start | bytes 6148
  4.1 8.1 %collective-permute-start = (f32[2,3,64,128]{3,2,1,0:T(8,128)S(1)}, f32[2,3,64,128]{3,2,1,0:T(8,128)S(1)}, u32[]{:S(2)}, u32[]{:S(2)}) collective-permute-start(f32[2,3,64,128]{3,2,1,0:T(8,128)S(1)} %get-tuple-element.52), channel_id=1, source_target_pairs={{0,1},{1,0},{2,3},{3,2},{4,5},{5,4},{6,7},{7,6},{8,9},{9,8},{10,11... | collective-permute-start | bytes 589832 | tf_op jit(solution)/shard_map/ppermute | solution.py:404
  4.6 10.6 %collective-permute-start.1 = (f32[2,3,64,128]{3,2,1,0:T(8,128)S(1)}, f32[2,3,64,128]{3,2,1,0:T(8,128)S(1)}, u32[]{:S(2)}, u32[]{:S(2)}) collective-permute-start(f32[2,3,64,128]{3,2,1,0:T(8,128)S(1)} %get-tuple-element.53), channel_id=1, source_target_pairs={{0,6},{1,7},{2,4},{3,5},{4,2},{5,3},{6,0},{7,1},{8,14},{9,15},{10,... | collective-permute-start | bytes 589832 | tf_op jit(solution)/shard_map/ppermute | solution.py:404
  9.3 13.9 %collective-permute-start.2 = (f32[2,3,64,128]{3,2,1,0:T(8,128)S(1)}, f32[2,3,64,128]{3,2,1,0:T(8,128)S(1)}, u32[]{:S(2)}, u32[]{:S(2)}) collective-permute-start(f32[2,3,64,128]{3,2,1,0:T(8,128)S(1)} %get-tuple-element.54), channel_id=1, source_target_pairs={{0,7},{1,6},{2,5},{3,4},{4,3},{5,2},{6,1},{7,0},{8,15},{9,14},{10,... | collective-permute-start | bytes 589832 | tf_op jit(solution)/shard_map/ppermute | solution.py:404
  9.3 14.0 %collective-permute-start.3 = (f32[2,3,64,128]{3,2,1,0:T(8,128)S(1)}, f32[2,3,64,128]{3,2,1,0:T(8,128)S(1)}, u32[]{:S(2)}, u32[]{:S(2)}) collective-permute-start(f32[2,3,64,128]{3,2,1,0:T(8,128)S(1)} %get-tuple-element.55), channel_id=1, source_target_pairs={{0,2},{1,3},{2,0},{3,1},{4,6},{5,7},{6,4},{7,5},{8,10},{9,11},{10,... | collective-permute-start | bytes 589832 | tf_op jit(solution)/shard_map/ppermute | solution.py:404
  9.3 19.1 %collective-permute-start.4 = (f32[2,3,64,128]{3,2,1,0:T(8,128)S(1)}, f32[2,3,64,128]{3,2,1,0:T(8,128)S(1)}, u32[]{:S(2)}, u32[]{:S(2)}) collective-permute-start(f32[2,3,64,128]{3,2,1,0:T(8,128)S(1)} %get-tuple-element.56), channel_id=1, source_target_pairs={{0,3},{1,2},{2,1},{3,0},{4,7},{5,6},{6,5},{7,4},{8,11},{9,10},{10,... | collective-permute-start | bytes 589832 | tf_op jit(solution)/shard_map/ppermute | solution.py:404
  12.2 27.4 %collective-permute-start.5 = (f32[2,3,64,128]{3,2,1,0:T(8,128)S(1)}, f32[2,3,64,128]{3,2,1,0:T(8,128)S(1)}, u32[]{:S(2)}, u32[]{:S(2)}) collective-permute-start(f32[2,3,64,128]{3,2,1,0:T(8,128)S(1)} %get-tuple-element.57), channel_id=1, source_target_pairs={{0,4},{1,5},{2,6},{3,7},{4,0},{5,1},{6,2},{7,3},{8,12},{9,13},{10,... | collective-permute-start | bytes 589832 | tf_op jit(solution)/shard_map/ppermute | solution.py:404
  15.2 27.7 %collective-permute-start.6 = (f32[2,3,64,128]{3,2,1,0:T(8,128)S(1)}, f32[2,3,64,128]{3,2,1,0:T(8,128)S(1)}, u32[]{:S(2)}, u32[]{:S(2)}) collective-permute-start(f32[2,3,64,128]{3,2,1,0:T(8,128)S(1)} %get-tuple-element.58), channel_id=1, source_target_pairs={{0,5},{1,4},{2,7},{3,6},{4,1},{5,0},{6,3},{7,2},{8,13},{9,12},{10,... | collective-permute-start | bytes 589832 | tf_op jit(solution)/shard_map/ppermute | solution.py:404
  44.5 5.6 %collective-permute-start.7 = (f32[3,64,128]{2,1,0:T(8,128)S(1)}, f32[3,64,128]{2,1,0:T(8,128)S(1)}, u32[]{:S(2)}, u32[]{:S(2)}) collective-permute-start(f32[3,64,128]{2,1,0:T(8,128)S(1)} %get-tuple-element.60), channel_id=1, source_target_pairs={{0,1},{1,0},{2,3},{3,2},{4,5},{5,4},{6,7},{7,6},{8,9},{9,8},{10,11... | collective-permute-start | bytes 294920 | tf_op jit(solution)/shard_map/ppermute | solution.py:404
  44.8 6.9 %collective-permute-start.8 = (f32[3,64,128]{2,1,0:T(8,128)S(1)}, f32[3,64,128]{2,1,0:T(8,128)S(1)}, u32[]{:S(2)}, u32[]{:S(2)}) collective-permute-start(f32[3,64,128]{2,1,0:T(8,128)S(1)} %get-tuple-element.61), channel_id=1, source_target_pairs={{0,6},{1,7},{2,4},{3,5},{4,2},{5,3},{6,0},{7,1},{8,14},{9,15},{10,... | collective-permute-start | bytes 294920 | tf_op jit(solution)/shard_map/ppermute | solution.py:404
  47.4 6.9 %collective-permute-start.9 = (f32[3,64,128]{2,1,0:T(8,128)S(1)}, f32[3,64,128]{2,1,0:T(8,128)S(1)}, u32[]{:S(2)}, u32[]{:S(2)}) collective-permute-start(f32[3,64,128]{2,1,0:T(8,128)S(1)} %get-tuple-element.62), channel_id=1, source_target_pairs={{0,7},{1,6},{2,5},{3,4},{4,3},{5,2},{6,1},{7,0},{8,15},{9,14},{10,... | collective-permute-start | bytes 294920 | tf_op jit(solution)/shard_map/ppermute | solution.py:404
  48.2 10.6 %collective-permute-start.10 = (f32[3,64,128]{2,1,0:T(8,128)S(1)}, f32[3,64,128]{2,1,0:T(8,128)S(1)}, u32[]{:S(2)}, u32[]{:S(2)}) collective-permute-start(f32[3,64,128]{2,1,0:T(8,128)S(1)} %get-tuple-element.63), channel_id=1, source_target_pairs={{0,2},{1,3},{2,0},{3,1},{4,6},{5,7},{6,4},{7,5},{8,10},{9,11},{10,... | collective-permute-start | bytes 294920 | tf_op jit(solution)/shard_map/ppermute | solution.py:404
  48.2 12.5 %collective-permute-start.11 = (f32[3,64,128]{2,1,0:T(8,128)S(1)}, f32[3,64,128]{2,1,0:T(8,128)S(1)}, u32[]{:S(2)}, u32[]{:S(2)}) collective-permute-start(f32[3,64,128]{2,1,0:T(8,128)S(1)} %get-tuple-element.64), channel_id=1, source_target_pairs={{0,3},{1,2},{2,1},{3,0},{4,7},{5,6},{6,5},{7,4},{8,11},{9,10},{10,... | collective-permute-start | bytes 294920 | tf_op jit(solution)/shard_map/ppermute | solution.py:404
  50.1 11.6 %collective-permute-start.12 = (f32[3,64,128]{2,1,0:T(8,128)S(1)}, f32[3,64,128]{2,1,0:T(8,128)S(1)}, u32[]{:S(2)}, u32[]{:S(2)}) collective-permute-start(f32[3,64,128]{2,1,0:T(8,128)S(1)} %get-tuple-element.65), channel_id=1, source_target_pairs={{0,4},{1,5},{2,6},{3,7},{4,0},{5,1},{6,2},{7,3},{8,12},{9,13},{10,... | collective-permute-start | bytes 294920 | tf_op jit(solution)/shard_map/ppermute | solution.py:404
  51.7 12.0 %collective-permute-start.13 = (f32[3,64,128]{2,1,0:T(8,128)S(1)}, f32[3,64,128]{2,1,0:T(8,128)S(1)}, u32[]{:S(2)}, u32[]{:S(2)}) collective-permute-start(f32[3,64,128]{2,1,0:T(8,128)S(1)} %get-tuple-element.66), channel_id=1, source_target_pairs={{0,5},{1,4},{2,7},{3,6},{4,1},{5,0},{6,3},{7,2},{8,13},{9,12},{10,... | collective-permute-start | bytes 294920 | tf_op jit(solution)/shard_map/ppermute | solution.py:404
  63.7 6.5 %copy-start.3 = (f32[6,64,512]{2,1,0:T(8,128)S(1)}, f32[6,64,512]{2,1,0:T(8,128)}, u32[]{:S(2)}) copy-start(f32[6,64,512]{2,1,0:T(8,128)} %velocity_ref.1) | copy-start | bytes 2359300
  63.7 6.5 %copy-start.4 = (s32[2,512]{1,0:T(2,128)S(1)}, s32[2,512]{1,0:T(2,128)}, u32[]{:S(2)}) copy-start(s32[2,512]{1,0:T(2,128)} %modes_ref.1) | copy-start | bytes 12292
  64.3 4.1 %collective-permute-start.14 = (f32[3,64,128]{2,1,0:T(8,128)S(1)}, f32[3,64,128]{2,1,0:T(8,128)S(1)}, u32[]{:S(2)}, u32[]{:S(2)}) collective-permute-start(f32[3,64,128]{2,1,0:T(8,128)S(1)} %get-tuple-element.69), channel_id=1, source_target_pairs={{0,1},{1,0},{2,3},{3,2},{4,5},{5,4},{6,7},{7,6},{8,9},{9,8},{10,11... | collective-permute-start | bytes 294920 | tf_op jit(solution)/shard_map/ppermute | solution.py:404
  64.7 19.0 %collective-permute-start.15 = (f32[3,64,128]{2,1,0:T(8,128)S(1)}, f32[3,64,128]{2,1,0:T(8,128)S(1)}, u32[]{:S(2)}, u32[]{:S(2)}) collective-permute-start(f32[3,64,128]{2,1,0:T(8,128)S(1)} %get-tuple-element.72), channel_id=1, source_target_pairs={{0,4},{1,5},{2,6},{3,7},{4,0},{5,1},{6,2},{7,3},{8,12},{9,13},{10,... | collective-permute-start | bytes 294920 | tf_op jit(solution)/shard_map/ppermute | solution.py:404
  64.7 7.6 %collective-permute-start.20 = (f32[3,64,128]{2,1,0:T(8,128)S(1)}, f32[3,64,128]{2,1,0:T(8,128)S(1)}, u32[]{:S(2)}, u32[]{:S(2)}) collective-permute-start(f32[3,64,128]{2,1,0:T(8,128)S(1)} %get-tuple-element.76), channel_id=1, source_target_pairs={{0,6},{1,7},{2,4},{3,5},{4,2},{5,3},{6,0},{7,1},{8,14},{9,15},{10,... | collective-permute-start | bytes 294920 | tf_op jit(solution)/shard_map/ppermute | solution.py:404
  66.4 12.6 %collective-permute-start.21 = (f32[3,64,128]{2,1,0:T(8,128)S(1)}, f32[3,64,128]{2,1,0:T(8,128)S(1)}, u32[]{:S(2)}, u32[]{:S(2)}) collective-permute-start(f32[3,64,128]{2,1,0:T(8,128)S(1)} %get-tuple-element.77), channel_id=1, source_target_pairs={{0,7},{1,6},{2,5},{3,4},{4,3},{5,2},{6,1},{7,0},{8,15},{9,14},{10,... | collective-permute-start | bytes 294920 | tf_op jit(solution)/shard_map/ppermute | solution.py:404
  68.0 13.3 %collective-permute-start.23 = (f32[3,64,128]{2,1,0:T(8,128)S(1)}, f32[3,64,128]{2,1,0:T(8,128)S(1)}, u32[]{:S(2)}, u32[]{:S(2)}) collective-permute-start(f32[3,64,128]{2,1,0:T(8,128)S(1)} %get-tuple-element.80), channel_id=1, source_target_pairs={{0,3},{1,2},{2,1},{3,0},{4,7},{5,6},{6,5},{7,4},{8,11},{9,10},{10,... | collective-permute-start | bytes 294920 | tf_op jit(solution)/shard_map/ppermute | solution.py:404
  68.4 13.5 %collective-permute-start.22 = (f32[3,64,128]{2,1,0:T(8,128)S(1)}, f32[3,64,128]{2,1,0:T(8,128)S(1)}, u32[]{:S(2)}, u32[]{:S(2)}) collective-permute-start(f32[3,64,128]{2,1,0:T(8,128)S(1)} %get-tuple-element.79), channel_id=1, source_target_pairs={{0,2},{1,3},{2,0},{3,1},{4,6},{5,7},{6,4},{7,5},{8,10},{9,11},{10,... | collective-permute-start | bytes 294920 | tf_op jit(solution)/shard_map/ppermute | solution.py:404
  72.2 11.4 %collective-permute-start.16 = (f32[3,64,128]{2,1,0:T(8,128)S(1)}, f32[3,64,128]{2,1,0:T(8,128)S(1)}, u32[]{:S(2)}, u32[]{:S(2)}) collective-permute-start(f32[3,64,128]{2,1,0:T(8,128)S(1)} %get-tuple-element.73), channel_id=1, source_target_pairs={{0,5},{1,4},{2,7},{3,6},{4,1},{5,0},{6,3},{7,2},{8,13},{9,12},{10,... | collective-permute-start | bytes 294920 | tf_op jit(solution)/shard_map/ppermute | solution.py:404
  78.9 4.8 %collective-permute-start.19 = (f32[3,64]{1,0:T(4,128)S(1)}, f32[3,64]{1,0:T(4,128)S(1)}, u32[]{:S(2)}, u32[]{:S(2)}) collective-permute-start(f32[3,64]{1,0:T(4,128)S(1)} %get-tuple-element.74.refs_2_), channel_id=1, source_target_pairs={{0,24},{8,16},{16,8},{24,0},{1,25},{9,17},{17,9},{25,1},{2,26},{10... | collective-permute-start | bytes 2312 | tf_op jit(solution)/shard_map/ppermute | solution.py:412
  81.4 3.6 %collective-permute-start.18 = (f32[3,64]{1,0:T(4,128)S(1)}, f32[3,64]{1,0:T(4,128)S(1)}, u32[]{:S(2)}, u32[]{:S(2)}) collective-permute-start(f32[3,64]{1,0:T(4,128)S(1)} %get-tuple-element.74.refs_2_), channel_id=1, source_target_pairs={{0,16},{8,24},{16,0},{24,8},{1,17},{9,25},{17,1},{25,9},{2,18},{10... | collective-permute-start | bytes 2312 | tf_op jit(solution)/shard_map/ppermute | solution.py:412
  81.9 3.6 %collective-permute-start.17 = (f32[3,64]{1,0:T(4,128)S(1)}, f32[3,64]{1,0:T(4,128)S(1)}, u32[]{:S(2)}, u32[]{:S(2)}) collective-permute-start(f32[3,64]{1,0:T(4,128)S(1)} %get-tuple-element.74.refs_2_), channel_id=1, source_target_pairs={{0,8},{8,0},{16,24},{24,16},{1,9},{9,1},{17,25},{25,17},{2,10},{10... | collective-permute-start | bytes 2312 | tf_op jit(solution)/shard_map/ppermute | solution.py:412
